TPU v7x, 512 devices: a whole 4x4x16 slice. The times are simulated.
512 devices in a mesh: leaf: 128 (over y, z, core), col: 4 (over x).
Axes of the slice: x: 4, y: 4, z: 16, core: 2. Of those that a mesh axis runs over, the one named last changes fastest.
Arguments:
- leaf_rhs: float32 [114688, 512], P('leaf', 'col'), may hold values from -6 to 6
- leaf_inverse: float32 [896, 128, 128], P('leaf'), may hold values from -0.5 to 0.5
- leaf_blocks: float32 [2688, 128, 128], P('leaf'), may hold values from -0.1875 to 0.1875
- leaf_pattern: int32 [128, 21], P('leaf'), may hold values 0 or 1
- leaf_coupling: float32 [65536, 512], P('leaf'), may hold values from -0.0625 to 0.0625
- sep_rhs: float32 [22016, 512], P('leaf', 'col'), may hold values from -6 to 6
- sep_inverse: float32 [22016, 512], P('leaf', 'col'), may hold values from -0.25 to 0.25
- sep_coupling: float32 [21504, 512], P('leaf', 'col'), may hold values from -0.09375 to 0.09375
Outputs:
- leaf_solution: float32 [114688, 512], P('leaf', 'col')
- sep_solution: float32 [22016, 512], P('leaf', 'col')
Inputs may be any that keep to these rules, and one draw needn't show every extreme that they name: `leaf_pattern`: 1 where a factor block below the diagonal is nonzero, 0 where it is zero.
All inputs are finite; a program needn't handle non-finite values.
Results may differ from a plain program's by a relative error of at most 0.00011.
Values sent between devices are 32-bit elements; how exact they have to be, the bound alone decides.
No kernel may reach another device: no remote copies, remote signals or barrier semaphores. Data moves between devices by JAX's collectives and lax.ppermute only.
A program may use at most 64 MiB of HBM per device.

v0:
```python
import jax
import jax.numpy as jnp
from jax import lax
from jax.sharding import PartitionSpec as P

HIGH = lax.Precision.HIGHEST


def from_partner(shard, axis, apart):
    return lax.ppermute(shard, axis, [(i, i ^ 1 << apart) for i in range(lax.axis_size(axis))])


def product(left_side, right_side):
    return jnp.dot(left_side, right_side, precision=HIGH, preferred_element_type=jnp.float32)


def product_first(left_side, right_side):
    return lax.dot_general(
        left_side,
        right_side,
        (((0,), (0,)), ((), ())),
        precision=HIGH,
        preferred_element_type=jnp.float32,
    )


def group_sizes(leaf_count):
    result = []
    for level_index in range(1, 5):
        group_span = 4**level_index
        result.append(min(group_span, leaf_count))
    return result


def group_total(partial_value, group_size):
    bit_count = group_size.bit_length() - 1
    for bit_place in range(bit_count):
        partial_value = partial_value + from_partner(partial_value, "leaf", bit_place)
    return partial_value


def shards(
    leaf_rhs,
    leaf_inverse,
    leaf_blocks,
    leaf_pattern,
    leaf_coupling,
    sep_rhs,
    sep_inverse,
    sep_coupling,
):
    inverse_full, coupling_full = (
        lax.all_gather(sep_inverse, "col", axis=1, tiled=True),
        lax.all_gather(sep_coupling, "col", axis=1, tiled=True),
    )
    leaf_count = lax.axis_size("leaf")
    position = lax.axis_index("leaf")
    block_count = leaf_inverse.shape[0]
    block_rows = leaf_inverse.shape[1]
    columns = leaf_rhs.shape[1]
    sep_rows = inverse_full.shape[1]
    weighted = leaf_blocks * leaf_pattern[0].astype(jnp.float32)[:, None, None]
    rhs_blocks = leaf_rhs.reshape(block_count, block_rows, columns)
    column_starts = []
    running = 0
    for column_index in range(block_count):
        column_starts.append(running)
        running = running + block_count - 1 - column_index
    pending = [rhs_blocks[i] for i in range(block_count)]
    forward = []
    for column_index in range(block_count):
        solved = product(leaf_inverse[column_index], pending[column_index])
        forward.append(solved)
        below_count = block_count - 1 - column_index
        if below_count:
            pair_start = column_starts[column_index]
            column_blocks = weighted[pair_start : pair_start + below_count].reshape(
                below_count * block_rows, block_rows
            )
            update = product(column_blocks, solved).reshape(below_count, block_rows, columns)
            for later_index in range(below_count):
                pending[column_index + 1 + later_index] = (
                    pending[column_index + 1 + later_index] - update[later_index]
                )
    sizes_list = group_sizes(leaf_count)
    level_total = len(sizes_list)
    row_counts = [sep_rows // size_item for size_item in sizes_list]
    offsets = []
    running = 0
    for row_count in row_counts:
        offsets.append(running)
        running = running + row_count
    last_block = forward[-1]
    level_pieces = []
    for level_index in range(level_total):
        group_size = sizes_list[level_index]
        row_count = row_counts[level_index]
        row_offset = offsets[level_index]
        row_start = position % group_size * row_count
        coupling_rows = leaf_coupling[level_index * block_rows : (level_index + 1) * block_rows]
        partial_value = -product_first(coupling_rows, last_block)
        if level_index > 0:
            child_offset = offsets[level_index - 1]
            child_count = row_counts[level_index - 1]
            partial_value = partial_value - product_first(
                coupling_full[child_offset : child_offset + child_count], level_pieces[-1]
            )
        own_rows = (
            lax.dynamic_slice_in_dim(partial_value, row_start, row_count, 0)
            + sep_rhs[row_offset : row_offset + row_count]
        )
        partial_value = lax.dynamic_update_slice_in_dim(partial_value, own_rows, row_start, 0)
        summed = group_total(partial_value, group_size)
        level_pieces.append(product(inverse_full[row_offset : row_offset + row_count], summed))
    correction = jnp.zeros((block_rows, columns), jnp.float32)
    solution_pieces = [None] * level_total
    parent_full = None
    for level_index in reversed(range(level_total)):
        group_size = sizes_list[level_index]
        row_count = row_counts[level_index]
        row_offset = offsets[level_index]
        row_start = position % group_size * row_count
        target = level_pieces[level_index]
        if parent_full is not None:
            target = target - product(
                coupling_full[row_offset : row_offset + row_count], parent_full
            )
        partial_value = product_first(inverse_full[row_offset : row_offset + row_count], target)
        parent_full = group_total(partial_value, group_size)
        solution_pieces[level_index] = lax.dynamic_slice_in_dim(
            parent_full, row_start, row_count, 0
        )
        correction = correction + product(
            leaf_coupling[level_index * block_rows : (level_index + 1) * block_rows], parent_full
        )
    pending = list(forward)
    pending[-1] = pending[-1] - correction
    backward = [None] * block_count
    for column_index in reversed(range(block_count)):
        target = pending[column_index]
        below_count = block_count - 1 - column_index
        if below_count:
            pair_start = column_starts[column_index]
            column_blocks = weighted[pair_start : pair_start + below_count].reshape(
                below_count * block_rows, block_rows
            )
            later_blocks = jnp.concatenate(backward[column_index + 1 :], 0)
            target = target - product_first(column_blocks, later_blocks)
        backward[column_index] = product_first(leaf_inverse[column_index], target)
    return (jnp.concatenate(backward, 0), jnp.concatenate(solution_pieces, 0))


def solution(mesh):
    return jax.shard_map(
        shards,
        mesh=mesh,
        in_specs=(
            P("leaf", "col"),
            P("leaf", None, None),
            P("leaf", None, None),
            P("leaf", None),
            P("leaf", None),
            P("leaf", "col"),
            P("leaf", "col"),
            P("leaf", "col"),
        ),
        out_specs=(P("leaf", "col"), P("leaf", "col")),
        check_vma=False,
    )
```

profile of v0, /device:TPU:1, one launch (start us, length us, event | category | flops | bytes accessed | tf_op | source)
XLA Modules:
  0.0 635.7 jit_solution(7210796794714294757)
XLA Ops:
  15.1 8.8 %collective-permute-start = (f32[512,128]{0,1:T(8,128)S(1)}, f32[512,128]{0,1:T(8,128)S(1)}, u32[]{:S(2)}, u32[]{:S(2)}) collective-permute-start(f32[512,128]{0,1:T(8,128)S(1)} %fusion.47), channel_id=1, source_target_pairs={{0,4},{4,0},{8,12},{12,8},{16,20},{20,16},{24,28},{28,24},{32,36},... | collective-permute-start | bytes 786440 | tf_op jit(solution)/shard_map/ppermute | solution.py:10
  23.9 10.2 %all_gather.6 = f32[172,512]{1,0:T(8,128)S(1)} all-gather(f32[172,128]{1,0:T(8,128)} %param.14), channel_id=1, replica_groups=mesh['leaf'=128,'col'=4] {'col'}, dimensions={1}, use_global_device_ids=true | all-gather | bytes 440320 | tf_op jit(solution)/shard_map/all_gather | solution.py:53
  36.7 10.1 %all_gather.7 = f32[168,512]{1,0:T(8,128)S(1)} all-gather(f32[168,128]{1,0:T(8,128)S(1)} %copy-done.30), channel_id=1, replica_groups=mesh['leaf'=128,'col'=4] {'col'}, dimensions={1}, use_global_device_ids=true | all-gather | bytes 430080 | tf_op jit(solution)/shard_map/all_gather | solution.py:54
  53.8 6.8 %collective-permute-start.2 = (f32[512,128]{0,1:T(8,128)}, f32[512,128]{0,1:T(8,128)S(1)}, u32[]{:S(2)}, u32[]{:S(2)}) collective-permute-start(f32[512,128]{0,1:T(8,128)} %dynamic_update_slice.13), channel_id=1, source_target_pairs={{0,4},{4,0},{8,12},{12,8},{16,20},{20,16},{24,28},{28,24},{32,36},... | collective-permute-start | bytes 786440 | tf_op jit(solution)/shard_map/ppermute | solution.py:10
  66.7 6.4 %collective-permute-done.3 = f32[512,128]{0,1:T(8,128)S(1)} collective-permute-done((f32[512,128]{0,1:T(8,128)S(1)}, f32[512,128]{0,1:T(8,128)S(1)}, u32[]{:S(2)}, u32[]{:S(2)}) %collective-permute-start.3) | collective-permute-done | bytes 262176 | tf_op jit(solution)/shard_map/ppermute | solution.py:10
  75.1 13.8 %collective-permute-done.4 = f32[512,128]{0,1:T(8,128)S(1)} collective-permute-done((f32[512,128]{0,1:T(8,128)S(1)}, f32[512,128]{0,1:T(8,128)S(1)}, u32[]{:S(2)}, u32[]{:S(2)}) %collective-permute-start.4) | collective-permute-done | bytes 262176 | tf_op jit(solution)/shard_map/ppermute | solution.py:10
  98.0 21.5 %collective-permute-done.5 = f32[512,128]{0,1:T(8,128)} collective-permute-done((f32[512,128]{0,1:T(8,128)}, f32[512,128]{0,1:T(8,128)}, u32[]{:S(2)}, u32[]{:S(2)}) %collective-permute-start.5) | collective-permute-done | bytes 262176 | tf_op jit(solution)/shard_map/ppermute | solution.py:10
  131.8 7.5 %collective-permute-done.7 = f32[512,128]{0,1:T(8,128)S(1)} collective-permute-done((f32[512,128]{0,1:T(8,128)S(1)}, f32[512,128]{0,1:T(8,128)S(1)}, u32[]{:S(2)}, u32[]{:S(2)}) %collective-permute-start.7) | collective-permute-done | bytes 262176 | tf_op jit(solution)/shard_map/ppermute | solution.py:10
  141.3 14.7 %collective-permute-done.8 = f32[512,128]{0,1:T(8,128)S(1)} collective-permute-done((f32[512,128]{0,1:T(8,128)S(1)}, f32[512,128]{0,1:T(8,128)S(1)}, u32[]{:S(2)}, u32[]{:S(2)}) %collective-permute-start.8) | collective-permute-done | bytes 262176 | tf_op jit(solution)/shard_map/ppermute | solution.py:10
  160.0 24.5 %collective-permute-done.9 = f32[512,128]{0,1:T(8,128)S(1)} collective-permute-done((f32[512,128]{0,1:T(8,128)S(1)}, f32[512,128]{0,1:T(8,128)S(1)}, u32[]{:S(2)}, u32[]{:S(2)}) %collective-permute-start.9) | collective-permute-done | bytes 262176 | tf_op jit(solution)/shard_map/ppermute | solution.py:10
  184.5 15.6 %collective-permute-start.10 = (f32[512,128]{0,1:T(8,128)S(1)}, f32[512,128]{0,1:T(8,128)S(1)}, u32[]{:S(2)}, u32[]{:S(2)}) collective-permute-start(f32[512,128]{0,1:T(8,128)S(1)} %add.193), channel_id=1, source_target_pairs={{0,64},{4,68},{8,72},{12,76},{16,80},{20,84},{24,88},{28,92},{32,9... | collective-permute-start | bytes 786440 | tf_op jit(solution)/shard_map/ppermute | solution.py:10
  200.1 17.2 %collective-permute-done.10 = f32[512,128]{0,1:T(8,128)S(1)} collective-permute-done((f32[512,128]{0,1:T(8,128)S(1)}, f32[512,128]{0,1:T(8,128)S(1)}, u32[]{:S(2)}, u32[]{:S(2)}) %collective-permute-start.10) | collective-permute-done | bytes 262176 | tf_op jit(solution)/shard_map/ppermute | solution.py:10
  239.9 7.5 %collective-permute-done.13 = f32[512,128]{0,1:T(8,128)S(1)} collective-permute-done((f32[512,128]{0,1:T(8,128)S(1)}, f32[512,128]{0,1:T(8,128)S(1)}, u32[]{:S(2)}, u32[]{:S(2)}) %collective-permute-start.13) | collective-permute-done | bytes 262176 | tf_op jit(solution)/shard_map/ppermute | solution.py:10
  249.4 14.7 %collective-permute-done.14 = f32[512,128]{0,1:T(8,128)S(1)} collective-permute-done((f32[512,128]{0,1:T(8,128)S(1)}, f32[512,128]{0,1:T(8,128)S(1)}, u32[]{:S(2)}, u32[]{:S(2)}) %collective-permute-start.14) | collective-permute-done | bytes 262176 | tf_op jit(solution)/shard_map/ppermute | solution.py:10
  266.0 25.1 %collective-permute-done.15 = f32[512,128]{0,1:T(8,128)S(1)} collective-permute-done((f32[512,128]{0,1:T(8,128)S(1)}, f32[512,128]{0,1:T(8,128)S(1)}, u32[]{:S(2)}, u32[]{:S(2)}) %collective-permute-start.15) | collective-permute-done | bytes 262176 | tf_op jit(solution)/shard_map/ppermute | solution.py:10
  291.1 13.5 %collective-permute-start.16 = (f32[512,128]{0,1:T(8,128)S(1)}, f32[512,128]{0,1:T(8,128)S(1)}, u32[]{:S(2)}, u32[]{:S(2)}) collective-permute-start(f32[512,128]{0,1:T(8,128)S(1)} %add.202), channel_id=1, source_target_pairs={{0,64},{4,68},{8,72},{12,76},{16,80},{20,84},{24,88},{28,92},{32,9... | collective-permute-start | bytes 786440 | tf_op jit(solution)/shard_map/ppermute | solution.py:10
  304.7 11.3 %collective-permute-done.16 = f32[512,128]{0,1:T(8,128)S(1)} collective-permute-done((f32[512,128]{0,1:T(8,128)S(1)}, f32[512,128]{0,1:T(8,128)S(1)}, u32[]{:S(2)}, u32[]{:S(2)}) %collective-permute-start.16) | collective-permute-done | bytes 262176 | tf_op jit(solution)/shard_map/ppermute | solution.py:10
  343.0 7.5 %collective-permute-done.20 = f32[512,128]{0,1:T(8,128)S(1)} collective-permute-done((f32[512,128]{0,1:T(8,128)S(1)}, f32[512,128]{0,1:T(8,128)S(1)}, u32[]{:S(2)}, u32[]{:S(2)}) %collective-permute-start.20) | collective-permute-done | bytes 262176 | tf_op jit(solution)/shard_map/ppermute | solution.py:10
  353.9 13.2 %collective-permute-done.21 = f32[512,128]{0,1:T(8,128)S(1)} collective-permute-done((f32[512,128]{0,1:T(8,128)S(1)}, f32[512,128]{0,1:T(8,128)S(1)}, u32[]{:S(2)}, u32[]{:S(2)}) %collective-permute-start.21) | collective-permute-done | bytes 262176 | tf_op jit(solution)/shard_map/ppermute | solution.py:10
  367.1 8.6 %collective-permute-start.22 = (f32[512,128]{0,1:T(8,128)S(1)}, f32[512,128]{0,1:T(8,128)S(1)}, u32[]{:S(2)}, u32[]{:S(2)}) collective-permute-start(f32[512,128]{0,1:T(8,128)S(1)} %add.208), channel_id=1, source_target_pairs={{0,32},{4,36},{8,40},{12,44},{16,48},{20,52},{24,56},{28,60},{32,0... | collective-permute-start | bytes 786440 | tf_op jit(solution)/shard_map/ppermute | solution.py:10
  375.8 22.6 %collective-permute-done.22 = f32[512,128]{0,1:T(8,128)S(1)} collective-permute-done((f32[512,128]{0,1:T(8,128)S(1)}, f32[512,128]{0,1:T(8,128)S(1)}, u32[]{:S(2)}, u32[]{:S(2)}) %collective-permute-start.22) | collective-permute-done | bytes 262176 | tf_op jit(solution)/shard_map/ppermute | solution.py:10
  398.4 7.8 %collective-permute-start.23 = (f32[512,128]{0,1:T(8,128)S(1)}, f32[512,128]{0,1:T(8,128)S(1)}, u32[]{:S(2)}, u32[]{:S(2)}) collective-permute-start(f32[512,128]{0,1:T(8,128)S(1)} %add.209), channel_id=1, source_target_pairs={{0,64},{4,68},{8,72},{12,76},{16,80},{20,84},{24,88},{28,92},{32,9... | collective-permute-start | bytes 786440 | tf_op jit(solution)/shard_map/ppermute | solution.py:10
  406.2 25.2 %collective-permute-done.23 = f32[512,128]{0,1:T(8,128)S(1)} collective-permute-done((f32[512,128]{0,1:T(8,128)S(1)}, f32[512,128]{0,1:T(8,128)S(1)}, u32[]{:S(2)}, u32[]{:S(2)}) %collective-permute-start.23) | collective-permute-done | bytes 262176 | tf_op jit(solution)/shard_map/ppermute | solution.py:10
  458.6 7.5 %collective-permute-done.27 = f32[512,128]{0,1:T(8,128)S(1)} collective-permute-done((f32[512,128]{0,1:T(8,128)S(1)}, f32[512,128]{0,1:T(8,128)S(1)}, u32[]{:S(2)}, u32[]{:S(2)}) %collective-permute-start.27) | collective-permute-done | bytes 262176 | tf_op jit(solution)/shard_map/ppermute | solution.py:10
  468.1 14.7 %collective-permute-done.28 = f32[512,128]{0,1:T(8,128)S(1)} collective-permute-done((f32[512,128]{0,1:T(8,128)S(1)}, f32[512,128]{0,1:T(8,128)S(1)}, u32[]{:S(2)}, u32[]{:S(2)}) %collective-permute-start.28) | collective-permute-done | bytes 262176 | tf_op jit(solution)/shard_map/ppermute | solution.py:10
  484.7 25.1 %collective-permute-done.29 = f32[512,128]{0,1:T(8,128)S(1)} collective-permute-done((f32[512,128]{0,1:T(8,128)S(1)}, f32[512,128]{0,1:T(8,128)S(1)}, u32[]{:S(2)}, u32[]{:S(2)}) %collective-permute-start.29) | collective-permute-done | bytes 262176 | tf_op jit(solution)/shard_map/ppermute | solution.py:10
  509.9 13.3 %collective-permute-start.30 = (f32[512,128]{0,1:T(8,128)S(1)}, f32[512,128]{0,1:T(8,128)S(1)}, u32[]{:S(2)}, u32[]{:S(2)}) collective-permute-start(f32[512,128]{0,1:T(8,128)S(1)} %add.216), channel_id=1, source_target_pairs={{0,64},{4,68},{8,72},{12,76},{16,80},{20,84},{24,88},{28,92},{32,9... | collective-permute-start | bytes 786440 | tf_op jit(solution)/shard_map/ppermute | solution.py:10
  523.2 13.9 %collective-permute-done.30 = f32[512,128]{0,1:T(8,128)S(1)} collective-permute-done((f32[512,128]{0,1:T(8,128)S(1)}, f32[512,128]{0,1:T(8,128)S(1)}, u32[]{:S(2)}, u32[]{:S(2)}) %collective-permute-start.30) | collective-permute-done | bytes 262176 | tf_op jit(solution)/shard_map/ppermute | solution.py:10
  553.7 7.5 %collective-permute-done.33 = f32[512,128]{0,1:T(8,128)S(1)} collective-permute-done((f32[512,128]{0,1:T(8,128)S(1)}, f32[512,128]{0,1:T(8,128)S(1)}, u32[]{:S(2)}, u32[]{:S(2)}) %collective-permute-start.33) | collective-permute-done | bytes 262176 | tf_op jit(solution)/shard_map/ppermute | solution.py:10
  563.2 14.7 %collective-permute-done.34 = f32[512,128]{0,1:T(8,128)S(1)} collective-permute-done((f32[512,128]{0,1:T(8,128)S(1)}, f32[512,128]{0,1:T(8,128)S(1)}, u32[]{:S(2)}, u32[]{:S(2)}) %collective-permute-start.34) | collective-permute-done | bytes 262176 | tf_op jit(solution)/shard_map/ppermute | solution.py:10
  583.7 24.1 %collective-permute-done.35 = f32[512,128]{0,1:T(8,128)S(1)} collective-permute-done((f32[512,128]{0,1:T(8,128)S(1)}, f32[512,128]{0,1:T(8,128)S(1)}, u32[]{:S(2)}, u32[]{:S(2)}) %collective-permute-start.35) | collective-permute-done | bytes 262176 | tf_op jit(solution)/shard_map/ppermute | solution.py:10
  615.2 6.4 %collective-permute-done.37 = f32[512,128]{0,1:T(8,128)S(1)} collective-permute-done((f32[512,128]{0,1:T(8,128)S(1)}, f32[512,128]{0,1:T(8,128)S(1)}, u32[]{:S(2)}, u32[]{:S(2)}) %collective-permute-start.37) | collective-permute-done | bytes 262176 | tf_op jit(solution)/shard_map/ppermute | solution.py:10
  (239 shorter events, 192.7 us)
Async XLA Ops:
  15.1 19.0 %collective-permute-start = (f32[512,128]{0,1:T(8,128)S(1)}, f32[512,128]{0,1:T(8,128)S(1)}, u32[]{:S(2)}, u32[]{:S(2)}) collective-permute-start(f32[512,128]{0,1:T(8,128)S(1)} %fusion.47), channel_id=1, source_target_pairs={{0,4},{4,0},{8,12},{12,8},{16,20},{20,16},{24,28},{28,24},{32,36},... | collective-permute-start | bytes 786440 | tf_op jit(solution)/shard_map/ppermute | solution.py:10
  34.8 14.0 %collective-permute-start.1 = (f32[512,128]{0,1:T(8,128)}, f32[512,128]{0,1:T(8,128)}, u32[]{:S(2)}, u32[]{:S(2)}) collective-permute-start(f32[512,128]{0,1:T(8,128)} %add.178), channel_id=1, source_target_pairs={{0,8},{4,12},{8,0},{12,4},{16,24},{20,28},{24,16},{28,20},{32,40},... | collective-permute-start | bytes 786440 | tf_op jit(solution)/shard_map/ppermute | solution.py:10
  53.8 8.2 %collective-permute-start.2 = (f32[512,128]{0,1:T(8,128)}, f32[512,128]{0,1:T(8,128)S(1)}, u32[]{:S(2)}, u32[]{:S(2)}) collective-permute-start(f32[512,128]{0,1:T(8,128)} %dynamic_update_slice.13), channel_id=1, source_target_pairs={{0,4},{4,0},{8,12},{12,8},{16,20},{20,16},{24,28},{28,24},{32,36},... | collective-permute-start | bytes 786440 | tf_op jit(solution)/shard_map/ppermute | solution.py:10
  62.9 10.2 %collective-permute-start.3 = (f32[512,128]{0,1:T(8,128)S(1)}, f32[512,128]{0,1:T(8,128)S(1)}, u32[]{:S(2)}, u32[]{:S(2)}) collective-permute-start(f32[512,128]{0,1:T(8,128)S(1)} %add.183), channel_id=1, source_target_pairs={{0,8},{4,12},{8,0},{12,4},{16,24},{20,28},{24,16},{28,20},{32,40},... | collective-permute-start | bytes 786440 | tf_op jit(solution)/shard_map/ppermute | solution.py:10
  73.1 15.7 %collective-permute-start.4 = (f32[512,128]{0,1:T(8,128)S(1)}, f32[512,128]{0,1:T(8,128)S(1)}, u32[]{:S(2)}, u32[]{:S(2)}) collective-permute-start(f32[512,128]{0,1:T(8,128)S(1)} %add.184), channel_id=1, source_target_pairs={{0,16},{4,20},{8,24},{12,28},{16,0},{20,4},{24,8},{28,12},{32,48},... | collective-permute-start | bytes 786440 | tf_op jit(solution)/shard_map/ppermute | solution.py:10
  89.6 29.8 %collective-permute-start.5 = (f32[512,128]{0,1:T(8,128)}, f32[512,128]{0,1:T(8,128)}, u32[]{:S(2)}, u32[]{:S(2)}) collective-permute-start(f32[512,128]{0,1:T(8,128)} %add.185), channel_id=1, source_target_pairs={{0,32},{4,36},{8,40},{12,44},{16,48},{20,52},{24,56},{28,60},{32,0... | collective-permute-start | bytes 786440 | tf_op jit(solution)/shard_map/ppermute | solution.py:10
  129.9 9.5 %collective-permute-start.7 = (f32[512,128]{0,1:T(8,128)S(1)}, f32[512,128]{0,1:T(8,128)S(1)}, u32[]{:S(2)}, u32[]{:S(2)}) collective-permute-start(f32[512,128]{0,1:T(8,128)S(1)} %add.190), channel_id=1, source_target_pairs={{0,8},{4,12},{8,0},{12,4},{16,24},{20,28},{24,16},{28,20},{32,40},... | collective-permute-start | bytes 786440 | tf_op jit(solution)/shard_map/ppermute | solution.py:10
  139.4 16.6 %collective-permute-start.8 = (f32[512,128]{0,1:T(8,128)S(1)}, f32[512,128]{0,1:T(8,128)S(1)}, u32[]{:S(2)}, u32[]{:S(2)}) collective-permute-start(f32[512,128]{0,1:T(8,128)S(1)} %add.191), channel_id=1, source_target_pairs={{0,16},{4,20},{8,24},{12,28},{16,0},{20,4},{24,8},{28,12},{32,48},... | collective-permute-start | bytes 786440 | tf_op jit(solution)/shard_map/ppermute | solution.py:10
  156.0 28.5 %collective-permute-start.9 = (f32[512,128]{0,1:T(8,128)S(1)}, f32[512,128]{0,1:T(8,128)S(1)}, u32[]{:S(2)}, u32[]{:S(2)}) collective-permute-start(f32[512,128]{0,1:T(8,128)S(1)} %add.192), channel_id=1, source_target_pairs={{0,32},{4,36},{8,40},{12,44},{16,48},{20,52},{24,56},{28,60},{32,0... | collective-permute-start | bytes 786440 | tf_op jit(solution)/shard_map/ppermute | solution.py:10
  184.5 32.8 %collective-permute-start.10 = (f32[512,128]{0,1:T(8,128)S(1)}, f32[512,128]{0,1:T(8,128)S(1)}, u32[]{:S(2)}, u32[]{:S(2)}) collective-permute-start(f32[512,128]{0,1:T(8,128)S(1)} %add.193), channel_id=1, source_target_pairs={{0,64},{4,68},{8,72},{12,76},{16,80},{20,84},{24,88},{28,92},{32,9... | collective-permute-start | bytes 786440 | tf_op jit(solution)/shard_map/ppermute | solution.py:10
  218.0 9.6 %collective-permute-start.11 = (f32[512,128]{0,1:T(8,128)}, f32[512,128]{0,1:T(8,128)}, u32[]{:S(2)}, u32[]{:S(2)}) collective-permute-start(f32[512,128]{0,1:T(8,128)} %add.194), channel_id=1, source_target_pairs={{0,128},{4,132},{8,136},{12,140},{16,144},{20,148},{24,152},{28,15... | collective-permute-start | bytes 786440 | tf_op jit(solution)/shard_map/ppermute | solution.py:10
  238.0 9.4 %collective-permute-start.13 = (f32[512,128]{0,1:T(8,128)S(1)}, f32[512,128]{0,1:T(8,128)S(1)}, u32[]{:S(2)}, u32[]{:S(2)}) collective-permute-start(f32[512,128]{0,1:T(8,128)S(1)} %add.199), channel_id=1, source_target_pairs={{0,8},{4,12},{8,0},{12,4},{16,24},{20,28},{24,16},{28,20},{32,40},... | collective-permute-start | bytes 786440 | tf_op jit(solution)/shard_map/ppermute | solution.py:10
  247.4 16.6 %collective-permute-start.14 = (f32[512,128]{0,1:T(8,128)S(1)}, f32[512,128]{0,1:T(8,128)S(1)}, u32[]{:S(2)}, u32[]{:S(2)}) collective-permute-start(f32[512,128]{0,1:T(8,128)S(1)} %add.200), channel_id=1, source_target_pairs={{0,16},{4,20},{8,24},{12,28},{16,0},{20,4},{24,8},{28,12},{32,48},... | collective-permute-start | bytes 786440 | tf_op jit(solution)/shard_map/ppermute | solution.py:10
  264.1 27.0 %collective-permute-start.15 = (f32[512,128]{0,1:T(8,128)S(1)}, f32[512,128]{0,1:T(8,128)S(1)}, u32[]{:S(2)}, u32[]{:S(2)}) collective-permute-start(f32[512,128]{0,1:T(8,128)S(1)} %add.201), channel_id=1, source_target_pairs={{0,32},{4,36},{8,40},{12,44},{16,48},{20,52},{24,56},{28,60},{32,0... | collective-permute-start | bytes 786440 | tf_op jit(solution)/shard_map/ppermute | solution.py:10
  291.1 24.9 %collective-permute-start.16 = (f32[512,128]{0,1:T(8,128)S(1)}, f32[512,128]{0,1:T(8,128)S(1)}, u32[]{:S(2)}, u32[]{:S(2)}) collective-permute-start(f32[512,128]{0,1:T(8,128)S(1)} %add.202), channel_id=1, source_target_pairs={{0,64},{4,68},{8,72},{12,76},{16,80},{20,84},{24,88},{28,92},{32,9... | collective-permute-start | bytes 786440 | tf_op jit(solution)/shard_map/ppermute | solution.py:10
  316.0 9.0 %collective-permute-start.17 = (f32[512,128]{0,1:T(8,128)S(1)}, f32[512,128]{0,1:T(8,128)S(1)}, u32[]{:S(2)}, u32[]{:S(2)}) collective-permute-start(f32[512,128]{0,1:T(8,128)S(1)} %add.203), channel_id=1, source_target_pairs={{0,128},{4,132},{8,136},{12,140},{16,144},{20,148},{24,152},{28,15... | collective-permute-start | bytes 786440 | tf_op jit(solution)/shard_map/ppermute | solution.py:10
  325.1 9.6 %collective-permute-start.18 = (f32[512,128]{0,1:T(8,128)S(1)}, f32[512,128]{0,1:T(8,128)S(1)}, u32[]{:S(2)}, u32[]{:S(2)}) collective-permute-start(f32[512,128]{0,1:T(8,128)S(1)} %add.204), channel_id=1, source_target_pairs={{0,256},{4,260},{8,264},{12,268},{16,272},{20,276},{24,280},{28,28... | collective-permute-start | bytes 786440 | tf_op jit(solution)/shard_map/ppermute | solution.py:10
  341.0 9.4 %collective-permute-start.20 = (f32[512,128]{0,1:T(8,128)S(1)}, f32[512,128]{0,1:T(8,128)S(1)}, u32[]{:S(2)}, u32[]{:S(2)}) collective-permute-start(f32[512,128]{0,1:T(8,128)S(1)} %add.206), channel_id=1, source_target_pairs={{0,8},{4,12},{8,0},{12,4},{16,24},{20,28},{24,16},{28,20},{32,40},... | collective-permute-start | bytes 786440 | tf_op jit(solution)/shard_map/ppermute | solution.py:10
  350.5 16.6 %collective-permute-start.21 = (f32[512,128]{0,1:T(8,128)S(1)}, f32[512,128]{0,1:T(8,128)S(1)}, u32[]{:S(2)}, u32[]{:S(2)}) collective-permute-start(f32[512,128]{0,1:T(8,128)S(1)} %add.207), channel_id=1, source_target_pairs={{0,16},{4,20},{8,24},{12,28},{16,0},{20,4},{24,8},{28,12},{32,48},... | collective-permute-start | bytes 786440 | tf_op jit(solution)/shard_map/ppermute | solution.py:10
  367.1 31.2 %collective-permute-start.22 = (f32[512,128]{0,1:T(8,128)S(1)}, f32[512,128]{0,1:T(8,128)S(1)}, u32[]{:S(2)}, u32[]{:S(2)}) collective-permute-start(f32[512,128]{0,1:T(8,128)S(1)} %add.208), channel_id=1, source_target_pairs={{0,32},{4,36},{8,40},{12,44},{16,48},{20,52},{24,56},{28,60},{32,0... | collective-permute-start | bytes 786440 | tf_op jit(solution)/shard_map/ppermute | solution.py:10
  398.4 32.9 %collective-permute-start.23 = (f32[512,128]{0,1:T(8,128)S(1)}, f32[512,128]{0,1:T(8,128)S(1)}, u32[]{:S(2)}, u32[]{:S(2)}) collective-permute-start(f32[512,128]{0,1:T(8,128)S(1)} %add.209), channel_id=1, source_target_pairs={{0,64},{4,68},{8,72},{12,76},{16,80},{20,84},{24,88},{28,92},{32,9... | collective-permute-start | bytes 786440 | tf_op jit(solution)/shard_map/ppermute | solution.py:10
  431.4 9.3 %collective-permute-start.24 = (f32[512,128]{0,1:T(8,128)S(1)}, f32[512,128]{0,1:T(8,128)S(1)}, u32[]{:S(2)}, u32[]{:S(2)}) collective-permute-start(f32[512,128]{0,1:T(8,128)S(1)} %add.210), channel_id=1, source_target_pairs={{0,128},{4,132},{8,136},{12,140},{16,144},{20,148},{24,152},{28,15... | collective-permute-start | bytes 786440 | tf_op jit(solution)/shard_map/ppermute | solution.py:10
  440.7 9.9 %collective-permute-start.25 = (f32[512,128]{0,1:T(8,128)S(1)}, f32[512,128]{0,1:T(8,128)S(1)}, u32[]{:S(2)}, u32[]{:S(2)}) collective-permute-start(f32[512,128]{0,1:T(8,128)S(1)} %add.211), channel_id=1, source_target_pairs={{0,256},{4,260},{8,264},{12,268},{16,272},{20,276},{24,280},{28,28... | collective-permute-start | bytes 786440 | tf_op jit(solution)/shard_map/ppermute | solution.py:10
  456.7 9.4 %collective-permute-start.27 = (f32[512,128]{0,1:T(8,128)S(1)}, f32[512,128]{0,1:T(8,128)S(1)}, u32[]{:S(2)}, u32[]{:S(2)}) collective-permute-start(f32[512,128]{0,1:T(8,128)S(1)} %add.213), channel_id=1, source_target_pairs={{0,8},{4,12},{8,0},{12,4},{16,24},{20,28},{24,16},{28,20},{32,40},... | collective-permute-start | bytes 786440 | tf_op jit(solution)/shard_map/ppermute | solution.py:10
  466.2 16.6 %collective-permute-start.28 = (f32[512,128]{0,1:T(8,128)S(1)}, f32[512,128]{0,1:T(8,128)S(1)}, u32[]{:S(2)}, u32[]{:S(2)}) collective-permute-start(f32[512,128]{0,1:T(8,128)S(1)} %add.214), channel_id=1, source_target_pairs={{0,16},{4,20},{8,24},{12,28},{16,0},{20,4},{24,8},{28,12},{32,48},... | collective-permute-start | bytes 786440 | tf_op jit(solution)/shard_map/ppermute | solution.py:10
  482.8 27.0 %collective-permute-start.29 = (f32[512,128]{0,1:T(8,128)S(1)}, f32[512,128]{0,1:T(8,128)S(1)}, u32[]{:S(2)}, u32[]{:S(2)}) collective-permute-start(f32[512,128]{0,1:T(8,128)S(1)} %add.215), channel_id=1, source_target_pairs={{0,32},{4,36},{8,40},{12,44},{16,48},{20,52},{24,56},{28,60},{32,0... | collective-permute-start | bytes 786440 | tf_op jit(solution)/shard_map/ppermute | solution.py:10
  509.9 27.2 %collective-permute-start.30 = (f32[512,128]{0,1:T(8,128)S(1)}, f32[512,128]{0,1:T(8,128)S(1)}, u32[]{:S(2)}, u32[]{:S(2)}) collective-permute-start(f32[512,128]{0,1:T(8,128)S(1)} %add.216), channel_id=1, source_target_pairs={{0,64},{4,68},{8,72},{12,76},{16,80},{20,84},{24,88},{28,92},{32,9... | collective-permute-start | bytes 786440 | tf_op jit(solution)/shard_map/ppermute | solution.py:10
  537.1 9.1 %collective-permute-start.31 = (f32[512,128]{0,1:T(8,128)S(1)}, f32[512,128]{0,1:T(8,128)S(1)}, u32[]{:S(2)}, u32[]{:S(2)}) collective-permute-start(f32[512,128]{0,1:T(8,128)S(1)} %add.217), channel_id=1, source_target_pairs={{0,128},{4,132},{8,136},{12,140},{16,144},{20,148},{24,152},{28,15... | collective-permute-start | bytes 786440 | tf_op jit(solution)/shard_map/ppermute | solution.py:10
  551.7 9.5 %collective-permute-start.33 = (f32[512,128]{0,1:T(8,128)S(1)}, f32[512,128]{0,1:T(8,128)S(1)}, u32[]{:S(2)}, u32[]{:S(2)}) collective-permute-start(f32[512,128]{0,1:T(8,128)S(1)} %add.220), channel_id=1, source_target_pairs={{0,8},{4,12},{8,0},{12,4},{16,24},{20,28},{24,16},{28,20},{32,40},... | collective-permute-start | bytes 786440 | tf_op jit(solution)/shard_map/ppermute | solution.py:10
  561.3 16.6 %collective-permute-start.34 = (f32[512,128]{0,1:T(8,128)S(1)}, f32[512,128]{0,1:T(8,128)S(1)}, u32[]{:S(2)}, u32[]{:S(2)}) collective-permute-start(f32[512,128]{0,1:T(8,128)S(1)} %add.221), channel_id=1, source_target_pairs={{0,16},{4,20},{8,24},{12,28},{16,0},{20,4},{24,8},{28,12},{32,48},... | collective-permute-start | bytes 786440 | tf_op jit(solution)/shard_map/ppermute | solution.py:10
  577.9 29.9 %collective-permute-start.35 = (f32[512,128]{0,1:T(8,128)S(1)}, f32[512,128]{0,1:T(8,128)S(1)}, u32[]{:S(2)}, u32[]{:S(2)}) collective-permute-start(f32[512,128]{0,1:T(8,128)S(1)} %add.222), channel_id=1, source_target_pairs={{0,32},{4,36},{8,40},{12,44},{16,48},{20,52},{24,56},{28,60},{32,0... | collective-permute-start | bytes 786440 | tf_op jit(solution)/shard_map/ppermute | solution.py:10
  612.1 9.4 %collective-permute-start.37 = (f32[512,128]{0,1:T(8,128)S(1)}, f32[512,128]{0,1:T(8,128)S(1)}, u32[]{:S(2)}, u32[]{:S(2)}) collective-permute-start(f32[512,128]{0,1:T(8,128)S(1)} %add.225), channel_id=1, source_target_pairs={{0,8},{4,12},{8,0},{12,4},{16,24},{20,28},{24,16},{28,20},{32,40},... | collective-permute-start | bytes 786440 | tf_op jit(solution)/shard_map/ppermute | solution.py:10
  (41 other events, 533.1 us)
where the time goes:
time: 638 us; the launch traced here: 636 us
  waiting for transfers between devices  387 us (61%)
  starting transfers between devices  166 us (26%)
  matrix products  33.7 us (5%)
  blocking collectives  20.3 us (3%)
  local copies, waits for them, and re-layouts  15.7 us (2%)
  other arithmetic  11.4 us (2%)
    ppermute x38, waiting for transfers between devices, from_partner(): lax.ppermute(shard, axis, [(i, i ^ 1 << apart) for i in range(lax.axis_si...  387 us
    ppermute x38, starting transfers between devices, from_partner(): lax.ppermute(shard, axis, [(i, i ^ 1 << apart) for i in range(lax.axis_si...  166 us
    dot_general x24, matrix products, product_first(): lax.dot_general(left_side, right_side, (((0,), (0,)), ((), ())), precisio...  17.3 us
    dot_general x24, matrix products, product(): jnp.dot(left_side, right_side, precision=HIGH, preferred_element_type=jnp...  16.3 us
  transfers between devices with their start and end apart: 38, of which 35 were waited for; matrix products, arithmetic and copies ran while one was open for 1% of the time, Pallas kernels for 0%

commit v1 on v0

v1 whole, which is shorter than its diff:
```python
import functools

import jax
import jax.numpy as jnp
from jax import lax
from jax.experimental import pallas as pl
from jax.experimental.pallas import tpu as pltpu
from jax.sharding import PartitionSpec as P

F32 = jnp.float32
BF16 = jnp.bfloat16
NN = (((1,), (0,)), ((), ()))
NT = (((1,), (1,)), ((), ()))
TN = (((0,), (0,)), ((), ()))
LEVELS = 4
CORE, Z1, Z2, Z4, Z8, Y1, Y2 = range(7)


def halves(value):
    high = value.astype(BF16)
    low = (value - high.astype(F32)).astype(BF16)
    return high, low


def mm(left, right, dims):
    left_high, left_low = halves(left)
    right_high, right_low = halves(right)
    dot = functools.partial(lax.dot_general, dimension_numbers=dims, preferred_element_type=F32)
    return dot(left_high, right_high) + (dot(left_high, right_low) + dot(left_low, right_high))


def exact(left, right, dims):
    return lax.dot_general(left, right, dims, precision=lax.Precision.HIGHEST, preferred_element_type=F32)


def swap(value, axis, mask):
    return lax.ppermute(value, axis, [(i, i ^ mask) for i in range(lax.axis_size(axis))])


def across(value, bit):
    return swap(value, "leaf", 1 << bit)


def grow(value, bit):
    return jnp.concatenate([value, across(value, bit)], axis=1)


def pair_starts(blocks):
    starts, running = [], 0
    for column in range(blocks):
        starts.append(running)
        running += blocks - 1 - column
    return starts


def placement(rows, offset, count, start, width):
    row = lax.broadcasted_iota(jnp.int32, (rows, width), 0)
    column = lax.broadcasted_iota(jnp.int32, (rows, width), 1)
    inside = (row >= offset) & (row < offset + count)
    return jnp.where(inside & (row - offset == column - start), 1.0, 0.0).astype(F32)


def forward_kernel(sizes, where, pattern, rhs, inverse, blocks, coupling, sep_rhs, y_out, t_out):
    count, size = inverse.shape[0], inverse.shape[1]
    starts = pair_starts(count)
    pending = [rhs[i * size : (i + 1) * size, :] for i in range(count)]
    for column in range(count):
        solved = mm(inverse[column], pending[column], NN)
        y_out[column * size : (column + 1) * size, :] = solved
        for later in range(column + 1, count):
            pair = starts[column] + later - column - 1
            weight = pattern[0, pair].astype(F32)
            pending[later] = pending[later] - weight * mm(blocks[pair], solved, NN)
    last = y_out[(count - 1) * size :, :]
    right = sep_rhs[...]
    width = coupling.shape[1]
    offset = 0
    for level, rows in enumerate(sizes):
        spread = placement(right.shape[0], offset, rows, where[level], width)
        offset += rows
        t_out[:, level * width : (level + 1) * width] = exact(right, spread, TN) - mm(
            last, coupling[level * size : (level + 1) * size, :], TN
        )


def backward_kernel(sizes, where, pattern, y, x, inverse, blocks, coupling, out, sep_out):
    count, size = inverse.shape[0], inverse.shape[1]
    starts = pair_starts(count)
    width = coupling.shape[1]
    place = where[LEVELS]
    quarter = x.shape[0]
    xs = jnp.concatenate([x[jnp.bitwise_xor(place, q)] for q in range(quarter)], axis=0)
    correction = jnp.zeros((size, y.shape[1]), F32)
    pieces = jnp.zeros((sep_out.shape[0], y.shape[1]), F32)
    offset = 0
    for level, rows in enumerate(sizes):
        part = xs[:, level * width : (level + 1) * width]
        correction = correction + mm(coupling[level * size : (level + 1) * size, :], part, NT)
        spread = placement(sep_out.shape[0], offset, rows, where[level], width)
        pieces = pieces + exact(spread, part, NT)
        offset += rows
    sep_out[...] = pieces
    pending = [y[i * size : (i + 1) * size, :] for i in range(count)]
    pending[-1] = pending[-1] - correction
    for column in reversed(range(count)):
        solved = mm(inverse[column], pending[column], TN)
        out[column * size : (column + 1) * size, :] = solved
        for earlier in reversed(range(column)):
            pair = starts[earlier] + column - earlier - 1
            weight = pattern[0, pair].astype(F32)
            pending[earlier] = pending[earlier] - weight * mm(blocks[pair], solved, TN)


def spans(plane, count):
    return [pl.ds(pl.multiple_of(jnp.bitwise_xor(plane, r) * 128, 128), 128) for r in range(count)]


def times_rows(value, spots, mats):
    result = []
    for half in mats:
        total = None
        for spot, block in zip(spots, half):
            term = mm(value[:, spot], block[0], NT)
            total = term if total is None else total + term
        result.append(total)
    return result


def times_matrix(value, mats, r):
    total = None
    for piece, half in zip(value, mats):
        term = mm(piece, half[r][0], NN)
        total = term if total is None else total + term
    return total


def split(refs, count):
    per = 2 * count
    return [[refs[i * per + h * count : i * per + (h + 1) * count] for h in range(2)] for i in range(len(refs) // per)]


def level_kernel(count, plane, right, base, *refs):
    mats, (z_out, v_out) = refs[:-2], refs[-2:]
    diagonal, below = split(mats, count)
    spots = spans(plane[0], count)
    z = times_rows(right, spots, diagonal)
    z_out[...] = jnp.concatenate(z, axis=1)
    for r, spot in enumerate(spots):
        v_out[:, spot] = base[:, spot] - times_matrix(z, below, r)


def top_kernel(count, plane, right, z1, z2, z3, *refs):
    mats, x_out = refs[:-1], refs[-1]
    d4, d3, c3, d2, c2, d1, c1 = split(mats, count)
    width = right.shape[1]
    spots = spans(plane[0], count)
    z = times_rows(right, spots, d4)
    level = 3
    order = [(z3, d3, c3), (z2, d2, c2), (z1, d1, c1)]
    diagonal = d4
    while True:
        places = [pl.ds(pl.multiple_of(level * width + jnp.bitwise_xor(plane[0], r) * 128, 128), 128) for r in range(count)]
        for r, place in enumerate(places):
            x_out[:, place] = times_matrix(z, diagonal, r)
        if not order:
            break
        held, diagonal, below = order.pop(0)
        moved = times_rows(x_out, places, below)
        half = held.shape[1] // 2
        z = [held[:, :half] - moved[0], held[:, half:] - moved[1]]
        level -= 1


SMEM = pl.BlockSpec(memory_space=pltpu.SMEM)
VMEM = pl.BlockSpec(memory_space=pltpu.VMEM)


def params():
    return pltpu.CompilerParams(vmem_limit_bytes=40 * 1024 * 1024)


def mat_specs(gathered, index):
    rows = gathered[0].shape[1]
    spec = pl.BlockSpec((1, rows, 128), lambda step: (index, 0, 0))
    return [spec] * len(gathered), list(gathered)


def with_mats(kernel, plane, small, mats, outs):
    specs, arrays = [], []
    for gathered, index in mats:
        more, given = mat_specs(gathered, index)
        specs += more
        arrays += given
    whole = [pl.BlockSpec(v.shape, lambda step: (0, 0)) for v in small]
    return pl.pallas_call(
        kernel,
        grid=(1,),
        out_shape=[jax.ShapeDtypeStruct(s, F32) for s in outs],
        in_specs=[SMEM] + whole + specs,
        out_specs=[pl.BlockSpec(s, lambda step: (0, 0)) for s in outs],
        compiler_params=params(),
    )(plane, *small, *arrays)


def over_col(value):
    return [value] + [swap(value, "col", r) for r in range(1, lax.axis_size("col"))]


def gathered(value):
    mine = over_col(value)
    return mine + [across(v, CORE) for v in mine]


def shards(leaf_rhs, leaf_inverse, leaf_blocks, leaf_pattern, leaf_coupling, sep_rhs, sep_inverse, sep_coupling):
    position = lax.axis_index("leaf")
    planes = lax.axis_size("col")
    columns = leaf_rhs.shape[1]
    width = leaf_coupling.shape[1]
    groups = [4, 16, 64, 128]
    sizes = [width // g for g in groups]
    offsets = [sum(sizes[:i]) for i in range(LEVELS)]
    where = jnp.stack([position % g * r for g, r in zip(groups, sizes)] + [position % 4]).astype(jnp.int32)
    plane = lax.axis_index("col").astype(jnp.int32)[None]

    def rows(array, level):
        return array[offsets[level] : offsets[level] + sizes[level]][None]

    def both(level):
        return jnp.concatenate([rows(sep_inverse, level), rows(sep_coupling, level)], 0)

    first = gathered(grow(both(0), Z1))
    far = grow(rows(sep_inverse, 3), Y2)
    far = grow(jnp.concatenate([far, both(2)], 0), Y1)
    far = grow(far, Z8)
    far = grow(jnp.concatenate([far, both(1)], 0), Z4)
    far = gathered(grow(grow(far, Z2), Z1))

    padded = jnp.pad(sep_rhs, ((0, 4), (0, 0)))
    y, t = pl.pallas_call(
        functools.partial(forward_kernel, sizes),
        out_shape=[
            jax.ShapeDtypeStruct(leaf_rhs.shape, F32),
            jax.ShapeDtypeStruct((columns, LEVELS * width), F32),
        ],
        in_specs=[SMEM, SMEM] + [VMEM] * 5,
        out_specs=[VMEM, VMEM],
        compiler_params=params(),
    )(where, leaf_pattern, leaf_rhs, leaf_inverse, leaf_blocks, leaf_coupling, padded)

    near = [[g * 4 + m for m in range(4)] for g in range(lax.axis_size("leaf") // 4)]
    t = lax.all_to_all(t, "leaf", 0, 0, axis_index_groups=near, tiled=True)
    t = t.reshape(4, columns // 4, LEVELS * width).sum(0)
    t1, t2, t3, t4 = [t[:, i * width : (i + 1) * width] for i in range(LEVELS)]

    def total(value, bits):
        for bit in bits:
            value = value + across(value, bit)
        return value

    shape = t1.shape
    upper = total(jnp.concatenate([t3, t4], 1), (Z2, Z4))
    t3, t4 = upper[:, :width], upper[:, width:]
    t4 = total(t4, (Z8, Y1))
    level = functools.partial(level_kernel, planes)
    z1, v = with_mats(level, plane, [t1, t2], [(first, 0), (first, 1)], [shape] * 2)
    v = total(v, (Z2, Z4))
    z2, v = with_mats(level, plane, [v, t3], [(far, 3), (far, 4)], [shape] * 2)
    v = total(v, (Z8, Y1))
    z3, v = with_mats(level, plane, [v, t4], [(far, 1), (far, 2)], [shape] * 2)
    v = total(v, (Y2,))
    (x,) = with_mats(
        functools.partial(top_kernel, planes),
        plane,
        [v, z1, z2, z3],
        [(far, 0), (far, 1), (far, 2), (far, 3), (far, 4), (first, 0), (first, 1)],
        [(shape[0], LEVELS * width)],
    )
    x = grow(x[None, None], Z1)[0]
    other = across(x, CORE)
    x = jnp.stack([x[0], other[0], x[1], other[1]], 0)

    return pl.pallas_call(
        functools.partial(backward_kernel, sizes),
        out_shape=[jax.ShapeDtypeStruct(leaf_rhs.shape, F32), jax.ShapeDtypeStruct(padded.shape, F32)],
        in_specs=[SMEM, SMEM] + [VMEM] * 5,
        out_specs=[VMEM, VMEM],
        compiler_params=params(),
    )(where, leaf_pattern, y, x, leaf_inverse, leaf_blocks, leaf_coupling)


def program(*arrays):
    leaf, sep = shards(*arrays)
    return leaf, sep[: arrays[5].shape[0]]


def solution(mesh):
    return jax.shard_map(
        program,
        mesh=mesh,
        in_specs=(
            P("leaf", "col"),
            P("leaf", None, None),
            P("leaf", None, None),
            P("leaf", None),
            P("leaf", None),
            P("leaf", "col"),
            P("leaf", "col"),
            P("leaf", "col"),
        ),
        out_specs=(P("leaf", "col"), P("leaf", "col")),
        check_vma=False,
    )
```

time: 638 us -> 246 us (0.39)
  waiting for transfers between devices: 387 us -> 72.1 us
  matrix products: 33.7 us -> 0 us
  starting transfers between devices: 166 us -> 138 us
  blocking collectives: 20.3 us -> 0 us
  Pallas kernels: 0 us -> 19.1 us
  other arithmetic: 11.4 us -> 2.43 us
    ppermute x38 -> x32, waiting for transfers between devices: 387 us -> 72.1 us  [swap(): lax.ppermute(value, axis, [(i, i ^ mask) for i in range(lax.axis_size(axi...]
    ppermute x38 -> x32, starting transfers between devices: 166 us -> 126 us  [swap(): lax.ppermute(value, axis, [(i, i ^ mask) for i in range(lax.axis_size(axi...]
    dot_general x48 -> x0, matrix products: 33.7 us -> none  [the longest x24 17.3 us: product_first(): lax.dot_general(left_side, right_side, (((0,), (0,)), ((), ())), precisio...]
    all_gather x2 -> x0, blocking collectives: 20.3 us -> none  [the longest x1 10.2 us: shards(): lax.all_gather(sep_inverse, 'col', axis=1, tiled=True)]
    pallas_call x0 -> x6, Pallas kernels: none -> 19.1 us  [the longest x4 9.15 us: with_mats(): pl.pallas_call(kernel, grid=(1,), out_shape=[jax.ShapeDtypeStruct(s, F32)...]
    all_to_all x0 -> x1, starting transfers between devices: none -> 11.2 us  [shards(): t = lax.all_to_all(t, 'leaf', 0, 0, axis_index_groups=near, tiled=True)]
    add x37 -> x9, other arithmetic: 9.15 us -> 0.12 us  [total(): value = value + across(value, bit)]
  transfers between devices with their start and end apart: 38 -> 33, of which waited for: 35 -> 16; matrix products, arithmetic and copies ran while one was open for 1% -> 2% of each run, Pallas kernels for 0% -> 1%
where the time goes in v1:
time: 246 us; the launch traced here: 245 us
  starting transfers between devices  138 us (56%)
  waiting for transfers between devices  72.1 us (29%)
  Pallas kernels  19.1 us (8%)
  local copies, waits for them, and re-layouts  12.2 us (5%)
    ppermute x32, starting transfers between devices, swap(): lax.ppermute(value, axis, [(i, i ^ mask) for i in range(lax.axis_size(axi...  126 us
    ppermute x32, waiting for transfers between devices, swap(): lax.ppermute(value, axis, [(i, i ^ mask) for i in range(lax.axis_size(axi...  72.1 us
    all_to_all x1, starting transfers between devices, shards(): t = lax.all_to_all(t, 'leaf', 0, 0, axis_index_groups=near, tiled=True)  11.2 us
    unnamed x40, local copies, waits for them, and re-layouts  9.37 us
    pallas_call x4, Pallas kernels, with_mats(): pl.pallas_call(kernel, grid=(1,), out_shape=[jax.ShapeDtypeStruct(s, F32)...  9.15 us
    pallas_call x1, Pallas kernels, shards(): pl.pallas_call(functools.partial(forward_kernel, sizes), out_shape=[jax.S...  5.13 us
  transfers between devices with their start and end apart: 33, of which 16 were waited for; matrix products, arithmetic and copies ran while one was open for 2% of the time, Pallas kernels for 1%

profile of v1, /device:TPU:1, one launch (start us, length us, event | category | flops | bytes accessed | tf_op | source)
XLA Modules:
  0.0 244.8 jit_solution(5430906936575072506)
XLA Ops:
  6.9 5.1 %shard_map.95 = (f32[896,128]{1,0:T(8,128)S(1)}, f32[128,2048]{1,0:T(8,128)}) custom-call(s32[5]{0:T(128)S(1)} %stack.26.where, s32[1,21]{1,0:T(1,128)S(1)} %copy-done.15, f32[896,128]{1,0:T(8,128)S(1)} %copy-done.14, f32[7,128,128]{2,1,0:T(8,128)S(1)} %copy-done.10, f32[21,128,128]{2,1,0:T(8,128)S(1)} %copy-done, f32[512,512]{1,0:T(8,128)S(1)} %copy-done.8, ...), custom_call_target="tpu_custom_call" | custom-call | tf_op jit(solution)/shard_map/pallas_call | solution.py:239
  12.8 11.2 %all-to-all-start = ((f32[4,32,2048]{2,1,0:T(8,128)}), f32[4,32,2048]{2,1,0:T(8,128)}, u32[]{:S(2)}, u32[]{:S(2)}) async-start(f32[4,32,2048]{2,1,0:T(8,128)} %bitcast.6), calls=%async_computation | async-start | bytes 2097152 | tf_op jit(solution)/shard_map/all_to_all | solution.py:251
  26.0 3.9 %collective-permute-done.12 = f32[1,4,128]{2,1,0:T(4,128)S(1)} collective-permute-done((f32[1,4,128]{2,1,0:T(4,128)S(1)}, f32[1,4,128]{2,1,0:T(4,128)S(1)}, u32[]{:S(2)}, u32[]{:S(2)}) %collective-permute-start.12) | collective-permute-done | bytes 2080 | tf_op jit(solution)/shard_map/ppermute | solution.py:37
  34.7 10.1 %collective-permute-start.14 = (f32[3,16,128]{2,1,0:T(8,128)S(1)}, f32[3,16,128]{2,1,0:T(8,128)S(1)}, u32[]{:S(2)}, u32[]{:S(2)}) collective-permute-start(f32[3,16,128]{2,1,0:T(8,128)S(1)} %pad_maximum_fusion.7), channel_id=1, source_target_pairs={{0,64},{4,68},{8,72},{12,76},{16,80},{20,84},{24,88},{28,92},{32,9... | collective-permute-start | bytes 73736 | tf_op jit(solution)/shard_map/ppermute | solution.py:37
  44.8 3.2 %collective-permute-done.14 = f32[3,16,128]{2,1,0:T(8,128)S(1)} collective-permute-done((f32[3,16,128]{2,1,0:T(8,128)S(1)}, f32[3,16,128]{2,1,0:T(8,128)S(1)}, u32[]{:S(2)}, u32[]{:S(2)}) %collective-permute-start.14) | collective-permute-done | bytes 24608 | tf_op jit(solution)/shard_map/ppermute | solution.py:37
  48.1 3.4 %collective-permute-start.15 = (f32[5,32,128]{2,1,0:T(8,128)S(1)}, f32[5,32,128]{2,1,0:T(8,128)S(1)}, u32[]{:S(2)}, u32[]{:S(2)}) collective-permute-start(f32[5,32,128]{2,1,0:T(8,128)S(1)} %pad_maximum_fusion.6), channel_id=1, source_target_pairs={{0,32},{4,36},{8,40},{12,44},{16,48},{20,52},{24,56},{28,60},{32,0... | collective-permute-start | bytes 245768 | tf_op jit(solution)/shard_map/ppermute | solution.py:37
  51.5 8.3 %collective-permute-done.15 = f32[5,32,128]{2,1,0:T(8,128)S(1)} collective-permute-done((f32[5,32,128]{2,1,0:T(8,128)S(1)}, f32[5,32,128]{2,1,0:T(8,128)S(1)}, u32[]{:S(2)}, u32[]{:S(2)}) %collective-permute-start.15) | collective-permute-done | bytes 81952 | tf_op jit(solution)/shard_map/ppermute | solution.py:37
  63.7 3.4 %collective-permute-done.16 = f32[5,64,128]{2,1,0:T(8,128)S(1)} collective-permute-done((f32[5,64,128]{2,1,0:T(8,128)S(1)}, f32[5,64,128]{2,1,0:T(8,128)S(1)}, u32[]{:S(2)}, u32[]{:S(2)}) %collective-permute-start.16) | collective-permute-done | bytes 163872 | tf_op jit(solution)/shard_map/ppermute | solution.py:37
  71.0 3.6 %collective-permute-start.2 = (f32[2,256,128]{2,1,0:T(8,128)S(1)}, f32[2,256,128]{2,1,0:T(8,128)S(1)}, u32[]{:S(2)}, u32[]{:S(2)}) collective-permute-start(f32[2,256,128]{2,1,0:T(8,128)S(1)} %pad_maximum_fusion.3.refs_0_.refs_8_.refs_40_.refs_48_), channel_id=1, source_target_pairs={{0,2},{1,3},{2,0},{3,1},{4,6},{5,7},{6,4},{7,5},{8,10},{9,11},{10,... | collective-permute-start | bytes 786440 | tf_op jit(solution)/shard_map/ppermute | solution.py:37
  74.6 4.1 %collective-permute-start.3 = (f32[2,256,128]{2,1,0:T(8,128)S(1)}, f32[2,256,128]{2,1,0:T(8,128)}, u32[]{:S(2)}, u32[]{:S(2)}) collective-permute-start(f32[2,256,128]{2,1,0:T(8,128)S(1)} %pad_maximum_fusion.3.refs_0_.refs_8_.refs_40_.refs_48_), channel_id=1, source_target_pairs={{0,3},{1,2},{2,1},{3,0},{4,7},{5,6},{6,5},{7,4},{8,11},{9,10},{10,... | collective-permute-start | bytes 786440 | tf_op jit(solution)/shard_map/ppermute | solution.py:37
  78.7 8.6 %collective-permute-start.4 = (f32[2,256,128]{2,1,0:T(8,128)S(1)}, f32[2,256,128]{2,1,0:T(8,128)S(1)}, u32[]{:S(2)}, u32[]{:S(2)}) collective-permute-start(f32[2,256,128]{2,1,0:T(8,128)S(1)} %pad_maximum_fusion.3.refs_0_.refs_8_.refs_40_.refs_48_), channel_id=1, source_target_pairs={{0,4},{4,0},{8,12},{12,8},{16,20},{20,16},{24,28},{28,24},{32,36},... | collective-permute-start | bytes 786440 | tf_op jit(solution)/shard_map/ppermute | solution.py:37
  89.3 4.6 %collective-permute-start.19 = (f32[5,256,128]{2,1,0:T(8,128)S(1)}, f32[5,256,128]{2,1,0:T(8,128)S(1)}, u32[]{:S(2)}, u32[]{:S(2)}) collective-permute-start(f32[5,256,128]{2,1,0:T(8,128)S(1)} %pad_maximum_fusion.1.refs_0_.refs_8_.refs_16_.refs_24_.refs_32_), channel_id=1, source_target_pairs={{0,2},{1,3},{2,0},{3,1},{4,6},{5,7},{6,4},{7,5},{8,10},{9,11},{10,... | collective-permute-start | bytes 1966088 | tf_op jit(solution)/shard_map/ppermute | solution.py:37
  93.9 3.0 %collective-permute-start.20 = (f32[5,256,128]{2,1,0:T(8,128)S(1)}, f32[5,256,128]{2,1,0:T(8,128)S(1)}, u32[]{:S(2)}, u32[]{:S(2)}) collective-permute-start(f32[5,256,128]{2,1,0:T(8,128)S(1)} %pad_maximum_fusion.1.refs_0_.refs_8_.refs_16_.refs_24_.refs_32_), channel_id=1, source_target_pairs={{0,3},{1,2},{2,1},{3,0},{4,7},{5,6},{6,5},{7,4},{8,11},{9,10},{10,... | collective-permute-start | bytes 1966088 | tf_op jit(solution)/shard_map/ppermute | solution.py:37
  108.5 3.1 %collective-permute-start.10 = (f32[32,1024]{1,0:T(8,128)S(1)}, f32[32,1024]{1,0:T(8,128)S(1)}, u32[]{:S(2)}, u32[]{:S(2)}) collective-permute-start(f32[32,1024]{1,0:T(8,128)S(1)} %concatenate.51), channel_id=1, source_target_pairs={{0,16},{4,20},{8,24},{12,28},{16,0},{20,4},{24,8},{28,12},{32,48},... | collective-permute-start | bytes 393224 | tf_op jit(solution)/shard_map/ppermute | solution.py:37
  116.8 4.1 %collective-permute-done.19.refs_2_.refs_10_.refs_18_.refs_26_.refs_34_ = f32[5,256,128]{2,1,0:T(8,128)S(1)} collective-permute-done((f32[5,256,128]{2,1,0:T(8,128)S(1)}, f32[5,256,128]{2,1,0:T(8,128)S(1)}, u32[]{:S(2)}, u32[]{:S(2)}) %collective-permute-start.19) | collective-permute-done | bytes 655392 | tf_op jit(solution)/shard_map/ppermute | solution.py:37
  123.7 3.1 %collective-permute-done.20.refs_3_.refs_11_.refs_19_.refs_27_.refs_35_ = f32[5,256,128]{2,1,0:T(8,128)S(1)} collective-permute-done((f32[5,256,128]{2,1,0:T(8,128)S(1)}, f32[5,256,128]{2,1,0:T(8,128)S(1)}, u32[]{:S(2)}, u32[]{:S(2)}) %collective-permute-start.20) | collective-permute-done | bytes 655392 | tf_op jit(solution)/shard_map/ppermute | solution.py:37
  126.8 3.3 %collective-permute-start.24 = (f32[5,256,128]{2,1,0:T(8,128)S(1)}, f32[5,256,128]{2,1,0:T(8,128)S(1)}, u32[]{:S(2)}, u32[]{:S(2)}) collective-permute-start(f32[5,256,128]{2,1,0:T(8,128)S(1)} %collective-permute-done.20.refs_3_.refs_11_.refs_19_.refs_27_.refs_35_), channel_id=1, source_target_pairs={{0,4},{4,0},{8,12},{12,8},{16,20},{20,16},{24,28},{28,24},{32,36},... | collective-permute-start | bytes 1966088 | tf_op jit(solution)/shard_map/ppermute | solution.py:37
  134.2 3.0 %collective-permute-start.8 = (f32[32,512]{1,0:T(8,128)S(1)}, f32[32,512]{1,0:T(8,128)S(1)}, u32[]{:S(2)}, u32[]{:S(2)}) collective-permute-start(f32[32,512]{1,0:T(8,128)S(1)} %get-tuple-element.14), channel_id=1, source_target_pairs={{0,16},{4,20},{8,24},{12,28},{16,0},{20,4},{24,8},{28,12},{32,48},... | collective-permute-start | bytes 196616 | tf_op jit(solution)/shard_map/ppermute | solution.py:37
  137.2 3.5 %collective-permute-done.8 = f32[32,512]{1,0:T(8,128)S(1)} collective-permute-done((f32[32,512]{1,0:T(8,128)S(1)}, f32[32,512]{1,0:T(8,128)S(1)}, u32[]{:S(2)}, u32[]{:S(2)}) %collective-permute-start.8) | collective-permute-done | bytes 65568 | tf_op jit(solution)/shard_map/ppermute | solution.py:37
  140.8 7.8 %collective-permute-start.11 = (f32[32,1024]{1,0:T(8,128)S(1)}, f32[32,1024]{1,0:T(8,128)S(1)}, u32[]{:S(2)}, u32[]{:S(2)}) collective-permute-start(f32[32,1024]{1,0:T(8,128)S(1)} %slice_add_fusion.1), channel_id=1, source_target_pairs={{0,32},{4,36},{8,40},{12,44},{16,48},{20,52},{24,56},{28,60},{32,0... | collective-permute-start | bytes 393224 | tf_op jit(solution)/shard_map/ppermute | solution.py:37
  148.5 11.9 %collective-permute-done.11 = f32[32,1024]{1,0:T(8,128)S(1)} collective-permute-done((f32[32,1024]{1,0:T(8,128)S(1)}, f32[32,1024]{1,0:T(8,128)S(1)}, u32[]{:S(2)}, u32[]{:S(2)}) %collective-permute-start.11) | collective-permute-done | bytes 131104 | tf_op jit(solution)/shard_map/ppermute | solution.py:37
  162.4 9.9 %collective-permute-done.9 = f32[32,512]{1,0:T(8,128)S(1)} collective-permute-done((f32[32,512]{1,0:T(8,128)S(1)}, f32[32,512]{1,0:T(8,128)S(1)}, u32[]{:S(2)}, u32[]{:S(2)}) %collective-permute-start.9) | collective-permute-done | bytes 65568 | tf_op jit(solution)/shard_map/ppermute | solution.py:37
  172.4 9.6 %collective-permute-start.27 = (f32[32,512]{1,0:T(8,128)S(1)}, f32[32,512]{1,0:T(8,128)S(1)}, u32[]{:S(2)}, u32[]{:S(2)}) collective-permute-start(f32[32,512]{1,0:T(8,128)S(1)} %slice.72), channel_id=1, source_target_pairs={{0,64},{4,68},{8,72},{12,76},{16,80},{20,84},{24,88},{28,92},{32,9... | collective-permute-start | bytes 196616 | tf_op jit(solution)/shard_map/ppermute | solution.py:37
  182.0 5.3 %collective-permute-done.27 = f32[32,512]{1,0:T(8,128)S(1)} collective-permute-done((f32[32,512]{1,0:T(8,128)S(1)}, f32[32,512]{1,0:T(8,128)S(1)}, u32[]{:S(2)}, u32[]{:S(2)}) %collective-permute-start.27) | collective-permute-done | bytes 65568 | tf_op jit(solution)/shard_map/ppermute | solution.py:37
  188.4 8.3 %collective-permute-start.25 = (f32[32,512]{1,0:T(8,128)S(1)}, f32[32,512]{1,0:T(8,128)S(1)}, u32[]{:S(2)}, u32[]{:S(2)}) collective-permute-start(f32[32,512]{1,0:T(8,128)S(1)} %get-tuple-element.15), channel_id=1, source_target_pairs={{0,64},{4,68},{8,72},{12,76},{16,80},{20,84},{24,88},{28,92},{32,9... | collective-permute-start | bytes 196616 | tf_op jit(solution)/shard_map/ppermute | solution.py:37
  196.8 3.2 %collective-permute-start.28 = (f32[32,512]{1,0:T(8,128)S(1)}, f32[32,512]{1,0:T(8,128)S(1)}, u32[]{:S(2)}, u32[]{:S(2)}) collective-permute-start(f32[32,512]{1,0:T(8,128)S(1)} %get-tuple-element.26), channel_id=1, source_target_pairs={{0,128},{4,132},{8,136},{12,140},{16,144},{20,148},{24,152},{28,15... | collective-permute-start | bytes 196616 | tf_op jit(solution)/shard_map/ppermute | solution.py:37
  202.1 3.2 %collective-permute-start.26 = (f32[32,512]{1,0:T(8,128)S(1)}, f32[32,512]{1,0:T(8,128)S(1)}, u32[]{:S(2)}, u32[]{:S(2)}) collective-permute-start(f32[32,512]{1,0:T(8,128)S(1)} %add.51), channel_id=1, source_target_pairs={{0,128},{4,132},{8,136},{12,140},{16,144},{20,148},{24,152},{28,15... | collective-permute-start | bytes 196616 | tf_op jit(solution)/shard_map/ppermute | solution.py:37
  208.4 4.8 %collective-permute-start.29 = (f32[32,512]{1,0:T(8,128)S(1)}, f32[32,512]{1,0:T(8,128)S(1)}, u32[]{:S(2)}, u32[]{:S(2)}) collective-permute-start(f32[32,512]{1,0:T(8,128)S(1)} %get-tuple-element.16), channel_id=1, source_target_pairs={{0,256},{4,260},{8,264},{12,268},{16,272},{20,276},{24,280},{28,28... | collective-permute-start | bytes 196616 | tf_op jit(solution)/shard_map/ppermute | solution.py:37
  214.9 5.0 %shard_map.99 = f32[32,2048]{1,0:T(8,128)S(1)} custom-call(s32[1]{0:T(128)} %bitcast.5.plane, f32[32,512]{1,0:T(8,128)S(1)} %add.55.right, f32[32,512]{1,0:T(8,128)S(1)} %get-tuple-element.17.z1, f32[32,512]{1,0:T(8,128)S(1)} %get-tuple-element.18.z2, f32[32,512]{1,0:T(8,128)S(1)} %get-tuple-element.19.z3, ...), custom_call_target="tpu_custom_call" | custom-call | tf_op jit(solution)/shard_map/pallas_call | solution.py:195
  221.9 5.2 %collective-permute-done.30 = f32[1,1,32,2048]{3,2,1,0:T(8,128)S(1)} collective-permute-done((f32[1,1,32,2048]{3,2,1,0:T(8,128)S(1)}, f32[1,1,32,2048]{3,2,1,0:T(8,128)S(1)}, u32[]{:S(2)}, u32[]{:S(2)}) %collective-permute-start.30) | collective-permute-done | bytes 262176 | tf_op jit(solution)/shard_map/ppermute | solution.py:37
  227.2 11.2 %collective-permute-start.31 = (f32[2,32,2048]{2,1,0:T(8,128)S(1)}, f32[2,32,2048]{2,1,0:T(8,128)S(1)}, u32[]{:S(2)}, u32[]{:S(2)}) collective-permute-start(f32[2,32,2048]{2,1,0:T(8,128)S(1)} %maximum_bitcast_fusion), channel_id=1, source_target_pairs={{0,4},{4,0},{8,12},{12,8},{16,20},{20,16},{24,28},{28,24},{32,36},... | collective-permute-start | bytes 1572872 | tf_op jit(solution)/shard_map/ppermute | solution.py:37
  240.0 4.8 %shard_map.100 = (f32[896,128]{1,0:T(8,128)}, f32[176,128]{1,0:T(8,128)}) custom-call(s32[5]{0:T(128)S(1)} %stack.26.where, s32[1,21]{1,0:T(1,128)S(1)} %copy-done.16, f32[896,128]{1,0:T(8,128)S(1)} %copy-done.13, f32[4,32,2048]{2,1,0:T(8,128)S(1)} %pad_maximum_fusion.x, f32[7,128,128]{2,1,0:T(8,128)S(1)} %copy-done.11, f32[21,128,128]{2,1,0:T(8,128)S(1)} %copy-done.1, ...), custom_call_target="tpu_custom_call" | custom-call | tf_op jit(solution)/shard_map/pallas_call | solution.py:282
  (110 shorter events, 60.3 us)
Async XLA Ops:
  12.8 92.7 %all-to-all-start = ((f32[4,32,2048]{2,1,0:T(8,128)}), f32[4,32,2048]{2,1,0:T(8,128)}, u32[]{:S(2)}, u32[]{:S(2)}) async-start(f32[4,32,2048]{2,1,0:T(8,128)} %bitcast.6), calls=%async_computation | async-start | bytes 2097152 | tf_op jit(solution)/shard_map/all_to_all | solution.py:251
  24.1 5.8 %collective-permute-start.12 = (f32[1,4,128]{2,1,0:T(4,128)S(1)}, f32[1,4,128]{2,1,0:T(4,128)S(1)}, u32[]{:S(2)}, u32[]{:S(2)}) collective-permute-start(f32[1,4,128]{2,1,0:T(4,128)S(1)} %slice_bitcast_fusion.6), channel_id=1, source_target_pairs={{0,256},{4,260},{8,264},{12,268},{16,272},{20,276},{24,280},{28,28... | collective-permute-start | bytes 6152 | tf_op jit(solution)/shard_map/ppermute | solution.py:37
  34.7 13.3 %collective-permute-start.14 = (f32[3,16,128]{2,1,0:T(8,128)S(1)}, f32[3,16,128]{2,1,0:T(8,128)S(1)}, u32[]{:S(2)}, u32[]{:S(2)}) collective-permute-start(f32[3,16,128]{2,1,0:T(8,128)S(1)} %pad_maximum_fusion.7), channel_id=1, source_target_pairs={{0,64},{4,68},{8,72},{12,76},{16,80},{20,84},{24,88},{28,92},{32,9... | collective-permute-start | bytes 73736 | tf_op jit(solution)/shard_map/ppermute | solution.py:37
  48.1 11.7 %collective-permute-start.15 = (f32[5,32,128]{2,1,0:T(8,128)S(1)}, f32[5,32,128]{2,1,0:T(8,128)S(1)}, u32[]{:S(2)}, u32[]{:S(2)}) collective-permute-start(f32[5,32,128]{2,1,0:T(8,128)S(1)} %pad_maximum_fusion.6), channel_id=1, source_target_pairs={{0,32},{4,36},{8,40},{12,44},{16,48},{20,52},{24,56},{28,60},{32,0... | collective-permute-start | bytes 245768 | tf_op jit(solution)/shard_map/ppermute | solution.py:37
  59.8 7.3 %collective-permute-start.16 = (f32[5,64,128]{2,1,0:T(8,128)S(1)}, f32[5,64,128]{2,1,0:T(8,128)S(1)}, u32[]{:S(2)}, u32[]{:S(2)}) collective-permute-start(f32[5,64,128]{2,1,0:T(8,128)S(1)} %pad_maximum_fusion.4), channel_id=1, source_target_pairs={{0,16},{4,20},{8,24},{12,28},{16,0},{20,4},{24,8},{28,12},{32,48},... | collective-permute-start | bytes 491528 | tf_op jit(solution)/shard_map/ppermute | solution.py:37
  61.7 7.3 %collective-permute-start = (f32[2,128,128]{2,1,0:T(8,128)S(1)}, f32[2,128,128]{2,1,0:T(8,128)S(1)}, u32[]{:S(2)}, u32[]{:S(2)}) collective-permute-start(f32[2,128,128]{2,1,0:T(8,128)S(1)} %pad_maximum_fusion.5), channel_id=1, source_target_pairs={{0,8},{4,12},{8,0},{12,4},{16,24},{20,28},{24,16},{28,20},{32,40},... | collective-permute-start | bytes 393224 | tf_op jit(solution)/shard_map/ppermute | solution.py:37
  67.1 20.2 %collective-permute-start.17 = (f32[5,128,128]{2,1,0:T(8,128)S(1)}, f32[5,128,128]{2,1,0:T(8,128)S(1)}, u32[]{:S(2)}, u32[]{:S(2)}) collective-permute-start(f32[5,128,128]{2,1,0:T(8,128)S(1)} %pad_maximum_fusion.2), channel_id=1, source_target_pairs={{0,8},{4,12},{8,0},{12,4},{16,24},{20,28},{24,16},{28,20},{32,40},... | collective-permute-start | bytes 983048 | tf_op jit(solution)/shard_map/ppermute | solution.py:37
  69.1 20.2 %collective-permute-start.1 = (f32[2,256,128]{2,1,0:T(8,128)S(1)}, f32[2,256,128]{2,1,0:T(8,128)S(1)}, u32[]{:S(2)}, u32[]{:S(2)}) collective-permute-start(f32[2,256,128]{2,1,0:T(8,128)S(1)} %pad_maximum_fusion.3.refs_0_.refs_8_.refs_40_.refs_48_), channel_id=1, source_target_pairs={{0,1},{1,0},{2,3},{3,2},{4,5},{5,4},{6,7},{7,6},{8,9},{9,8},{10,11... | collective-permute-start | bytes 786440 | tf_op jit(solution)/shard_map/ppermute | solution.py:37
  71.0 22.9 %collective-permute-start.2 = (f32[2,256,128]{2,1,0:T(8,128)S(1)}, f32[2,256,128]{2,1,0:T(8,128)S(1)}, u32[]{:S(2)}, u32[]{:S(2)}) collective-permute-start(f32[2,256,128]{2,1,0:T(8,128)S(1)} %pad_maximum_fusion.3.refs_0_.refs_8_.refs_40_.refs_48_), channel_id=1, source_target_pairs={{0,2},{1,3},{2,0},{3,1},{4,6},{5,7},{6,4},{7,5},{8,10},{9,11},{10,... | collective-permute-start | bytes 786440 | tf_op jit(solution)/shard_map/ppermute | solution.py:37
  74.6 22.4 %collective-permute-start.3 = (f32[2,256,128]{2,1,0:T(8,128)S(1)}, f32[2,256,128]{2,1,0:T(8,128)}, u32[]{:S(2)}, u32[]{:S(2)}) collective-permute-start(f32[2,256,128]{2,1,0:T(8,128)S(1)} %pad_maximum_fusion.3.refs_0_.refs_8_.refs_40_.refs_48_), channel_id=1, source_target_pairs={{0,3},{1,2},{2,1},{3,0},{4,7},{5,6},{6,5},{7,4},{8,11},{9,10},{10,... | collective-permute-start | bytes 786440 | tf_op jit(solution)/shard_map/ppermute | solution.py:37
  78.7 21.1 %collective-permute-start.4 = (f32[2,256,128]{2,1,0:T(8,128)S(1)}, f32[2,256,128]{2,1,0:T(8,128)S(1)}, u32[]{:S(2)}, u32[]{:S(2)}) collective-permute-start(f32[2,256,128]{2,1,0:T(8,128)S(1)} %pad_maximum_fusion.3.refs_0_.refs_8_.refs_40_.refs_48_), channel_id=1, source_target_pairs={{0,4},{4,0},{8,12},{12,8},{16,20},{20,16},{24,28},{28,24},{32,36},... | collective-permute-start | bytes 786440 | tf_op jit(solution)/shard_map/ppermute | solution.py:37
  87.3 27.4 %collective-permute-start.18 = (f32[5,256,128]{2,1,0:T(8,128)S(1)}, f32[5,256,128]{2,1,0:T(8,128)S(1)}, u32[]{:S(2)}, u32[]{:S(2)}) collective-permute-start(f32[5,256,128]{2,1,0:T(8,128)S(1)} %pad_maximum_fusion.1.refs_0_.refs_8_.refs_16_.refs_24_.refs_32_), channel_id=1, source_target_pairs={{0,1},{1,0},{2,3},{3,2},{4,5},{5,4},{6,7},{7,6},{8,9},{9,8},{10,11... | collective-permute-start | bytes 1966088 | tf_op jit(solution)/shard_map/ppermute | solution.py:37
  89.3 31.7 %collective-permute-start.19 = (f32[5,256,128]{2,1,0:T(8,128)S(1)}, f32[5,256,128]{2,1,0:T(8,128)S(1)}, u32[]{:S(2)}, u32[]{:S(2)}) collective-permute-start(f32[5,256,128]{2,1,0:T(8,128)S(1)} %pad_maximum_fusion.1.refs_0_.refs_8_.refs_16_.refs_24_.refs_32_), channel_id=1, source_target_pairs={{0,2},{1,3},{2,0},{3,1},{4,6},{5,7},{6,4},{7,5},{8,10},{9,11},{10,... | collective-permute-start | bytes 1966088 | tf_op jit(solution)/shard_map/ppermute | solution.py:37
  93.9 32.9 %collective-permute-start.20 = (f32[5,256,128]{2,1,0:T(8,128)S(1)}, f32[5,256,128]{2,1,0:T(8,128)S(1)}, u32[]{:S(2)}, u32[]{:S(2)}) collective-permute-start(f32[5,256,128]{2,1,0:T(8,128)S(1)} %pad_maximum_fusion.1.refs_0_.refs_8_.refs_16_.refs_24_.refs_32_), channel_id=1, source_target_pairs={{0,3},{1,2},{2,1},{3,0},{4,7},{5,6},{6,5},{7,4},{8,11},{9,10},{10,... | collective-permute-start | bytes 1966088 | tf_op jit(solution)/shard_map/ppermute | solution.py:37
  97.0 5.4 %collective-permute-start.5 = (f32[2,256,128]{2,1,0:T(8,128)S(1)}, f32[2,256,128]{2,1,0:T(8,128)S(1)}, u32[]{:S(2)}, u32[]{:S(2)}) collective-permute-start(f32[2,256,128]{2,1,0:T(8,128)S(1)} %collective-permute-done.1.refs_1_.refs_9_.refs_41_.refs_49_), channel_id=1, source_target_pairs={{0,4},{4,0},{8,12},{12,8},{16,20},{20,16},{24,28},{28,24},{32,36},... | collective-permute-start | bytes 786440 | tf_op jit(solution)/shard_map/ppermute | solution.py:37
  100.5 8.0 %collective-permute-start.6 = (f32[2,256,128]{2,1,0:T(8,128)S(1)}, f32[2,256,128]{2,1,0:T(8,128)}, u32[]{:S(2)}, u32[]{:S(2)}) collective-permute-start(f32[2,256,128]{2,1,0:T(8,128)S(1)} %collective-permute-done.2.refs_2_.refs_10_.refs_42_.refs_50_), channel_id=1, source_target_pairs={{0,4},{4,0},{8,12},{12,8},{16,20},{20,16},{24,28},{28,24},{32,36},... | collective-permute-start | bytes 786440 | tf_op jit(solution)/shard_map/ppermute | solution.py:37
  103.1 9.4 %collective-permute-start.7 = (f32[2,256,128]{2,1,0:T(8,128)}, f32[2,256,128]{2,1,0:T(8,128)}, u32[]{:S(2)}, u32[]{:S(2)}) collective-permute-start(f32[2,256,128]{2,1,0:T(8,128)} %collective-permute-done.3.refs_3_.refs_11_.refs_43_.refs_51_), channel_id=1, source_target_pairs={{0,4},{4,0},{8,12},{12,8},{16,20},{20,16},{24,28},{28,24},{32,36},... | collective-permute-start | bytes 786440 | tf_op jit(solution)/shard_map/ppermute | solution.py:37
  108.5 25.7 %collective-permute-start.10 = (f32[32,1024]{1,0:T(8,128)S(1)}, f32[32,1024]{1,0:T(8,128)S(1)}, u32[]{:S(2)}, u32[]{:S(2)}) collective-permute-start(f32[32,1024]{1,0:T(8,128)S(1)} %concatenate.51), channel_id=1, source_target_pairs={{0,16},{4,20},{8,24},{12,28},{16,0},{20,4},{24,8},{28,12},{32,48},... | collective-permute-start | bytes 393224 | tf_op jit(solution)/shard_map/ppermute | solution.py:37
  112.5 74.9 %collective-permute-start.21 = (f32[5,256,128]{2,1,0:T(8,128)S(1)}, f32[5,256,128]{2,1,0:T(8,128)S(1)}, u32[]{:S(2)}, u32[]{:S(2)}) collective-permute-start(f32[5,256,128]{2,1,0:T(8,128)S(1)} %pad_maximum_fusion.1.refs_0_.refs_8_.refs_16_.refs_24_.refs_32_), channel_id=1, source_target_pairs={{0,4},{4,0},{8,12},{12,8},{16,20},{20,16},{24,28},{28,24},{32,36},... | collective-permute-start | bytes 1966088 | tf_op jit(solution)/shard_map/ppermute | solution.py:37
  114.7 72.7 %collective-permute-start.22 = (f32[5,256,128]{2,1,0:T(8,128)S(1)}, f32[5,256,128]{2,1,0:T(8,128)S(1)}, u32[]{:S(2)}, u32[]{:S(2)}) collective-permute-start(f32[5,256,128]{2,1,0:T(8,128)S(1)} %collective-permute-done.18.refs_1_.refs_9_.refs_17_.refs_25_.refs_33_), channel_id=1, source_target_pairs={{0,4},{4,0},{8,12},{12,8},{16,20},{20,16},{24,28},{28,24},{32,36},... | collective-permute-start | bytes 1966088 | tf_op jit(solution)/shard_map/ppermute | solution.py:37
  121.0 66.4 %collective-permute-start.23 = (f32[5,256,128]{2,1,0:T(8,128)S(1)}, f32[5,256,128]{2,1,0:T(8,128)S(1)}, u32[]{:S(2)}, u32[]{:S(2)}) collective-permute-start(f32[5,256,128]{2,1,0:T(8,128)S(1)} %collective-permute-done.19.refs_2_.refs_10_.refs_18_.refs_26_.refs_34_), channel_id=1, source_target_pairs={{0,4},{4,0},{8,12},{12,8},{16,20},{20,16},{24,28},{28,24},{32,36},... | collective-permute-start | bytes 1966088 | tf_op jit(solution)/shard_map/ppermute | solution.py:37
  126.8 60.6 %collective-permute-start.24 = (f32[5,256,128]{2,1,0:T(8,128)S(1)}, f32[5,256,128]{2,1,0:T(8,128)S(1)}, u32[]{:S(2)}, u32[]{:S(2)}) collective-permute-start(f32[5,256,128]{2,1,0:T(8,128)S(1)} %collective-permute-done.20.refs_3_.refs_11_.refs_19_.refs_27_.refs_35_), channel_id=1, source_target_pairs={{0,4},{4,0},{8,12},{12,8},{16,20},{20,16},{24,28},{28,24},{32,36},... | collective-permute-start | bytes 1966088 | tf_op jit(solution)/shard_map/ppermute | solution.py:37
  134.2 6.5 %collective-permute-start.8 = (f32[32,512]{1,0:T(8,128)S(1)}, f32[32,512]{1,0:T(8,128)S(1)}, u32[]{:S(2)}, u32[]{:S(2)}) collective-permute-start(f32[32,512]{1,0:T(8,128)S(1)} %get-tuple-element.14), channel_id=1, source_target_pairs={{0,16},{4,20},{8,24},{12,28},{16,0},{20,4},{24,8},{28,12},{32,48},... | collective-permute-start | bytes 196616 | tf_op jit(solution)/shard_map/ppermute | solution.py:37
  140.8 19.7 %collective-permute-start.11 = (f32[32,1024]{1,0:T(8,128)S(1)}, f32[32,1024]{1,0:T(8,128)S(1)}, u32[]{:S(2)}, u32[]{:S(2)}) collective-permute-start(f32[32,1024]{1,0:T(8,128)S(1)} %slice_add_fusion.1), channel_id=1, source_target_pairs={{0,32},{4,36},{8,40},{12,44},{16,48},{20,52},{24,56},{28,60},{32,0... | collective-permute-start | bytes 393224 | tf_op jit(solution)/shard_map/ppermute | solution.py:37
  160.5 11.9 %collective-permute-start.9 = (f32[32,512]{1,0:T(8,128)S(1)}, f32[32,512]{1,0:T(8,128)S(1)}, u32[]{:S(2)}, u32[]{:S(2)}) collective-permute-start(f32[32,512]{1,0:T(8,128)S(1)} %add.47), channel_id=1, source_target_pairs={{0,32},{4,36},{8,40},{12,44},{16,48},{20,52},{24,56},{28,60},{32,0... | collective-permute-start | bytes 196616 | tf_op jit(solution)/shard_map/ppermute | solution.py:37
  172.4 15.0 %collective-permute-start.27 = (f32[32,512]{1,0:T(8,128)S(1)}, f32[32,512]{1,0:T(8,128)S(1)}, u32[]{:S(2)}, u32[]{:S(2)}) collective-permute-start(f32[32,512]{1,0:T(8,128)S(1)} %slice.72), channel_id=1, source_target_pairs={{0,64},{4,68},{8,72},{12,76},{16,80},{20,84},{24,88},{28,92},{32,9... | collective-permute-start | bytes 196616 | tf_op jit(solution)/shard_map/ppermute | solution.py:37
  188.4 13.7 %collective-permute-start.25 = (f32[32,512]{1,0:T(8,128)S(1)}, f32[32,512]{1,0:T(8,128)S(1)}, u32[]{:S(2)}, u32[]{:S(2)}) collective-permute-start(f32[32,512]{1,0:T(8,128)S(1)} %get-tuple-element.15), channel_id=1, source_target_pairs={{0,64},{4,68},{8,72},{12,76},{16,80},{20,84},{24,88},{28,92},{32,9... | collective-permute-start | bytes 196616 | tf_op jit(solution)/shard_map/ppermute | solution.py:37
  196.8 8.6 %collective-permute-start.28 = (f32[32,512]{1,0:T(8,128)S(1)}, f32[32,512]{1,0:T(8,128)S(1)}, u32[]{:S(2)}, u32[]{:S(2)}) collective-permute-start(f32[32,512]{1,0:T(8,128)S(1)} %get-tuple-element.26), channel_id=1, source_target_pairs={{0,128},{4,132},{8,136},{12,140},{16,144},{20,148},{24,152},{28,15... | collective-permute-start | bytes 196616 | tf_op jit(solution)/shard_map/ppermute | solution.py:37
  202.1 5.3 %collective-permute-start.26 = (f32[32,512]{1,0:T(8,128)S(1)}, f32[32,512]{1,0:T(8,128)S(1)}, u32[]{:S(2)}, u32[]{:S(2)}) collective-permute-start(f32[32,512]{1,0:T(8,128)S(1)} %add.51), channel_id=1, source_target_pairs={{0,128},{4,132},{8,136},{12,140},{16,144},{20,148},{24,152},{28,15... | collective-permute-start | bytes 196616 | tf_op jit(solution)/shard_map/ppermute | solution.py:37
  208.4 6.5 %collective-permute-start.29 = (f32[32,512]{1,0:T(8,128)S(1)}, f32[32,512]{1,0:T(8,128)S(1)}, u32[]{:S(2)}, u32[]{:S(2)}) collective-permute-start(f32[32,512]{1,0:T(8,128)S(1)} %get-tuple-element.16), channel_id=1, source_target_pairs={{0,256},{4,260},{8,264},{12,268},{16,272},{20,276},{24,280},{28,28... | collective-permute-start | bytes 196616 | tf_op jit(solution)/shard_map/ppermute | solution.py:37
  220.0 7.1 %collective-permute-start.30 = (f32[1,1,32,2048]{3,2,1,0:T(8,128)S(1)}, f32[1,1,32,2048]{3,2,1,0:T(8,128)S(1)}, u32[]{:S(2)}, u32[]{:S(2)}) collective-permute-start(f32[1,1,32,2048]{3,2,1,0:T(8,128)S(1)} %bitcast.27), channel_id=1, source_target_pairs={{0,8},{4,12},{8,0},{12,4},{16,24},{20,28},{24,16},{28,20},{32,40},... | collective-permute-start | bytes 786440 | tf_op jit(solution)/shard_map/ppermute | solution.py:37
  227.2 12.6 %collective-permute-start.31 = (f32[2,32,2048]{2,1,0:T(8,128)S(1)}, f32[2,32,2048]{2,1,0:T(8,128)S(1)}, u32[]{:S(2)}, u32[]{:S(2)}) collective-permute-start(f32[2,32,2048]{2,1,0:T(8,128)S(1)} %maximum_bitcast_fusion), channel_id=1, source_target_pairs={{0,4},{4,0},{8,12},{12,8},{16,20},{20,16},{24,28},{28,24},{32,36},... | collective-permute-start | bytes 1572872 | tf_op jit(solution)/shard_map/ppermute | solution.py:37
  (21 other events, 122.6 us)

commit v2 on v1

v2 whole, which is shorter than its diff:
```python
import functools

import jax
import jax.numpy as jnp
from jax import lax
from jax.experimental import pallas as pl
from jax.experimental.pallas import tpu as pltpu
from jax.sharding import PartitionSpec as P

F32 = jnp.float32
BF16 = jnp.bfloat16
NN = (((1,), (0,)), ((), ()))
NT = (((1,), (1,)), ((), ()))
TN = (((0,), (0,)), ((), ()))
LEVELS = 4
Z1, Z2, Z4, Z8, Y1, Y2 = range(1, 7)
CORE_MASK = 1


def halves(value):
    high = value.astype(BF16)
    low = (value - high.astype(F32)).astype(BF16)
    return high, low


def mm(left, right, dims):
    left_high, left_low = halves(left)
    right_high, right_low = halves(right)
    dot = functools.partial(lax.dot_general, dimension_numbers=dims, preferred_element_type=F32)
    return dot(left_high, right_high) + (dot(left_high, right_low) + dot(left_low, right_high))


def exact(left, right, dims):
    return lax.dot_general(left, right, dims, precision=lax.Precision.HIGHEST, preferred_element_type=F32)


def swap(value, axis, mask):
    return lax.ppermute(value, axis, [(i, i ^ mask) for i in range(lax.axis_size(axis))])


def across(value, mask):
    return swap(value, "leaf", mask)


def grow(value, mask):
    return jnp.concatenate([value, across(value, mask)], axis=1)


def pair_starts(blocks):
    starts, running = [], 0
    for column in range(blocks):
        starts.append(running)
        running += blocks - 1 - column
    return starts


def placement(rows, offset, count, start, width):
    row = lax.broadcasted_iota(jnp.int32, (rows, width), 0)
    column = lax.broadcasted_iota(jnp.int32, (rows, width), 1)
    inside = (row >= offset) & (row < offset + count)
    return jnp.where(inside & (row - offset == column - start), 1.0, 0.0).astype(F32)


def forward_kernel(sizes, where, pattern, rhs, inverse, blocks, coupling, sep_rhs, y_out, t_out):
    count, size = inverse.shape[0], inverse.shape[1]
    starts = pair_starts(count)
    pending = [rhs[i * size : (i + 1) * size, :] for i in range(count)]
    for column in range(count):
        solved = mm(inverse[column], pending[column], NN)
        y_out[column * size : (column + 1) * size, :] = solved
        for later in range(column + 1, count):
            pair = starts[column] + later - column - 1
            weight = pattern[0, pair].astype(F32)
            pending[later] = pending[later] - weight * mm(blocks[pair], solved, NN)
    last = y_out[(count - 1) * size :, :]
    right = sep_rhs[...]
    width = coupling.shape[1]
    offset = 0
    for level, rows in enumerate(sizes):
        spread = placement(right.shape[0], offset, rows, where[level], width)
        offset += rows
        t_out[:, level * width : (level + 1) * width] = exact(right, spread, TN) - mm(
            last, coupling[level * size : (level + 1) * size, :], TN
        )


def backward_kernel(sizes, where, pattern, y, x, inverse, blocks, coupling, out, sep_out):
    count, size = inverse.shape[0], inverse.shape[1]
    starts = pair_starts(count)
    width = coupling.shape[1]
    place = where[LEVELS]
    quarter = x.shape[0]
    xs = jnp.concatenate([x[jnp.bitwise_xor(place, q)] for q in range(quarter)], axis=0)
    correction = jnp.zeros((size, y.shape[1]), F32)
    pieces = jnp.zeros((sep_out.shape[0], y.shape[1]), F32)
    offset = 0
    for level, rows in enumerate(sizes):
        part = xs[:, level * width : (level + 1) * width]
        correction = correction + mm(coupling[level * size : (level + 1) * size, :], part, NT)
        spread = placement(sep_out.shape[0], offset, rows, where[level], width)
        pieces = pieces + exact(spread, part, NT)
        offset += rows
    sep_out[...] = pieces
    pending = [y[i * size : (i + 1) * size, :] for i in range(count)]
    pending[-1] = pending[-1] - correction
    for column in reversed(range(count)):
        solved = mm(inverse[column], pending[column], TN)
        out[column * size : (column + 1) * size, :] = solved
        for earlier in reversed(range(column)):
            pair = starts[earlier] + column - earlier - 1
            weight = pattern[0, pair].astype(F32)
            pending[earlier] = pending[earlier] - weight * mm(blocks[pair], solved, TN)


def times_rows(value, mats, index):
    result = []
    for half in mats:
        total = None
        for r in range(half.shape[0]):
            term = mm(value[:, r * 128 : (r + 1) * 128], half[r, index], NT)
            total = term if total is None else total + term
        result.append(total)
    return result


def times_matrix(value, mats, index, r):
    total = None
    for piece, half in zip(value, mats):
        term = mm(piece, half[r, index], NN)
        total = term if total is None else total + term
    return total


def level_kernel(index, right, base, mine, other, z_out, v_out):
    mats = (mine, other)
    z = times_rows(right, mats, index)
    z_out[...] = jnp.concatenate(z, axis=1)
    for r in range(mine.shape[0]):
        spot = slice(r * 128, (r + 1) * 128)
        v_out[:, spot] = base[:, spot] - times_matrix(z, mats, index + 1, r)


def top_kernel(right, z1, z2, z3, m1, o1, m2, o2, m3, o3, x_out):
    width = right.shape[1]
    top = (m3, o3)
    z = times_rows(right, top, 0)
    order = [(z3, top, 1), (z2, (m2, o2), 0), (z1, (m1, o1), 0)]
    mats, index = top, 0
    level = 3
    while True:
        for r in range(mats[0].shape[0]):
            start = level * width + r * 128
            x_out[:, start : start + 128] = times_matrix(z, mats, index, r)
        if not order:
            break
        held, mats, index = order.pop(0)
        moved = times_rows(x_out[:, level * width : (level + 1) * width], mats, index + 1)
        half = held.shape[1] // 2
        z = [held[:, :half] - moved[0], held[:, half:] - moved[1]]
        level -= 1


SMEM = pl.BlockSpec(memory_space=pltpu.SMEM)
VMEM = pl.BlockSpec(memory_space=pltpu.VMEM)


def params():
    return pltpu.CompilerParams(vmem_limit_bytes=40 * 1024 * 1024)


def call(kernel, outs, *arrays):
    return pl.pallas_call(
        kernel,
        out_shape=[jax.ShapeDtypeStruct(s, F32) for s in outs],
        in_specs=[SMEM if v.dtype == jnp.int32 else VMEM for v in arrays],
        out_specs=[VMEM] * len(outs),
        compiler_params=params(),
    )(*arrays)


def shards(leaf_rhs, leaf_inverse, leaf_blocks, leaf_pattern, leaf_coupling, sep_rhs, sep_inverse, sep_coupling):
    position = lax.axis_index("leaf")
    columns = leaf_rhs.shape[1]
    width = leaf_coupling.shape[1]
    leaves = lax.axis_size("leaf")
    groups = [4, 16, 64, 128]
    sizes = [width // g for g in groups]
    offsets = [sum(sizes[:i]) for i in range(LEVELS)]
    where = jnp.stack([position % g * r for g, r in zip(groups, sizes)] + [position % 4]).astype(jnp.int32)

    def rows(array, level):
        return array[offsets[level] : offsets[level] + sizes[level]]

    def both(level):
        return jnp.stack([rows(sep_inverse, level), rows(sep_coupling, level)])

    count = leaves // 4
    far = jnp.concatenate([rows(sep_inverse, 2), rows(sep_coupling, 2), rows(sep_inverse, 3)], 0)
    far = jnp.broadcast_to(far[None], (count, *far.shape))
    apart = [[m + 4 * k for k in range(count)] for m in range(4)]
    far = lax.all_to_all(far, "leaf", 0, 0, axis_index_groups=apart, tiled=True)

    first = grow(both(0), 1 << Z1)
    second = grow(both(1), 1 << Z4)
    padded = jnp.pad(sep_rhs, ((0, 4), (0, 0)))
    where, first, second = lax.optimization_barrier((where, first, second))
    y, t = call(
        functools.partial(forward_kernel, sizes),
        [leaf_rhs.shape, (columns, LEVELS * width)],
        where, leaf_pattern, leaf_rhs, leaf_inverse, leaf_blocks, leaf_coupling, padded,
    )
    first = lax.all_gather(first, "col", axis=0)
    near = [[g * 4 + m for m in range(4)] for g in range(leaves // 4)]
    second = grow(second, 1 << Z2)
    far, second, t = lax.optimization_barrier((far, second, t))
    t = lax.all_to_all(t, "leaf", 0, 0, axis_index_groups=near, tiled=True)
    t = t.reshape(4, columns // 4, LEVELS * width).sum(0)
    upper = t[:, 2 * width :]
    upper = upper + across(upper, 1 << Z2)
    first, upper = lax.optimization_barrier((first, upper))
    upper = upper + across(upper, 1 << Z4)
    first = (first, across(first, CORE_MASK))
    second = lax.all_gather(grow(second, 1 << Z1), "col", axis=0)
    own = lax.dynamic_slice_in_dim(far, position // 64 * 16, 16, 0)
    third = [
        far[:, 2 * sizes[2] :].reshape(-1, 128),
        own[:, : sizes[2]].reshape(-1, 128),
        own[:, sizes[2] : 2 * sizes[2]].reshape(-1, 128),
    ]
    third = lax.all_gather(grow(jnp.stack(third), 1 << Z1), "col", axis=0)

    t1, t2 = t[:, :width], t[:, width : 2 * width]
    t3, t4 = upper[:, :width], upper[:, width:]

    def total(value, *masks):
        for mask in masks:
            value = value + across(value, mask)
        return value

    shape = t1.shape
    halves_z, wrap_z, wrap_y = 1 << Z4, (1 << Z8) | (1 << Z4) | (1 << Z2), (1 << Y2) | (1 << Y1)
    t4 = total(t4, wrap_z, 1 << Y1)
    z1, v = call(functools.partial(level_kernel, 0), [shape] * 2, t1, t2, *first)
    v = total(v, 1 << Z2)
    v, second = lax.optimization_barrier((v, second))
    second = (second, across(second, CORE_MASK))
    v = total(v, halves_z)
    z2, v = call(functools.partial(level_kernel, 0), [shape] * 2, v, t3, *second)
    v, third = lax.optimization_barrier((v, third))
    third = (third, across(third, CORE_MASK))
    v = total(v, wrap_z, 1 << Y1)
    z3, v = call(functools.partial(level_kernel, 1), [shape] * 2, v, t4, *third)
    v = total(v, wrap_y)
    (x,) = call(top_kernel, [(shape[0], LEVELS * width)], v, z1, z2, z3, *first, *second, *third)
    x = jnp.stack([x, across(x, 1 << Z1)])
    other = across(x, CORE_MASK)
    x = jnp.stack([x[0], other[0], x[1], other[1]], 0)
    return call(
        functools.partial(backward_kernel, sizes),
        [leaf_rhs.shape, padded.shape],
        where, leaf_pattern, y, x, leaf_inverse, leaf_blocks, leaf_coupling,
    )


def program(*arrays):
    leaf, sep = shards(*arrays)
    return leaf, sep[: arrays[5].shape[0]]


def solution(mesh):
    return jax.shard_map(
        program,
        mesh=mesh,
        in_specs=(
            P("leaf", "col"),
            P("leaf", None, None),
            P("leaf", None, None),
            P("leaf", None),
            P("leaf", None),
            P("leaf", "col"),
            P("leaf", "col"),
            P("leaf", "col"),
        ),
        out_specs=(P("leaf", "col"), P("leaf", "col")),
        check_vma=False,
    )
```

time: 246 us -> 244 us (level)
  starting transfers between devices: 138 us -> 105 us
  between operations: 1.39 us -> 14.3 us
  other arithmetic: 2.43 us -> 12.7 us
  local copies, waits for them, and re-layouts: 12.2 us -> 18.8 us
  Pallas kernels: 19.1 us -> 16.2 us
    ppermute x32 -> x19, starting transfers between devices: 126 us -> 81 us  [swap(): lax.ppermute(value, axis, [(i, i ^ mask) for i in range(lax.axis_size(axi...]
    all_to_all x0 -> x1, starting transfers between devices: none -> 18.7 us  [shards(): far = lax.all_to_all(far, 'leaf', 0, 0, axis_index_groups=apart, tiled=True)]
    all_gather x0 -> x3, waiting for transfers between devices: none -> 12.6 us  [the longest x1 12.6 us: shards(): second = lax.all_gather(grow(second, 1 << Z1), 'col', axis=0)]
    ppermute x32 -> x19, waiting for transfers between devices: 72.1 us -> 60.6 us  [swap(): lax.ppermute(value, axis, [(i, i ^ mask) for i in range(lax.axis_size(axi...]
    add x9, other arithmetic: 0.12 us -> 6.37 us  [the longest x7 3.86 us: total(): value = value + across(value, mask)]
    all_to_all x1, starting transfers between devices: 11.2 us -> 5.21 us  [shards(): t = lax.all_to_all(t, 'leaf', 0, 0, axis_index_groups=near, tiled=True)]
    concatenate x8 -> x6, other arithmetic: 0.14 us -> 4.76 us  [the longest x5 4.75 us: grow(): return jnp.concatenate([value, across(value, mask)], axis=1)]
    slice x1 -> x6, local copies, waits for them, and re-layouts: 0.88 us -> 4.13 us  [the longest x3 2.22 us: rows(): return array[offsets[level]:offsets[level] + sizes[level]]]
  transfers between devices with their start and end apart: 33 -> 24, of which waited for: 16 -> 14; matrix products, arithmetic and copies ran while one was open for 2% -> 7% of each run, Pallas kernels for 1% -> 3%
where the time goes in v2:
time: 244 us; the launch traced here: 241 us
  starting transfers between devices  105 us (43%)
  waiting for transfers between devices  73.9 us (30%)
  local copies, waits for them, and re-layouts  18.8 us (8%)
  Pallas kernels  16.2 us (7%)
  between operations  14.3 us (6%)
  other arithmetic  12.7 us (5%)
    ppermute x19, starting transfers between devices, swap(): lax.ppermute(value, axis, [(i, i ^ mask) for i in range(lax.axis_size(axi...  81 us
    ppermute x19, waiting for transfers between devices, swap(): lax.ppermute(value, axis, [(i, i ^ mask) for i in range(lax.axis_size(axi...  60.6 us
    all_to_all x1, starting transfers between devices, shards(): far = lax.all_to_all(far, 'leaf', 0, 0, axis_index_groups=apart, tiled=True)  18.7 us
    pallas_call x6, Pallas kernels, call(): pl.pallas_call(kernel, out_shape=[jax.ShapeDtypeStruct(s, F32) for s in o...  16.2 us
    all_gather x1, waiting for transfers between devices, shards(): second = lax.all_gather(grow(second, 1 << Z1), 'col', axis=0)  12.6 us
    unnamed x50, local copies, waits for them, and re-layouts  11.3 us
    all_to_all x1, starting transfers between devices, shards(): t = lax.all_to_all(t, 'leaf', 0, 0, axis_index_groups=near, tiled=True)  5.21 us
  transfers between devices with their start and end apart: 24, of which 14 were waited for; matrix products, arithmetic and copies ran while one was open for 7% of the time, Pallas kernels for 3%

profile of v2, /device:TPU:1, one launch (start us, length us, event | category | flops | bytes accessed | tf_op | source)
XLA Modules:
  0.0 241.0 jit_solution(12810133728770161140)
XLA Ops:
  10.2 18.7 %all-to-all-start = ((f32[32,20,128]{2,1,0:T(8,128)}), f32[32,20,128]{2,1,0:T(8,128)S(1)}, u32[]{:S(2)}, u32[]{:S(2)}) async-start(f32[32,20,128]{2,1,0:T(8,128)} %broadcast_in_dim.2), calls=%async_computation | async-start | bytes 786432 | tf_op jit(solution)/shard_map/all_to_all | solution.py:201
  29.6 7.0 %collective-permute-start.1 = (f32[2,32,128]{2,1,0:T(8,128)S(1)}, f32[2,32,128]{2,1,0:T(8,128)S(1)}, u32[]{:S(2)}, u32[]{:S(2)}) collective-permute-start(f32[2,32,128]{2,1,0:T(8,128)S(1)} %pad_maximum_fusion.9), channel_id=1, source_target_pairs={{0,32},{4,36},{8,40},{12,44},{16,48},{20,52},{24,56},{28,60},{32,0... | collective-permute-start | bytes 98312 | tf_op jit(solution)/shard_map/ppermute | solution.py:38
  37.6 2.6 %collective-permute-start = (f32[2,128,128]{2,1,0:T(8,128)S(1)}, f32[2,128,128]{2,1,0:T(8,128)S(1)}, u32[]{:S(2)}, u32[]{:S(2)}) collective-permute-start(f32[2,128,128]{2,1,0:T(8,128)S(1)} %pad_maximum_fusion.6), channel_id=1, source_target_pairs={{0,8},{4,12},{8,0},{12,4},{16,24},{20,28},{24,16},{28,20},{32,40},... | collective-permute-start | bytes 393224 | tf_op jit(solution)/shard_map/ppermute | solution.py:38
  40.4 11.0 %collective-permute-done.1 = f32[2,32,128]{2,1,0:T(8,128)S(1)} collective-permute-done((f32[2,32,128]{2,1,0:T(8,128)S(1)}, f32[2,32,128]{2,1,0:T(8,128)S(1)}, u32[]{:S(2)}, u32[]{:S(2)}) %collective-permute-start.1) | collective-permute-done | bytes 32800 | tf_op jit(solution)/shard_map/ppermute | solution.py:38
  52.1 4.5 %collective-permute-start.2 = (f32[2,64,128]{2,1,0:T(8,128)S(1)}, f32[2,64,128]{2,1,0:T(8,128)S(1)}, u32[]{:S(2)}, u32[]{:S(2)}) collective-permute-start(f32[2,64,128]{2,1,0:T(8,128)S(1)} %pad_maximum_fusion.8), channel_id=1, source_target_pairs={{0,16},{4,20},{8,24},{12,28},{16,0},{20,4},{24,8},{28,12},{32,48},... | collective-permute-start | bytes 196616 | tf_op jit(solution)/shard_map/ppermute | solution.py:38
  58.8 5.1 %shard_map.95 = (f32[896,128]{1,0:T(8,128)S(1)}, f32[128,2048]{1,0:T(8,128)}) custom-call(s32[5]{0:T(128)S(1)} %stack.56.where, s32[1,21]{1,0:T(1,128)S(1)} %copy-done.19, f32[896,128]{1,0:T(8,128)S(1)} %copy-done.15, f32[7,128,128]{2,1,0:T(8,128)S(1)} %copy-done.11, f32[21,128,128]{2,1,0:T(8,128)S(1)} %copy-done.2, f32[512,512]{1,0:T(8,128)S(1)} %copy-done.3, ...), custom_call_target="tpu_custom_call" | custom-call | tf_op jit(solution)/shard_map/pallas_call | solution.py:172
  66.1 5.2 %all-to-all-start.1 = ((f32[4,32,2048]{2,1,0:T(8,128)}), f32[4,32,2048]{2,1,0:T(8,128)S(1)}, u32[]{:S(2)}, u32[]{:S(2)}) async-start(f32[4,32,2048]{2,1,0:T(8,128)} %bitcast.9), calls=%async_computation.1 | async-start | bytes 2097152 | tf_op jit(solution)/shard_map/all_to_all | solution.py:216
  72.1 3.3 %collective-permute-start.6 = (f32[2,128,128]{2,1,0:T(8,128)}, f32[2,128,128]{2,1,0:T(8,128)S(1)}, u32[]{:S(2)}, u32[]{:S(2)}) collective-permute-start(f32[2,128,128]{2,1,0:T(8,128)} %pad_maximum_fusion.7), channel_id=1, source_target_pairs={{0,8},{4,12},{8,0},{12,4},{16,24},{20,28},{24,16},{28,20},{32,40},... | collective-permute-start | bytes 393224 | tf_op jit(solution)/shard_map/ppermute | solution.py:38
  75.4 12.3 %collective-permute-done.6 = f32[2,128,128]{2,1,0:T(8,128)S(1)} collective-permute-done((f32[2,128,128]{2,1,0:T(8,128)}, f32[2,128,128]{2,1,0:T(8,128)S(1)}, u32[]{:S(2)}, u32[]{:S(2)}) %collective-permute-start.6) | collective-permute-done | bytes 131104 | tf_op jit(solution)/shard_map/ppermute | solution.py:38
  92.0 2.3 collective-permute-start.10
  96.0 3.3 %collective-permute-start.3 = (f32[32,1024]{1,0:T(8,128)S(1)}, f32[32,1024]{1,0:T(8,128)S(1)}, u32[]{:S(2)}, u32[]{:S(2)}) collective-permute-start(f32[32,1024]{1,0:T(8,128)S(1)} %slice.74), channel_id=1, source_target_pairs={{0,16},{4,20},{8,24},{12,28},{16,0},{20,4},{24,8},{28,12},{32,48},... | collective-permute-start | bytes 393224 | tf_op jit(solution)/shard_map/ppermute | solution.py:38
  101.5 4.7 %collective-permute-done.3 = f32[32,1024]{1,0:T(8,128)S(1)} collective-permute-done((f32[32,1024]{1,0:T(8,128)S(1)}, f32[32,1024]{1,0:T(8,128)S(1)}, u32[]{:S(2)}, u32[]{:S(2)}) %collective-permute-start.3) | collective-permute-done | bytes 131104 | tf_op jit(solution)/shard_map/ppermute | solution.py:38
  107.8 3.3 %collective-permute-start.4 = (f32[4,2,256,128]{3,2,1,0:T(8,128)}, f32[4,2,256,128]{3,2,1,0:T(8,128)S(1)}, u32[]{:S(2)}, u32[]{:S(2)}) collective-permute-start(f32[4,2,256,128]{3,2,1,0:T(8,128)} %bitcast.28), channel_id=1, source_target_pairs={{0,4},{4,0},{8,12},{12,8},{16,20},{20,16},{24,28},{28,24},{32,36},... | collective-permute-start | bytes 3145736 | tf_op jit(solution)/shard_map/ppermute | solution.py:38
  111.1 2.4 %collective-permute-done.4.other.o1 = f32[4,2,256,128]{3,2,1,0:T(8,128)S(1)} collective-permute-done((f32[4,2,256,128]{3,2,1,0:T(8,128)}, f32[4,2,256,128]{3,2,1,0:T(8,128)S(1)}, u32[]{:S(2)}, u32[]{:S(2)}) %collective-permute-start.4) | collective-permute-done | bytes 1048608 | tf_op jit(solution)/shard_map/ppermute | solution.py:38
  118.0 6.0 %collective-permute-done.5 = f32[32,512]{1,0:T(8,128)S(1)} collective-permute-done((f32[32,512]{1,0:T(8,128)S(1)}, f32[32,512]{1,0:T(8,128)S(1)}, u32[]{:S(2)}, u32[]{:S(2)}) %collective-permute-start.5) | collective-permute-done | bytes 65568 | tf_op jit(solution)/shard_map/ppermute | solution.py:38
  124.6 12.6 %all-gather.9.cloned.1.call-done = f32[8,256,128]{2,1,0:T(8,128)} async-done(((f32[2,256,128]{2,1,0:T(8,128)}), f32[8,256,128]{2,1,0:T(8,128)}) %all-gather.9.cloned.1.call-update) | async-done | bytes 1048592 | tf_op jit(solution)/shard_map/all_gather | solution.py:223
  137.2 3.6 %collective-permute-start.9 = (f32[4,2,256,128]{3,2,1,0:T(8,128)}, f32[4,2,256,128]{3,2,1,0:T(8,128)S(1)}, u32[]{:S(2)}, u32[]{:S(2)}) collective-permute-start(f32[4,2,256,128]{3,2,1,0:T(8,128)} %bitcast.31), channel_id=1, source_target_pairs={{0,4},{4,0},{8,12},{12,8},{16,20},{20,16},{24,28},{28,24},{32,36},... | collective-permute-start | bytes 3145736 | tf_op jit(solution)/shard_map/ppermute | solution.py:38
  140.8 7.4 %collective-permute-start.8 = (f32[32,1024]{1,0:T(8,128)}, f32[32,1024]{1,0:T(8,128)S(1)}, u32[]{:S(2)}, u32[]{:S(2)}) collective-permute-start(f32[32,1024]{1,0:T(8,128)} %slice_add_fusion.1), channel_id=1, source_target_pairs={{0,32},{4,36},{8,40},{12,44},{16,48},{20,52},{24,56},{28,60},{32,0... | collective-permute-start | bytes 393224 | tf_op jit(solution)/shard_map/ppermute | solution.py:38
  148.2 12.4 %collective-permute-done.8 = f32[32,1024]{1,0:T(8,128)S(1)} collective-permute-done((f32[32,1024]{1,0:T(8,128)}, f32[32,1024]{1,0:T(8,128)S(1)}, u32[]{:S(2)}, u32[]{:S(2)}) %collective-permute-start.8) | collective-permute-done | bytes 131104 | tf_op jit(solution)/shard_map/ppermute | solution.py:38
  161.5 3.5 %collective-permute-start.13 = (f32[32,512]{1,0:T(8,128)S(1)}, f32[32,512]{1,0:T(8,128)S(1)}, u32[]{:S(2)}, u32[]{:S(2)}) collective-permute-start(f32[32,512]{1,0:T(8,128)S(1)} %slice.76), channel_id=1, source_target_pairs={{0,112},{4,116},{8,120},{12,124},{16,96},{20,100},{24,104},{28,108... | collective-permute-start | bytes 196616 | tf_op jit(solution)/shard_map/ppermute | solution.py:38
  165.1 5.9 %collective-permute-start.7 = (f32[32,512]{1,0:T(8,128)}, f32[32,512]{1,0:T(8,128)S(1)}, u32[]{:S(2)}, u32[]{:S(2)}) collective-permute-start(f32[32,512]{1,0:T(8,128)} %add.52), channel_id=1, source_target_pairs={{0,32},{4,36},{8,40},{12,44},{16,48},{20,52},{24,56},{28,60},{32,0... | collective-permute-start | bytes 196616 | tf_op jit(solution)/shard_map/ppermute | solution.py:38
  171.6 2.6 %collective-permute-done.7 = f32[32,512]{1,0:T(8,128)S(1)} collective-permute-done((f32[32,512]{1,0:T(8,128)}, f32[32,512]{1,0:T(8,128)S(1)}, u32[]{:S(2)}, u32[]{:S(2)}) %collective-permute-start.7) | collective-permute-done | bytes 65568 | tf_op jit(solution)/shard_map/ppermute | solution.py:38
  178.2 4.2 %collective-permute-start.15 = (f32[4,3,256,128]{3,2,1,0:T(8,128)}, f32[4,3,256,128]{3,2,1,0:T(8,128)S(1)}, u32[]{:S(2)}, u32[]{:S(2)}) collective-permute-start(f32[4,3,256,128]{3,2,1,0:T(8,128)} %bitcast.25), channel_id=1, source_target_pairs={{0,4},{4,0},{8,12},{12,8},{16,20},{20,16},{24,28},{28,24},{32,36},... | collective-permute-start | bytes 4718600 | tf_op jit(solution)/shard_map/ppermute | solution.py:38
  182.4 4.0 %collective-permute-start.11 = (f32[32,512]{1,0:T(8,128)}, f32[32,512]{1,0:T(8,128)S(1)}, u32[]{:S(2)}, u32[]{:S(2)}) collective-permute-start(f32[32,512]{1,0:T(8,128)} %copy-done.18), channel_id=1, source_target_pairs={{0,112},{4,116},{8,120},{12,124},{16,96},{20,100},{24,104},{28,108... | collective-permute-start | bytes 196616 | tf_op jit(solution)/shard_map/ppermute | solution.py:38
  186.4 3.1 %collective-permute-start.14 = (f32[32,512]{1,0:T(8,128)}, f32[32,512]{1,0:T(8,128)S(1)}, u32[]{:S(2)}, u32[]{:S(2)}) collective-permute-start(f32[32,512]{1,0:T(8,128)} %get-tuple-element.52), channel_id=1, source_target_pairs={{0,128},{4,132},{8,136},{12,140},{16,144},{20,148},{24,152},{28,15... | collective-permute-start | bytes 196616 | tf_op jit(solution)/shard_map/ppermute | solution.py:38
  191.2 3.1 %collective-permute-start.12 = (f32[32,512]{1,0:T(8,128)S(1)}, f32[32,512]{1,0:T(8,128)S(1)}, u32[]{:S(2)}, u32[]{:S(2)}) collective-permute-start(f32[32,512]{1,0:T(8,128)S(1)} %add.56), channel_id=1, source_target_pairs={{0,128},{4,132},{8,136},{12,140},{16,144},{20,148},{24,152},{28,15... | collective-permute-start | bytes 196616 | tf_op jit(solution)/shard_map/ppermute | solution.py:38
  198.6 4.4 %collective-permute-start.16 = (f32[32,512]{1,0:T(8,128)S(1)}, f32[32,512]{1,0:T(8,128)S(1)}, u32[]{:S(2)}, u32[]{:S(2)}) collective-permute-start(f32[32,512]{1,0:T(8,128)S(1)} %get-tuple-element.40), channel_id=1, source_target_pairs={{0,384},{4,388},{8,392},{12,396},{16,400},{20,404},{24,408},{28,41... | collective-permute-start | bytes 196616 | tf_op jit(solution)/shard_map/ppermute | solution.py:38
  207.3 3.4 %shard_map.99 = f32[32,2048]{1,0:T(8,128)S(1)} custom-call(f32[32,512]{1,0:T(8,128)S(1)} %add.60.right, f32[32,512]{1,0:T(8,128)S(1)} %get-tuple-element.41.z1, f32[32,512]{1,0:T(8,128)S(1)} %copy-done.17, f32[32,512]{1,0:T(8,128)S(1)} %get-tuple-element.43.z3, f32[4,2,256,128]{3,2,1,0:T(8,128)S(1)} %bitcast.30, f32[4,2,256,128]{3,2,1,0:T(8,128)S(1)} %copy-done.8, ...), custom_call_target="tpu_custom_call" | custom-call | tf_op jit(solution)/shard_map/pallas_call | solution.py:172
  210.7 6.0 %collective-permute-start.17 = (f32[32,2048]{1,0:T(8,128)S(1)}, f32[32,2048]{1,0:T(8,128)S(1)}, u32[]{:S(2)}, u32[]{:S(2)}) collective-permute-start(f32[32,2048]{1,0:T(8,128)S(1)} %shard_map.99), channel_id=1, source_target_pairs={{0,8},{4,12},{8,0},{12,4},{16,24},{20,28},{24,16},{28,20},{32,40},... | collective-permute-start | bytes 786440 | tf_op jit(solution)/shard_map/ppermute | solution.py:38
  216.7 3.7 %collective-permute-done.17 = f32[32,2048]{1,0:T(8,128)S(1)} collective-permute-done((f32[32,2048]{1,0:T(8,128)S(1)}, f32[32,2048]{1,0:T(8,128)S(1)}, u32[]{:S(2)}, u32[]{:S(2)}) %collective-permute-start.17) | collective-permute-done | bytes 262176 | tf_op jit(solution)/shard_map/ppermute | solution.py:38
  220.5 7.6 %collective-permute-start.18 = (f32[2,32,2048]{2,1,0:T(8,128)S(1)}, f32[2,32,2048]{2,1,0:T(8,128)S(1)}, u32[]{:S(2)}, u32[]{:S(2)}) collective-permute-start(f32[2,32,2048]{2,1,0:T(8,128)S(1)} %pad_maximum_fusion.1), channel_id=1, source_target_pairs={{0,4},{4,0},{8,12},{12,8},{16,20},{20,16},{24,28},{28,24},{32,36},... | collective-permute-start | bytes 1572872 | tf_op jit(solution)/shard_map/ppermute | solution.py:38
  229.6 4.8 %shard_map.100 = (f32[896,128]{1,0:T(8,128)}, f32[176,128]{1,0:T(8,128)}) custom-call(s32[5]{0:T(128)S(1)} %stack.56.where, s32[1,21]{1,0:T(1,128)S(1)} %copy-done.19, f32[896,128]{1,0:T(8,128)S(1)} %copy-done.14, f32[4,32,2048]{2,1,0:T(8,128)S(1)} %pad_maximum_fusion.x, f32[7,128,128]{2,1,0:T(8,128)S(1)} %copy-done.12, f32[21,128,128]{2,1,0:T(8,128)S(1)} %copy-done.2, ...), custom_call_target="tpu_custom_call" | custom-call | tf_op jit(solution)/shard_map/pallas_call | solution.py:172
  (110 shorter events, 42.6 us)
Async XLA Ops:
  7.2 49.5 %copy-start.24 = (f32[172,128]{1,0:T(8,128)S(1)}, f32[172,128]{1,0:T(8,128)}, u32[]{:S(2)}) copy-start(f32[172,128]{1,0:T(8,128)} %param.13) | copy-start | bytes 264196
  7.2 49.5 %copy-start.3 = (f32[512,512]{1,0:T(8,128)S(1)}, f32[512,512]{1,0:T(8,128)}, u32[]{:S(2)}) copy-start(f32[512,512]{1,0:T(8,128)} %coupling.3) | copy-start | bytes 3145732
  7.2 49.5 %copy-start.19 = (s32[1,21]{1,0:T(1,128)S(1)}, s32[1,21]{1,0:T(1,128)}, u32[]{:S(2)}) copy-start(s32[1,21]{1,0:T(1,128)} %pattern.3) | copy-start | bytes 256
  7.2 49.5 %copy-start.2 = (f32[21,128,128]{2,1,0:T(8,128)S(1)}, f32[21,128,128]{2,1,0:T(8,128)}, u32[]{:S(2)}) copy-start(f32[21,128,128]{2,1,0:T(8,128)} %blocks.3) | copy-start | bytes 4128772
  10.2 55.2 %all-to-all-start = ((f32[32,20,128]{2,1,0:T(8,128)}), f32[32,20,128]{2,1,0:T(8,128)S(1)}, u32[]{:S(2)}, u32[]{:S(2)}) async-start(f32[32,20,128]{2,1,0:T(8,128)} %broadcast_in_dim.2), calls=%async_computation | async-start | bytes 786432 | tf_op jit(solution)/shard_map/all_to_all | solution.py:201
  29.6 21.8 %collective-permute-start.1 = (f32[2,32,128]{2,1,0:T(8,128)S(1)}, f32[2,32,128]{2,1,0:T(8,128)S(1)}, u32[]{:S(2)}, u32[]{:S(2)}) collective-permute-start(f32[2,32,128]{2,1,0:T(8,128)S(1)} %pad_maximum_fusion.9), channel_id=1, source_target_pairs={{0,32},{4,36},{8,40},{12,44},{16,48},{20,52},{24,56},{28,60},{32,0... | collective-permute-start | bytes 98312 | tf_op jit(solution)/shard_map/ppermute | solution.py:38
  37.6 13.8 %collective-permute-start = (f32[2,128,128]{2,1,0:T(8,128)S(1)}, f32[2,128,128]{2,1,0:T(8,128)S(1)}, u32[]{:S(2)}, u32[]{:S(2)}) collective-permute-start(f32[2,128,128]{2,1,0:T(8,128)S(1)} %pad_maximum_fusion.6), channel_id=1, source_target_pairs={{0,8},{4,12},{8,0},{12,4},{16,24},{20,28},{24,16},{28,20},{32,40},... | collective-permute-start | bytes 393224 | tf_op jit(solution)/shard_map/ppermute | solution.py:38
  52.1 12.6 %collective-permute-start.2 = (f32[2,64,128]{2,1,0:T(8,128)S(1)}, f32[2,64,128]{2,1,0:T(8,128)S(1)}, u32[]{:S(2)}, u32[]{:S(2)}) collective-permute-start(f32[2,64,128]{2,1,0:T(8,128)S(1)} %pad_maximum_fusion.8), channel_id=1, source_target_pairs={{0,16},{4,20},{8,24},{12,28},{16,0},{20,4},{24,8},{28,12},{32,48},... | collective-permute-start | bytes 196616 | tf_op jit(solution)/shard_map/ppermute | solution.py:38
  66.1 28.1 %all-to-all-start.1 = ((f32[4,32,2048]{2,1,0:T(8,128)}), f32[4,32,2048]{2,1,0:T(8,128)S(1)}, u32[]{:S(2)}, u32[]{:S(2)}) async-start(f32[4,32,2048]{2,1,0:T(8,128)} %bitcast.9), calls=%async_computation.1 | async-start | bytes 2097152 | tf_op jit(solution)/shard_map/all_to_all | solution.py:216
  71.3 36.4 %all-gather.7.cloned.1.call-start = ((), (), s32[]{:S(2)}) async-start(), calls=%async_computation.2 | async-start | bytes 1310720 | tf_op jit(solution)/shard_map/all_gather | solution.py:212
  72.0 65.1 %all-gather.9.cloned.1.call-start = ((), (), s32[]{:S(2)}) async-start(), calls=%async_computation.3 | async-start | bytes 1310720 | tf_op jit(solution)/shard_map/all_gather | solution.py:223
  72.1 15.6 %collective-permute-start.6 = (f32[2,128,128]{2,1,0:T(8,128)}, f32[2,128,128]{2,1,0:T(8,128)S(1)}, u32[]{:S(2)}, u32[]{:S(2)}) collective-permute-start(f32[2,128,128]{2,1,0:T(8,128)} %pad_maximum_fusion.7), channel_id=1, source_target_pairs={{0,8},{4,12},{8,0},{12,4},{16,24},{20,28},{24,16},{28,20},{32,40},... | collective-permute-start | bytes 393224 | tf_op jit(solution)/shard_map/ppermute | solution.py:38
  89.4 88.8 %all-gather.11.cloned.1.call-start = ((), (), s32[]{:S(2)}) async-start(), calls=%async_computation.4 | async-start | bytes 1966080 | tf_op jit(solution)/shard_map/all_gather | solution.py:230
  92.0 7.7 %collective-permute-start.10 = (f32[3,128,128]{2,1,0:T(8,128)}, f32[3,128,128]{2,1,0:T(8,128)}, u32[]{:S(2)}, u32[]{:S(2)}) collective-permute-start(f32[3,128,128]{2,1,0:T(8,128)} %pad_maximum_fusion.5), channel_id=1, source_target_pairs={{0,8},{4,12},{8,0},{12,4},{16,24},{20,28},{24,16},{28,20},{32,40},... | collective-permute-start | bytes 589832 | tf_op jit(solution)/shard_map/ppermute | solution.py:38
  95.0 16.0 %copy-start.20 = (f32[32,2048]{1,0:T(8,128)S(1)}, f32[32,2048]{1,0:T(8,128)}, u32[]{:S(2)}) copy-start(f32[32,2048]{1,0:T(8,128)} %reduce_sum.9) | copy-start | bytes 786436
  96.0 10.1 %collective-permute-start.3 = (f32[32,1024]{1,0:T(8,128)S(1)}, f32[32,1024]{1,0:T(8,128)S(1)}, u32[]{:S(2)}, u32[]{:S(2)}) collective-permute-start(f32[32,1024]{1,0:T(8,128)S(1)} %slice.74), channel_id=1, source_target_pairs={{0,16},{4,20},{8,24},{12,28},{16,0},{20,4},{24,8},{28,12},{32,48},... | collective-permute-start | bytes 393224 | tf_op jit(solution)/shard_map/ppermute | solution.py:38
  107.8 5.7 %collective-permute-start.4 = (f32[4,2,256,128]{3,2,1,0:T(8,128)}, f32[4,2,256,128]{3,2,1,0:T(8,128)S(1)}, u32[]{:S(2)}, u32[]{:S(2)}) collective-permute-start(f32[4,2,256,128]{3,2,1,0:T(8,128)} %bitcast.28), channel_id=1, source_target_pairs={{0,4},{4,0},{8,12},{12,8},{16,20},{20,16},{24,28},{28,24},{32,36},... | collective-permute-start | bytes 3145736 | tf_op jit(solution)/shard_map/ppermute | solution.py:38
  116.1 7.9 %collective-permute-start.5 = (f32[32,512]{1,0:T(8,128)S(1)}, f32[32,512]{1,0:T(8,128)S(1)}, u32[]{:S(2)}, u32[]{:S(2)}) collective-permute-start(f32[32,512]{1,0:T(8,128)S(1)} %get-tuple-element.31), channel_id=1, source_target_pairs={{0,16},{4,20},{8,24},{12,28},{16,0},{20,4},{24,8},{28,12},{32,48},... | collective-permute-start | bytes 196616 | tf_op jit(solution)/shard_map/ppermute | solution.py:38
  137.2 37.8 %copy-start.6 = (f32[8,256,128]{2,1,0:T(8,128)S(1)}, f32[8,256,128]{2,1,0:T(8,128)}, u32[]{:S(2)}) copy-start(f32[8,256,128]{2,1,0:T(8,128)} %all-gather.9.cloned.1.call-done) | copy-start | bytes 3145732
  137.2 37.8 %collective-permute-start.9 = (f32[4,2,256,128]{3,2,1,0:T(8,128)}, f32[4,2,256,128]{3,2,1,0:T(8,128)S(1)}, u32[]{:S(2)}, u32[]{:S(2)}) collective-permute-start(f32[4,2,256,128]{3,2,1,0:T(8,128)} %bitcast.31), channel_id=1, source_target_pairs={{0,4},{4,0},{8,12},{12,8},{16,20},{20,16},{24,28},{28,24},{32,36},... | collective-permute-start | bytes 3145736 | tf_op jit(solution)/shard_map/ppermute | solution.py:38
  140.8 19.8 %collective-permute-start.8 = (f32[32,1024]{1,0:T(8,128)}, f32[32,1024]{1,0:T(8,128)S(1)}, u32[]{:S(2)}, u32[]{:S(2)}) collective-permute-start(f32[32,1024]{1,0:T(8,128)} %slice_add_fusion.1), channel_id=1, source_target_pairs={{0,32},{4,36},{8,40},{12,44},{16,48},{20,52},{24,56},{28,60},{32,0... | collective-permute-start | bytes 393224 | tf_op jit(solution)/shard_map/ppermute | solution.py:38
  161.5 9.4 %collective-permute-start.13 = (f32[32,512]{1,0:T(8,128)S(1)}, f32[32,512]{1,0:T(8,128)S(1)}, u32[]{:S(2)}, u32[]{:S(2)}) collective-permute-start(f32[32,512]{1,0:T(8,128)S(1)} %slice.76), channel_id=1, source_target_pairs={{0,112},{4,116},{8,120},{12,124},{16,96},{20,100},{24,104},{28,108... | collective-permute-start | bytes 196616 | tf_op jit(solution)/shard_map/ppermute | solution.py:38
  165.1 9.1 %collective-permute-start.7 = (f32[32,512]{1,0:T(8,128)}, f32[32,512]{1,0:T(8,128)S(1)}, u32[]{:S(2)}, u32[]{:S(2)}) collective-permute-start(f32[32,512]{1,0:T(8,128)} %add.52), channel_id=1, source_target_pairs={{0,32},{4,36},{8,40},{12,44},{16,48},{20,52},{24,56},{28,60},{32,0... | collective-permute-start | bytes 196616 | tf_op jit(solution)/shard_map/ppermute | solution.py:38
  178.2 18.0 %collective-permute-start.15 = (f32[4,3,256,128]{3,2,1,0:T(8,128)}, f32[4,3,256,128]{3,2,1,0:T(8,128)S(1)}, u32[]{:S(2)}, u32[]{:S(2)}) collective-permute-start(f32[4,3,256,128]{3,2,1,0:T(8,128)} %bitcast.25), channel_id=1, source_target_pairs={{0,4},{4,0},{8,12},{12,8},{16,20},{20,16},{24,28},{28,24},{32,36},... | collective-permute-start | bytes 4718600 | tf_op jit(solution)/shard_map/ppermute | solution.py:38
  182.4 7.9 %collective-permute-start.11 = (f32[32,512]{1,0:T(8,128)}, f32[32,512]{1,0:T(8,128)S(1)}, u32[]{:S(2)}, u32[]{:S(2)}) collective-permute-start(f32[32,512]{1,0:T(8,128)} %copy-done.18), channel_id=1, source_target_pairs={{0,112},{4,116},{8,120},{12,124},{16,96},{20,100},{24,104},{28,108... | collective-permute-start | bytes 196616 | tf_op jit(solution)/shard_map/ppermute | solution.py:38
  186.4 7.9 %collective-permute-start.14 = (f32[32,512]{1,0:T(8,128)}, f32[32,512]{1,0:T(8,128)S(1)}, u32[]{:S(2)}, u32[]{:S(2)}) collective-permute-start(f32[32,512]{1,0:T(8,128)} %get-tuple-element.52), channel_id=1, source_target_pairs={{0,128},{4,132},{8,136},{12,140},{16,144},{20,148},{24,152},{28,15... | collective-permute-start | bytes 196616 | tf_op jit(solution)/shard_map/ppermute | solution.py:38
  191.2 5.0 %collective-permute-start.12 = (f32[32,512]{1,0:T(8,128)S(1)}, f32[32,512]{1,0:T(8,128)S(1)}, u32[]{:S(2)}, u32[]{:S(2)}) collective-permute-start(f32[32,512]{1,0:T(8,128)S(1)} %add.56), channel_id=1, source_target_pairs={{0,128},{4,132},{8,136},{12,140},{16,144},{20,148},{24,152},{28,15... | collective-permute-start | bytes 196616 | tf_op jit(solution)/shard_map/ppermute | solution.py:38
  198.6 6.2 %collective-permute-start.16 = (f32[32,512]{1,0:T(8,128)S(1)}, f32[32,512]{1,0:T(8,128)S(1)}, u32[]{:S(2)}, u32[]{:S(2)}) collective-permute-start(f32[32,512]{1,0:T(8,128)S(1)} %get-tuple-element.40), channel_id=1, source_target_pairs={{0,384},{4,388},{8,392},{12,396},{16,400},{20,404},{24,408},{28,41... | collective-permute-start | bytes 196616 | tf_op jit(solution)/shard_map/ppermute | solution.py:38
  210.7 9.7 %collective-permute-start.17 = (f32[32,2048]{1,0:T(8,128)S(1)}, f32[32,2048]{1,0:T(8,128)S(1)}, u32[]{:S(2)}, u32[]{:S(2)}) collective-permute-start(f32[32,2048]{1,0:T(8,128)S(1)} %shard_map.99), channel_id=1, source_target_pairs={{0,8},{4,12},{8,0},{12,4},{16,24},{20,28},{24,16},{28,20},{32,40},... | collective-permute-start | bytes 786440 | tf_op jit(solution)/shard_map/ppermute | solution.py:38
  220.5 9.1 %copy-start.12 = (f32[7,128,128]{2,1,0:T(8,128)S(1)}, f32[7,128,128]{2,1,0:T(8,128)}, u32[]{:S(2)}) copy-start(f32[7,128,128]{2,1,0:T(8,128)} %inverse.3) | copy-start | bytes 1376260
  220.5 9.1 %copy-start.14 = (f32[896,128]{1,0:T(8,128)S(1)}, f32[896,128]{1,0:T(8,128)}, u32[]{:S(2)}) copy-start(f32[896,128]{1,0:T(8,128)} %copy-done.13) | copy-start | bytes 1376260
  220.5 8.9 %collective-permute-start.18 = (f32[2,32,2048]{2,1,0:T(8,128)S(1)}, f32[2,32,2048]{2,1,0:T(8,128)S(1)}, u32[]{:S(2)}, u32[]{:S(2)}) collective-permute-start(f32[2,32,2048]{2,1,0:T(8,128)S(1)} %pad_maximum_fusion.1), channel_id=1, source_target_pairs={{0,4},{4,0},{8,12},{12,8},{16,20},{20,16},{24,28},{28,24},{32,36},... | collective-permute-start | bytes 1572872 | tf_op jit(solution)/shard_map/ppermute | solution.py:38
  (17 other events, 36.9 us)
Sparse Core Ops, SparseCore 0:
  74.2 28.7 all-gather.6
  105.1 32.0 all-gather.8
  139.3 35.4 all-gather.10

commit v3 on v2

--- a/solution.py
+++ b/solution.py
@@ -112,12 +112,16 @@
             pending[earlier] = pending[earlier] - weight * mm(blocks[pair], solved, TN)
 
 
-def times_rows(value, mats, index):
+def spots(start, plane, count):
+    return [pl.ds(pl.multiple_of(start + (plane ^ r) * 128, 128), 128) for r in range(count)]
+
+
+def times_rows(value, places, mats, index):
     result = []
     for half in mats:
         total = None
-        for r in range(half.shape[0]):
-            term = mm(value[:, r * 128 : (r + 1) * 128], half[r, index], NT)
+        for r, place in enumerate(places):
+            term = mm(value[:, place], half[r, index], NT)
             total = term if total is None else total + term
         result.append(total)
     return result
@@ -131,30 +135,30 @@
     return total
 
 
-def level_kernel(index, right, base, mine, other, z_out, v_out):
+def level_kernel(index, plane, right, base, mine, other, z_out, v_out):
     mats = (mine, other)
-    z = times_rows(right, mats, index)
+    places = spots(0, plane[0], mine.shape[0])
+    z = times_rows(right, places, mats, index)
     z_out[...] = jnp.concatenate(z, axis=1)
-    for r in range(mine.shape[0]):
-        spot = slice(r * 128, (r + 1) * 128)
-        v_out[:, spot] = base[:, spot] - times_matrix(z, mats, index + 1, r)
-
-
-def top_kernel(right, z1, z2, z3, m1, o1, m2, o2, m3, o3, x_out):
+    for r, place in enumerate(places):
+        v_out[:, place] = base[:, place] - times_matrix(z, mats, index + 1, r)
+
+
+def top_kernel(plane, right, z1, z2, z3, m1, o1, m2, o2, m3, o3, x_out):
     width = right.shape[1]
+    count = m3.shape[0]
     top = (m3, o3)
-    z = times_rows(right, top, 0)
-    order = [(z3, top, 1), (z2, (m2, o2), 0), (z1, (m1, o1), 0)]
-    mats, index = top, 0
+    z = times_rows(right, spots(0, 0, count), top, 0)
+    order = [(z3, top, 1, 0), (z2, (m2, o2), 0, plane[0]), (z1, (m1, o1), 0, plane[0])]
+    mats, index, turn = top, 0, 0
     level = 3
     while True:
-        for r in range(mats[0].shape[0]):
-            start = level * width + r * 128
-            x_out[:, start : start + 128] = times_matrix(z, mats, index, r)
+        for r, place in enumerate(spots(level * width, turn, count)):
+            x_out[:, place] = times_matrix(z, mats, index, r)
         if not order:
             break
-        held, mats, index = order.pop(0)
-        moved = times_rows(x_out[:, level * width : (level + 1) * width], mats, index + 1)
+        held, mats, index, turn = order.pop(0)
+        moved = times_rows(x_out, spots(level * width, turn, count), mats, index + 1)
         half = held.shape[1] // 2
         z = [held[:, :half] - moved[0], held[:, half:] - moved[1]]
         level -= 1
@@ -188,70 +192,84 @@
     offsets = [sum(sizes[:i]) for i in range(LEVELS)]
     where = jnp.stack([position % g * r for g, r in zip(groups, sizes)] + [position % 4]).astype(jnp.int32)
 
+    plane = lax.axis_index("col").astype(jnp.int32)[None]
+
     def rows(array, level):
         return array[offsets[level] : offsets[level] + sizes[level]]
 
     def both(level):
         return jnp.stack([rows(sep_inverse, level), rows(sep_coupling, level)])
 
-    count = leaves // 4
+    def planes(value):
+        return jnp.stack([value] + [swap(value, "col", r) for r in range(1, lax.axis_size("col"))])
+
+    tie = lax.optimization_barrier
+    halves_z, wrap_z, wrap_y = 1 << Z4, (1 << Z8) | (1 << Z4) | (1 << Z2), (1 << Y2) | (1 << Y1)
+
+    padded = jnp.pad(sep_rhs, ((0, 4), (0, 0)))
+    first, second = both(0), both(1)
     far = jnp.concatenate([rows(sep_inverse, 2), rows(sep_coupling, 2), rows(sep_inverse, 3)], 0)
-    far = jnp.broadcast_to(far[None], (count, *far.shape))
-    apart = [[m + 4 * k for k in range(count)] for m in range(4)]
-    far = lax.all_to_all(far, "leaf", 0, 0, axis_index_groups=apart, tiled=True)
-
-    first = grow(both(0), 1 << Z1)
-    second = grow(both(1), 1 << Z4)
-    padded = jnp.pad(sep_rhs, ((0, 4), (0, 0)))
-    where, first, second = lax.optimization_barrier((where, first, second))
+    first = grow(first, 1 << Z1)
     y, t = call(
         functools.partial(forward_kernel, sizes),
         [leaf_rhs.shape, (columns, LEVELS * width)],
         where, leaf_pattern, leaf_rhs, leaf_inverse, leaf_blocks, leaf_coupling, padded,
     )
-    first = lax.all_gather(first, "col", axis=0)
+    t, first, second, far = tie((t, first, second, far))
+
     near = [[g * 4 + m for m in range(4)] for g in range(leaves // 4)]
+    t = lax.all_to_all(t, "leaf", 0, 0, axis_index_groups=near, tiled=True)
+    first = planes(first)
+    second = grow(second, halves_z)
+    t, first, second, far = tie((t, first, second, far))
+
+    count = leaves // 4
+    far = jnp.broadcast_to(far[None], (count, *far.shape))
+    apart = [[m + 4 * k for k in range(count)] for m in range(4)]
+    far = lax.all_to_all(far, "leaf", 0, 0, axis_index_groups=apart, tiled=True)
+    t = t.reshape(4, columns // 4, LEVELS * width).sum(0)
+    t1, t2, upper = t[:, :width], t[:, width : 2 * width], t[:, 2 * width :]
+    first = (first, across(first, CORE_MASK))
     second = grow(second, 1 << Z2)
-    far, second, t = lax.optimization_barrier((far, second, t))
-    t = lax.all_to_all(t, "leaf", 0, 0, axis_index_groups=near, tiled=True)
-    t = t.reshape(4, columns // 4, LEVELS * width).sum(0)
-    upper = t[:, 2 * width :]
-    upper = upper + across(upper, 1 << Z2)
-    first, upper = lax.optimization_barrier((first, upper))
-    upper = upper + across(upper, 1 << Z4)
-    first = (first, across(first, CORE_MASK))
-    second = lax.all_gather(grow(second, 1 << Z1), "col", axis=0)
+    upper_z2 = across(upper, 1 << Z2)
+    shape = t1.shape
+    z1, v = call(functools.partial(level_kernel, 0), [shape] * 2, plane, t1, t2, *first)
+    v, second, upper, upper_z2 = tie((v, second, upper, upper_z2))
+
+    upper = upper + upper_z2
+    second = grow(second, 1 << Z1)
+    upper_z4 = across(upper, halves_z)
+    v = v + across(v, 1 << Z2)
+    v, second, far = tie((v, second, far))
+
     own = lax.dynamic_slice_in_dim(far, position // 64 * 16, 16, 0)
-    third = [
+    third = jnp.stack([
         far[:, 2 * sizes[2] :].reshape(-1, 128),
         own[:, : sizes[2]].reshape(-1, 128),
         own[:, sizes[2] : 2 * sizes[2]].reshape(-1, 128),
-    ]
-    third = lax.all_gather(grow(jnp.stack(third), 1 << Z1), "col", axis=0)
-
-    t1, t2 = t[:, :width], t[:, width : 2 * width]
+    ])
+    second = planes(second)
+    third = grow(third, 1 << Z1)
+    v = v + across(v, halves_z)
+    v, second, third, upper, upper_z4 = tie((v, second, third, upper, upper_z4))
+
+    third = lax.all_gather(third, "col", axis=0)
+    second = (second, across(second, CORE_MASK))
+    upper = upper + upper_z4
     t3, t4 = upper[:, :width], upper[:, width:]
-
-    def total(value, *masks):
-        for mask in masks:
-            value = value + across(value, mask)
-        return value
-
-    shape = t1.shape
-    halves_z, wrap_z, wrap_y = 1 << Z4, (1 << Z8) | (1 << Z4) | (1 << Z2), (1 << Y2) | (1 << Y1)
-    t4 = total(t4, wrap_z, 1 << Y1)
-    z1, v = call(functools.partial(level_kernel, 0), [shape] * 2, t1, t2, *first)
-    v = total(v, 1 << Z2)
-    v, second = lax.optimization_barrier((v, second))
-    second = (second, across(second, CORE_MASK))
-    v = total(v, halves_z)
-    z2, v = call(functools.partial(level_kernel, 0), [shape] * 2, v, t3, *second)
-    v, third = lax.optimization_barrier((v, third))
+    t4_far = across(t4, wrap_z)
+    z2, v = call(functools.partial(level_kernel, 0), [shape] * 2, plane, v, t3, *second)
+    v, t4, t4_far = tie((v, t4, t4_far))
+
+    t4 = t4 + t4_far
+    t4_y = across(t4, 1 << Y1)
+    v = v + across(v, wrap_z)
+    v, t4, t4_y, third = tie((v, t4, t4_y, third))
     third = (third, across(third, CORE_MASK))
-    v = total(v, wrap_z, 1 << Y1)
-    z3, v = call(functools.partial(level_kernel, 1), [shape] * 2, v, t4, *third)
-    v = total(v, wrap_y)
-    (x,) = call(top_kernel, [(shape[0], LEVELS * width)], v, z1, z2, z3, *first, *second, *third)
+    v = v + across(v, 1 << Y1)
+    z3, v = call(functools.partial(level_kernel, 1), [shape] * 2, plane * 0, v, t4 + t4_y, *third)
+    v = v + across(v, wrap_y)
+    (x,) = call(top_kernel, [(shape[0], LEVELS * width)], plane, v, z1, z2, z3, *first, *second, *third)
     x = jnp.stack([x, across(x, 1 << Z1)])
     other = across(x, CORE_MASK)
     x = jnp.stack([x[0], other[0], x[1], other[1]], 0)

time: 244 us -> 234 us (0.959)
  other arithmetic: 12.7 us -> 4.98 us
  starting transfers between devices: 105 us -> 108 us
    ppermute x19 -> x25, starting transfers between devices: 81 us -> 86.8 us  [swap(): lax.ppermute(value, axis, [(i, i ^ mask) for i in range(lax.axis_size(axi...]
    all_to_all x1, starting transfers between devices: 18.7 us -> 13.6 us  [shards(): far = lax.all_to_all(far, 'leaf', 0, 0, axis_index_groups=apart, tiled=True)]
    concatenate x5, other arithmetic: 4.75 us -> 0.81 us  [grow(): return jnp.concatenate([value, across(value, mask)], axis=1)]
    add x9, other arithmetic: 6.37 us -> 2.66 us  [the longest x1 1.59 us: shards(): upper = upper + upper_z2]
    all_to_all x1, starting transfers between devices: 5.21 us -> 7.92 us  [shards(): t = lax.all_to_all(t, 'leaf', 0, 0, axis_index_groups=near, tiled=True)]
    unnamed x50 -> x34, local copies, waits for them, and re-layouts: 11.3 us -> 9.24 us
    ppermute x19 -> x25, waiting for transfers between devices: 60.6 us -> 58.6 us  [swap(): lax.ppermute(value, axis, [(i, i ^ mask) for i in range(lax.axis_size(axi...]
    all_gather x3 -> x1, waiting for transfers between devices: 12.6 us -> 13.1 us  [shards(): third = lax.all_gather(third, 'col', axis=0)]
  transfers between devices with their start and end apart: 24 -> 28, of which waited for: 14 -> 15; matrix products, arithmetic and copies ran while one was open for 7% -> 4% of each run, Pallas kernels for 3% -> 3%
where the time goes in v3:
time: 234 us; the launch traced here: 233 us
  starting transfers between devices  108 us (46%)
  waiting for transfers between devices  71.7 us (31%)
  local copies, waits for them, and re-layouts  16.6 us (7%)
  Pallas kernels  16.5 us (7%)
  between operations  14.7 us (6%)
  other arithmetic  4.98 us (2%)
    ppermute x25, starting transfers between devices, swap(): lax.ppermute(value, axis, [(i, i ^ mask) for i in range(lax.axis_size(axi...  86.8 us
    ppermute x25, waiting for transfers between devices, swap(): lax.ppermute(value, axis, [(i, i ^ mask) for i in range(lax.axis_size(axi...  58.6 us
    pallas_call x6, Pallas kernels, call(): pl.pallas_call(kernel, out_shape=[jax.ShapeDtypeStruct(s, F32) for s in o...  16.5 us
    all_to_all x1, starting transfers between devices, shards(): far = lax.all_to_all(far, 'leaf', 0, 0, axis_index_groups=apart, tiled=True)  13.6 us
    all_gather x1, waiting for transfers between devices, shards(): third = lax.all_gather(third, 'col', axis=0)  13.1 us
    unnamed x34, local copies, waits for them, and re-layouts  9.24 us
    all_to_all x1, starting transfers between devices, shards(): t = lax.all_to_all(t, 'leaf', 0, 0, axis_index_groups=near, tiled=True)  7.92 us
  transfers between devices with their start and end apart: 28, of which 15 were waited for; matrix products, arithmetic and copies ran while one was open for 4% of the time, Pallas kernels for 3%

profile of v3, /device:TPU:1, one launch (start us, length us, event | category | flops | bytes accessed | tf_op | source)
XLA Modules:
  0.0 232.7 jit_solution(8550967646877330747)
XLA Ops:
  8.1 4.4 %collective-permute-start = (f32[2,128,128]{2,1,0:T(8,128)S(1)}, f32[2,128,128]{2,1,0:T(8,128)S(1)}, u32[]{:S(2)}, u32[]{:S(2)}) collective-permute-start(f32[2,128,128]{2,1,0:T(8,128)S(1)} %pad_maximum_fusion.8), channel_id=1, source_target_pairs={{0,8},{4,12},{8,0},{12,4},{16,24},{20,28},{24,16},{28,20},{32,40},... | collective-permute-start | bytes 393224 | tf_op jit(solution)/shard_map/ppermute | solution.py:38
  21.5 5.2 %shard_map.95 = (f32[896,128]{1,0:T(8,128)S(1)}, f32[128,2048]{1,0:T(8,128)}) custom-call(s32[5]{0:T(128)S(1)} %stack.86.where, s32[1,21]{1,0:T(1,128)S(1)} %copy-done.12, f32[896,128]{1,0:T(8,128)S(1)} %copy-done.11, f32[7,128,128]{2,1,0:T(8,128)S(1)} %copy-done.7, f32[21,128,128]{2,1,0:T(8,128)S(1)} %copy-done.1, f32[512,512]{1,0:T(8,128)S(1)} %copy-done.5, ...), custom_call_target="tpu_custom_call" | custom-call | tf_op jit(solution)/shard_map/pallas_call | solution.py:176
  27.5 7.9 %all-to-all-start = ((f32[4,32,2048]{2,1,0:T(8,128)}), f32[4,32,2048]{2,1,0:T(8,128)S(1)}, u32[]{:S(2)}, u32[]{:S(2)}) async-start(f32[4,32,2048]{2,1,0:T(8,128)} %bitcast.10), calls=%async_computation | async-start | bytes 2097152 | tf_op jit(solution)/shard_map/all_to_all | solution.py:221
  39.3 5.1 %collective-permute-start.1 = (f32[2,256,128]{2,1,0:T(8,128)S(1)}, f32[2,256,128]{2,1,0:T(8,128)S(1)}, u32[]{:S(2)}, u32[]{:S(2)}) collective-permute-start(f32[2,256,128]{2,1,0:T(8,128)S(1)} %pad_maximum_fusion.5), channel_id=1, source_target_pairs={{0,1},{1,0},{2,3},{3,2},{4,5},{5,4},{6,7},{7,6},{8,9},{9,8},{10,11... | collective-permute-start | bytes 786440 | tf_op jit(solution)/shard_map/ppermute | solution.py:38
  44.4 5.3 %collective-permute-start.4 = (f32[2,32,128]{2,1,0:T(8,128)S(1)}, f32[2,32,128]{2,1,0:T(8,128)S(1)}, u32[]{:S(2)}, u32[]{:S(2)}) collective-permute-start(f32[2,32,128]{2,1,0:T(8,128)S(1)} %pad_maximum_fusion.11), channel_id=1, source_target_pairs={{0,32},{4,36},{8,40},{12,44},{16,48},{20,52},{24,56},{28,60},{32,0... | collective-permute-start | bytes 98312 | tf_op jit(solution)/shard_map/ppermute | solution.py:38
  49.8 3.2 %collective-permute-done.4 = f32[2,32,128]{2,1,0:T(8,128)S(1)} collective-permute-done((f32[2,32,128]{2,1,0:T(8,128)S(1)}, f32[2,32,128]{2,1,0:T(8,128)S(1)}, u32[]{:S(2)}, u32[]{:S(2)}) %collective-permute-start.4) | collective-permute-done | bytes 32800 | tf_op jit(solution)/shard_map/ppermute | solution.py:38
  54.3 3.1 %collective-permute-start.5 = (f32[4,2,256,128]{3,2,1,0:T(8,128)S(1)}, f32[4,2,256,128]{3,2,1,0:T(8,128)S(1)}, u32[]{:S(2)}, u32[]{:S(2)}) collective-permute-start(f32[4,2,256,128]{3,2,1,0:T(8,128)S(1)} %pad_maximum_fusion.mine.m1), channel_id=1, source_target_pairs={{0,4},{4,0},{8,12},{12,8},{16,20},{20,16},{24,28},{28,24},{32,36},... | collective-permute-start | bytes 3145736 | tf_op jit(solution)/shard_map/ppermute | solution.py:38
  58.2 13.6 %all-to-all-start.1 = ((f32[32,20,128]{2,1,0:T(8,128)}), f32[32,20,128]{2,1,0:T(8,128)}, u32[]{:S(2)}, u32[]{:S(2)}) async-start(f32[32,20,128]{2,1,0:T(8,128)} %broadcast_in_dim.10), calls=%async_computation.1 | async-start | bytes 786432 | tf_op jit(solution)/shard_map/all_to_all | solution.py:229
  71.9 4.0 %collective-permute-start.6 = (f32[2,64,128]{2,1,0:T(8,128)S(1)}, f32[2,64,128]{2,1,0:T(8,128)S(1)}, u32[]{:S(2)}, u32[]{:S(2)}) collective-permute-start(f32[2,64,128]{2,1,0:T(8,128)S(1)} %pad_maximum_fusion.10), channel_id=1, source_target_pairs={{0,16},{4,20},{8,24},{12,28},{16,0},{20,4},{24,8},{28,12},{32,48},... | collective-permute-start | bytes 196616 | tf_op jit(solution)/shard_map/ppermute | solution.py:38
  78.1 16.7 %collective-permute-done.6 = f32[2,64,128]{2,1,0:T(8,128)S(1)} collective-permute-done((f32[2,64,128]{2,1,0:T(8,128)S(1)}, f32[2,64,128]{2,1,0:T(8,128)S(1)}, u32[]{:S(2)}, u32[]{:S(2)}) %collective-permute-start.6) | collective-permute-done | bytes 65568 | tf_op jit(solution)/shard_map/ppermute | solution.py:38
  95.8 3.9 %collective-permute-done.7 = f32[32,1024]{1,0:T(8,128)S(1)} collective-permute-done((f32[32,1024]{1,0:T(8,128)S(1)}, f32[32,1024]{1,0:T(8,128)S(1)}, u32[]{:S(2)}, u32[]{:S(2)}) %collective-permute-start.7) | collective-permute-done | bytes 131104 | tf_op jit(solution)/shard_map/ppermute | solution.py:38
  101.7 3.6 %collective-permute-start.8 = (f32[32,512]{1,0:T(8,128)S(1)}, f32[32,512]{1,0:T(8,128)S(1)}, u32[]{:S(2)}, u32[]{:S(2)}) collective-permute-start(f32[32,512]{1,0:T(8,128)S(1)} %get-tuple-element.49), channel_id=1, source_target_pairs={{0,16},{4,20},{8,24},{12,28},{16,0},{20,4},{24,8},{28,12},{32,48},... | collective-permute-start | bytes 196616 | tf_op jit(solution)/shard_map/ppermute | solution.py:38
  109.6 3.3 %collective-permute-start.14 = (f32[3,128,128]{2,1,0:T(8,128)S(1)}, f32[3,128,128]{2,1,0:T(8,128)S(1)}, u32[]{:S(2)}, u32[]{:S(2)}) collective-permute-start(f32[3,128,128]{2,1,0:T(8,128)S(1)} %pad_maximum_fusion.7), channel_id=1, source_target_pairs={{0,8},{4,12},{8,0},{12,4},{16,24},{20,28},{24,16},{28,20},{32,40},... | collective-permute-start | bytes 589832 | tf_op jit(solution)/shard_map/ppermute | solution.py:38
  112.9 4.4 %collective-permute-start.13 = (f32[2,256,128]{2,1,0:T(8,128)S(1)}, f32[2,256,128]{2,1,0:T(8,128)S(1)}, u32[]{:S(2)}, u32[]{:S(2)}) collective-permute-start(f32[2,256,128]{2,1,0:T(8,128)S(1)} %pad_maximum_fusion.6), channel_id=1, source_target_pairs={{0,3},{1,2},{2,1},{3,0},{4,7},{5,6},{6,5},{7,4},{8,11},{9,10},{10,... | collective-permute-start | bytes 786440 | tf_op jit(solution)/shard_map/ppermute | solution.py:38
  117.3 2.4 %collective-permute-start.12 = (f32[2,256,128]{2,1,0:T(8,128)S(1)}, f32[2,256,128]{2,1,0:T(8,128)S(1)}, u32[]{:S(2)}, u32[]{:S(2)}) collective-permute-start(f32[2,256,128]{2,1,0:T(8,128)S(1)} %pad_maximum_fusion.6), channel_id=1, source_target_pairs={{0,2},{1,3},{2,0},{3,1},{4,6},{5,7},{6,4},{7,5},{8,10},{9,11},{10,... | collective-permute-start | bytes 786440 | tf_op jit(solution)/shard_map/ppermute | solution.py:38
  121.9 7.1 %collective-permute-start.10 = (f32[32,512]{1,0:T(8,128)S(1)}, f32[32,512]{1,0:T(8,128)S(1)}, u32[]{:S(2)}, u32[]{:S(2)}) collective-permute-start(f32[32,512]{1,0:T(8,128)S(1)} %add.51), channel_id=1, source_target_pairs={{0,32},{4,36},{8,40},{12,44},{16,48},{20,52},{24,56},{28,60},{32,0... | collective-permute-start | bytes 196616 | tf_op jit(solution)/shard_map/ppermute | solution.py:38
  132.7 5.2 %collective-permute-start.15 = (f32[32,1024]{1,0:T(8,128)}, f32[32,1024]{1,0:T(8,128)}, u32[]{:S(2)}, u32[]{:S(2)}) collective-permute-start(f32[32,1024]{1,0:T(8,128)} %add.54), channel_id=1, source_target_pairs={{0,32},{4,36},{8,40},{12,44},{16,48},{20,52},{24,56},{28,60},{32,0... | collective-permute-start | bytes 393224 | tf_op jit(solution)/shard_map/ppermute | solution.py:38
  140.8 10.7 %collective-permute-done.15 = f32[32,1024]{1,0:T(8,128)} collective-permute-done((f32[32,1024]{1,0:T(8,128)}, f32[32,1024]{1,0:T(8,128)}, u32[]{:S(2)}, u32[]{:S(2)}) %collective-permute-start.15) | collective-permute-done | bytes 131104 | tf_op jit(solution)/shard_map/ppermute | solution.py:38
  151.4 2.5 %collective-permute-start.16 = (f32[4,2,256,128]{3,2,1,0:T(8,128)S(1)}, f32[4,2,256,128]{3,2,1,0:T(8,128)S(1)}, u32[]{:S(2)}, u32[]{:S(2)}) collective-permute-start(f32[4,2,256,128]{3,2,1,0:T(8,128)S(1)} %pad_maximum_fusion.1.mine.m2), channel_id=1, source_target_pairs={{0,4},{4,0},{8,12},{12,8},{16,20},{20,16},{24,28},{28,24},{32,36},... | collective-permute-start | bytes 3145736 | tf_op jit(solution)/shard_map/ppermute | solution.py:38
  154.9 3.0 %collective-permute-start.17 = (f32[32,512]{1,0:T(8,128)S(1)}, f32[32,512]{1,0:T(8,128)S(1)}, u32[]{:S(2)}, u32[]{:S(2)}) collective-permute-start(f32[32,512]{1,0:T(8,128)S(1)} %get-tuple-element.63), channel_id=1, source_target_pairs={{0,112},{4,116},{8,120},{12,124},{16,96},{20,100},{24,104},{28,108... | collective-permute-start | bytes 196616 | tf_op jit(solution)/shard_map/ppermute | solution.py:38
  159.9 5.7 %collective-permute-done.17 = f32[32,512]{1,0:T(8,128)S(1)} collective-permute-done((f32[32,512]{1,0:T(8,128)S(1)}, f32[32,512]{1,0:T(8,128)S(1)}, u32[]{:S(2)}, u32[]{:S(2)}) %collective-permute-start.17) | collective-permute-done | bytes 65568 | tf_op jit(solution)/shard_map/ppermute | solution.py:38
  167.5 2.9 %collective-permute-start.19 = (f32[32,512]{1,0:T(8,128)S(1)}, f32[32,512]{1,0:T(8,128)S(1)}, u32[]{:S(2)}, u32[]{:S(2)}) collective-permute-start(f32[32,512]{1,0:T(8,128)S(1)} %add.57), channel_id=1, source_target_pairs={{0,128},{4,132},{8,136},{12,140},{16,144},{20,148},{24,152},{28,15... | collective-permute-start | bytes 196616 | tf_op jit(solution)/shard_map/ppermute | solution.py:38
  172.9 13.1 %all-gather.3.cloned.1.call-done = f32[12,256,128]{2,1,0:T(8,128)} async-done(((f32[3,256,128]{2,1,0:T(8,128)}), f32[12,256,128]{2,1,0:T(8,128)}) %all-gather.3.cloned.1.call-update) | async-done | bytes 1572880 | tf_op jit(solution)/shard_map/all_gather | solution.py:256
  186.0 2.6 %collective-permute-start.21 = (f32[4,3,256,128]{3,2,1,0:T(8,128)}, f32[4,3,256,128]{3,2,1,0:T(8,128)S(1)}, u32[]{:S(2)}, u32[]{:S(2)}) collective-permute-start(f32[4,3,256,128]{3,2,1,0:T(8,128)} %bitcast.34), channel_id=1, source_target_pairs={{0,4},{4,0},{8,12},{12,8},{16,20},{20,16},{24,28},{28,24},{32,36},... | collective-permute-start | bytes 4718600 | tf_op jit(solution)/shard_map/ppermute | solution.py:38
  188.6 3.1 %collective-permute-start.20 = (f32[32,512]{1,0:T(8,128)S(1)}, f32[32,512]{1,0:T(8,128)S(1)}, u32[]{:S(2)}, u32[]{:S(2)}) collective-permute-start(f32[32,512]{1,0:T(8,128)S(1)} %add.56), channel_id=1, source_target_pairs={{0,128},{4,132},{8,136},{12,140},{16,144},{20,148},{24,152},{28,15... | collective-permute-start | bytes 196616 | tf_op jit(solution)/shard_map/ppermute | solution.py:38
  191.7 2.5 %collective-permute-done.20 = f32[32,512]{1,0:T(8,128)S(1)} collective-permute-done((f32[32,512]{1,0:T(8,128)S(1)}, f32[32,512]{1,0:T(8,128)S(1)}, u32[]{:S(2)}, u32[]{:S(2)}) %collective-permute-start.20) | collective-permute-done | bytes 65568 | tf_op jit(solution)/shard_map/ppermute | solution.py:38
  196.6 4.4 %collective-permute-start.22 = (f32[32,512]{1,0:T(8,128)S(1)}, f32[32,512]{1,0:T(8,128)S(1)}, u32[]{:S(2)}, u32[]{:S(2)}) collective-permute-start(f32[32,512]{1,0:T(8,128)S(1)} %get-tuple-element.70), channel_id=1, source_target_pairs={{0,384},{4,388},{8,392},{12,396},{16,400},{20,404},{24,408},{28,41... | collective-permute-start | bytes 196616 | tf_op jit(solution)/shard_map/ppermute | solution.py:38
  202.8 3.6 %shard_map.99 = f32[32,2048]{1,0:T(8,128)S(1)} custom-call(s32[1]{0:T(128)} %bitcast.5.plane, f32[32,512]{1,0:T(8,128)S(1)} %add.60.right, f32[32,512]{1,0:T(8,128)S(1)} %get-tuple-element.71.z1, f32[32,512]{1,0:T(8,128)S(1)} %get-tuple-element.72.z2, f32[32,512]{1,0:T(8,128)S(1)} %get-tuple-element.73.z3, f32[4,2,256,128]{3,2,1,0:T(8,128)S(1)} %pad_maximum_fusion.mine.m1, ...), custom_call_target="tpu_custom_call" | custom-call | tf_op jit(solution)/shard_map/pallas_call | solution.py:176
  206.5 3.2 %collective-permute-start.23 = (f32[32,2048]{1,0:T(8,128)S(1)}, f32[32,2048]{1,0:T(8,128)S(1)}, u32[]{:S(2)}, u32[]{:S(2)}) collective-permute-start(f32[32,2048]{1,0:T(8,128)S(1)} %shard_map.99), channel_id=1, source_target_pairs={{0,8},{4,12},{8,0},{12,4},{16,24},{20,28},{24,16},{28,20},{32,40},... | collective-permute-start | bytes 786440 | tf_op jit(solution)/shard_map/ppermute | solution.py:38
  209.7 4.6 %collective-permute-done.23 = f32[32,2048]{1,0:T(8,128)S(1)} collective-permute-done((f32[32,2048]{1,0:T(8,128)S(1)}, f32[32,2048]{1,0:T(8,128)S(1)}, u32[]{:S(2)}, u32[]{:S(2)}) %collective-permute-start.23) | collective-permute-done | bytes 262176 | tf_op jit(solution)/shard_map/ppermute | solution.py:38
  214.3 5.2 %collective-permute-start.24 = (f32[2,32,2048]{2,1,0:T(8,128)S(1)}, f32[2,32,2048]{2,1,0:T(8,128)S(1)}, u32[]{:S(2)}, u32[]{:S(2)}) collective-permute-start(f32[2,32,2048]{2,1,0:T(8,128)S(1)} %pad_maximum_fusion.3), channel_id=1, source_target_pairs={{0,4},{4,0},{8,12},{12,8},{16,20},{20,16},{24,28},{28,24},{32,36},... | collective-permute-start | bytes 1572872 | tf_op jit(solution)/shard_map/ppermute | solution.py:38
  221.1 4.8 %shard_map.100 = (f32[896,128]{1,0:T(8,128)}, f32[176,128]{1,0:T(8,128)}) custom-call(s32[5]{0:T(128)S(1)} %stack.86.where, s32[1,21]{1,0:T(1,128)S(1)} %copy-done.13, f32[896,128]{1,0:T(8,128)S(1)} %copy-done.10, f32[4,32,2048]{2,1,0:T(8,128)S(1)} %pad_maximum_fusion.2.x, f32[7,128,128]{2,1,0:T(8,128)S(1)} %copy-done.8, f32[21,128,128]{2,1,0:T(8,128)S(1)} %copy-done.2, ...), custom_call_target="tpu_custom_call" | custom-call | tf_op jit(solution)/shard_map/pallas_call | solution.py:176
  (102 shorter events, 47.9 us)
Async XLA Ops:
  8.1 19.4 %collective-permute-start = (f32[2,128,128]{2,1,0:T(8,128)S(1)}, f32[2,128,128]{2,1,0:T(8,128)S(1)}, u32[]{:S(2)}, u32[]{:S(2)}) collective-permute-start(f32[2,128,128]{2,1,0:T(8,128)S(1)} %pad_maximum_fusion.8), channel_id=1, source_target_pairs={{0,8},{4,12},{8,0},{12,4},{16,24},{20,28},{24,16},{28,20},{32,40},... | collective-permute-start | bytes 393224 | tf_op jit(solution)/shard_map/ppermute | solution.py:38
  27.5 26.8 %all-to-all-start = ((f32[4,32,2048]{2,1,0:T(8,128)}), f32[4,32,2048]{2,1,0:T(8,128)S(1)}, u32[]{:S(2)}, u32[]{:S(2)}) async-start(f32[4,32,2048]{2,1,0:T(8,128)} %bitcast.10), calls=%async_computation | async-start | bytes 2097152 | tf_op jit(solution)/shard_map/all_to_all | solution.py:221
  35.4 17.6 %collective-permute-start.3 = (f32[2,256,128]{2,1,0:T(8,128)S(1)}, f32[2,256,128]{2,1,0:T(8,128)S(1)}, u32[]{:S(2)}, u32[]{:S(2)}) collective-permute-start(f32[2,256,128]{2,1,0:T(8,128)S(1)} %pad_maximum_fusion.5), channel_id=1, source_target_pairs={{0,3},{1,2},{2,1},{3,0},{4,7},{5,6},{6,5},{7,4},{8,11},{9,10},{10,... | collective-permute-start | bytes 786440 | tf_op jit(solution)/shard_map/ppermute | solution.py:38
  37.3 15.7 %collective-permute-start.2 = (f32[2,256,128]{2,1,0:T(8,128)S(1)}, f32[2,256,128]{2,1,0:T(8,128)S(1)}, u32[]{:S(2)}, u32[]{:S(2)}) collective-permute-start(f32[2,256,128]{2,1,0:T(8,128)S(1)} %pad_maximum_fusion.5), channel_id=1, source_target_pairs={{0,2},{1,3},{2,0},{3,1},{4,6},{5,7},{6,4},{7,5},{8,10},{9,11},{10,... | collective-permute-start | bytes 786440 | tf_op jit(solution)/shard_map/ppermute | solution.py:38
  39.3 15.0 %collective-permute-start.1 = (f32[2,256,128]{2,1,0:T(8,128)S(1)}, f32[2,256,128]{2,1,0:T(8,128)S(1)}, u32[]{:S(2)}, u32[]{:S(2)}) collective-permute-start(f32[2,256,128]{2,1,0:T(8,128)S(1)} %pad_maximum_fusion.5), channel_id=1, source_target_pairs={{0,1},{1,0},{2,3},{3,2},{4,5},{5,4},{6,7},{7,6},{8,9},{9,8},{10,11... | collective-permute-start | bytes 786440 | tf_op jit(solution)/shard_map/ppermute | solution.py:38
  44.4 8.6 %collective-permute-start.4 = (f32[2,32,128]{2,1,0:T(8,128)S(1)}, f32[2,32,128]{2,1,0:T(8,128)S(1)}, u32[]{:S(2)}, u32[]{:S(2)}) collective-permute-start(f32[2,32,128]{2,1,0:T(8,128)S(1)} %pad_maximum_fusion.11), channel_id=1, source_target_pairs={{0,32},{4,36},{8,40},{12,44},{16,48},{20,52},{24,56},{28,60},{32,0... | collective-permute-start | bytes 98312 | tf_op jit(solution)/shard_map/ppermute | solution.py:38
  54.3 40.6 %collective-permute-start.5 = (f32[4,2,256,128]{3,2,1,0:T(8,128)S(1)}, f32[4,2,256,128]{3,2,1,0:T(8,128)S(1)}, u32[]{:S(2)}, u32[]{:S(2)}) collective-permute-start(f32[4,2,256,128]{3,2,1,0:T(8,128)S(1)} %pad_maximum_fusion.mine.m1), channel_id=1, source_target_pairs={{0,4},{4,0},{8,12},{12,8},{16,20},{20,16},{24,28},{28,24},{32,36},... | collective-permute-start | bytes 3145736 | tf_op jit(solution)/shard_map/ppermute | solution.py:38
  58.2 49.6 %all-to-all-start.1 = ((f32[32,20,128]{2,1,0:T(8,128)}), f32[32,20,128]{2,1,0:T(8,128)}, u32[]{:S(2)}, u32[]{:S(2)}) async-start(f32[32,20,128]{2,1,0:T(8,128)} %broadcast_in_dim.10), calls=%async_computation.1 | async-start | bytes 786432 | tf_op jit(solution)/shard_map/all_to_all | solution.py:229
  71.8 114.3 %all-gather.3.cloned.1.call-start = ((), (), s32[]{:S(2)}) async-start(), calls=%async_computation.2 | async-start | bytes 1966080 | tf_op jit(solution)/shard_map/all_gather | solution.py:256
  71.9 23.0 %collective-permute-start.6 = (f32[2,64,128]{2,1,0:T(8,128)S(1)}, f32[2,64,128]{2,1,0:T(8,128)S(1)}, u32[]{:S(2)}, u32[]{:S(2)}) collective-permute-start(f32[2,64,128]{2,1,0:T(8,128)S(1)} %pad_maximum_fusion.10), channel_id=1, source_target_pairs={{0,16},{4,20},{8,24},{12,28},{16,0},{20,4},{24,8},{28,12},{32,48},... | collective-permute-start | bytes 196616 | tf_op jit(solution)/shard_map/ppermute | solution.py:38
  75.9 23.9 %collective-permute-start.7 = (f32[32,1024]{1,0:T(8,128)S(1)}, f32[32,1024]{1,0:T(8,128)S(1)}, u32[]{:S(2)}, u32[]{:S(2)}) collective-permute-start(f32[32,1024]{1,0:T(8,128)S(1)} %slice.74), channel_id=1, source_target_pairs={{0,16},{4,20},{8,24},{12,28},{16,0},{20,4},{24,8},{28,12},{32,48},... | collective-permute-start | bytes 393224 | tf_op jit(solution)/shard_map/ppermute | solution.py:38
  99.8 8.0 %copy-start.16 = (f32[32,1024]{1,0:T(8,128)}, f32[32,1024]{1,0:T(8,128)S(1)}, u32[]{:S(2)}) copy-start(f32[32,1024]{1,0:T(8,128)S(1)} %collective-permute-done.7) | copy-start | bytes 393220
  99.8 7.9 %collective-permute-start.9 = (f32[2,128,128]{2,1,0:T(8,128)S(1)}, f32[2,128,128]{2,1,0:T(8,128)S(1)}, u32[]{:S(2)}, u32[]{:S(2)}) collective-permute-start(f32[2,128,128]{2,1,0:T(8,128)S(1)} %pad_maximum_fusion.9), channel_id=1, source_target_pairs={{0,8},{4,12},{8,0},{12,4},{16,24},{20,28},{24,16},{28,20},{32,40},... | collective-permute-start | bytes 393224 | tf_op jit(solution)/shard_map/ppermute | solution.py:38
  101.7 6.0 %collective-permute-start.8 = (f32[32,512]{1,0:T(8,128)S(1)}, f32[32,512]{1,0:T(8,128)S(1)}, u32[]{:S(2)}, u32[]{:S(2)}) collective-permute-start(f32[32,512]{1,0:T(8,128)S(1)} %get-tuple-element.49), channel_id=1, source_target_pairs={{0,16},{4,20},{8,24},{12,28},{16,0},{20,4},{24,8},{28,12},{32,48},... | collective-permute-start | bytes 196616 | tf_op jit(solution)/shard_map/ppermute | solution.py:38
  109.6 28.3 %collective-permute-start.14 = (f32[3,128,128]{2,1,0:T(8,128)S(1)}, f32[3,128,128]{2,1,0:T(8,128)S(1)}, u32[]{:S(2)}, u32[]{:S(2)}) collective-permute-start(f32[3,128,128]{2,1,0:T(8,128)S(1)} %pad_maximum_fusion.7), channel_id=1, source_target_pairs={{0,8},{4,12},{8,0},{12,4},{16,24},{20,28},{24,16},{28,20},{32,40},... | collective-permute-start | bytes 589832 | tf_op jit(solution)/shard_map/ppermute | solution.py:38
  112.9 25.8 %collective-permute-start.13 = (f32[2,256,128]{2,1,0:T(8,128)S(1)}, f32[2,256,128]{2,1,0:T(8,128)S(1)}, u32[]{:S(2)}, u32[]{:S(2)}) collective-permute-start(f32[2,256,128]{2,1,0:T(8,128)S(1)} %pad_maximum_fusion.6), channel_id=1, source_target_pairs={{0,3},{1,2},{2,1},{3,0},{4,7},{5,6},{6,5},{7,4},{8,11},{9,10},{10,... | collective-permute-start | bytes 786440 | tf_op jit(solution)/shard_map/ppermute | solution.py:38
  117.3 21.4 %collective-permute-start.12 = (f32[2,256,128]{2,1,0:T(8,128)S(1)}, f32[2,256,128]{2,1,0:T(8,128)S(1)}, u32[]{:S(2)}, u32[]{:S(2)}) collective-permute-start(f32[2,256,128]{2,1,0:T(8,128)S(1)} %pad_maximum_fusion.6), channel_id=1, source_target_pairs={{0,2},{1,3},{2,0},{3,1},{4,6},{5,7},{6,4},{7,5},{8,10},{9,11},{10,... | collective-permute-start | bytes 786440 | tf_op jit(solution)/shard_map/ppermute | solution.py:38
  119.7 19.0 %collective-permute-start.11 = (f32[2,256,128]{2,1,0:T(8,128)S(1)}, f32[2,256,128]{2,1,0:T(8,128)}, u32[]{:S(2)}, u32[]{:S(2)}) collective-permute-start(f32[2,256,128]{2,1,0:T(8,128)S(1)} %pad_maximum_fusion.6), channel_id=1, source_target_pairs={{0,1},{1,0},{2,3},{3,2},{4,5},{5,4},{6,7},{7,6},{8,9},{9,8},{10,11... | collective-permute-start | bytes 786440 | tf_op jit(solution)/shard_map/ppermute | solution.py:38
  121.9 10.8 %collective-permute-start.10 = (f32[32,512]{1,0:T(8,128)S(1)}, f32[32,512]{1,0:T(8,128)S(1)}, u32[]{:S(2)}, u32[]{:S(2)}) collective-permute-start(f32[32,512]{1,0:T(8,128)S(1)} %add.51), channel_id=1, source_target_pairs={{0,32},{4,36},{8,40},{12,44},{16,48},{20,52},{24,56},{28,60},{32,0... | collective-permute-start | bytes 196616 | tf_op jit(solution)/shard_map/ppermute | solution.py:38
  132.7 18.7 %collective-permute-start.15 = (f32[32,1024]{1,0:T(8,128)}, f32[32,1024]{1,0:T(8,128)}, u32[]{:S(2)}, u32[]{:S(2)}) collective-permute-start(f32[32,1024]{1,0:T(8,128)} %add.54), channel_id=1, source_target_pairs={{0,32},{4,36},{8,40},{12,44},{16,48},{20,52},{24,56},{28,60},{32,0... | collective-permute-start | bytes 393224 | tf_op jit(solution)/shard_map/ppermute | solution.py:38
  151.4 6.5 %collective-permute-start.16 = (f32[4,2,256,128]{3,2,1,0:T(8,128)S(1)}, f32[4,2,256,128]{3,2,1,0:T(8,128)S(1)}, u32[]{:S(2)}, u32[]{:S(2)}) collective-permute-start(f32[4,2,256,128]{3,2,1,0:T(8,128)S(1)} %pad_maximum_fusion.1.mine.m2), channel_id=1, source_target_pairs={{0,4},{4,0},{8,12},{12,8},{16,20},{20,16},{24,28},{28,24},{32,36},... | collective-permute-start | bytes 3145736 | tf_op jit(solution)/shard_map/ppermute | solution.py:38
  154.9 10.7 %collective-permute-start.17 = (f32[32,512]{1,0:T(8,128)S(1)}, f32[32,512]{1,0:T(8,128)S(1)}, u32[]{:S(2)}, u32[]{:S(2)}) collective-permute-start(f32[32,512]{1,0:T(8,128)S(1)} %get-tuple-element.63), channel_id=1, source_target_pairs={{0,112},{4,116},{8,120},{12,124},{16,96},{20,100},{24,104},{28,108... | collective-permute-start | bytes 196616 | tf_op jit(solution)/shard_map/ppermute | solution.py:38
  165.6 7.1 %collective-permute-start.18 = (f32[32,512]{1,0:T(8,128)S(1)}, f32[32,512]{1,0:T(8,128)S(1)}, u32[]{:S(2)}, u32[]{:S(2)}) collective-permute-start(f32[32,512]{1,0:T(8,128)S(1)} %get-tuple-element.62), channel_id=1, source_target_pairs={{0,112},{4,116},{8,120},{12,124},{16,96},{20,100},{24,104},{28,108... | collective-permute-start | bytes 196616 | tf_op jit(solution)/shard_map/ppermute | solution.py:38
  167.5 5.4 %collective-permute-start.19 = (f32[32,512]{1,0:T(8,128)S(1)}, f32[32,512]{1,0:T(8,128)S(1)}, u32[]{:S(2)}, u32[]{:S(2)}) collective-permute-start(f32[32,512]{1,0:T(8,128)S(1)} %add.57), channel_id=1, source_target_pairs={{0,128},{4,132},{8,136},{12,140},{16,144},{20,148},{24,152},{28,15... | collective-permute-start | bytes 196616 | tf_op jit(solution)/shard_map/ppermute | solution.py:38
  186.0 8.2 %collective-permute-start.21 = (f32[4,3,256,128]{3,2,1,0:T(8,128)}, f32[4,3,256,128]{3,2,1,0:T(8,128)S(1)}, u32[]{:S(2)}, u32[]{:S(2)}) collective-permute-start(f32[4,3,256,128]{3,2,1,0:T(8,128)} %bitcast.34), channel_id=1, source_target_pairs={{0,4},{4,0},{8,12},{12,8},{16,20},{20,16},{24,28},{28,24},{32,36},... | collective-permute-start | bytes 4718600 | tf_op jit(solution)/shard_map/ppermute | solution.py:38
  188.6 5.6 %collective-permute-start.20 = (f32[32,512]{1,0:T(8,128)S(1)}, f32[32,512]{1,0:T(8,128)S(1)}, u32[]{:S(2)}, u32[]{:S(2)}) collective-permute-start(f32[32,512]{1,0:T(8,128)S(1)} %add.56), channel_id=1, source_target_pairs={{0,128},{4,132},{8,136},{12,140},{16,144},{20,148},{24,152},{28,15... | collective-permute-start | bytes 196616 | tf_op jit(solution)/shard_map/ppermute | solution.py:38
  195.6 7.2 %copy-start.4 = (f32[4,2,256,128]{3,2,1,0:T(8,128)S(1)}, f32[4,2,256,128]{3,2,1,0:T(8,128)}, u32[]{:S(2)}) copy-start(f32[4,2,256,128]{3,2,1,0:T(8,128)} %copy-done.3) | copy-start | bytes 3145732
  196.6 6.2 %collective-permute-start.22 = (f32[32,512]{1,0:T(8,128)S(1)}, f32[32,512]{1,0:T(8,128)S(1)}, u32[]{:S(2)}, u32[]{:S(2)}) collective-permute-start(f32[32,512]{1,0:T(8,128)S(1)} %get-tuple-element.70), channel_id=1, source_target_pairs={{0,384},{4,388},{8,392},{12,396},{16,400},{20,404},{24,408},{28,41... | collective-permute-start | bytes 196616 | tf_op jit(solution)/shard_map/ppermute | solution.py:38
  206.5 7.8 %collective-permute-start.23 = (f32[32,2048]{1,0:T(8,128)S(1)}, f32[32,2048]{1,0:T(8,128)S(1)}, u32[]{:S(2)}, u32[]{:S(2)}) collective-permute-start(f32[32,2048]{1,0:T(8,128)S(1)} %shard_map.99), channel_id=1, source_target_pairs={{0,8},{4,12},{8,0},{12,4},{16,24},{20,28},{24,16},{28,20},{32,40},... | collective-permute-start | bytes 786440 | tf_op jit(solution)/shard_map/ppermute | solution.py:38
  214.2 6.8 %copy-start.10 = (f32[896,128]{1,0:T(8,128)S(1)}, f32[896,128]{1,0:T(8,128)}, u32[]{:S(2)}) copy-start(f32[896,128]{1,0:T(8,128)} %copy-done.9) | copy-start | bytes 1376260
  214.3 6.8 %copy-start.2 = (f32[21,128,128]{2,1,0:T(8,128)S(1)}, f32[21,128,128]{2,1,0:T(8,128)}, u32[]{:S(2)}) copy-start(f32[21,128,128]{2,1,0:T(8,128)} %blocks.3) | copy-start | bytes 4128772
  214.3 6.6 %collective-permute-start.24 = (f32[2,32,2048]{2,1,0:T(8,128)S(1)}, f32[2,32,2048]{2,1,0:T(8,128)S(1)}, u32[]{:S(2)}, u32[]{:S(2)}) collective-permute-start(f32[2,32,2048]{2,1,0:T(8,128)S(1)} %pad_maximum_fusion.3), channel_id=1, source_target_pairs={{0,4},{4,0},{8,12},{12,8},{16,20},{20,16},{24,28},{28,24},{32,36},... | collective-permute-start | bytes 1572872 | tf_op jit(solution)/shard_map/ppermute | solution.py:38
  (13 other events, 30.2 us)
Sparse Core Ops, SparseCore 0:
  151.6 34.4 all-gather.2

commit v4 on v3

--- a/solution.py
+++ b/solution.py
@@ -30,8 +30,18 @@
     return dot(left_high, right_high) + (dot(left_high, right_low) + dot(left_low, right_high))
 
 
-def exact(left, right, dims):
-    return lax.dot_general(left, right, dims, precision=lax.Precision.HIGHEST, preferred_element_type=F32)
+def pick_left(spread, value, dims):
+    high, low = halves(value)
+    rest = (value - high.astype(F32) - low.astype(F32)).astype(BF16)
+    dot = functools.partial(lax.dot_general, spread, dimension_numbers=dims, preferred_element_type=F32)
+    return dot(high) + (dot(low) + dot(rest))
+
+
+def pick_right(value, spread, dims):
+    high, low = halves(value)
+    rest = (value - high.astype(F32) - low.astype(F32)).astype(BF16)
+    dot = functools.partial(lax.dot_general, dimension_numbers=dims, preferred_element_type=F32)
+    return dot(high, spread) + (dot(low, spread) + dot(rest, spread))
 
 
 def swap(value, axis, mask):
@@ -58,7 +68,7 @@
     row = lax.broadcasted_iota(jnp.int32, (rows, width), 0)
     column = lax.broadcasted_iota(jnp.int32, (rows, width), 1)
     inside = (row >= offset) & (row < offset + count)
-    return jnp.where(inside & (row - offset == column - start), 1.0, 0.0).astype(F32)
+    return jnp.where(inside & (row - offset == column - start), 1.0, 0.0).astype(BF16)
 
 
 def forward_kernel(sizes, where, pattern, rhs, inverse, blocks, coupling, sep_rhs, y_out, t_out):
@@ -79,7 +89,7 @@
     for level, rows in enumerate(sizes):
         spread = placement(right.shape[0], offset, rows, where[level], width)
         offset += rows
-        t_out[:, level * width : (level + 1) * width] = exact(right, spread, TN) - mm(
+        t_out[:, level * width : (level + 1) * width] = pick_right(right, spread, TN) - mm(
             last, coupling[level * size : (level + 1) * size, :], TN
         )
 
@@ -98,7 +108,7 @@
         part = xs[:, level * width : (level + 1) * width]
         correction = correction + mm(coupling[level * size : (level + 1) * size, :], part, NT)
         spread = placement(sep_out.shape[0], offset, rows, where[level], width)
-        pieces = pieces + exact(spread, part, NT)
+        pieces = pieces + pick_left(spread, part, NT)
         offset += rows
     sep_out[...] = pieces
     pending = [y[i * size : (i + 1) * size, :] for i in range(count)]
@@ -112,8 +122,8 @@
             pending[earlier] = pending[earlier] - weight * mm(blocks[pair], solved, TN)
 
 
-def spots(start, plane, count):
-    return [pl.ds(pl.multiple_of(start + (plane ^ r) * 128, 128), 128) for r in range(count)]
+def spots(start, count):
+    return [slice(start + r * 128, start + (r + 1) * 128) for r in range(count)]
 
 
 def times_rows(value, places, mats, index):
@@ -135,30 +145,30 @@
     return total
 
 
-def level_kernel(index, plane, right, base, mine, other, z_out, v_out):
+def level_kernel(index, right, base, mine, other, z_out, v_out):
     mats = (mine, other)
-    places = spots(0, plane[0], mine.shape[0])
+    places = spots(0, mine.shape[0])
     z = times_rows(right, places, mats, index)
     z_out[...] = jnp.concatenate(z, axis=1)
     for r, place in enumerate(places):
         v_out[:, place] = base[:, place] - times_matrix(z, mats, index + 1, r)
 
 
-def top_kernel(plane, right, z1, z2, z3, m1, o1, m2, o2, m3, o3, x_out):
+def top_kernel(right, z1, z2, z3, m1, o1, m2, o2, m3, o3, x_out):
     width = right.shape[1]
     count = m3.shape[0]
     top = (m3, o3)
-    z = times_rows(right, spots(0, 0, count), top, 0)
-    order = [(z3, top, 1, 0), (z2, (m2, o2), 0, plane[0]), (z1, (m1, o1), 0, plane[0])]
-    mats, index, turn = top, 0, 0
+    z = times_rows(right, spots(0, count), top, 0)
+    order = [(z3, top, 1), (z2, (m2, o2), 0), (z1, (m1, o1), 0)]
+    mats, index = top, 0
     level = 3
     while True:
-        for r, place in enumerate(spots(level * width, turn, count)):
+        for r, place in enumerate(spots(level * width, count)):
             x_out[:, place] = times_matrix(z, mats, index, r)
         if not order:
             break
-        held, mats, index, turn = order.pop(0)
-        moved = times_rows(x_out, spots(level * width, turn, count), mats, index + 1)
+        held, mats, index = order.pop(0)
+        moved = times_rows(x_out, spots(level * width, count), mats, index + 1)
         half = held.shape[1] // 2
         z = [held[:, :half] - moved[0], held[:, half:] - moved[1]]
         level -= 1
@@ -192,8 +202,6 @@
     offsets = [sum(sizes[:i]) for i in range(LEVELS)]
     where = jnp.stack([position % g * r for g, r in zip(groups, sizes)] + [position % 4]).astype(jnp.int32)
 
-    plane = lax.axis_index("col").astype(jnp.int32)[None]
-
     def rows(array, level):
         return array[offsets[level] : offsets[level] + sizes[level]]
 
@@ -201,75 +209,62 @@
         return jnp.stack([rows(sep_inverse, level), rows(sep_coupling, level)])
 
     def planes(value):
-        return jnp.stack([value] + [swap(value, "col", r) for r in range(1, lax.axis_size("col"))])
+        count = lax.axis_size("col")
+        return lax.all_to_all(jnp.broadcast_to(value[None], (count, *value.shape)), "col", 0, 0, tiled=True)
 
     tie = lax.optimization_barrier
     halves_z, wrap_z, wrap_y = 1 << Z4, (1 << Z8) | (1 << Z4) | (1 << Z2), (1 << Y2) | (1 << Y1)
-
+    near = [[g * 4 + m for m in range(4)] for g in range(leaves // 4)]
+    level = lambda kernel, *arrays: call(kernel, [(columns // 4, width)] * 2, *arrays)
+
+    first = grow(both(0), 1 << Z1)
+    far = grow(rows(sep_inverse, 3)[None], wrap_y)
     padded = jnp.pad(sep_rhs, ((0, 4), (0, 0)))
-    first, second = both(0), both(1)
-    far = jnp.concatenate([rows(sep_inverse, 2), rows(sep_coupling, 2), rows(sep_inverse, 3)], 0)
-    first = grow(first, 1 << Z1)
     y, t = call(
         functools.partial(forward_kernel, sizes),
         [leaf_rhs.shape, (columns, LEVELS * width)],
         where, leaf_pattern, leaf_rhs, leaf_inverse, leaf_blocks, leaf_coupling, padded,
     )
-    t, first, second, far = tie((t, first, second, far))
-
-    near = [[g * 4 + m for m in range(4)] for g in range(leaves // 4)]
+    t, first, far = tie((t, first, far))
+
     t = lax.all_to_all(t, "leaf", 0, 0, axis_index_groups=near, tiled=True)
+    far = grow(jnp.concatenate([far, both(2)], 0), 1 << Y1)
     first = planes(first)
-    second = grow(second, halves_z)
-    t, first, second, far = tie((t, first, second, far))
-
-    count = leaves // 4
-    far = jnp.broadcast_to(far[None], (count, *far.shape))
-    apart = [[m + 4 * k for k in range(count)] for m in range(4)]
-    far = lax.all_to_all(far, "leaf", 0, 0, axis_index_groups=apart, tiled=True)
+    t, far = tie((t, far))
+
+    far = grow(far, wrap_z)
     t = t.reshape(4, columns // 4, LEVELS * width).sum(0)
-    t1, t2, upper = t[:, :width], t[:, width : 2 * width], t[:, 2 * width :]
+    first, t, far = tie((first, t, far))
+
+    far = grow(jnp.concatenate([far, both(1)], 0), halves_z)
     first = (first, across(first, CORE_MASK))
-    second = grow(second, 1 << Z2)
-    upper_z2 = across(upper, 1 << Z2)
-    shape = t1.shape
-    z1, v = call(functools.partial(level_kernel, 0), [shape] * 2, plane, t1, t2, *first)
-    v, second, upper, upper_z2 = tie((v, second, upper, upper_z2))
-
-    upper = upper + upper_z2
-    second = grow(second, 1 << Z1)
-    upper_z4 = across(upper, halves_z)
+    z1, v = level(functools.partial(level_kernel, 0), t[:, :width], t[:, width : 2 * width], *first)
+    v = jnp.concatenate([v, t[:, 2 * width :]], 1)
+    v, far = tie((v, far))
+
+    far = grow(far, 1 << Z2)
     v = v + across(v, 1 << Z2)
-    v, second, far = tie((v, second, far))
-
-    own = lax.dynamic_slice_in_dim(far, position // 64 * 16, 16, 0)
-    third = jnp.stack([
-        far[:, 2 * sizes[2] :].reshape(-1, 128),
-        own[:, : sizes[2]].reshape(-1, 128),
-        own[:, sizes[2] : 2 * sizes[2]].reshape(-1, 128),
-    ])
-    second = planes(second)
-    third = grow(third, 1 << Z1)
-    v = v + across(v, halves_z)
-    v, second, third, upper, upper_z4 = tie((v, second, third, upper, upper_z4))
-
-    third = lax.all_gather(third, "col", axis=0)
+    v, far = tie((v, far))
+
+    far = grow(far, 1 << Z1)
+    v_far = across(v, halves_z)
+    far, v = tie((far, v))
+
+    third = lax.all_gather(far[:3], "col", axis=0)
+    second = planes(far[3:])
+    second, v, v_far = tie((second, v, v_far))
     second = (second, across(second, CORE_MASK))
-    upper = upper + upper_z4
-    t3, t4 = upper[:, :width], upper[:, width:]
-    t4_far = across(t4, wrap_z)
-    z2, v = call(functools.partial(level_kernel, 0), [shape] * 2, plane, v, t3, *second)
-    v, t4, t4_far = tie((v, t4, t4_far))
-
-    t4 = t4 + t4_far
-    t4_y = across(t4, 1 << Y1)
+    v = v + v_far
+    z2, v3 = level(functools.partial(level_kernel, 0), v[:, :width], v[:, width : 2 * width], *second)
+    v = jnp.concatenate([v3, v[:, 2 * width :]], 1)
     v = v + across(v, wrap_z)
-    v, t4, t4_y, third = tie((v, t4, t4_y, third))
+    v, third = tie((v, third))
+
     third = (third, across(third, CORE_MASK))
     v = v + across(v, 1 << Y1)
-    z3, v = call(functools.partial(level_kernel, 1), [shape] * 2, plane * 0, v, t4 + t4_y, *third)
+    z3, v = level(functools.partial(level_kernel, 1), v[:, :width], v[:, width:], *third)
     v = v + across(v, wrap_y)
-    (x,) = call(top_kernel, [(shape[0], LEVELS * width)], plane, v, z1, z2, z3, *first, *second, *third)
+    (x,) = call(top_kernel, [(columns // 4, LEVELS * width)], v, z1, z2, z3, *first, *second, *third)
     x = jnp.stack([x, across(x, 1 << Z1)])
     other = across(x, CORE_MASK)
     x = jnp.stack([x[0], other[0], x[1], other[1]], 0)

time: 234 us -> 221 us (0.944)
  starting transfers between devices: 108 us -> 74.5 us
  blocking collectives: 0 us -> 18.2 us
  waiting for transfers between devices: 71.7 us -> 80 us
  other arithmetic: 4.98 us -> 1.39 us
    ppermute x25 -> x17, waiting for transfers between devices: 58.6 us -> 80 us  [swap(): lax.ppermute(value, axis, [(i, i ^ mask) for i in range(lax.axis_size(axi...]
    ppermute x25 -> x17, starting transfers between devices: 86.8 us -> 66.6 us  [swap(): lax.ppermute(value, axis, [(i, i ^ mask) for i in range(lax.axis_size(axi...]
    all_to_all x0 -> x1, blocking collectives: none -> 18.2 us  [shards(): t = lax.all_to_all(t, 'leaf', 0, 0, axis_index_groups=near, tiled=True)]
    all_to_all x2, starting transfers between devices: 21.5 us -> 7.92 us  [planes(): lax.all_to_all(jnp.broadcast_to(value[None], (count, *value.shape)), 'col...]
    all_gather x1, waiting for transfers between devices: 13.1 us -> 0.02 us  [shards(): third = lax.all_gather(far[:3], 'col', axis=0)]
    unnamed x34 -> x28, local copies, waits for them, and re-layouts: 9.24 us -> 7.66 us
  transfers between devices with their start and end apart: 28 -> 20, of which waited for: 15 -> 13; matrix products, arithmetic and copies ran while one was open for 4% -> 3% of each run, Pallas kernels for 3% -> 2%
where the time goes in v4:
time: 221 us; the launch traced here: 219 us
  waiting for transfers between devices  80 us (36%)
  starting transfers between devices  74.5 us (34%)
  blocking collectives  18.2 us (8%)
  local copies, waits for them, and re-layouts  16 us (7%)
  Pallas kernels  14.7 us (7%)
  between operations  14.5 us (7%)
    ppermute x17, waiting for transfers between devices, swap(): lax.ppermute(value, axis, [(i, i ^ mask) for i in range(lax.axis_size(axi...  80 us
    ppermute x17, starting transfers between devices, swap(): lax.ppermute(value, axis, [(i, i ^ mask) for i in range(lax.axis_size(axi...  66.6 us
    all_to_all x1, blocking collectives, shards(): t = lax.all_to_all(t, 'leaf', 0, 0, axis_index_groups=near, tiled=True)  18.2 us
    pallas_call x6, Pallas kernels, call(): pl.pallas_call(kernel, out_shape=[jax.ShapeDtypeStruct(s, F32) for s in o...  14.7 us
    all_to_all x2, starting transfers between devices, planes(): lax.all_to_all(jnp.broadcast_to(value[None], (count, *value.shape)), 'col...  7.92 us
    unnamed x28, local copies, waits for them, and re-layouts  7.66 us
  transfers between devices with their start and end apart: 20, of which 13 were waited for; matrix products, arithmetic and copies ran while one was open for 3% of the time, Pallas kernels for 2%

profile of v4, /device:TPU:1, one launch (start us, length us, event | category | flops | bytes accessed | tf_op | source)
XLA Modules:
  0.0 219.4 jit_solution(11811171664745136719)
XLA Ops:
  8.1 4.4 %collective-permute-start = (f32[2,128,128]{2,1,0:T(8,128)S(1)}, f32[2,128,128]{2,1,0:T(8,128)S(1)}, u32[]{:S(2)}, u32[]{:S(2)}) collective-permute-start(f32[2,128,128]{2,1,0:T(8,128)S(1)} %pad_maximum_fusion.7), channel_id=1, source_target_pairs={{0,8},{4,12},{8,0},{12,4},{16,24},{20,28},{24,16},{28,20},{32,40},... | collective-permute-start | bytes 393224 | tf_op jit(solution)/shard_map/ppermute | solution.py:48
  13.1 4.6 %collective-permute-start.1 = (f32[1,4,128]{2,1,0:T(4,128)S(1)}, f32[1,4,128]{2,1,0:T(4,128)S(1)}, u32[]{:S(2)}, u32[]{:S(2)}) collective-permute-start(f32[1,4,128]{2,1,0:T(4,128)S(1)} %slice_bitcast_fusion.6), channel_id=1, source_target_pairs={{0,384},{4,388},{8,392},{12,396},{16,400},{20,404},{24,408},{28,41... | collective-permute-start | bytes 6152 | tf_op jit(solution)/shard_map/ppermute | solution.py:48
  24.1 3.8 %shard_map.95 = (f32[896,128]{1,0:T(8,128)S(1)}, f32[128,2048]{1,0:T(8,128)S(1)}) custom-call(s32[5]{0:T(128)S(1)} %stack.56.where, s32[1,21]{1,0:T(1,128)S(1)} %copy-done.12, f32[896,128]{1,0:T(8,128)S(1)} %copy-done.11, f32[7,128,128]{2,1,0:T(8,128)S(1)} %copy-done.7, f32[21,128,128]{2,1,0:T(8,128)S(1)} %copy-done.1, f32[512,512]{1,0:T(8,128)S(1)} %copy-done.3, ...), custom_call_target="tpu_custom_call" | custom-call | tf_op jit(solution)/shard_map/pallas_call | solution.py:186
  27.9 18.2 %all_to_all.22 = f32[4,32,2048]{2,1,0:T(8,128)S(1)} all-to-all(f32[4,32,2048]{2,1,0:T(8,128)S(1)} %bitcast.31), channel_id=1, replica_groups={{0,4,8,12},{16,20,24,28},{32,36,40,44},{48,52,56,60},{64,68,72,76},{80,..., dimensions={0} | all-to-all | bytes 2097152 | tf_op jit(solution)/shard_map/all_to_all | solution.py:230
  47.2 3.5 %all-to-all-start = ((f32[4,2,256,128]{3,2,1,0:T(8,128)}), f32[4,2,256,128]{3,2,1,0:T(8,128)S(1)}, u32[]{:S(2)}, u32[]{:S(2)}) async-start(f32[4,2,256,128]{3,2,1,0:T(8,128)} %broadcast_in_dim.7), calls=%async_computation | async-start | bytes 2097152 | tf_op jit(solution)/shard_map/all_to_all | solution.py:213
  54.1 2.8 %collective-permute-done.2 = f32[3,8,128]{2,1,0:T(8,128)S(1)} collective-permute-done((f32[3,8,128]{2,1,0:T(8,128)S(1)}, f32[3,8,128]{2,1,0:T(8,128)S(1)}, u32[]{:S(2)}, u32[]{:S(2)}) %collective-permute-start.2) | collective-permute-done | bytes 12320 | tf_op jit(solution)/shard_map/ppermute | solution.py:48
  56.9 10.0 %collective-permute-start.3 = (f32[3,16,128]{2,1,0:T(8,128)S(1)}, f32[3,16,128]{2,1,0:T(8,128)S(1)}, u32[]{:S(2)}, u32[]{:S(2)}) collective-permute-start(f32[3,16,128]{2,1,0:T(8,128)S(1)} %pad_maximum_fusion.11), channel_id=1, source_target_pairs={{0,112},{4,116},{8,120},{12,124},{16,96},{20,100},{24,104},{28,108... | collective-permute-start | bytes 73736 | tf_op jit(solution)/shard_map/ppermute | solution.py:48
  68.1 5.1 %collective-permute-start.4 = (f32[4,2,256,128]{3,2,1,0:T(8,128)S(1)}, f32[4,2,256,128]{3,2,1,0:T(8,128)S(1)}, u32[]{:S(2)}, u32[]{:S(2)}) collective-permute-start(f32[4,2,256,128]{3,2,1,0:T(8,128)S(1)} %all-to-all-done.mine.m1), channel_id=1, source_target_pairs={{0,4},{4,0},{8,12},{12,8},{16,20},{20,16},{24,28},{28,24},{32,36},... | collective-permute-start | bytes 3145736 | tf_op jit(solution)/shard_map/ppermute | solution.py:48
  74.6 7.4 %collective-permute-start.5 = (f32[5,32,128]{2,1,0:T(8,128)S(1)}, f32[5,32,128]{2,1,0:T(8,128)S(1)}, u32[]{:S(2)}, u32[]{:S(2)}) collective-permute-start(f32[5,32,128]{2,1,0:T(8,128)S(1)} %pad_maximum_fusion.9), channel_id=1, source_target_pairs={{0,32},{4,36},{8,40},{12,44},{16,48},{20,52},{24,56},{28,60},{32,0... | collective-permute-start | bytes 245768 | tf_op jit(solution)/shard_map/ppermute | solution.py:48
  82.1 7.9 %collective-permute-done.5 = f32[5,32,128]{2,1,0:T(8,128)S(1)} collective-permute-done((f32[5,32,128]{2,1,0:T(8,128)S(1)}, f32[5,32,128]{2,1,0:T(8,128)S(1)}, u32[]{:S(2)}, u32[]{:S(2)}) %collective-permute-start.5) | collective-permute-done | bytes 81952 | tf_op jit(solution)/shard_map/ppermute | solution.py:48
  91.0 1.9 collective-permute-start.7
  93.0 4.3 %collective-permute-start.6 = (f32[32,1536]{1,0:T(8,128)S(1)}, f32[32,1536]{1,0:T(8,128)S(1)}, u32[]{:S(2)}, u32[]{:S(2)}) collective-permute-start(f32[32,1536]{1,0:T(8,128)S(1)} %pad_maximum_fusion.5), channel_id=1, source_target_pairs={{0,16},{4,20},{8,24},{12,28},{16,0},{20,4},{24,8},{28,12},{32,48},... | collective-permute-start | bytes 589832 | tf_op jit(solution)/shard_map/ppermute | solution.py:48
  97.2 6.5 %collective-permute-done.7 = f32[5,64,128]{2,1,0:T(8,128)S(1)} collective-permute-done((f32[5,64,128]{2,1,0:T(8,128)S(1)}, f32[5,64,128]{2,1,0:T(8,128)S(1)}, u32[]{:S(2)}, u32[]{:S(2)}) %collective-permute-start.7) | collective-permute-done | bytes 163872 | tf_op jit(solution)/shard_map/ppermute | solution.py:48
  103.8 4.2 %collective-permute-done.6 = f32[32,1536]{1,0:T(8,128)S(1)} collective-permute-done((f32[32,1536]{1,0:T(8,128)S(1)}, f32[32,1536]{1,0:T(8,128)S(1)}, u32[]{:S(2)}, u32[]{:S(2)}) %collective-permute-start.6) | collective-permute-done | bytes 196640 | tf_op jit(solution)/shard_map/ppermute | solution.py:48
  108.0 1.9 collective-permute-start.8
  109.9 8.3 %collective-permute-done.8 = f32[5,128,128]{2,1,0:T(8,128)S(1)} collective-permute-done((f32[5,128,128]{2,1,0:T(8,128)S(1)}, f32[5,128,128]{2,1,0:T(8,128)S(1)}, u32[]{:S(2)}, u32[]{:S(2)}) %collective-permute-start.8) | collective-permute-done | bytes 327712 | tf_op jit(solution)/shard_map/ppermute | solution.py:48
  120.2 4.4 %all-to-all-start.2 = ((f32[4,2,256,128]{3,2,1,0:T(8,128)}), f32[4,2,256,128]{3,2,1,0:T(8,128)S(1)}, u32[]{:S(2)}, u32[]{:S(2)}) async-start(f32[4,2,256,128]{3,2,1,0:T(8,128)} %broadcast_in_dim.8), calls=%async_computation.2 | async-start | bytes 2097152 | tf_op jit(solution)/shard_map/all_to_all | solution.py:213
  124.6 3.3 %collective-permute-start.9 = (f32[32,1536]{1,0:T(8,128)S(1)}, f32[32,1536]{1,0:T(8,128)}, u32[]{:S(2)}, u32[]{:S(2)}) collective-permute-start(f32[32,1536]{1,0:T(8,128)S(1)} %add.35), channel_id=1, source_target_pairs={{0,32},{4,36},{8,40},{12,44},{16,48},{20,52},{24,56},{28,60},{32,0... | collective-permute-start | bytes 589832 | tf_op jit(solution)/shard_map/ppermute | solution.py:48
  127.9 21.0 %collective-permute-done.9 = f32[32,1536]{1,0:T(8,128)} collective-permute-done((f32[32,1536]{1,0:T(8,128)S(1)}, f32[32,1536]{1,0:T(8,128)}, u32[]{:S(2)}, u32[]{:S(2)}) %collective-permute-start.9) | collective-permute-done | bytes 196640 | tf_op jit(solution)/shard_map/ppermute | solution.py:48
  148.9 2.4 %collective-permute-start.10 = (f32[4,2,256,128]{3,2,1,0:T(8,128)S(1)}, f32[4,2,256,128]{3,2,1,0:T(8,128)S(1)}, u32[]{:S(2)}, u32[]{:S(2)}) collective-permute-start(f32[4,2,256,128]{3,2,1,0:T(8,128)S(1)} %all-to-all-done.2.mine.m2), channel_id=1, source_target_pairs={{0,4},{4,0},{8,12},{12,8},{16,20},{20,16},{24,28},{28,24},{32,36},... | collective-permute-start | bytes 3145736 | tf_op jit(solution)/shard_map/ppermute | solution.py:48
  155.5 2.6 %collective-permute-start.11 = (f32[32,1024]{1,0:T(8,128)S(1)}, f32[32,1024]{1,0:T(8,128)S(1)}, u32[]{:S(2)}, u32[]{:S(2)}) collective-permute-start(f32[32,1024]{1,0:T(8,128)S(1)} %pad_maximum_fusion.8), channel_id=1, source_target_pairs={{0,112},{4,116},{8,120},{12,124},{16,96},{20,100},{24,104},{28,108... | collective-permute-start | bytes 393224 | tf_op jit(solution)/shard_map/ppermute | solution.py:48
  158.1 11.3 %collective-permute-done.11 = f32[32,1024]{1,0:T(8,128)S(1)} collective-permute-done((f32[32,1024]{1,0:T(8,128)S(1)}, f32[32,1024]{1,0:T(8,128)S(1)}, u32[]{:S(2)}, u32[]{:S(2)}) %collective-permute-start.11) | collective-permute-done | bytes 131104 | tf_op jit(solution)/shard_map/ppermute | solution.py:48
  169.4 2.4 %collective-permute-start.13 = (f32[4,3,256,128]{3,2,1,0:T(8,128)}, f32[4,3,256,128]{3,2,1,0:T(8,128)S(1)}, u32[]{:S(2)}, u32[]{:S(2)}) collective-permute-start(f32[4,3,256,128]{3,2,1,0:T(8,128)} %bitcast.26), channel_id=1, source_target_pairs={{0,4},{4,0},{8,12},{12,8},{16,20},{20,16},{24,28},{28,24},{32,36},... | collective-permute-start | bytes 4718600 | tf_op jit(solution)/shard_map/ppermute | solution.py:48
  171.9 1.9 collective-permute-start.12
  173.8 5.1 %collective-permute-done.12 = f32[32,1024]{1,0:T(8,128)S(1)} collective-permute-done((f32[32,1024]{1,0:T(8,128)S(1)}, f32[32,1024]{1,0:T(8,128)S(1)}, u32[]{:S(2)}, u32[]{:S(2)}) %collective-permute-start.12) | collective-permute-done | bytes 131104 | tf_op jit(solution)/shard_map/ppermute | solution.py:48
  181.3 1.9 collective-permute-start.14
  183.2 4.3 %collective-permute-done.14 = f32[32,512]{1,0:T(8,128)S(1)} collective-permute-done((f32[32,512]{1,0:T(8,128)S(1)}, f32[32,512]{1,0:T(8,128)S(1)}, u32[]{:S(2)}, u32[]{:S(2)}) %collective-permute-start.14) | collective-permute-done | bytes 65568 | tf_op jit(solution)/shard_map/ppermute | solution.py:48
  187.6 3.4 %shard_map.99 = f32[32,2048]{1,0:T(8,128)S(1)} custom-call(f32[32,512]{1,0:T(8,128)S(1)} %add.39.right, f32[32,512]{1,0:T(8,128)S(1)} %get-tuple-element.55.z1, f32[32,512]{1,0:T(8,128)S(1)} %get-tuple-element.56.z2, f32[32,512]{1,0:T(8,128)S(1)} %get-tuple-element.57.z3, f32[4,2,256,128]{3,2,1,0:T(8,128)S(1)} %all-to-all-done.mine.m1, ...), custom_call_target="tpu_custom_call" | custom-call | tf_op jit(solution)/shard_map/pallas_call | solution.py:186
  191.0 5.7 %collective-permute-start.15 = (f32[32,2048]{1,0:T(8,128)S(1)}, f32[32,2048]{1,0:T(8,128)S(1)}, u32[]{:S(2)}, u32[]{:S(2)}) collective-permute-start(f32[32,2048]{1,0:T(8,128)S(1)} %shard_map.99), channel_id=1, source_target_pairs={{0,8},{4,12},{8,0},{12,4},{16,24},{20,28},{24,16},{28,20},{32,40},... | collective-permute-start | bytes 786440 | tf_op jit(solution)/shard_map/ppermute | solution.py:48
  196.7 4.6 %collective-permute-done.15 = f32[32,2048]{1,0:T(8,128)S(1)} collective-permute-done((f32[32,2048]{1,0:T(8,128)S(1)}, f32[32,2048]{1,0:T(8,128)S(1)}, u32[]{:S(2)}, u32[]{:S(2)}) %collective-permute-start.15) | collective-permute-done | bytes 262176 | tf_op jit(solution)/shard_map/ppermute | solution.py:48
  201.4 4.8 %collective-permute-start.16 = (f32[2,32,2048]{2,1,0:T(8,128)S(1)}, f32[2,32,2048]{2,1,0:T(8,128)S(1)}, u32[]{:S(2)}, u32[]{:S(2)}) collective-permute-start(f32[2,32,2048]{2,1,0:T(8,128)S(1)} %pad_maximum_fusion.2), channel_id=1, source_target_pairs={{0,4},{4,0},{8,12},{12,8},{16,20},{20,16},{24,28},{28,24},{32,36},... | collective-permute-start | bytes 1572872 | tf_op jit(solution)/shard_map/ppermute | solution.py:48
  207.9 4.6 %shard_map.100 = (f32[896,128]{1,0:T(8,128)}, f32[176,128]{1,0:T(8,128)}) custom-call(s32[5]{0:T(128)S(1)} %stack.56.where, s32[1,21]{1,0:T(1,128)S(1)} %copy-done.13, f32[896,128]{1,0:T(8,128)S(1)} %copy-done.10, f32[4,32,2048]{2,1,0:T(8,128)S(1)} %pad_maximum_fusion.x, f32[7,128,128]{2,1,0:T(8,128)S(1)} %copy-done.8, f32[21,128,128]{2,1,0:T(8,128)S(1)} %copy-done.2, ...), custom_call_target="tpu_custom_call" | custom-call | tf_op jit(solution)/shard_map/pallas_call | solution.py:186
  (81 shorter events, 26.2 us)
Async XLA Ops:
  8.1 19.8 %collective-permute-start = (f32[2,128,128]{2,1,0:T(8,128)S(1)}, f32[2,128,128]{2,1,0:T(8,128)S(1)}, u32[]{:S(2)}, u32[]{:S(2)}) collective-permute-start(f32[2,128,128]{2,1,0:T(8,128)S(1)} %pad_maximum_fusion.7), channel_id=1, source_target_pairs={{0,8},{4,12},{8,0},{12,4},{16,24},{20,28},{24,16},{28,20},{32,40},... | collective-permute-start | bytes 393224 | tf_op jit(solution)/shard_map/ppermute | solution.py:48
  13.1 14.7 %collective-permute-start.1 = (f32[1,4,128]{2,1,0:T(4,128)S(1)}, f32[1,4,128]{2,1,0:T(4,128)S(1)}, u32[]{:S(2)}, u32[]{:S(2)}) collective-permute-start(f32[1,4,128]{2,1,0:T(4,128)S(1)} %slice_bitcast_fusion.6), channel_id=1, source_target_pairs={{0,384},{4,388},{8,392},{12,396},{16,400},{20,404},{24,408},{28,41... | collective-permute-start | bytes 6152 | tf_op jit(solution)/shard_map/ppermute | solution.py:48
  18.8 1.3 copy-start.1
  20.1 1.2 copy-start.3
  21.4 1.0 copy-start.7
  22.4 1.0 copy-start.11
  27.9 18.3 %copy-start.9 = (f32[896,128]{1,0:T(8,128)}, f32[896,128]{1,0:T(8,128)S(1)}, u32[]{:S(2)}) copy-start(f32[896,128]{1,0:T(8,128)S(1)} %get-tuple-element.31.y) | copy-start | bytes 1376260
  47.2 20.9 %all-to-all-start = ((f32[4,2,256,128]{3,2,1,0:T(8,128)}), f32[4,2,256,128]{3,2,1,0:T(8,128)S(1)}, u32[]{:S(2)}, u32[]{:S(2)}) async-start(f32[4,2,256,128]{3,2,1,0:T(8,128)} %broadcast_in_dim.7), calls=%async_computation | async-start | bytes 2097152 | tf_op jit(solution)/shard_map/all_to_all | solution.py:213
  50.7 118.7 %all-gather.3.cloned.1.call-start = ((), (), s32[]{:S(2)}) async-start(), calls=%async_computation.3 | async-start | bytes 1966080 | tf_op jit(solution)/shard_map/all_gather | solution.py:253
  52.2 4.7 %collective-permute-start.2 = (f32[3,8,128]{2,1,0:T(8,128)S(1)}, f32[3,8,128]{2,1,0:T(8,128)S(1)}, u32[]{:S(2)}, u32[]{:S(2)}) collective-permute-start(f32[3,8,128]{2,1,0:T(8,128)S(1)} %pad_maximum_fusion.12), channel_id=1, source_target_pairs={{0,128},{4,132},{8,136},{12,140},{16,144},{20,148},{24,152},{28,15... | collective-permute-start | bytes 36872 | tf_op jit(solution)/shard_map/ppermute | solution.py:48
  56.9 11.2 %collective-permute-start.3 = (f32[3,16,128]{2,1,0:T(8,128)S(1)}, f32[3,16,128]{2,1,0:T(8,128)S(1)}, u32[]{:S(2)}, u32[]{:S(2)}) collective-permute-start(f32[3,16,128]{2,1,0:T(8,128)S(1)} %pad_maximum_fusion.11), channel_id=1, source_target_pairs={{0,112},{4,116},{8,120},{12,124},{16,96},{20,100},{24,104},{28,108... | collective-permute-start | bytes 73736 | tf_op jit(solution)/shard_map/ppermute | solution.py:48
  68.1 21.9 %collective-permute-start.4 = (f32[4,2,256,128]{3,2,1,0:T(8,128)S(1)}, f32[4,2,256,128]{3,2,1,0:T(8,128)S(1)}, u32[]{:S(2)}, u32[]{:S(2)}) collective-permute-start(f32[4,2,256,128]{3,2,1,0:T(8,128)S(1)} %all-to-all-done.mine.m1), channel_id=1, source_target_pairs={{0,4},{4,0},{8,12},{12,8},{16,20},{20,16},{24,28},{28,24},{32,36},... | collective-permute-start | bytes 3145736 | tf_op jit(solution)/shard_map/ppermute | solution.py:48
  74.6 15.4 %collective-permute-start.5 = (f32[5,32,128]{2,1,0:T(8,128)S(1)}, f32[5,32,128]{2,1,0:T(8,128)S(1)}, u32[]{:S(2)}, u32[]{:S(2)}) collective-permute-start(f32[5,32,128]{2,1,0:T(8,128)S(1)} %pad_maximum_fusion.9), channel_id=1, source_target_pairs={{0,32},{4,36},{8,40},{12,44},{16,48},{20,52},{24,56},{28,60},{32,0... | collective-permute-start | bytes 245768 | tf_op jit(solution)/shard_map/ppermute | solution.py:48
  91.0 12.7 %collective-permute-start.7 = (f32[5,64,128]{2,1,0:T(8,128)S(1)}, f32[5,64,128]{2,1,0:T(8,128)S(1)}, u32[]{:S(2)}, u32[]{:S(2)}) collective-permute-start(f32[5,64,128]{2,1,0:T(8,128)S(1)} %pad_maximum_fusion.6), channel_id=1, source_target_pairs={{0,16},{4,20},{8,24},{12,28},{16,0},{20,4},{24,8},{28,12},{32,48},... | collective-permute-start | bytes 491528 | tf_op jit(solution)/shard_map/ppermute | solution.py:48
  93.0 15.0 %collective-permute-start.6 = (f32[32,1536]{1,0:T(8,128)S(1)}, f32[32,1536]{1,0:T(8,128)S(1)}, u32[]{:S(2)}, u32[]{:S(2)}) collective-permute-start(f32[32,1536]{1,0:T(8,128)S(1)} %pad_maximum_fusion.5), channel_id=1, source_target_pairs={{0,16},{4,20},{8,24},{12,28},{16,0},{20,4},{24,8},{28,12},{32,48},... | collective-permute-start | bytes 589832 | tf_op jit(solution)/shard_map/ppermute | solution.py:48
  108.0 10.2 %collective-permute-start.8 = (f32[5,128,128]{2,1,0:T(8,128)S(1)}, f32[5,128,128]{2,1,0:T(8,128)S(1)}, u32[]{:S(2)}, u32[]{:S(2)}) collective-permute-start(f32[5,128,128]{2,1,0:T(8,128)S(1)} %pad_maximum_fusion.3), channel_id=1, source_target_pairs={{0,8},{4,12},{8,0},{12,4},{16,24},{20,28},{24,16},{28,20},{32,40},... | collective-permute-start | bytes 983048 | tf_op jit(solution)/shard_map/ppermute | solution.py:48
  120.2 28.7 %all-to-all-start.2 = ((f32[4,2,256,128]{3,2,1,0:T(8,128)}), f32[4,2,256,128]{3,2,1,0:T(8,128)S(1)}, u32[]{:S(2)}, u32[]{:S(2)}) async-start(f32[4,2,256,128]{3,2,1,0:T(8,128)} %broadcast_in_dim.8), calls=%async_computation.2 | async-start | bytes 2097152 | tf_op jit(solution)/shard_map/all_to_all | solution.py:213
  124.6 24.3 %collective-permute-start.9 = (f32[32,1536]{1,0:T(8,128)S(1)}, f32[32,1536]{1,0:T(8,128)}, u32[]{:S(2)}, u32[]{:S(2)}) collective-permute-start(f32[32,1536]{1,0:T(8,128)S(1)} %add.35), channel_id=1, source_target_pairs={{0,32},{4,36},{8,40},{12,44},{16,48},{20,52},{24,56},{28,60},{32,0... | collective-permute-start | bytes 589832 | tf_op jit(solution)/shard_map/ppermute | solution.py:48
  148.9 4.7 %collective-permute-start.10 = (f32[4,2,256,128]{3,2,1,0:T(8,128)S(1)}, f32[4,2,256,128]{3,2,1,0:T(8,128)S(1)}, u32[]{:S(2)}, u32[]{:S(2)}) collective-permute-start(f32[4,2,256,128]{3,2,1,0:T(8,128)S(1)} %all-to-all-done.2.mine.m2), channel_id=1, source_target_pairs={{0,4},{4,0},{8,12},{12,8},{16,20},{20,16},{24,28},{28,24},{32,36},... | collective-permute-start | bytes 3145736 | tf_op jit(solution)/shard_map/ppermute | solution.py:48
  155.5 13.9 %collective-permute-start.11 = (f32[32,1024]{1,0:T(8,128)S(1)}, f32[32,1024]{1,0:T(8,128)S(1)}, u32[]{:S(2)}, u32[]{:S(2)}) collective-permute-start(f32[32,1024]{1,0:T(8,128)S(1)} %pad_maximum_fusion.8), channel_id=1, source_target_pairs={{0,112},{4,116},{8,120},{12,124},{16,96},{20,100},{24,104},{28,108... | collective-permute-start | bytes 393224 | tf_op jit(solution)/shard_map/ppermute | solution.py:48
  169.4 9.5 %collective-permute-start.13 = (f32[4,3,256,128]{3,2,1,0:T(8,128)}, f32[4,3,256,128]{3,2,1,0:T(8,128)S(1)}, u32[]{:S(2)}, u32[]{:S(2)}) collective-permute-start(f32[4,3,256,128]{3,2,1,0:T(8,128)} %bitcast.26), channel_id=1, source_target_pairs={{0,4},{4,0},{8,12},{12,8},{16,20},{20,16},{24,28},{28,24},{32,36},... | collective-permute-start | bytes 4718600 | tf_op jit(solution)/shard_map/ppermute | solution.py:48
  171.9 7.0 %collective-permute-start.12 = (f32[32,1024]{1,0:T(8,128)S(1)}, f32[32,1024]{1,0:T(8,128)S(1)}, u32[]{:S(2)}, u32[]{:S(2)}) collective-permute-start(f32[32,1024]{1,0:T(8,128)S(1)} %fusion), channel_id=1, source_target_pairs={{0,128},{4,132},{8,136},{12,140},{16,144},{20,148},{24,152},{28,15... | collective-permute-start | bytes 393224 | tf_op jit(solution)/shard_map/ppermute | solution.py:48
  178.9 1.4 copy-start
  180.3 7.2 %copy-start.6 = (f32[4,2,256,128]{3,2,1,0:T(8,128)S(1)}, f32[4,2,256,128]{3,2,1,0:T(8,128)}, u32[]{:S(2)}) copy-start(f32[4,2,256,128]{3,2,1,0:T(8,128)} %copy-done.5) | copy-start | bytes 3145732
  181.3 6.2 %collective-permute-start.14 = (f32[32,512]{1,0:T(8,128)S(1)}, f32[32,512]{1,0:T(8,128)S(1)}, u32[]{:S(2)}, u32[]{:S(2)}) collective-permute-start(f32[32,512]{1,0:T(8,128)S(1)} %get-tuple-element.54), channel_id=1, source_target_pairs={{0,384},{4,388},{8,392},{12,396},{16,400},{20,404},{24,408},{28,41... | collective-permute-start | bytes 196616 | tf_op jit(solution)/shard_map/ppermute | solution.py:48
  191.0 10.4 %collective-permute-start.15 = (f32[32,2048]{1,0:T(8,128)S(1)}, f32[32,2048]{1,0:T(8,128)S(1)}, u32[]{:S(2)}, u32[]{:S(2)}) collective-permute-start(f32[32,2048]{1,0:T(8,128)S(1)} %shard_map.99), channel_id=1, source_target_pairs={{0,8},{4,12},{8,0},{12,4},{16,24},{20,28},{24,16},{28,20},{32,40},... | collective-permute-start | bytes 786440 | tf_op jit(solution)/shard_map/ppermute | solution.py:48
  201.3 6.6 %copy-start.10 = (f32[896,128]{1,0:T(8,128)S(1)}, f32[896,128]{1,0:T(8,128)}, u32[]{:S(2)}) copy-start(f32[896,128]{1,0:T(8,128)} %copy-done.9) | copy-start | bytes 1376260
  201.4 6.5 %copy-start.2 = (f32[21,128,128]{2,1,0:T(8,128)S(1)}, f32[21,128,128]{2,1,0:T(8,128)}, u32[]{:S(2)}) copy-start(f32[21,128,128]{2,1,0:T(8,128)} %blocks.3) | copy-start | bytes 4128772
  201.4 6.5 %copy-start.4 = (f32[512,512]{1,0:T(8,128)S(1)}, f32[512,512]{1,0:T(8,128)}, u32[]{:S(2)}) copy-start(f32[512,512]{1,0:T(8,128)} %coupling.3) | copy-start | bytes 3145732
  201.4 6.5 %copy-start.8 = (f32[7,128,128]{2,1,0:T(8,128)S(1)}, f32[7,128,128]{2,1,0:T(8,128)}, u32[]{:S(2)}) copy-start(f32[7,128,128]{2,1,0:T(8,128)} %inverse.3) | copy-start | bytes 1376260
  201.4 6.5 %copy-start.13 = (s32[1,21]{1,0:T(1,128)S(1)}, s32[1,21]{1,0:T(1,128)}, u32[]{:S(2)}) copy-start(s32[1,21]{1,0:T(1,128)} %pattern.3) | copy-start | bytes 256
  201.4 6.3 %collective-permute-start.16 = (f32[2,32,2048]{2,1,0:T(8,128)S(1)}, f32[2,32,2048]{2,1,0:T(8,128)S(1)}, u32[]{:S(2)}, u32[]{:S(2)}) collective-permute-start(f32[2,32,2048]{2,1,0:T(8,128)S(1)} %pad_maximum_fusion.2), channel_id=1, source_target_pairs={{0,4},{4,0},{8,12},{12,8},{16,20},{20,16},{24,28},{28,24},{32,36},... | collective-permute-start | bytes 1572872 | tf_op jit(solution)/shard_map/ppermute | solution.py:48
  (2 other events, 1.6 us)
Sparse Core Ops, SparseCore 0:
  119.2 33.9 all-gather.2

commit v5 on v4

--- a/solution.py
+++ b/solution.py
@@ -71,13 +71,29 @@
     return jnp.where(inside & (row - offset == column - start), 1.0, 0.0).astype(BF16)
 
 
-def forward_kernel(sizes, where, pattern, rhs, inverse, blocks, coupling, sep_rhs, y_out, t_out):
+def forward_kernel(
+    sizes, where, pattern, rhs_far, inverse_far, blocks_far, coupling_far, sep_rhs, y_out, t_out, rhs, inverse, blocks, coupling, sems
+):
     count, size = inverse.shape[0], inverse.shape[1]
     starts = pair_starts(count)
+    copies = [
+        pltpu.make_async_copy(rhs_far, rhs, sems.at[0]),
+        pltpu.make_async_copy(inverse_far, inverse, sems.at[1]),
+        pltpu.make_async_copy(coupling_far, coupling, sems.at[2]),
+    ]
+    for column in range(count - 1):
+        part = pl.ds(starts[column], count - 1 - column)
+        copies.append(pltpu.make_async_copy(blocks_far.at[part], blocks.at[part], sems.at[3 + column]))
+    for copy in copies[:2] + copies[3:] + copies[2:3]:
+        copy.start()
+    copies[0].wait()
+    copies[1].wait()
     pending = [rhs[i * size : (i + 1) * size, :] for i in range(count)]
     for column in range(count):
         solved = mm(inverse[column], pending[column], NN)
         y_out[column * size : (column + 1) * size, :] = solved
+        if column < count - 1:
+            copies[3 + column].wait()
         for later in range(column + 1, count):
             pair = starts[column] + later - column - 1
             weight = pattern[0, pair].astype(F32)
@@ -85,6 +101,7 @@
     last = y_out[(count - 1) * size :, :]
     right = sep_rhs[...]
     width = coupling.shape[1]
+    copies[2].wait()
     offset = 0
     for level, rows in enumerate(sizes):
         spread = placement(right.shape[0], offset, rows, where[level], width)
@@ -102,15 +119,16 @@
     quarter = x.shape[0]
     xs = jnp.concatenate([x[jnp.bitwise_xor(place, q)] for q in range(quarter)], axis=0)
     correction = jnp.zeros((size, y.shape[1]), F32)
-    pieces = jnp.zeros((sep_out.shape[0], y.shape[1]), F32)
+    padded = -(-sep_out.shape[0] // 8) * 8
+    pieces = jnp.zeros((padded, y.shape[1]), F32)
     offset = 0
     for level, rows in enumerate(sizes):
         part = xs[:, level * width : (level + 1) * width]
         correction = correction + mm(coupling[level * size : (level + 1) * size, :], part, NT)
-        spread = placement(sep_out.shape[0], offset, rows, where[level], width)
+        spread = placement(padded, offset, rows, where[level], width)
         pieces = pieces + pick_left(spread, part, NT)
         offset += rows
-    sep_out[...] = pieces
+    sep_out[...] = pieces[: sep_out.shape[0], :]
     pending = [y[i * size : (i + 1) * size, :] for i in range(count)]
     pending[-1] = pending[-1] - correction
     for column in reversed(range(count)):
@@ -219,44 +237,57 @@
 
     first = grow(both(0), 1 << Z1)
     far = grow(rows(sep_inverse, 3)[None], wrap_y)
-    padded = jnp.pad(sep_rhs, ((0, 4), (0, 0)))
-    y, t = call(
+    where, first = tie((where, first))
+    first = planes(first)
+    y, t = pl.pallas_call(
         functools.partial(forward_kernel, sizes),
-        [leaf_rhs.shape, (columns, LEVELS * width)],
-        where, leaf_pattern, leaf_rhs, leaf_inverse, leaf_blocks, leaf_coupling, padded,
-    )
-    t, first, far = tie((t, first, far))
+        out_shape=[
+            jax.ShapeDtypeStruct(leaf_rhs.shape, F32),
+            jax.ShapeDtypeStruct((columns, LEVELS * width), F32),
+        ],
+        in_specs=[SMEM, SMEM] + [pl.BlockSpec(memory_space=pltpu.HBM)] * 4 + [VMEM],
+        out_specs=[VMEM, VMEM],
+        scratch_shapes=[pltpu.VMEM(v.shape, F32) for v in (leaf_rhs, leaf_inverse, leaf_blocks, leaf_coupling)]
+        + [pltpu.SemaphoreType.DMA((2 + leaf_inverse.shape[0],))],
+        compiler_params=params(),
+    )(where, leaf_pattern, leaf_rhs, leaf_inverse, leaf_blocks, leaf_coupling, sep_rhs)
+    second = both(1)
+    t, far, second = tie((t, far, second))
 
     t = lax.all_to_all(t, "leaf", 0, 0, axis_index_groups=near, tiled=True)
     far = grow(jnp.concatenate([far, both(2)], 0), 1 << Y1)
-    first = planes(first)
-    t, far = tie((t, far))
-
-    far = grow(far, wrap_z)
+    second = grow(second, halves_z)
+    far, second = tie((far, second))
+
+    line = [[m + 4 * k for k in range(8)] for m in range(leaves) if m % 32 < 4]
+    far = lax.all_to_all(jnp.broadcast_to(far[None], (8, *far.shape)), "leaf", 0, 0, axis_index_groups=line, tiled=True)
+    second = grow(second, 1 << Z2)
+    first, t, second = tie((first, t, second))
     t = t.reshape(4, columns // 4, LEVELS * width).sum(0)
-    first, t, far = tie((first, t, far))
-
-    far = grow(jnp.concatenate([far, both(1)], 0), halves_z)
+
+    upper = t[:, 2 * width :]
+    upper_z2 = across(upper, 1 << Z2)
     first = (first, across(first, CORE_MASK))
     z1, v = level(functools.partial(level_kernel, 0), t[:, :width], t[:, width : 2 * width], *first)
-    v = jnp.concatenate([v, t[:, 2 * width :]], 1)
-    v, far = tie((v, far))
-
-    far = grow(far, 1 << Z2)
-    v = v + across(v, 1 << Z2)
-    v, far = tie((v, far))
-
-    far = grow(far, 1 << Z1)
-    v_far = across(v, halves_z)
-    far, v = tie((far, v))
-
+    v, upper, upper_z2, second = tie((v, upper, upper_z2, second))
+
+    upper = upper + upper_z2
+    v_z2 = across(v, 1 << Z2)
+    far = far.transpose(1, 0, 2, 3).reshape(3, -1, 128)
+    far = grow(jnp.concatenate([far, second], 0), 1 << Z1)
+    v = v + v_z2
+    v, far, upper = tie((v, far, upper))
+
+    second = planes(far[3:])
     third = lax.all_gather(far[:3], "col", axis=0)
-    second = planes(far[3:])
-    second, v, v_far = tie((second, v, v_far))
+    v = v + across(v, halves_z)
+    v, second = tie((v, second))
+
+    upper_z4 = across(upper, halves_z)
     second = (second, across(second, CORE_MASK))
-    v = v + v_far
-    z2, v3 = level(functools.partial(level_kernel, 0), v[:, :width], v[:, width : 2 * width], *second)
-    v = jnp.concatenate([v3, v[:, 2 * width :]], 1)
+    upper = upper + upper_z4
+    z2, v3 = level(functools.partial(level_kernel, 0), v, upper[:, :width], *second)
+    v = jnp.concatenate([v3, upper[:, width:]], 1)
     v = v + across(v, wrap_z)
     v, third = tie((v, third))
 
@@ -270,19 +301,14 @@
     x = jnp.stack([x[0], other[0], x[1], other[1]], 0)
     return call(
         functools.partial(backward_kernel, sizes),
-        [leaf_rhs.shape, padded.shape],
+        [leaf_rhs.shape, sep_rhs.shape],
         where, leaf_pattern, y, x, leaf_inverse, leaf_blocks, leaf_coupling,
     )
 
 
-def program(*arrays):
-    leaf, sep = shards(*arrays)
-    return leaf, sep[: arrays[5].shape[0]]
-
-
 def solution(mesh):
     return jax.shard_map(
-        program,
+        shards,
         mesh=mesh,
         in_specs=(
             P("leaf", "col"),

time: 221 us -> 236 us (1.068)
  waiting for transfers between devices: 80 us -> 50 us
  starting transfers between devices: 74.5 us -> 101 us
  blocking collectives: 18.2 us -> 26.8 us
  other arithmetic: 1.39 us -> 6.98 us
  local copies, waits for them, and re-layouts: 16 us -> 18.8 us
    ppermute x17 -> x18, waiting for transfers between devices: 80 us -> 50 us  [swap(): lax.ppermute(value, axis, [(i, i ^ mask) for i in range(lax.axis_size(axi...]
    ppermute x17 -> x18, starting transfers between devices: 66.6 us -> 81.1 us  [swap(): lax.ppermute(value, axis, [(i, i ^ mask) for i in range(lax.axis_size(axi...]
    all_to_all x0 -> x1, starting transfers between devices: none -> 10.3 us  [shards(): t = lax.all_to_all(t, 'leaf', 0, 0, axis_index_groups=near, tiled=True)]
    all_to_all x1, blocking collectives: 18.2 us -> 26.8 us  [shards(): lax.all_to_all(jnp.broadcast_to(far[None], (8, *far.shape)), 'leaf', 0, 0...]
    pallas_call x0 -> x1, Pallas kernels: none -> 5.51 us  [shards(): pl.pallas_call(functools.partial(forward_kernel, sizes), out_shape=[jax.S...]
    pallas_call x6 -> x5, Pallas kernels: 14.7 us -> 10.9 us  [call(): pl.pallas_call(kernel, out_shape=[jax.ShapeDtypeStruct(s, F32) for s in o...]
    unnamed x28 -> x48, local copies, waits for them, and re-layouts: 7.66 us -> 8.77 us
  transfers between devices with their start and end apart: 20 -> 22, of which waited for: 13 -> 13; matrix products, arithmetic and copies ran while one was open for 3% -> 6% of each run, Pallas kernels for 2% -> 3%
where the time goes in v5:
time: 236 us; the launch traced here: 234 us
  starting transfers between devices  101 us (43%)
  waiting for transfers between devices  50 us (21%)
  blocking collectives  26.8 us (11%)
  local copies, waits for them, and re-layouts  18.8 us (8%)
  Pallas kernels  16.4 us (7%)
  between operations  14.6 us (6%)
  other arithmetic  6.98 us (3%)
    ppermute x18, starting transfers between devices, swap(): lax.ppermute(value, axis, [(i, i ^ mask) for i in range(lax.axis_size(axi...  81.1 us
    ppermute x18, waiting for transfers between devices, swap(): lax.ppermute(value, axis, [(i, i ^ mask) for i in range(lax.axis_size(axi...  50 us
    all_to_all x1, blocking collectives, shards(): lax.all_to_all(jnp.broadcast_to(far[None], (8, *far.shape)), 'leaf', 0, 0...  26.8 us
    pallas_call x5, Pallas kernels, call(): pl.pallas_call(kernel, out_shape=[jax.ShapeDtypeStruct(s, F32) for s in o...  10.9 us
    all_to_all x1, starting transfers between devices, shards(): t = lax.all_to_all(t, 'leaf', 0, 0, axis_index_groups=near, tiled=True)  10.3 us
    all_to_all x2, starting transfers between devices, planes(): lax.all_to_all(jnp.broadcast_to(value[None], (count, *value.shape)), 'col...  9.41 us
    unnamed x48, local copies, waits for them, and re-layouts  8.77 us
    pallas_call x1, Pallas kernels, shards(): pl.pallas_call(functools.partial(forward_kernel, sizes), out_shape=[jax.S...  5.51 us
  transfers between devices with their start and end apart: 22, of which 13 were waited for; matrix products, arithmetic and copies ran while one was open for 6% of the time, Pallas kernels for 3%

profile of v5, /device:TPU:1, one launch (start us, length us, event | category | flops | bytes accessed | tf_op | source)
XLA Modules:
  0.0 234.5 jit_solution(12045175471823352875)
XLA Ops:
  8.9 4.4 %collective-permute-start = (f32[2,128,128]{2,1,0:T(8,128)S(1)}, f32[2,128,128]{2,1,0:T(8,128)S(1)}, u32[]{:S(2)}, u32[]{:S(2)}) collective-permute-start(f32[2,128,128]{2,1,0:T(8,128)S(1)} %pad_maximum_fusion.5), channel_id=1, source_target_pairs={{0,8},{4,12},{8,0},{12,4},{16,24},{20,28},{24,16},{28,20},{32,40},... | collective-permute-start | bytes 393224 | tf_op jit(solution)/shard_map/ppermute | solution.py:48
  13.4 2.2 collective-permute-done
  16.7 4.9 %all-to-all-start = ((f32[4,2,256,128]{3,2,1,0:T(8,128)}), f32[4,2,256,128]{3,2,1,0:T(8,128)S(1)}, u32[]{:S(2)}, u32[]{:S(2)}) async-start(f32[4,2,256,128]{3,2,1,0:T(8,128)} %broadcast_in_dim.8), calls=%async_computation | async-start | bytes 2097152 | tf_op jit(solution)/shard_map/all_to_all | solution.py:231
  22.3 4.6 %collective-permute-start.1 = (f32[1,4,128]{2,1,0:T(4,128)S(1)}, f32[1,4,128]{2,1,0:T(4,128)S(1)}, u32[]{:S(2)}, u32[]{:S(2)}) collective-permute-start(f32[1,4,128]{2,1,0:T(4,128)S(1)} %slice_bitcast_fusion.6), channel_id=1, source_target_pairs={{0,384},{4,388},{8,392},{12,396},{16,400},{20,404},{24,408},{28,41... | collective-permute-start | bytes 6152 | tf_op jit(solution)/shard_map/ppermute | solution.py:48
  30.8 5.5 %shard_map.95 = (f32[896,128]{1,0:T(8,128)S(1)}, f32[128,2048]{1,0:T(8,128)S(1)}) custom-call(s32[5]{0:T(128)S(1)} %stack.59.where, s32[1,21]{1,0:T(1,128)S(1)} %copy-done.19, f32[896,128]{1,0:T(8,128)S(1)} %copy-done.13, f32[7,128,128]{2,1,0:T(8,128)S(1)} %copy-done.8, f32[21,128,128]{2,1,0:T(8,128)S(1)} %copy-done.1, f32[512,512]{1,0:T(8,128)S(1)} %copy-done.2, ...), custom_call_target="tpu_custom_call" | custom-call | tf_op jit(solution)/shard_map/pallas_call | solution.py:242
  38.1 10.3 %all-to-all-start.1 = ((f32[4,32,2048]{2,1,0:T(8,128)}), f32[4,32,2048]{2,1,0:T(8,128)S(1)}, u32[]{:S(2)}, u32[]{:S(2)}) async-start(f32[4,32,2048]{2,1,0:T(8,128)} %bitcast.33), calls=%async_computation.1 | async-start | bytes 2097152 | tf_op jit(solution)/shard_map/all_to_all | solution.py:257
  51.8 4.8 %collective-permute-start.3 = (f32[2,32,128]{2,1,0:T(8,128)S(1)}, f32[2,32,128]{2,1,0:T(8,128)S(1)}, u32[]{:S(2)}, u32[]{:S(2)}) collective-permute-start(f32[2,32,128]{2,1,0:T(8,128)S(1)} %pad_maximum_fusion.9), channel_id=1, source_target_pairs={{0,32},{4,36},{8,40},{12,44},{16,48},{20,52},{24,56},{28,60},{32,0... | collective-permute-start | bytes 98312 | tf_op jit(solution)/shard_map/ppermute | solution.py:48
  56.6 4.9 %collective-permute-done.3 = f32[2,32,128]{2,1,0:T(8,128)S(1)} collective-permute-done((f32[2,32,128]{2,1,0:T(8,128)S(1)}, f32[2,32,128]{2,1,0:T(8,128)S(1)}, u32[]{:S(2)}, u32[]{:S(2)}) %collective-permute-start.3) | collective-permute-done | bytes 32800 | tf_op jit(solution)/shard_map/ppermute | solution.py:48
  63.3 4.0 %collective-permute-done.4 = f32[2,64,128]{2,1,0:T(8,128)S(1)} collective-permute-done((f32[2,64,128]{2,1,0:T(8,128)S(1)}, f32[2,64,128]{2,1,0:T(8,128)S(1)}, u32[]{:S(2)}, u32[]{:S(2)}) %collective-permute-start.4) | collective-permute-done | bytes 65568 | tf_op jit(solution)/shard_map/ppermute | solution.py:48
  69.0 3.9 %collective-permute-start.5 = (f32[4,2,256,128]{3,2,1,0:T(8,128)S(1)}, f32[4,2,256,128]{3,2,1,0:T(8,128)S(1)}, u32[]{:S(2)}, u32[]{:S(2)}) collective-permute-start(f32[4,2,256,128]{3,2,1,0:T(8,128)S(1)} %all-to-all-done.mine.m1), channel_id=1, source_target_pairs={{0,4},{4,0},{8,12},{12,8},{16,20},{20,16},{24,28},{28,24},{32,36},... | collective-permute-start | bytes 3145736 | tf_op jit(solution)/shard_map/ppermute | solution.py:48
  72.9 26.8 %all_to_all.27 = f32[8,3,16,128]{3,2,1,0:T(8,128)S(1)} all-to-all(f32[8,3,16,128]{3,2,1,0:T(8,128)S(1)} %broadcast_in_dim.10), channel_id=1, replica_groups={{0,16,32,48,64,80,96,112},{4,20,36,52,68,84,100,116},{8,24,40,56,72,88,..., dimensions={0} | all-to-all | bytes 393216 | tf_op jit(solution)/shard_map/all_to_all | solution.py:263
  100.3 2.0 reduce_sum.9
  107.1 2.8 %collective-permute-done.6 = f32[32,1024]{1,0:T(8,128)S(1)} collective-permute-done((f32[32,1024]{1,0:T(8,128)S(1)}, f32[32,1024]{1,0:T(8,128)S(1)}, u32[]{:S(2)}, u32[]{:S(2)}) %collective-permute-start.6) | collective-permute-done | bytes 131104 | tf_op jit(solution)/shard_map/ppermute | solution.py:48
  110.0 4.7 %collective-permute-start.8 = (f32[5,128,128]{2,1,0:T(8,128)S(1)}, f32[5,128,128]{2,1,0:T(8,128)S(1)}, u32[]{:S(2)}, u32[]{:S(2)}) collective-permute-start(f32[5,128,128]{2,1,0:T(8,128)S(1)} %pad_maximum_fusion.3), channel_id=1, source_target_pairs={{0,8},{4,12},{8,0},{12,4},{16,24},{20,28},{24,16},{28,20},{32,40},... | collective-permute-start | bytes 983048 | tf_op jit(solution)/shard_map/ppermute | solution.py:48
  114.7 4.0 %collective-permute-start.7 = (f32[32,512]{1,0:T(8,128)S(1)}, f32[32,512]{1,0:T(8,128)S(1)}, u32[]{:S(2)}, u32[]{:S(2)}) collective-permute-start(f32[32,512]{1,0:T(8,128)S(1)} %get-tuple-element.43), channel_id=1, source_target_pairs={{0,16},{4,20},{8,24},{12,28},{16,0},{20,4},{24,8},{28,12},{32,48},... | collective-permute-start | bytes 196616 | tf_op jit(solution)/shard_map/ppermute | solution.py:48
  122.6 4.5 %all-to-all-start.3 = ((f32[4,2,256,128]{3,2,1,0:T(8,128)}), f32[4,2,256,128]{3,2,1,0:T(8,128)S(1)}, u32[]{:S(2)}, u32[]{:S(2)}) async-start(f32[4,2,256,128]{3,2,1,0:T(8,128)} %broadcast_in_dim.11), calls=%async_computation.3 | async-start | bytes 2097152 | tf_op jit(solution)/shard_map/all_to_all | solution.py:231
  127.1 3.9 %collective-permute-start.9 = (f32[32,512]{1,0:T(8,128)S(1)}, f32[32,512]{1,0:T(8,128)S(1)}, u32[]{:S(2)}, u32[]{:S(2)}) collective-permute-start(f32[32,512]{1,0:T(8,128)S(1)} %add.39), channel_id=1, source_target_pairs={{0,32},{4,36},{8,40},{12,44},{16,48},{20,52},{24,56},{28,60},{32,0... | collective-permute-start | bytes 196616 | tf_op jit(solution)/shard_map/ppermute | solution.py:48
  131.0 5.0 %collective-permute-done.9 = f32[32,512]{1,0:T(8,128)S(1)} collective-permute-done((f32[32,512]{1,0:T(8,128)S(1)}, f32[32,512]{1,0:T(8,128)S(1)}, u32[]{:S(2)}, u32[]{:S(2)}) %collective-permute-start.9) | collective-permute-done | bytes 65568 | tf_op jit(solution)/shard_map/ppermute | solution.py:48
  136.8 8.2 %collective-permute-start.11 = (f32[4,2,256,128]{3,2,1,0:T(8,128)S(1)}, f32[4,2,256,128]{3,2,1,0:T(8,128)S(1)}, u32[]{:S(2)}, u32[]{:S(2)}) collective-permute-start(f32[4,2,256,128]{3,2,1,0:T(8,128)S(1)} %all-to-all-done.3.mine.m2), channel_id=1, source_target_pairs={{0,4},{4,0},{8,12},{12,8},{16,20},{20,16},{24,28},{28,24},{32,36},... | collective-permute-start | bytes 3145736 | tf_op jit(solution)/shard_map/ppermute | solution.py:48
  145.0 3.9 %collective-permute-start.10 = (f32[32,1024]{1,0:T(8,128)}, f32[32,1024]{1,0:T(8,128)S(1)}, u32[]{:S(2)}, u32[]{:S(2)}) collective-permute-start(f32[32,1024]{1,0:T(8,128)} %add.40), channel_id=1, source_target_pairs={{0,32},{4,36},{8,40},{12,44},{16,48},{20,52},{24,56},{28,60},{32,0... | collective-permute-start | bytes 393224 | tf_op jit(solution)/shard_map/ppermute | solution.py:48
  148.9 7.2 %collective-permute-done.10 = f32[32,1024]{1,0:T(8,128)S(1)} collective-permute-done((f32[32,1024]{1,0:T(8,128)}, f32[32,1024]{1,0:T(8,128)S(1)}, u32[]{:S(2)}, u32[]{:S(2)}) %collective-permute-start.10) | collective-permute-done | bytes 131104 | tf_op jit(solution)/shard_map/ppermute | solution.py:48
  159.7 13.0 %collective-permute-start.12 = (f32[32,1024]{1,0:T(8,128)S(1)}, f32[32,1024]{1,0:T(8,128)S(1)}, u32[]{:S(2)}, u32[]{:S(2)}) collective-permute-start(f32[32,1024]{1,0:T(8,128)S(1)} %pad_maximum_fusion.7), channel_id=1, source_target_pairs={{0,112},{4,116},{8,120},{12,124},{16,96},{20,100},{24,104},{28,108... | collective-permute-start | bytes 393224 | tf_op jit(solution)/shard_map/ppermute | solution.py:48
  172.7 9.6 %collective-permute-done.12 = f32[32,1024]{1,0:T(8,128)S(1)} collective-permute-done((f32[32,1024]{1,0:T(8,128)S(1)}, f32[32,1024]{1,0:T(8,128)S(1)}, u32[]{:S(2)}, u32[]{:S(2)}) %collective-permute-start.12) | collective-permute-done | bytes 131104 | tf_op jit(solution)/shard_map/ppermute | solution.py:48
  183.0 2.5 %collective-permute-start.14 = (f32[4,3,256,128]{3,2,1,0:T(8,128)}, f32[4,3,256,128]{3,2,1,0:T(8,128)S(1)}, u32[]{:S(2)}, u32[]{:S(2)}) collective-permute-start(f32[4,3,256,128]{3,2,1,0:T(8,128)} %bitcast.28), channel_id=1, source_target_pairs={{0,4},{4,0},{8,12},{12,8},{16,20},{20,16},{24,28},{28,24},{32,36},... | collective-permute-start | bytes 4718600 | tf_op jit(solution)/shard_map/ppermute | solution.py:48
  185.5 2.5 %collective-permute-start.13 = (f32[32,1024]{1,0:T(8,128)}, f32[32,1024]{1,0:T(8,128)S(1)}, u32[]{:S(2)}, u32[]{:S(2)}) collective-permute-start(f32[32,1024]{1,0:T(8,128)} %fusion), channel_id=1, source_target_pairs={{0,128},{4,132},{8,136},{12,140},{16,144},{20,148},{24,152},{28,15... | collective-permute-start | bytes 393224 | tf_op jit(solution)/shard_map/ppermute | solution.py:48
  188.0 4.7 %collective-permute-done.13 = f32[32,1024]{1,0:T(8,128)S(1)} collective-permute-done((f32[32,1024]{1,0:T(8,128)}, f32[32,1024]{1,0:T(8,128)S(1)}, u32[]{:S(2)}, u32[]{:S(2)}) %collective-permute-start.13) | collective-permute-done | bytes 131104 | tf_op jit(solution)/shard_map/ppermute | solution.py:48
  196.1 5.6 %collective-permute-start.15 = (f32[32,512]{1,0:T(8,128)S(1)}, f32[32,512]{1,0:T(8,128)S(1)}, u32[]{:S(2)}, u32[]{:S(2)}) collective-permute-start(f32[32,512]{1,0:T(8,128)S(1)} %get-tuple-element.56), channel_id=1, source_target_pairs={{0,384},{4,388},{8,392},{12,396},{16,400},{20,404},{24,408},{28,41... | collective-permute-start | bytes 196616 | tf_op jit(solution)/shard_map/ppermute | solution.py:48
  203.4 3.4 %shard_map.99 = f32[32,2048]{1,0:T(8,128)S(1)} custom-call(f32[32,512]{1,0:T(8,128)S(1)} %add.45.right, f32[32,512]{1,0:T(8,128)S(1)} %copy-done.16, f32[32,512]{1,0:T(8,128)S(1)} %copy-done.18, f32[32,512]{1,0:T(8,128)S(1)} %get-tuple-element.59.z3, f32[4,2,256,128]{3,2,1,0:T(8,128)S(1)} %all-to-all-done.mine.m1, f32[4,2,256,128]{3,2,1,0:T(8,128)S(1)} %copy-done.5, ...), custom_call_target="tpu_custom_call" | custom-call | tf_op jit(solution)/shard_map/pallas_call | solution.py:204
  206.8 5.1 %collective-permute-start.16 = (f32[32,2048]{1,0:T(8,128)S(1)}, f32[32,2048]{1,0:T(8,128)S(1)}, u32[]{:S(2)}, u32[]{:S(2)}) collective-permute-start(f32[32,2048]{1,0:T(8,128)S(1)} %shard_map.99), channel_id=1, source_target_pairs={{0,8},{4,12},{8,0},{12,4},{16,24},{20,28},{24,16},{28,20},{32,40},... | collective-permute-start | bytes 786440 | tf_op jit(solution)/shard_map/ppermute | solution.py:48
  211.9 4.9 %collective-permute-done.16 = f32[32,2048]{1,0:T(8,128)S(1)} collective-permute-done((f32[32,2048]{1,0:T(8,128)S(1)}, f32[32,2048]{1,0:T(8,128)S(1)}, u32[]{:S(2)}, u32[]{:S(2)}) %collective-permute-start.16) | collective-permute-done | bytes 262176 | tf_op jit(solution)/shard_map/ppermute | solution.py:48
  216.9 4.4 %collective-permute-start.17 = (f32[2,32,2048]{2,1,0:T(8,128)S(1)}, f32[2,32,2048]{2,1,0:T(8,128)S(1)}, u32[]{:S(2)}, u32[]{:S(2)}) collective-permute-start(f32[2,32,2048]{2,1,0:T(8,128)S(1)} %pad_maximum_fusion.2), channel_id=1, source_target_pairs={{0,4},{4,0},{8,12},{12,8},{16,20},{20,16},{24,28},{28,24},{32,36},... | collective-permute-start | bytes 1572872 | tf_op jit(solution)/shard_map/ppermute | solution.py:48
  223.0 4.7 %shard_map.100 = (f32[896,128]{1,0:T(8,128)}, f32[172,128]{1,0:T(8,128)}) custom-call(s32[5]{0:T(128)S(1)} %stack.59.where, s32[1,21]{1,0:T(1,128)S(1)} %copy-done.19, f32[896,128]{1,0:T(8,128)S(1)} %copy-done.12, f32[4,32,2048]{2,1,0:T(8,128)S(1)} %pad_maximum_fusion.x, f32[7,128,128]{2,1,0:T(8,128)S(1)} %copy-done.9, f32[21,128,128]{2,1,0:T(8,128)S(1)} %copy-done.1, ...), custom_call_target="tpu_custom_call" | custom-call | tf_op jit(solution)/shard_map/pallas_call | solution.py:204
  (107 shorter events, 37.1 us)
Async XLA Ops:
  8.9 6.7 %collective-permute-start = (f32[2,128,128]{2,1,0:T(8,128)S(1)}, f32[2,128,128]{2,1,0:T(8,128)S(1)}, u32[]{:S(2)}, u32[]{:S(2)}) collective-permute-start(f32[2,128,128]{2,1,0:T(8,128)S(1)} %pad_maximum_fusion.5), channel_id=1, source_target_pairs={{0,8},{4,12},{8,0},{12,4},{16,24},{20,28},{24,16},{28,20},{32,40},... | collective-permute-start | bytes 393224 | tf_op jit(solution)/shard_map/ppermute | solution.py:48
  15.6 12.3 %copy-start.1 = (f32[21,128,128]{2,1,0:T(8,128)S(1)}, f32[21,128,128]{2,1,0:T(8,128)}, u32[]{:S(2)}) copy-start(f32[21,128,128]{2,1,0:T(8,128)} %blocks.1) | copy-start | bytes 4128772
  15.6 12.3 %copy-start.2 = (f32[512,512]{1,0:T(8,128)S(1)}, f32[512,512]{1,0:T(8,128)}, u32[]{:S(2)}) copy-start(f32[512,512]{1,0:T(8,128)} %coupling.1) | copy-start | bytes 3145732
  15.6 12.3 %copy-start.19 = (s32[1,21]{1,0:T(1,128)S(1)}, s32[1,21]{1,0:T(1,128)}, u32[]{:S(2)}) copy-start(s32[1,21]{1,0:T(1,128)} %pattern.3) | copy-start | bytes 256
  16.7 21.4 %all-to-all-start = ((f32[4,2,256,128]{3,2,1,0:T(8,128)}), f32[4,2,256,128]{3,2,1,0:T(8,128)S(1)}, u32[]{:S(2)}, u32[]{:S(2)}) async-start(f32[4,2,256,128]{3,2,1,0:T(8,128)} %broadcast_in_dim.8), calls=%async_computation | async-start | bytes 2097152 | tf_op jit(solution)/shard_map/all_to_all | solution.py:231
  22.3 5.6 %collective-permute-start.1 = (f32[1,4,128]{2,1,0:T(4,128)S(1)}, f32[1,4,128]{2,1,0:T(4,128)S(1)}, u32[]{:S(2)}, u32[]{:S(2)}) collective-permute-start(f32[1,4,128]{2,1,0:T(4,128)S(1)} %slice_bitcast_fusion.6), channel_id=1, source_target_pairs={{0,384},{4,388},{8,392},{12,396},{16,400},{20,404},{24,408},{28,41... | collective-permute-start | bytes 6152 | tf_op jit(solution)/shard_map/ppermute | solution.py:48
  38.1 29.8 %all-to-all-start.1 = ((f32[4,32,2048]{2,1,0:T(8,128)}), f32[4,32,2048]{2,1,0:T(8,128)S(1)}, u32[]{:S(2)}, u32[]{:S(2)}) async-start(f32[4,32,2048]{2,1,0:T(8,128)} %bitcast.33), calls=%async_computation.1 | async-start | bytes 2097152 | tf_op jit(solution)/shard_map/all_to_all | solution.py:257
  48.5 134.6 %all-gather.3.cloned.1.call-start = ((), (), s32[]{:S(2)}) async-start(), calls=%async_computation.4 | async-start | bytes 1966080 | tf_op jit(solution)/shard_map/all_gather | solution.py:282
  49.9 6.7 %collective-permute-start.2 = (f32[3,8,128]{2,1,0:T(8,128)S(1)}, f32[3,8,128]{2,1,0:T(8,128)S(1)}, u32[]{:S(2)}, u32[]{:S(2)}) collective-permute-start(f32[3,8,128]{2,1,0:T(8,128)S(1)} %pad_maximum_fusion.11), channel_id=1, source_target_pairs={{0,128},{4,132},{8,136},{12,140},{16,144},{20,148},{24,152},{28,15... | collective-permute-start | bytes 36872 | tf_op jit(solution)/shard_map/ppermute | solution.py:48
  51.8 9.6 %collective-permute-start.3 = (f32[2,32,128]{2,1,0:T(8,128)S(1)}, f32[2,32,128]{2,1,0:T(8,128)S(1)}, u32[]{:S(2)}, u32[]{:S(2)}) collective-permute-start(f32[2,32,128]{2,1,0:T(8,128)S(1)} %pad_maximum_fusion.9), channel_id=1, source_target_pairs={{0,32},{4,36},{8,40},{12,44},{16,48},{20,52},{24,56},{28,60},{32,0... | collective-permute-start | bytes 98312 | tf_op jit(solution)/shard_map/ppermute | solution.py:48
  61.4 5.9 %collective-permute-start.4 = (f32[2,64,128]{2,1,0:T(8,128)S(1)}, f32[2,64,128]{2,1,0:T(8,128)S(1)}, u32[]{:S(2)}, u32[]{:S(2)}) collective-permute-start(f32[2,64,128]{2,1,0:T(8,128)S(1)} %pad_maximum_fusion.8), channel_id=1, source_target_pairs={{0,16},{4,20},{8,24},{12,28},{16,0},{20,4},{24,8},{28,12},{32,48},... | collective-permute-start | bytes 196616 | tf_op jit(solution)/shard_map/ppermute | solution.py:48
  69.0 37.1 %collective-permute-start.5 = (f32[4,2,256,128]{3,2,1,0:T(8,128)S(1)}, f32[4,2,256,128]{3,2,1,0:T(8,128)S(1)}, u32[]{:S(2)}, u32[]{:S(2)}) collective-permute-start(f32[4,2,256,128]{3,2,1,0:T(8,128)S(1)} %all-to-all-done.mine.m1), channel_id=1, source_target_pairs={{0,4},{4,0},{8,12},{12,8},{16,20},{20,16},{24,28},{28,24},{32,36},... | collective-permute-start | bytes 3145736 | tf_op jit(solution)/shard_map/ppermute | solution.py:48
  102.3 7.6 %copy-start.22 = (f32[2,128,128]{2,1,0:T(8,128)S(1)}, f32[2,128,128]{2,1,0:T(8,128)}, u32[]{:S(2)}) copy-start(f32[2,128,128]{2,1,0:T(8,128)} %pad_maximum_fusion.6) | copy-start | bytes 393220
  103.3 6.6 %collective-permute-start.6 = (f32[32,1024]{1,0:T(8,128)S(1)}, f32[32,1024]{1,0:T(8,128)S(1)}, u32[]{:S(2)}, u32[]{:S(2)}) collective-permute-start(f32[32,1024]{1,0:T(8,128)S(1)} %slice.74), channel_id=1, source_target_pairs={{0,16},{4,20},{8,24},{12,28},{16,0},{20,4},{24,8},{28,12},{32,48},... | collective-permute-start | bytes 393224 | tf_op jit(solution)/shard_map/ppermute | solution.py:48
  106.1 13.2 %copy-start.4 = (f32[4,2,256,128]{3,2,1,0:T(8,128)}, f32[4,2,256,128]{3,2,1,0:T(8,128)S(1)}, u32[]{:S(2)}) copy-start(f32[4,2,256,128]{3,2,1,0:T(8,128)S(1)} %collective-permute-done.5.other.o1) | copy-start | bytes 3145732
  107.1 13.5 %copy-start.15 = (f32[32,512]{1,0:T(8,128)}, f32[32,512]{1,0:T(8,128)S(1)}, u32[]{:S(2)}) copy-start(f32[32,512]{1,0:T(8,128)S(1)} %get-tuple-element.57.z1) | copy-start | bytes 196612
  110.0 10.7 %collective-permute-start.8 = (f32[5,128,128]{2,1,0:T(8,128)S(1)}, f32[5,128,128]{2,1,0:T(8,128)S(1)}, u32[]{:S(2)}, u32[]{:S(2)}) collective-permute-start(f32[5,128,128]{2,1,0:T(8,128)S(1)} %pad_maximum_fusion.3), channel_id=1, source_target_pairs={{0,8},{4,12},{8,0},{12,4},{16,24},{20,28},{24,16},{28,20},{32,40},... | collective-permute-start | bytes 983048 | tf_op jit(solution)/shard_map/ppermute | solution.py:48
  114.7 5.9 %collective-permute-start.7 = (f32[32,512]{1,0:T(8,128)S(1)}, f32[32,512]{1,0:T(8,128)S(1)}, u32[]{:S(2)}, u32[]{:S(2)}) collective-permute-start(f32[32,512]{1,0:T(8,128)S(1)} %get-tuple-element.43), channel_id=1, source_target_pairs={{0,16},{4,20},{8,24},{12,28},{16,0},{20,4},{24,8},{28,12},{32,48},... | collective-permute-start | bytes 196616 | tf_op jit(solution)/shard_map/ppermute | solution.py:48
  122.6 14.3 %all-to-all-start.3 = ((f32[4,2,256,128]{3,2,1,0:T(8,128)}), f32[4,2,256,128]{3,2,1,0:T(8,128)S(1)}, u32[]{:S(2)}, u32[]{:S(2)}) async-start(f32[4,2,256,128]{3,2,1,0:T(8,128)} %broadcast_in_dim.11), calls=%async_computation.3 | async-start | bytes 2097152 | tf_op jit(solution)/shard_map/all_to_all | solution.py:231
  127.1 8.9 %collective-permute-start.9 = (f32[32,512]{1,0:T(8,128)S(1)}, f32[32,512]{1,0:T(8,128)S(1)}, u32[]{:S(2)}, u32[]{:S(2)}) collective-permute-start(f32[32,512]{1,0:T(8,128)S(1)} %add.39), channel_id=1, source_target_pairs={{0,32},{4,36},{8,40},{12,44},{16,48},{20,52},{24,56},{28,60},{32,0... | collective-permute-start | bytes 196616 | tf_op jit(solution)/shard_map/ppermute | solution.py:48
  136.8 20.3 %collective-permute-start.11 = (f32[4,2,256,128]{3,2,1,0:T(8,128)S(1)}, f32[4,2,256,128]{3,2,1,0:T(8,128)S(1)}, u32[]{:S(2)}, u32[]{:S(2)}) collective-permute-start(f32[4,2,256,128]{3,2,1,0:T(8,128)S(1)} %all-to-all-done.3.mine.m2), channel_id=1, source_target_pairs={{0,4},{4,0},{8,12},{12,8},{16,20},{20,16},{24,28},{28,24},{32,36},... | collective-permute-start | bytes 3145736 | tf_op jit(solution)/shard_map/ppermute | solution.py:48
  145.0 11.1 %collective-permute-start.10 = (f32[32,1024]{1,0:T(8,128)}, f32[32,1024]{1,0:T(8,128)S(1)}, u32[]{:S(2)}, u32[]{:S(2)}) collective-permute-start(f32[32,1024]{1,0:T(8,128)} %add.40), channel_id=1, source_target_pairs={{0,32},{4,36},{8,40},{12,44},{16,48},{20,52},{24,56},{28,60},{32,0... | collective-permute-start | bytes 393224 | tf_op jit(solution)/shard_map/ppermute | solution.py:48
  159.7 22.7 %collective-permute-start.12 = (f32[32,1024]{1,0:T(8,128)S(1)}, f32[32,1024]{1,0:T(8,128)S(1)}, u32[]{:S(2)}, u32[]{:S(2)}) collective-permute-start(f32[32,1024]{1,0:T(8,128)S(1)} %pad_maximum_fusion.7), channel_id=1, source_target_pairs={{0,112},{4,116},{8,120},{12,124},{16,96},{20,100},{24,104},{28,108... | collective-permute-start | bytes 393224 | tf_op jit(solution)/shard_map/ppermute | solution.py:48
  183.0 10.7 %collective-permute-start.14 = (f32[4,3,256,128]{3,2,1,0:T(8,128)}, f32[4,3,256,128]{3,2,1,0:T(8,128)S(1)}, u32[]{:S(2)}, u32[]{:S(2)}) collective-permute-start(f32[4,3,256,128]{3,2,1,0:T(8,128)} %bitcast.28), channel_id=1, source_target_pairs={{0,4},{4,0},{8,12},{12,8},{16,20},{20,16},{24,28},{28,24},{32,36},... | collective-permute-start | bytes 4718600 | tf_op jit(solution)/shard_map/ppermute | solution.py:48
  185.5 7.2 %collective-permute-start.13 = (f32[32,1024]{1,0:T(8,128)}, f32[32,1024]{1,0:T(8,128)S(1)}, u32[]{:S(2)}, u32[]{:S(2)}) collective-permute-start(f32[32,1024]{1,0:T(8,128)} %fusion), channel_id=1, source_target_pairs={{0,128},{4,132},{8,136},{12,140},{16,144},{20,148},{24,152},{28,15... | collective-permute-start | bytes 393224 | tf_op jit(solution)/shard_map/ppermute | solution.py:48
  195.1 8.3 %copy-start.5 = (f32[4,2,256,128]{3,2,1,0:T(8,128)S(1)}, f32[4,2,256,128]{3,2,1,0:T(8,128)}, u32[]{:S(2)}) copy-start(f32[4,2,256,128]{3,2,1,0:T(8,128)} %copy-done.4) | copy-start | bytes 3145732
  195.1 8.3 %copy-start.7 = (f32[4,2,256,128]{3,2,1,0:T(8,128)S(1)}, f32[4,2,256,128]{3,2,1,0:T(8,128)}, u32[]{:S(2)}) copy-start(f32[4,2,256,128]{3,2,1,0:T(8,128)} %copy-done.6) | copy-start | bytes 3145732
  195.1 8.3 %copy-start.16 = (f32[32,512]{1,0:T(8,128)S(1)}, f32[32,512]{1,0:T(8,128)}, u32[]{:S(2)}) copy-start(f32[32,512]{1,0:T(8,128)} %copy-done.15) | copy-start | bytes 196612
  195.1 8.3 %copy-start.18 = (f32[32,512]{1,0:T(8,128)S(1)}, f32[32,512]{1,0:T(8,128)}, u32[]{:S(2)}) copy-start(f32[32,512]{1,0:T(8,128)} %copy-done.17) | copy-start | bytes 196612
  196.1 7.3 %collective-permute-start.15 = (f32[32,512]{1,0:T(8,128)S(1)}, f32[32,512]{1,0:T(8,128)S(1)}, u32[]{:S(2)}, u32[]{:S(2)}) collective-permute-start(f32[32,512]{1,0:T(8,128)S(1)} %get-tuple-element.56), channel_id=1, source_target_pairs={{0,384},{4,388},{8,392},{12,396},{16,400},{20,404},{24,408},{28,41... | collective-permute-start | bytes 196616 | tf_op jit(solution)/shard_map/ppermute | solution.py:48
  206.8 10.0 %collective-permute-start.16 = (f32[32,2048]{1,0:T(8,128)S(1)}, f32[32,2048]{1,0:T(8,128)S(1)}, u32[]{:S(2)}, u32[]{:S(2)}) collective-permute-start(f32[32,2048]{1,0:T(8,128)S(1)} %shard_map.99), channel_id=1, source_target_pairs={{0,8},{4,12},{8,0},{12,4},{16,24},{20,28},{24,16},{28,20},{32,40},... | collective-permute-start | bytes 786440 | tf_op jit(solution)/shard_map/ppermute | solution.py:48
  216.9 5.9 %collective-permute-start.17 = (f32[2,32,2048]{2,1,0:T(8,128)S(1)}, f32[2,32,2048]{2,1,0:T(8,128)S(1)}, u32[]{:S(2)}, u32[]{:S(2)}) collective-permute-start(f32[2,32,2048]{2,1,0:T(8,128)S(1)} %pad_maximum_fusion.2), channel_id=1, source_target_pairs={{0,4},{4,0},{8,12},{12,8},{16,20},{20,16},{24,28},{28,24},{32,36},... | collective-permute-start | bytes 1572872 | tf_op jit(solution)/shard_map/ppermute | solution.py:48
  (14 other events, 41.0 us)
Sparse Core Ops, SparseCore 0:
  121.6 36.6 all-gather.2

commit v6 on v4

--- a/solution.py
+++ b/solution.py
@@ -94,23 +94,27 @@
         )
 
 
-def backward_kernel(sizes, where, pattern, y, x, inverse, blocks, coupling, out, sep_out):
+def backward_kernel(sizes, where, pattern, y, near, across_core, inverse, blocks, coupling, out, sep_out):
     count, size = inverse.shape[0], inverse.shape[1]
     starts = pair_starts(count)
     width = coupling.shape[1]
     place = where[LEVELS]
-    quarter = x.shape[0]
-    xs = jnp.concatenate([x[jnp.bitwise_xor(place, q)] for q in range(quarter)], axis=0)
+    chunks = []
+    for member in range(2 * near.shape[0]):
+        apart = place ^ member
+        chunks.append(jnp.where(apart % 2 == 1, across_core[apart // 2], near[apart // 2]))
+    xs = jnp.concatenate(chunks, axis=0)
     correction = jnp.zeros((size, y.shape[1]), F32)
-    pieces = jnp.zeros((sep_out.shape[0], y.shape[1]), F32)
+    padded = -(-sep_out.shape[0] // 8) * 8
+    pieces = jnp.zeros((padded, y.shape[1]), F32)
     offset = 0
     for level, rows in enumerate(sizes):
         part = xs[:, level * width : (level + 1) * width]
         correction = correction + mm(coupling[level * size : (level + 1) * size, :], part, NT)
-        spread = placement(sep_out.shape[0], offset, rows, where[level], width)
+        spread = placement(padded, offset, rows, where[level], width)
         pieces = pieces + pick_left(spread, part, NT)
         offset += rows
-    sep_out[...] = pieces
+    sep_out[...] = pieces[: sep_out.shape[0], :]
     pending = [y[i * size : (i + 1) * size, :] for i in range(count)]
     pending[-1] = pending[-1] - correction
     for column in reversed(range(count)):
@@ -122,8 +126,10 @@
             pending[earlier] = pending[earlier] - weight * mm(blocks[pair], solved, TN)
 
 
-def spots(start, count):
-    return [slice(start + r * 128, start + (r + 1) * 128) for r in range(count)]
+def spots(start, count, turn=None):
+    if turn is None:
+        return [slice(start + r * 128, start + (r + 1) * 128) for r in range(count)]
+    return [pl.ds(pl.multiple_of(start + (turn ^ r) * 128, 128), 128) for r in range(count)]
 
 
 def times_rows(value, places, mats, index):
@@ -145,30 +151,44 @@
     return total
 
 
-def level_kernel(index, right, base, mine, other, z_out, v_out):
+def summed(parts, rows):
+    total = None
+    for part in parts:
+        for start in range(0, part.shape[0], rows):
+            term = part[start : start + rows, :]
+            total = term if total is None else total + term
+    return total
+
+
+def level_kernel(index, turned, plane, *refs):
+    mine, other, z_out, v_out = refs[-4:]
     mats = (mine, other)
-    places = spots(0, mine.shape[0])
-    z = times_rows(right, places, mats, index)
+    total = summed(refs[:-4], z_out.shape[0])
+    places = spots(0, mine.shape[0], plane[0] if turned else None)
+    width = z_out.shape[1]
+    z_out[...] = total[:, :width]
+    v_out[...] = total[:, width:]
+    z = times_rows(z_out, places, mats, index)
     z_out[...] = jnp.concatenate(z, axis=1)
     for r, place in enumerate(places):
-        v_out[:, place] = base[:, place] - times_matrix(z, mats, index + 1, r)
-
-
-def top_kernel(right, z1, z2, z3, m1, o1, m2, o2, m3, o3, x_out):
+        v_out[:, place] = v_out[:, place] - times_matrix(z, mats, index + 1, r)
+
+
+def top_kernel(plane, right, right_far, z1, z2, z3, m1, o1, m2, o2, m3, o3, x_out):
     width = right.shape[1]
     count = m3.shape[0]
     top = (m3, o3)
-    z = times_rows(right, spots(0, count), top, 0)
-    order = [(z3, top, 1), (z2, (m2, o2), 0), (z1, (m1, o1), 0)]
-    mats, index = top, 0
+    z = times_rows(right[...] + right_far[...], spots(0, count), top, 0)
+    order = [(z3, top, 1, None), (z2, (m2, o2), 0, None), (z1, (m1, o1), 0, plane[0])]
+    mats, index, turn = top, 0, None
     level = 3
     while True:
-        for r, place in enumerate(spots(level * width, count)):
+        for r, place in enumerate(spots(level * width, count, turn)):
             x_out[:, place] = times_matrix(z, mats, index, r)
         if not order:
             break
-        held, mats, index = order.pop(0)
-        moved = times_rows(x_out, spots(level * width, count), mats, index + 1)
+        held, mats, index, turn = order.pop(0)
+        moved = times_rows(x_out, spots(level * width, count, turn), mats, index + 1)
         half = held.shape[1] // 2
         z = [held[:, :half] - moved[0], held[:, half:] - moved[1]]
         level -= 1
@@ -215,74 +235,67 @@
     tie = lax.optimization_barrier
     halves_z, wrap_z, wrap_y = 1 << Z4, (1 << Z8) | (1 << Z4) | (1 << Z2), (1 << Y2) | (1 << Y1)
     near = [[g * 4 + m for m in range(4)] for g in range(leaves // 4)]
-    level = lambda kernel, *arrays: call(kernel, [(columns // 4, width)] * 2, *arrays)
+    plane = lax.axis_index("col").astype(jnp.int32)[None]
+
+    def turned_planes(value):
+        return jnp.stack([value] + [swap(value, "col", r) for r in range(1, lax.axis_size("col"))])
+
+    def solve(index, turned, depth, *arrays):
+        outs = [(columns // 4, width), (columns // 4, depth * width)]
+        return call(functools.partial(level_kernel, index, turned), outs, plane, *arrays)
 
     first = grow(both(0), 1 << Z1)
     far = grow(rows(sep_inverse, 3)[None], wrap_y)
-    padded = jnp.pad(sep_rhs, ((0, 4), (0, 0)))
     y, t = call(
         functools.partial(forward_kernel, sizes),
         [leaf_rhs.shape, (columns, LEVELS * width)],
-        where, leaf_pattern, leaf_rhs, leaf_inverse, leaf_blocks, leaf_coupling, padded,
+        where, leaf_pattern, leaf_rhs, leaf_inverse, leaf_blocks, leaf_coupling, sep_rhs,
     )
     t, first, far = tie((t, first, far))
 
     t = lax.all_to_all(t, "leaf", 0, 0, axis_index_groups=near, tiled=True)
+    first = turned_planes(first)
     far = grow(jnp.concatenate([far, both(2)], 0), 1 << Y1)
-    first = planes(first)
-    t, far = tie((t, far))
-
     far = grow(far, wrap_z)
-    t = t.reshape(4, columns // 4, LEVELS * width).sum(0)
-    first, t, far = tie((first, t, far))
-
+    t, first, far = tie((t, first, far))
+
+    first = (first, across(first, CORE_MASK))
     far = grow(jnp.concatenate([far, both(1)], 0), halves_z)
-    first = (first, across(first, CORE_MASK))
-    z1, v = level(functools.partial(level_kernel, 0), t[:, :width], t[:, width : 2 * width], *first)
-    v = jnp.concatenate([v, t[:, 2 * width :]], 1)
+    z1, v = solve(0, True, 3, t, *first)
     v, far = tie((v, far))
+    v_far = across(v, 1 << Z2)
 
     far = grow(far, 1 << Z2)
-    v = v + across(v, 1 << Z2)
-    v, far = tie((v, far))
-
+    v = v + v_far
+    v_far = across(v, halves_z)
     far = grow(far, 1 << Z1)
-    v_far = across(v, halves_z)
     far, v = tie((far, v))
 
+    second = planes(far[3:])
     third = lax.all_gather(far[:3], "col", axis=0)
-    second = planes(far[3:])
     second, v, v_far = tie((second, v, v_far))
+
     second = (second, across(second, CORE_MASK))
-    v = v + v_far
-    z2, v3 = level(functools.partial(level_kernel, 0), v[:, :width], v[:, width : 2 * width], *second)
-    v = jnp.concatenate([v3, v[:, 2 * width :]], 1)
+    z2, v = solve(0, False, 2, v, v_far, *second)
     v = v + across(v, wrap_z)
     v, third = tie((v, third))
 
     third = (third, across(third, CORE_MASK))
-    v = v + across(v, 1 << Y1)
-    z3, v = level(functools.partial(level_kernel, 1), v[:, :width], v[:, width:], *third)
-    v = v + across(v, wrap_y)
-    (x,) = call(top_kernel, [(columns // 4, LEVELS * width)], v, z1, z2, z3, *first, *second, *third)
+    z3, v = solve(1, False, 1, v, across(v, 1 << Y1), *third)
+    (x,) = call(
+        top_kernel, [(columns // 4, LEVELS * width)], plane, v, across(v, wrap_y), z1, z2, z3, *first, *second, *third
+    )
     x = jnp.stack([x, across(x, 1 << Z1)])
-    other = across(x, CORE_MASK)
-    x = jnp.stack([x[0], other[0], x[1], other[1]], 0)
     return call(
         functools.partial(backward_kernel, sizes),
-        [leaf_rhs.shape, padded.shape],
-        where, leaf_pattern, y, x, leaf_inverse, leaf_blocks, leaf_coupling,
+        [leaf_rhs.shape, sep_rhs.shape],
+        where, leaf_pattern, y, x, across(x, CORE_MASK), leaf_inverse, leaf_blocks, leaf_coupling,
     )
-
-
-def program(*arrays):
-    leaf, sep = shards(*arrays)
-    return leaf, sep[: arrays[5].shape[0]]
 
 
 def solution(mesh):
     return jax.shard_map(
-        program,
+        shards,
         mesh=mesh,
         in_specs=(
             P("leaf", "col"),

time: 221 us -> 208 us (0.941)
  starting transfers between devices: 74.5 us -> 117 us
  waiting for transfers between devices: 80 us -> 43.6 us
  blocking collectives: 18.2 us -> 0 us
    ppermute x17 -> x20, starting transfers between devices: 66.6 us -> 107 us  [swap(): lax.ppermute(value, axis, [(i, i ^ mask) for i in range(lax.axis_size(axi...]
    ppermute x17 -> x20, waiting for transfers between devices: 80 us -> 42.6 us  [swap(): lax.ppermute(value, axis, [(i, i ^ mask) for i in range(lax.axis_size(axi...]
    all_to_all x1 -> x0, blocking collectives: 18.2 us -> none  [shards(): t = lax.all_to_all(t, 'leaf', 0, 0, axis_index_groups=near, tiled=True)]
    all_to_all x0 -> x1, starting transfers between devices: none -> 5.19 us  [shards(): t = lax.all_to_all(t, 'leaf', 0, 0, axis_index_groups=near, tiled=True)]
    all_to_all x2 -> x1, starting transfers between devices: 7.92 us -> 4.03 us  [planes(): lax.all_to_all(jnp.broadcast_to(value[None], (count, *value.shape)), 'col...]
    unnamed x28 -> x38, local copies, waits for them, and re-layouts: 7.66 us -> 9.95 us
  transfers between devices with their start and end apart: 20 -> 23, of which waited for: 13 -> 12; matrix products, arithmetic and copies ran while one was open for 3% -> 2% of each run, Pallas kernels for 2% -> 3%
where the time goes in v6:
time: 208 us; the launch traced here: 207 us
  starting transfers between devices  117 us (56%)
  waiting for transfers between devices  43.6 us (21%)
  local copies, waits for them, and re-layouts  16.3 us (8%)
  Pallas kernels  15.9 us (8%)
  between operations  14.5 us (7%)
    ppermute x20, starting transfers between devices, swap(): lax.ppermute(value, axis, [(i, i ^ mask) for i in range(lax.axis_size(axi...  107 us
    ppermute x20, waiting for transfers between devices, swap(): lax.ppermute(value, axis, [(i, i ^ mask) for i in range(lax.axis_size(axi...  42.6 us
    pallas_call x6, Pallas kernels, call(): pl.pallas_call(kernel, out_shape=[jax.ShapeDtypeStruct(s, F32) for s in o...  15.9 us
    unnamed x38, local copies, waits for them, and re-layouts  9.95 us
    all_to_all x1, starting transfers between devices, shards(): t = lax.all_to_all(t, 'leaf', 0, 0, axis_index_groups=near, tiled=True)  5.19 us
  transfers between devices with their start and end apart: 23, of which 12 were waited for; matrix products, arithmetic and copies ran while one was open for 2% of the time, Pallas kernels for 3%

profile of v6, /device:TPU:1, one launch (start us, length us, event | category | flops | bytes accessed | tf_op | source)
XLA Modules:
  0.0 207.2 jit_solution(6536967380689504997)
XLA Ops:
  8.1 4.4 %collective-permute-start = (f32[2,128,128]{2,1,0:T(8,128)S(1)}, f32[2,128,128]{2,1,0:T(8,128)S(1)}, u32[]{:S(2)}, u32[]{:S(2)}) collective-permute-start(f32[2,128,128]{2,1,0:T(8,128)S(1)} %pad_maximum_fusion.6), channel_id=1, source_target_pairs={{0,8},{4,12},{8,0},{12,4},{16,24},{20,28},{24,16},{28,20},{32,40},... | collective-permute-start | bytes 393224 | tf_op jit(solution)/shard_map/ppermute | solution.py:48
  13.1 4.6 %collective-permute-start.1 = (f32[1,4,128]{2,1,0:T(4,128)S(1)}, f32[1,4,128]{2,1,0:T(4,128)S(1)}, u32[]{:S(2)}, u32[]{:S(2)}) collective-permute-start(f32[1,4,128]{2,1,0:T(4,128)S(1)} %slice_bitcast_fusion.6), channel_id=1, source_target_pairs={{0,384},{4,388},{8,392},{12,396},{16,400},{20,404},{24,408},{28,41... | collective-permute-start | bytes 6152 | tf_op jit(solution)/shard_map/ppermute | solution.py:48
  24.1 4.8 %shard_map.95 = (f32[896,128]{1,0:T(8,128)S(1)}, f32[128,2048]{1,0:T(8,128)}) custom-call(s32[5]{0:T(128)S(1)} %stack.68.where, s32[1,21]{1,0:T(1,128)S(1)} %copy-done.17, f32[896,128]{1,0:T(8,128)S(1)} %copy-done.11, f32[7,128,128]{2,1,0:T(8,128)S(1)} %copy-done.7, f32[21,128,128]{2,1,0:T(8,128)S(1)} %copy-done.1, f32[512,512]{1,0:T(8,128)S(1)} %copy-done.3, ...), custom_call_target="tpu_custom_call" | custom-call | tf_op jit(solution)/shard_map/pallas_call | solution.py:206
  29.7 5.2 %all-to-all-start = ((f32[4,32,2048]{2,1,0:T(8,128)}), f32[4,32,2048]{2,1,0:T(8,128)S(1)}, u32[]{:S(2)}, u32[]{:S(2)}) async-start(f32[4,32,2048]{2,1,0:T(8,128)} %bitcast.9), calls=%async_computation | async-start | bytes 2097152 | tf_op jit(solution)/shard_map/all_to_all | solution.py:256
  38.2 3.9 %collective-permute-start.4 = (f32[2,256,128]{2,1,0:T(8,128)S(1)}, f32[2,256,128]{2,1,0:T(8,128)S(1)}, u32[]{:S(2)}, u32[]{:S(2)}) collective-permute-start(f32[2,256,128]{2,1,0:T(8,128)S(1)} %pad_maximum_fusion.4), channel_id=1, source_target_pairs={{0,3},{1,2},{2,1},{3,0},{4,7},{5,6},{6,5},{7,4},{8,11},{9,10},{10,... | collective-permute-start | bytes 786440 | tf_op jit(solution)/shard_map/ppermute | solution.py:48
  42.1 2.4 %collective-permute-start.3 = (f32[2,256,128]{2,1,0:T(8,128)S(1)}, f32[2,256,128]{2,1,0:T(8,128)S(1)}, u32[]{:S(2)}, u32[]{:S(2)}) collective-permute-start(f32[2,256,128]{2,1,0:T(8,128)S(1)} %pad_maximum_fusion.4), channel_id=1, source_target_pairs={{0,2},{1,3},{2,0},{3,1},{4,6},{5,7},{6,4},{7,5},{8,10},{9,11},{10,... | collective-permute-start | bytes 786440 | tf_op jit(solution)/shard_map/ppermute | solution.py:48
  44.5 2.6 %collective-permute-start.2 = (f32[2,256,128]{2,1,0:T(8,128)S(1)}, f32[2,256,128]{2,1,0:T(8,128)S(1)}, u32[]{:S(2)}, u32[]{:S(2)}) collective-permute-start(f32[2,256,128]{2,1,0:T(8,128)S(1)} %pad_maximum_fusion.4), channel_id=1, source_target_pairs={{0,1},{1,0},{2,3},{3,2},{4,5},{5,4},{6,7},{7,6},{8,9},{9,8},{10,11... | collective-permute-start | bytes 786440 | tf_op jit(solution)/shard_map/ppermute | solution.py:48
  47.2 10.2 %collective-permute-start.6 = (f32[3,16,128]{2,1,0:T(8,128)S(1)}, f32[3,16,128]{2,1,0:T(8,128)S(1)}, u32[]{:S(2)}, u32[]{:S(2)}) collective-permute-start(f32[3,16,128]{2,1,0:T(8,128)S(1)} %pad_maximum_fusion.9), channel_id=1, source_target_pairs={{0,112},{4,116},{8,120},{12,124},{16,96},{20,100},{24,104},{28,108... | collective-permute-start | bytes 73736 | tf_op jit(solution)/shard_map/ppermute | solution.py:48
  58.7 4.0 %collective-permute-start.7 = (f32[4,2,256,128]{3,2,1,0:T(8,128)S(1)}, f32[4,2,256,128]{3,2,1,0:T(8,128)S(1)}, u32[]{:S(2)}, u32[]{:S(2)}) collective-permute-start(f32[4,2,256,128]{3,2,1,0:T(8,128)S(1)} %pad_maximum_fusion.refs_1_.m1), channel_id=1, source_target_pairs={{0,4},{4,0},{8,12},{12,8},{16,20},{20,16},{24,28},{28,24},{32,36},... | collective-permute-start | bytes 3145736 | tf_op jit(solution)/shard_map/ppermute | solution.py:48
  64.2 7.3 %collective-permute-start.8 = (f32[5,32,128]{2,1,0:T(8,128)S(1)}, f32[5,32,128]{2,1,0:T(8,128)S(1)}, u32[]{:S(2)}, u32[]{:S(2)}) collective-permute-start(f32[5,32,128]{2,1,0:T(8,128)S(1)} %pad_maximum_fusion.7), channel_id=1, source_target_pairs={{0,32},{4,36},{8,40},{12,44},{16,48},{20,52},{24,56},{28,60},{32,0... | collective-permute-start | bytes 245768 | tf_op jit(solution)/shard_map/ppermute | solution.py:48
  71.5 2.7 %collective-permute-done.8 = f32[5,32,128]{2,1,0:T(8,128)S(1)} collective-permute-done((f32[5,32,128]{2,1,0:T(8,128)S(1)}, f32[5,32,128]{2,1,0:T(8,128)S(1)}, u32[]{:S(2)}, u32[]{:S(2)}) %collective-permute-start.8) | collective-permute-done | bytes 81952 | tf_op jit(solution)/shard_map/ppermute | solution.py:48
  75.2 5.9 %collective-permute-start.9 = (f32[5,64,128]{2,1,0:T(8,128)S(1)}, f32[5,64,128]{2,1,0:T(8,128)S(1)}, u32[]{:S(2)}, u32[]{:S(2)}) collective-permute-start(f32[5,64,128]{2,1,0:T(8,128)S(1)} %pad_maximum_fusion.5), channel_id=1, source_target_pairs={{0,16},{4,20},{8,24},{12,28},{16,0},{20,4},{24,8},{28,12},{32,48},... | collective-permute-start | bytes 491528 | tf_op jit(solution)/shard_map/ppermute | solution.py:48
  81.2 2.7 %collective-permute-done.9 = f32[5,64,128]{2,1,0:T(8,128)S(1)} collective-permute-done((f32[5,64,128]{2,1,0:T(8,128)S(1)}, f32[5,64,128]{2,1,0:T(8,128)S(1)}, u32[]{:S(2)}, u32[]{:S(2)}) %collective-permute-start.9) | collective-permute-done | bytes 163872 | tf_op jit(solution)/shard_map/ppermute | solution.py:48
  83.9 8.2 %collective-permute-start.10 = (f32[5,128,128]{2,1,0:T(8,128)S(1)}, f32[5,128,128]{2,1,0:T(8,128)S(1)}, u32[]{:S(2)}, u32[]{:S(2)}) collective-permute-start(f32[5,128,128]{2,1,0:T(8,128)S(1)} %pad_maximum_fusion.3), channel_id=1, source_target_pairs={{0,8},{4,12},{8,0},{12,4},{16,24},{20,28},{24,16},{28,20},{32,40},... | collective-permute-start | bytes 983048 | tf_op jit(solution)/shard_map/ppermute | solution.py:48
  92.1 5.0 %collective-permute-start.11 = (f32[32,1536]{1,0:T(8,128)S(1)}, f32[32,1536]{1,0:T(8,128)S(1)}, u32[]{:S(2)}, u32[]{:S(2)}) collective-permute-start(f32[32,1536]{1,0:T(8,128)S(1)} %get-tuple-element.35), channel_id=1, source_target_pairs={{0,16},{4,20},{8,24},{12,28},{16,0},{20,4},{24,8},{28,12},{32,48},... | collective-permute-start | bytes 589832 | tf_op jit(solution)/shard_map/ppermute | solution.py:48
  97.1 5.3 %collective-permute-done.11 = f32[32,1536]{1,0:T(8,128)S(1)} collective-permute-done((f32[32,1536]{1,0:T(8,128)S(1)}, f32[32,1536]{1,0:T(8,128)S(1)}, u32[]{:S(2)}, u32[]{:S(2)}) %collective-permute-start.11) | collective-permute-done | bytes 196640 | tf_op jit(solution)/shard_map/ppermute | solution.py:48
  104.4 4.0 %all-to-all-start.1 = ((f32[4,2,256,128]{3,2,1,0:T(8,128)}), f32[4,2,256,128]{3,2,1,0:T(8,128)S(1)}, u32[]{:S(2)}, u32[]{:S(2)}) async-start(f32[4,2,256,128]{3,2,1,0:T(8,128)} %broadcast_in_dim.14), calls=%async_computation.1 | async-start | bytes 2097152 | tf_op jit(solution)/shard_map/all_to_all | solution.py:233
  108.4 8.3 %collective-permute-start.12 = (f32[32,1536]{1,0:T(8,128)S(1)}, f32[32,1536]{1,0:T(8,128)S(1)}, u32[]{:S(2)}, u32[]{:S(2)}) collective-permute-start(f32[32,1536]{1,0:T(8,128)S(1)} %add.24.refs_0_), channel_id=1, source_target_pairs={{0,32},{4,36},{8,40},{12,44},{16,48},{20,52},{24,56},{28,60},{32,0... | collective-permute-start | bytes 589832 | tf_op jit(solution)/shard_map/ppermute | solution.py:48
  116.7 3.0 %collective-permute-done.12.refs_1_ = f32[32,1536]{1,0:T(8,128)S(1)} collective-permute-done((f32[32,1536]{1,0:T(8,128)S(1)}, f32[32,1536]{1,0:T(8,128)S(1)}, u32[]{:S(2)}, u32[]{:S(2)}) %collective-permute-start.12) | collective-permute-done | bytes 196640 | tf_op jit(solution)/shard_map/ppermute | solution.py:48
  120.7 16.7 %collective-permute-start.13 = (f32[4,2,256,128]{3,2,1,0:T(8,128)S(1)}, f32[4,2,256,128]{3,2,1,0:T(8,128)S(1)}, u32[]{:S(2)}, u32[]{:S(2)}) collective-permute-start(f32[4,2,256,128]{3,2,1,0:T(8,128)S(1)} %all-to-all-done.1.refs_2_.m2), channel_id=1, source_target_pairs={{0,4},{4,0},{8,12},{12,8},{16,20},{20,16},{24,28},{28,24},{32,36},... | collective-permute-start | bytes 3145736 | tf_op jit(solution)/shard_map/ppermute | solution.py:48
  142.2 2.5 %collective-permute-start.14 = (f32[32,1024]{1,0:T(8,128)S(1)}, f32[32,1024]{1,0:T(8,128)S(1)}, u32[]{:S(2)}, u32[]{:S(2)}) collective-permute-start(f32[32,1024]{1,0:T(8,128)S(1)} %get-tuple-element.41), channel_id=1, source_target_pairs={{0,112},{4,116},{8,120},{12,124},{16,96},{20,100},{24,104},{28,108... | collective-permute-start | bytes 393224 | tf_op jit(solution)/shard_map/ppermute | solution.py:48
  144.7 11.4 %collective-permute-done.14 = f32[32,1024]{1,0:T(8,128)S(1)} collective-permute-done((f32[32,1024]{1,0:T(8,128)S(1)}, f32[32,1024]{1,0:T(8,128)S(1)}, u32[]{:S(2)}, u32[]{:S(2)}) %collective-permute-start.14) | collective-permute-done | bytes 131104 | tf_op jit(solution)/shard_map/ppermute | solution.py:48
  156.1 2.7 %collective-permute-start.16 = (f32[4,3,256,128]{3,2,1,0:T(8,128)}, f32[4,3,256,128]{3,2,1,0:T(8,128)S(1)}, u32[]{:S(2)}, u32[]{:S(2)}) collective-permute-start(f32[4,3,256,128]{3,2,1,0:T(8,128)} %bitcast.29), channel_id=1, source_target_pairs={{0,4},{4,0},{8,12},{12,8},{16,20},{20,16},{24,28},{28,24},{32,36},... | collective-permute-start | bytes 4718600 | tf_op jit(solution)/shard_map/ppermute | solution.py:48
  158.8 4.4 %collective-permute-start.15 = (f32[32,1024]{1,0:T(8,128)S(1)}, f32[32,1024]{1,0:T(8,128)S(1)}, u32[]{:S(2)}, u32[]{:S(2)}) collective-permute-start(f32[32,1024]{1,0:T(8,128)S(1)} %add.25.refs_0_), channel_id=1, source_target_pairs={{0,128},{4,132},{8,136},{12,140},{16,144},{20,148},{24,152},{28,15... | collective-permute-start | bytes 393224 | tf_op jit(solution)/shard_map/ppermute | solution.py:48
  163.2 3.8 %collective-permute-done.15.refs_1_ = f32[32,1024]{1,0:T(8,128)S(1)} collective-permute-done((f32[32,1024]{1,0:T(8,128)S(1)}, f32[32,1024]{1,0:T(8,128)S(1)}, u32[]{:S(2)}, u32[]{:S(2)}) %collective-permute-start.15) | collective-permute-done | bytes 131104 | tf_op jit(solution)/shard_map/ppermute | solution.py:48
  169.5 2.3 %collective-permute-start.17 = (f32[32,512]{1,0:T(8,128)S(1)}, f32[32,512]{1,0:T(8,128)S(1)}, u32[]{:S(2)}, u32[]{:S(2)}) collective-permute-start(f32[32,512]{1,0:T(8,128)S(1)} %get-tuple-element.44.right), channel_id=1, source_target_pairs={{0,384},{4,388},{8,392},{12,396},{16,400},{20,404},{24,408},{28,41... | collective-permute-start | bytes 196616 | tf_op jit(solution)/shard_map/ppermute | solution.py:48
  171.8 3.9 %collective-permute-done.17.right_far = f32[32,512]{1,0:T(8,128)S(1)} collective-permute-done((f32[32,512]{1,0:T(8,128)S(1)}, f32[32,512]{1,0:T(8,128)S(1)}, u32[]{:S(2)}, u32[]{:S(2)}) %collective-permute-start.17) | collective-permute-done | bytes 65568 | tf_op jit(solution)/shard_map/ppermute | solution.py:48
  175.7 3.5 %shard_map.99 = f32[32,2048]{1,0:T(8,128)S(1)} custom-call(s32[1]{0:T(128)} %bitcast.5.plane, f32[32,512]{1,0:T(8,128)S(1)} %get-tuple-element.44.right, f32[32,512]{1,0:T(8,128)S(1)} %collective-permute-done.17.right_far, f32[32,512]{1,0:T(8,128)S(1)} %copy-done.14, f32[32,512]{1,0:T(8,128)S(1)} %copy-done.16, f32[32,512]{1,0:T(8,128)S(1)} %get-tuple-element.47.z3, ...), custom_call_target="tpu_custom_call" | custom-call | tf_op jit(solution)/shard_map/pallas_call | solution.py:206
  179.3 5.6 %collective-permute-start.18 = (f32[32,2048]{1,0:T(8,128)S(1)}, f32[32,2048]{1,0:T(8,128)S(1)}, u32[]{:S(2)}, u32[]{:S(2)}) collective-permute-start(f32[32,2048]{1,0:T(8,128)S(1)} %shard_map.99), channel_id=1, source_target_pairs={{0,8},{4,12},{8,0},{12,4},{16,24},{20,28},{24,16},{28,20},{32,40},... | collective-permute-start | bytes 786440 | tf_op jit(solution)/shard_map/ppermute | solution.py:48
  184.9 4.8 %collective-permute-done.18 = f32[32,2048]{1,0:T(8,128)S(1)} collective-permute-done((f32[32,2048]{1,0:T(8,128)S(1)}, f32[32,2048]{1,0:T(8,128)S(1)}, u32[]{:S(2)}, u32[]{:S(2)}) %collective-permute-start.18) | collective-permute-done | bytes 262176 | tf_op jit(solution)/shard_map/ppermute | solution.py:48
  189.8 4.3 %collective-permute-start.19 = (f32[2,32,2048]{2,1,0:T(8,128)S(1)}, f32[2,32,2048]{2,1,0:T(8,128)S(1)}, u32[]{:S(2)}, u32[]{:S(2)}) collective-permute-start(f32[2,32,2048]{2,1,0:T(8,128)S(1)} %pad_maximum_fusion.2.near), channel_id=1, source_target_pairs={{0,4},{4,0},{8,12},{12,8},{16,20},{20,16},{24,28},{28,24},{32,36},... | collective-permute-start | bytes 1572872 | tf_op jit(solution)/shard_map/ppermute | solution.py:48
  195.7 4.7 %shard_map.100 = (f32[896,128]{1,0:T(8,128)}, f32[172,128]{1,0:T(8,128)}) custom-call(s32[5]{0:T(128)S(1)} %stack.68.where, s32[1,21]{1,0:T(1,128)S(1)} %copy-done.18, f32[896,128]{1,0:T(8,128)S(1)} %copy-done.10, f32[2,32,2048]{2,1,0:T(8,128)S(1)} %pad_maximum_fusion.2.near, f32[2,32,2048]{2,1,0:T(8,128)S(1)} %collective-permute-done.19.across_core, ...), custom_call_target="tpu_custom_call" | custom-call | tf_op jit(solution)/shard_map/pallas_call | solution.py:206
  (83 shorter events, 27.4 us)
Async XLA Ops:
  8.1 21.6 %collective-permute-start = (f32[2,128,128]{2,1,0:T(8,128)S(1)}, f32[2,128,128]{2,1,0:T(8,128)S(1)}, u32[]{:S(2)}, u32[]{:S(2)}) collective-permute-start(f32[2,128,128]{2,1,0:T(8,128)S(1)} %pad_maximum_fusion.6), channel_id=1, source_target_pairs={{0,8},{4,12},{8,0},{12,4},{16,24},{20,28},{24,16},{28,20},{32,40},... | collective-permute-start | bytes 393224 | tf_op jit(solution)/shard_map/ppermute | solution.py:48
  13.1 16.5 %collective-permute-start.1 = (f32[1,4,128]{2,1,0:T(4,128)S(1)}, f32[1,4,128]{2,1,0:T(4,128)S(1)}, u32[]{:S(2)}, u32[]{:S(2)}) collective-permute-start(f32[1,4,128]{2,1,0:T(4,128)S(1)} %slice_bitcast_fusion.6), channel_id=1, source_target_pairs={{0,384},{4,388},{8,392},{12,396},{16,400},{20,404},{24,408},{28,41... | collective-permute-start | bytes 6152 | tf_op jit(solution)/shard_map/ppermute | solution.py:48
  29.7 29.0 %all-to-all-start = ((f32[4,32,2048]{2,1,0:T(8,128)}), f32[4,32,2048]{2,1,0:T(8,128)S(1)}, u32[]{:S(2)}, u32[]{:S(2)}) async-start(f32[4,32,2048]{2,1,0:T(8,128)} %bitcast.9), calls=%async_computation | async-start | bytes 2097152 | tf_op jit(solution)/shard_map/all_to_all | solution.py:256
  34.9 121.3 %all-gather.3.cloned.1.call-start = ((), (), s32[]{:S(2)}) async-start(), calls=%async_computation.2 | async-start | bytes 1966080 | tf_op jit(solution)/shard_map/all_gather | solution.py:275
  36.2 10.9 %collective-permute-start.5 = (f32[3,8,128]{2,1,0:T(8,128)S(1)}, f32[3,8,128]{2,1,0:T(8,128)S(1)}, u32[]{:S(2)}, u32[]{:S(2)}) collective-permute-start(f32[3,8,128]{2,1,0:T(8,128)S(1)} %pad_maximum_fusion.10), channel_id=1, source_target_pairs={{0,128},{4,132},{8,136},{12,140},{16,144},{20,148},{24,152},{28,15... | collective-permute-start | bytes 36872 | tf_op jit(solution)/shard_map/ppermute | solution.py:48
  38.2 20.4 %collective-permute-start.4 = (f32[2,256,128]{2,1,0:T(8,128)S(1)}, f32[2,256,128]{2,1,0:T(8,128)S(1)}, u32[]{:S(2)}, u32[]{:S(2)}) collective-permute-start(f32[2,256,128]{2,1,0:T(8,128)S(1)} %pad_maximum_fusion.4), channel_id=1, source_target_pairs={{0,3},{1,2},{2,1},{3,0},{4,7},{5,6},{6,5},{7,4},{8,11},{9,10},{10,... | collective-permute-start | bytes 786440 | tf_op jit(solution)/shard_map/ppermute | solution.py:48
  42.1 16.5 %collective-permute-start.3 = (f32[2,256,128]{2,1,0:T(8,128)S(1)}, f32[2,256,128]{2,1,0:T(8,128)S(1)}, u32[]{:S(2)}, u32[]{:S(2)}) collective-permute-start(f32[2,256,128]{2,1,0:T(8,128)S(1)} %pad_maximum_fusion.4), channel_id=1, source_target_pairs={{0,2},{1,3},{2,0},{3,1},{4,6},{5,7},{6,4},{7,5},{8,10},{9,11},{10,... | collective-permute-start | bytes 786440 | tf_op jit(solution)/shard_map/ppermute | solution.py:48
  44.5 14.1 %collective-permute-start.2 = (f32[2,256,128]{2,1,0:T(8,128)S(1)}, f32[2,256,128]{2,1,0:T(8,128)S(1)}, u32[]{:S(2)}, u32[]{:S(2)}) collective-permute-start(f32[2,256,128]{2,1,0:T(8,128)S(1)} %pad_maximum_fusion.4), channel_id=1, source_target_pairs={{0,1},{1,0},{2,3},{3,2},{4,5},{5,4},{6,7},{7,6},{8,9},{9,8},{10,11... | collective-permute-start | bytes 786440 | tf_op jit(solution)/shard_map/ppermute | solution.py:48
  47.2 11.4 %collective-permute-start.6 = (f32[3,16,128]{2,1,0:T(8,128)S(1)}, f32[3,16,128]{2,1,0:T(8,128)S(1)}, u32[]{:S(2)}, u32[]{:S(2)}) collective-permute-start(f32[3,16,128]{2,1,0:T(8,128)S(1)} %pad_maximum_fusion.9), channel_id=1, source_target_pairs={{0,112},{4,116},{8,120},{12,124},{16,96},{20,100},{24,104},{28,108... | collective-permute-start | bytes 73736 | tf_op jit(solution)/shard_map/ppermute | solution.py:48
  58.7 15.5 %collective-permute-start.7 = (f32[4,2,256,128]{3,2,1,0:T(8,128)S(1)}, f32[4,2,256,128]{3,2,1,0:T(8,128)S(1)}, u32[]{:S(2)}, u32[]{:S(2)}) collective-permute-start(f32[4,2,256,128]{3,2,1,0:T(8,128)S(1)} %pad_maximum_fusion.refs_1_.m1), channel_id=1, source_target_pairs={{0,4},{4,0},{8,12},{12,8},{16,20},{20,16},{24,28},{28,24},{32,36},... | collective-permute-start | bytes 3145736 | tf_op jit(solution)/shard_map/ppermute | solution.py:48
  64.2 10.0 %collective-permute-start.8 = (f32[5,32,128]{2,1,0:T(8,128)S(1)}, f32[5,32,128]{2,1,0:T(8,128)S(1)}, u32[]{:S(2)}, u32[]{:S(2)}) collective-permute-start(f32[5,32,128]{2,1,0:T(8,128)S(1)} %pad_maximum_fusion.7), channel_id=1, source_target_pairs={{0,32},{4,36},{8,40},{12,44},{16,48},{20,52},{24,56},{28,60},{32,0... | collective-permute-start | bytes 245768 | tf_op jit(solution)/shard_map/ppermute | solution.py:48
  75.2 27.2 %copy-start.13 = (f32[32,512]{1,0:T(8,128)}, f32[32,512]{1,0:T(8,128)S(1)}, u32[]{:S(2)}) copy-start(f32[32,512]{1,0:T(8,128)S(1)} %get-tuple-element.45.z1) | copy-start | bytes 196612
  75.2 8.6 %collective-permute-start.9 = (f32[5,64,128]{2,1,0:T(8,128)S(1)}, f32[5,64,128]{2,1,0:T(8,128)S(1)}, u32[]{:S(2)}, u32[]{:S(2)}) collective-permute-start(f32[5,64,128]{2,1,0:T(8,128)S(1)} %pad_maximum_fusion.5), channel_id=1, source_target_pairs={{0,16},{4,20},{8,24},{12,28},{16,0},{20,4},{24,8},{28,12},{32,48},... | collective-permute-start | bytes 491528 | tf_op jit(solution)/shard_map/ppermute | solution.py:48
  83.9 18.5 %collective-permute-start.10 = (f32[5,128,128]{2,1,0:T(8,128)S(1)}, f32[5,128,128]{2,1,0:T(8,128)S(1)}, u32[]{:S(2)}, u32[]{:S(2)}) collective-permute-start(f32[5,128,128]{2,1,0:T(8,128)S(1)} %pad_maximum_fusion.3), channel_id=1, source_target_pairs={{0,8},{4,12},{8,0},{12,4},{16,24},{20,28},{24,16},{28,20},{32,40},... | collective-permute-start | bytes 983048 | tf_op jit(solution)/shard_map/ppermute | solution.py:48
  92.1 10.3 %collective-permute-start.11 = (f32[32,1536]{1,0:T(8,128)S(1)}, f32[32,1536]{1,0:T(8,128)S(1)}, u32[]{:S(2)}, u32[]{:S(2)}) collective-permute-start(f32[32,1536]{1,0:T(8,128)S(1)} %get-tuple-element.35), channel_id=1, source_target_pairs={{0,16},{4,20},{8,24},{12,28},{16,0},{20,4},{24,8},{28,12},{32,48},... | collective-permute-start | bytes 589832 | tf_op jit(solution)/shard_map/ppermute | solution.py:48
  104.4 16.4 %all-to-all-start.1 = ((f32[4,2,256,128]{3,2,1,0:T(8,128)}), f32[4,2,256,128]{3,2,1,0:T(8,128)S(1)}, u32[]{:S(2)}, u32[]{:S(2)}) async-start(f32[4,2,256,128]{3,2,1,0:T(8,128)} %broadcast_in_dim.14), calls=%async_computation.1 | async-start | bytes 2097152 | tf_op jit(solution)/shard_map/all_to_all | solution.py:233
  108.4 11.3 %collective-permute-start.12 = (f32[32,1536]{1,0:T(8,128)S(1)}, f32[32,1536]{1,0:T(8,128)S(1)}, u32[]{:S(2)}, u32[]{:S(2)}) collective-permute-start(f32[32,1536]{1,0:T(8,128)S(1)} %add.24.refs_0_), channel_id=1, source_target_pairs={{0,32},{4,36},{8,40},{12,44},{16,48},{20,52},{24,56},{28,60},{32,0... | collective-permute-start | bytes 589832 | tf_op jit(solution)/shard_map/ppermute | solution.py:48
  120.7 19.0 %collective-permute-start.13 = (f32[4,2,256,128]{3,2,1,0:T(8,128)S(1)}, f32[4,2,256,128]{3,2,1,0:T(8,128)S(1)}, u32[]{:S(2)}, u32[]{:S(2)}) collective-permute-start(f32[4,2,256,128]{3,2,1,0:T(8,128)S(1)} %all-to-all-done.1.refs_2_.m2), channel_id=1, source_target_pairs={{0,4},{4,0},{8,12},{12,8},{16,20},{20,16},{24,28},{28,24},{32,36},... | collective-permute-start | bytes 3145736 | tf_op jit(solution)/shard_map/ppermute | solution.py:48
  142.2 13.9 %collective-permute-start.14 = (f32[32,1024]{1,0:T(8,128)S(1)}, f32[32,1024]{1,0:T(8,128)S(1)}, u32[]{:S(2)}, u32[]{:S(2)}) collective-permute-start(f32[32,1024]{1,0:T(8,128)S(1)} %get-tuple-element.41), channel_id=1, source_target_pairs={{0,112},{4,116},{8,120},{12,124},{16,96},{20,100},{24,104},{28,108... | collective-permute-start | bytes 393224 | tf_op jit(solution)/shard_map/ppermute | solution.py:48
  156.1 19.6 %copy-start.14 = (f32[32,512]{1,0:T(8,128)S(1)}, f32[32,512]{1,0:T(8,128)}, u32[]{:S(2)}) copy-start(f32[32,512]{1,0:T(8,128)} %copy-done.13) | copy-start | bytes 196612
  156.1 19.6 %copy-start.16 = (f32[32,512]{1,0:T(8,128)S(1)}, f32[32,512]{1,0:T(8,128)}, u32[]{:S(2)}) copy-start(f32[32,512]{1,0:T(8,128)} %copy-done.15) | copy-start | bytes 196612
  156.1 10.9 %collective-permute-start.16 = (f32[4,3,256,128]{3,2,1,0:T(8,128)}, f32[4,3,256,128]{3,2,1,0:T(8,128)S(1)}, u32[]{:S(2)}, u32[]{:S(2)}) collective-permute-start(f32[4,3,256,128]{3,2,1,0:T(8,128)} %bitcast.29), channel_id=1, source_target_pairs={{0,4},{4,0},{8,12},{12,8},{16,20},{20,16},{24,28},{28,24},{32,36},... | collective-permute-start | bytes 4718600 | tf_op jit(solution)/shard_map/ppermute | solution.py:48
  158.8 8.3 %collective-permute-start.15 = (f32[32,1024]{1,0:T(8,128)S(1)}, f32[32,1024]{1,0:T(8,128)S(1)}, u32[]{:S(2)}, u32[]{:S(2)}) collective-permute-start(f32[32,1024]{1,0:T(8,128)S(1)} %add.25.refs_0_), channel_id=1, source_target_pairs={{0,128},{4,132},{8,136},{12,140},{16,144},{20,148},{24,152},{28,15... | collective-permute-start | bytes 393224 | tf_op jit(solution)/shard_map/ppermute | solution.py:48
  168.5 7.2 %copy-start.6 = (f32[4,2,256,128]{3,2,1,0:T(8,128)S(1)}, f32[4,2,256,128]{3,2,1,0:T(8,128)}, u32[]{:S(2)}) copy-start(f32[4,2,256,128]{3,2,1,0:T(8,128)} %copy-done.5) | copy-start | bytes 3145732
  169.5 6.2 %collective-permute-start.17 = (f32[32,512]{1,0:T(8,128)S(1)}, f32[32,512]{1,0:T(8,128)S(1)}, u32[]{:S(2)}, u32[]{:S(2)}) collective-permute-start(f32[32,512]{1,0:T(8,128)S(1)} %get-tuple-element.44.right), channel_id=1, source_target_pairs={{0,384},{4,388},{8,392},{12,396},{16,400},{20,404},{24,408},{28,41... | collective-permute-start | bytes 196616 | tf_op jit(solution)/shard_map/ppermute | solution.py:48
  175.7 19.9 %copy-start.2 = (f32[21,128,128]{2,1,0:T(8,128)S(1)}, f32[21,128,128]{2,1,0:T(8,128)}, u32[]{:S(2)}) copy-start(f32[21,128,128]{2,1,0:T(8,128)} %blocks.3) | copy-start | bytes 4128772
  175.7 19.9 %copy-start.8 = (f32[7,128,128]{2,1,0:T(8,128)S(1)}, f32[7,128,128]{2,1,0:T(8,128)}, u32[]{:S(2)}) copy-start(f32[7,128,128]{2,1,0:T(8,128)} %inverse.3) | copy-start | bytes 1376260
  175.7 19.9 %copy-start.10 = (f32[896,128]{1,0:T(8,128)S(1)}, f32[896,128]{1,0:T(8,128)}, u32[]{:S(2)}) copy-start(f32[896,128]{1,0:T(8,128)} %copy-done.9) | copy-start | bytes 1376260
  175.7 19.9 %copy-start.18 = (s32[1,21]{1,0:T(1,128)S(1)}, s32[1,21]{1,0:T(1,128)}, u32[]{:S(2)}) copy-start(s32[1,21]{1,0:T(1,128)} %pattern.3) | copy-start | bytes 256
  179.3 16.3 %copy-start.4 = (f32[512,512]{1,0:T(8,128)S(1)}, f32[512,512]{1,0:T(8,128)}, u32[]{:S(2)}) copy-start(f32[512,512]{1,0:T(8,128)} %coupling.3) | copy-start | bytes 3145732
  179.3 10.4 %collective-permute-start.18 = (f32[32,2048]{1,0:T(8,128)S(1)}, f32[32,2048]{1,0:T(8,128)S(1)}, u32[]{:S(2)}, u32[]{:S(2)}) collective-permute-start(f32[32,2048]{1,0:T(8,128)S(1)} %shard_map.99), channel_id=1, source_target_pairs={{0,8},{4,12},{8,0},{12,4},{16,24},{20,28},{24,16},{28,20},{32,40},... | collective-permute-start | bytes 786440 | tf_op jit(solution)/shard_map/ppermute | solution.py:48
  189.8 5.9 %collective-permute-start.19 = (f32[2,32,2048]{2,1,0:T(8,128)S(1)}, f32[2,32,2048]{2,1,0:T(8,128)S(1)}, u32[]{:S(2)}, u32[]{:S(2)}) collective-permute-start(f32[2,32,2048]{2,1,0:T(8,128)S(1)} %pad_maximum_fusion.2.near), channel_id=1, source_target_pairs={{0,4},{4,0},{8,12},{12,8},{16,20},{20,16},{24,28},{28,24},{32,36},... | collective-permute-start | bytes 1572872 | tf_op jit(solution)/shard_map/ppermute | solution.py:48
  (10 other events, 9.9 us)
Sparse Core Ops, SparseCore 0:
  103.4 36.8 all-gather.2

commit v7 on v6

--- a/solution.py
+++ b/solution.py
@@ -233,7 +233,7 @@
         return lax.all_to_all(jnp.broadcast_to(value[None], (count, *value.shape)), "col", 0, 0, tiled=True)
 
     tie = lax.optimization_barrier
-    halves_z, wrap_z, wrap_y = 1 << Z4, (1 << Z8) | (1 << Z4) | (1 << Z2), (1 << Y2) | (1 << Y1)
+    halves_z, wrap_z, wrap_y = 1 << Z4, (1 << Z8) | (1 << Z4), (1 << Y2) | (1 << Y1)
     near = [[g * 4 + m for m in range(4)] for g in range(leaves // 4)]
     plane = lax.axis_index("col").astype(jnp.int32)[None]
 
@@ -251,30 +251,30 @@
         [leaf_rhs.shape, (columns, LEVELS * width)],
         where, leaf_pattern, leaf_rhs, leaf_inverse, leaf_blocks, leaf_coupling, sep_rhs,
     )
-    t, first, far = tie((t, first, far))
+    t, first, far, second = tie((t, first, far, both(1)))
 
     t = lax.all_to_all(t, "leaf", 0, 0, axis_index_groups=near, tiled=True)
+    far = grow(jnp.concatenate([far, both(2)], 0), 1 << Y1)
+    second = grow(second, halves_z)
     first = turned_planes(first)
-    far = grow(jnp.concatenate([far, both(2)], 0), 1 << Y1)
     far = grow(far, wrap_z)
-    t, first, far = tie((t, first, far))
+    second = grow(second, 1 << Z2)
+    t, first, far, second = tie((t, first, far, second))
 
     first = (first, across(first, CORE_MASK))
-    far = grow(jnp.concatenate([far, both(1)], 0), halves_z)
+    second = grow(second, 1 << Z1)
+    far = grow(far, halves_z)
     z1, v = solve(0, True, 3, t, *first)
-    v, far = tie((v, far))
     v_far = across(v, 1 << Z2)
-
-    far = grow(far, 1 << Z2)
+    v, v_far, second, far = tie((v, v_far, second, far))
+
+    second = planes(second)
     v = v + v_far
     v_far = across(v, halves_z)
-    far = grow(far, 1 << Z1)
-    far, v = tie((far, v))
-
-    second = planes(far[3:])
-    third = lax.all_gather(far[:3], "col", axis=0)
-    second, v, v_far = tie((second, v, v_far))
-
+    far = grow(grow(far, 1 << Z2), 1 << Z1)
+    far, second, v, v_far = tie((far, second, v, v_far))
+
+    third = lax.all_gather(far, "col", axis=0)
     second = (second, across(second, CORE_MASK))
     z2, v = solve(0, False, 2, v, v_far, *second)
     v = v + across(v, wrap_z)

time: 208 us -> 217 us (1.043)
  waiting for transfers between devices: 43.6 us -> 68.4 us
  starting transfers between devices: 117 us -> 96.9 us
  other arithmetic: 0.29 us -> 5.34 us
    ppermute x20 -> x23, starting transfers between devices: 107 us -> 87.6 us  [swap(): lax.ppermute(value, axis, [(i, i ^ mask) for i in range(lax.axis_size(axi...]
    ppermute x20 -> x23, waiting for transfers between devices: 42.6 us -> 57 us  [swap(): lax.ppermute(value, axis, [(i, i ^ mask) for i in range(lax.axis_size(axi...]
    all_gather x1, waiting for transfers between devices: 0.02 us -> 11.4 us  [shards(): third = lax.all_gather(far, 'col', axis=0)]
    concatenate x7 -> x10, other arithmetic: 0.12 us -> 4.23 us  [grow(): return jnp.concatenate([value, across(value, mask)], axis=1)]
    unnamed x38 -> x44, local copies, waits for them, and re-layouts: 9.95 us -> 9.97 us
  transfers between devices with their start and end apart: 23 -> 26, of which waited for: 12 -> 11; matrix products, arithmetic and copies ran while one was open for 2% -> 4% of each run, Pallas kernels for 3% -> 3%
where the time goes in v7:
time: 217 us; the launch traced here: 216 us
  starting transfers between devices  96.9 us (45%)
  waiting for transfers between devices  68.4 us (32%)
  Pallas kernels  15.9 us (7%)
  local copies, waits for them, and re-layouts  14.8 us (7%)
  between operations  14.5 us (7%)
  other arithmetic  5.34 us (2%)
    ppermute x23, starting transfers between devices, swap(): lax.ppermute(value, axis, [(i, i ^ mask) for i in range(lax.axis_size(axi...  87.6 us
    ppermute x23, waiting for transfers between devices, swap(): lax.ppermute(value, axis, [(i, i ^ mask) for i in range(lax.axis_size(axi...  57 us
    pallas_call x6, Pallas kernels, call(): pl.pallas_call(kernel, out_shape=[jax.ShapeDtypeStruct(s, F32) for s in o...  15.9 us
    all_gather x1, waiting for transfers between devices, shards(): third = lax.all_gather(far, 'col', axis=0)  11.4 us
    unnamed x44, local copies, waits for them, and re-layouts  9.97 us
    all_to_all x1, starting transfers between devices, shards(): t = lax.all_to_all(t, 'leaf', 0, 0, axis_index_groups=near, tiled=True)  5.19 us
  transfers between devices with their start and end apart: 26, of which 11 were waited for; matrix products, arithmetic and copies ran while one was open for 4% of the time, Pallas kernels for 3%

profile of v7, /device:TPU:1, one launch (start us, length us, event | category | flops | bytes accessed | tf_op | source)
XLA Modules:
  0.0 215.8 jit_solution(9854052298278460618)
XLA Ops:
  7.9 5.5 %collective-permute-start.1 = (f32[1,4,128]{2,1,0:T(4,128)S(1)}, f32[1,4,128]{2,1,0:T(4,128)S(1)}, u32[]{:S(2)}, u32[]{:S(2)}) collective-permute-start(f32[1,4,128]{2,1,0:T(4,128)S(1)} %slice_bitcast_fusion.6), channel_id=1, source_target_pairs={{0,384},{4,388},{8,392},{12,396},{16,400},{20,404},{24,408},{28,41... | collective-permute-start | bytes 6152 | tf_op jit(solution)/shard_map/ppermute | solution.py:48
  14.2 3.5 %collective-permute-start = (f32[2,128,128]{2,1,0:T(8,128)S(1)}, f32[2,128,128]{2,1,0:T(8,128)S(1)}, u32[]{:S(2)}, u32[]{:S(2)}) collective-permute-start(f32[2,128,128]{2,1,0:T(8,128)S(1)} %pad_maximum_fusion.6), channel_id=1, source_target_pairs={{0,8},{4,12},{8,0},{12,4},{16,24},{20,28},{24,16},{28,20},{32,40},... | collective-permute-start | bytes 393224 | tf_op jit(solution)/shard_map/ppermute | solution.py:48
  24.8 4.8 %shard_map.95 = (f32[896,128]{1,0:T(8,128)S(1)}, f32[128,2048]{1,0:T(8,128)}) custom-call(s32[5]{0:T(128)S(1)} %stack.71.where, s32[1,21]{1,0:T(1,128)S(1)} %copy-done.17, f32[896,128]{1,0:T(8,128)S(1)} %copy-done.11, f32[7,128,128]{2,1,0:T(8,128)S(1)} %copy-done.7, f32[21,128,128]{2,1,0:T(8,128)S(1)} %copy-done.1, f32[512,512]{1,0:T(8,128)S(1)} %copy-done.3, ...), custom_call_target="tpu_custom_call" | custom-call | tf_op jit(solution)/shard_map/pallas_call | solution.py:206
  30.4 5.2 %all-to-all-start = ((f32[4,32,2048]{2,1,0:T(8,128)}), f32[4,32,2048]{2,1,0:T(8,128)S(1)}, u32[]{:S(2)}, u32[]{:S(2)}) async-start(f32[4,32,2048]{2,1,0:T(8,128)} %bitcast.11), calls=%async_computation | async-start | bytes 2097152 | tf_op jit(solution)/shard_map/all_to_all | solution.py:256
  38.9 3.9 %collective-permute-start.4 = (f32[2,256,128]{2,1,0:T(8,128)S(1)}, f32[2,256,128]{2,1,0:T(8,128)S(1)}, u32[]{:S(2)}, u32[]{:S(2)}) collective-permute-start(f32[2,256,128]{2,1,0:T(8,128)S(1)} %pad_maximum_fusion.3), channel_id=1, source_target_pairs={{0,3},{1,2},{2,1},{3,0},{4,7},{5,6},{6,5},{7,4},{8,11},{9,10},{10,... | collective-permute-start | bytes 786440 | tf_op jit(solution)/shard_map/ppermute | solution.py:48
  42.8 2.4 %collective-permute-start.3 = (f32[2,256,128]{2,1,0:T(8,128)S(1)}, f32[2,256,128]{2,1,0:T(8,128)S(1)}, u32[]{:S(2)}, u32[]{:S(2)}) collective-permute-start(f32[2,256,128]{2,1,0:T(8,128)S(1)} %pad_maximum_fusion.3), channel_id=1, source_target_pairs={{0,2},{1,3},{2,0},{3,1},{4,6},{5,7},{6,4},{7,5},{8,10},{9,11},{10,... | collective-permute-start | bytes 786440 | tf_op jit(solution)/shard_map/ppermute | solution.py:48
  45.3 2.6 %collective-permute-start.2 = (f32[2,256,128]{2,1,0:T(8,128)S(1)}, f32[2,256,128]{2,1,0:T(8,128)S(1)}, u32[]{:S(2)}, u32[]{:S(2)}) collective-permute-start(f32[2,256,128]{2,1,0:T(8,128)S(1)} %pad_maximum_fusion.3), channel_id=1, source_target_pairs={{0,1},{1,0},{2,3},{3,2},{4,5},{5,4},{6,7},{7,6},{8,9},{9,8},{10,11... | collective-permute-start | bytes 786440 | tf_op jit(solution)/shard_map/ppermute | solution.py:48
  47.9 8.4 %collective-permute-start.7 = (f32[2,32,128]{2,1,0:T(8,128)S(1)}, f32[2,32,128]{2,1,0:T(8,128)S(1)}, u32[]{:S(2)}, u32[]{:S(2)}) collective-permute-start(f32[2,32,128]{2,1,0:T(8,128)S(1)} %pad_maximum_fusion.11), channel_id=1, source_target_pairs={{0,32},{4,36},{8,40},{12,44},{16,48},{20,52},{24,56},{28,60},{32,0... | collective-permute-start | bytes 98312 | tf_op jit(solution)/shard_map/ppermute | solution.py:48
  56.3 7.9 %collective-permute-start.6 = (f32[3,16,128]{2,1,0:T(8,128)S(1)}, f32[3,16,128]{2,1,0:T(8,128)S(1)}, u32[]{:S(2)}, u32[]{:S(2)}) collective-permute-start(f32[3,16,128]{2,1,0:T(8,128)S(1)} %pad_maximum_fusion.12), channel_id=1, source_target_pairs={{0,96},{4,100},{8,104},{12,108},{16,112},{20,116},{24,120},{28,124... | collective-permute-start | bytes 73736 | tf_op jit(solution)/shard_map/ppermute | solution.py:48
  64.2 3.1 %collective-permute-start.8 = (f32[2,64,128]{2,1,0:T(8,128)S(1)}, f32[2,64,128]{2,1,0:T(8,128)S(1)}, u32[]{:S(2)}, u32[]{:S(2)}) collective-permute-start(f32[2,64,128]{2,1,0:T(8,128)S(1)} %pad_maximum_fusion.9), channel_id=1, source_target_pairs={{0,16},{4,20},{8,24},{12,28},{16,0},{20,4},{24,8},{28,12},{32,48},... | collective-permute-start | bytes 196616 | tf_op jit(solution)/shard_map/ppermute | solution.py:48
  67.4 3.0 %collective-permute-done.8 = f32[2,64,128]{2,1,0:T(8,128)S(1)} collective-permute-done((f32[2,64,128]{2,1,0:T(8,128)S(1)}, f32[2,64,128]{2,1,0:T(8,128)S(1)}, u32[]{:S(2)}, u32[]{:S(2)}) %collective-permute-start.8) | collective-permute-done | bytes 65568 | tf_op jit(solution)/shard_map/ppermute | solution.py:48
  71.2 4.4 %collective-permute-start.9 = (f32[4,2,256,128]{3,2,1,0:T(8,128)S(1)}, f32[4,2,256,128]{3,2,1,0:T(8,128)S(1)}, u32[]{:S(2)}, u32[]{:S(2)}) collective-permute-start(f32[4,2,256,128]{3,2,1,0:T(8,128)S(1)} %pad_maximum_fusion.refs_1_.m1), channel_id=1, source_target_pairs={{0,4},{4,0},{8,12},{12,8},{16,20},{20,16},{24,28},{28,24},{32,36},... | collective-permute-start | bytes 3145736 | tf_op jit(solution)/shard_map/ppermute | solution.py:48
  75.5 4.0 %collective-permute-start.12 = (f32[3,32,128]{2,1,0:T(8,128)S(1)}, f32[3,32,128]{2,1,0:T(8,128)}, u32[]{:S(2)}, u32[]{:S(2)}) collective-permute-start(f32[3,32,128]{2,1,0:T(8,128)S(1)} %pad_maximum_fusion.10), channel_id=1, source_target_pairs={{0,32},{4,36},{8,40},{12,44},{16,48},{20,52},{24,56},{28,60},{32,0... | collective-permute-start | bytes 147464 | tf_op jit(solution)/shard_map/ppermute | solution.py:48
  79.5 3.6 %collective-permute-start.11 = (f32[2,128,128]{2,1,0:T(8,128)}, f32[2,128,128]{2,1,0:T(8,128)}, u32[]{:S(2)}, u32[]{:S(2)}) collective-permute-start(f32[2,128,128]{2,1,0:T(8,128)} %pad_maximum_fusion.7), channel_id=1, source_target_pairs={{0,8},{4,12},{8,0},{12,4},{16,24},{20,28},{24,16},{28,20},{32,40},... | collective-permute-start | bytes 393224 | tf_op jit(solution)/shard_map/ppermute | solution.py:48
  84.2 3.3 %collective-permute-start.10 = (f32[32,1536]{1,0:T(8,128)S(1)}, f32[32,1536]{1,0:T(8,128)S(1)}, u32[]{:S(2)}, u32[]{:S(2)}) collective-permute-start(f32[32,1536]{1,0:T(8,128)S(1)} %get-tuple-element.41), channel_id=1, source_target_pairs={{0,16},{4,20},{8,24},{12,28},{16,0},{20,4},{24,8},{28,12},{32,48},... | collective-permute-start | bytes 589832 | tf_op jit(solution)/shard_map/ppermute | solution.py:48
  89.4 8.3 %collective-permute-done.10 = f32[32,1536]{1,0:T(8,128)S(1)} collective-permute-done((f32[32,1536]{1,0:T(8,128)S(1)}, f32[32,1536]{1,0:T(8,128)S(1)}, u32[]{:S(2)}, u32[]{:S(2)}) %collective-permute-start.10) | collective-permute-done | bytes 196640 | tf_op jit(solution)/shard_map/ppermute | solution.py:48
  98.8 4.0 %all-to-all-start.1 = ((f32[4,2,256,128]{3,2,1,0:T(8,128)}), f32[4,2,256,128]{3,2,1,0:T(8,128)S(1)}, u32[]{:S(2)}, u32[]{:S(2)}) async-start(f32[4,2,256,128]{3,2,1,0:T(8,128)} %broadcast_in_dim.14), calls=%async_computation.1 | async-start | bytes 2097152 | tf_op jit(solution)/shard_map/all_to_all | solution.py:233
  104.7 6.2 %collective-permute-done.13 = f32[3,64,128]{2,1,0:T(8,128)S(1)} collective-permute-done((f32[3,64,128]{2,1,0:T(8,128)S(1)}, f32[3,64,128]{2,1,0:T(8,128)S(1)}, u32[]{:S(2)}, u32[]{:S(2)}) %collective-permute-start.13) | collective-permute-done | bytes 98336 | tf_op jit(solution)/shard_map/ppermute | solution.py:48
  113.8 5.6 %collective-permute-start.15 = (f32[32,1536]{1,0:T(8,128)S(1)}, f32[32,1536]{1,0:T(8,128)S(1)}, u32[]{:S(2)}, u32[]{:S(2)}) collective-permute-start(f32[32,1536]{1,0:T(8,128)S(1)} %add.24.refs_0_), channel_id=1, source_target_pairs={{0,32},{4,36},{8,40},{12,44},{16,48},{20,52},{24,56},{28,60},{32,0... | collective-permute-start | bytes 589832 | tf_op jit(solution)/shard_map/ppermute | solution.py:48
  121.1 16.8 %collective-permute-done.15.refs_1_ = f32[32,1536]{1,0:T(8,128)S(1)} collective-permute-done((f32[32,1536]{1,0:T(8,128)S(1)}, f32[32,1536]{1,0:T(8,128)S(1)}, u32[]{:S(2)}, u32[]{:S(2)}) %collective-permute-start.15) | collective-permute-done | bytes 196640 | tf_op jit(solution)/shard_map/ppermute | solution.py:48
  137.9 3.6 %collective-permute-start.16 = (f32[4,2,256,128]{3,2,1,0:T(8,128)S(1)}, f32[4,2,256,128]{3,2,1,0:T(8,128)S(1)}, u32[]{:S(2)}, u32[]{:S(2)}) collective-permute-start(f32[4,2,256,128]{3,2,1,0:T(8,128)S(1)} %all-to-all-done.1.refs_2_.m2), channel_id=1, source_target_pairs={{0,4},{4,0},{8,12},{12,8},{16,20},{20,16},{24,28},{28,24},{32,36},... | collective-permute-start | bytes 3145736 | tf_op jit(solution)/shard_map/ppermute | solution.py:48
  148.3 8.6 %collective-permute-done.17 = f32[32,1024]{1,0:T(8,128)S(1)} collective-permute-done((f32[32,1024]{1,0:T(8,128)S(1)}, f32[32,1024]{1,0:T(8,128)S(1)}, u32[]{:S(2)}, u32[]{:S(2)}) %collective-permute-start.17) | collective-permute-done | bytes 131104 | tf_op jit(solution)/shard_map/ppermute | solution.py:48
  156.9 11.4 %all-gather.3.cloned.1.call-done = f32[12,256,128]{2,1,0:T(8,128)} async-done(((f32[3,256,128]{2,1,0:T(8,128)}), f32[12,256,128]{2,1,0:T(8,128)}) %all-gather.3.cloned.1.call-update) | async-done | bytes 1572880 | tf_op jit(solution)/shard_map/all_gather | solution.py:277
  168.3 2.6 %collective-permute-start.19 = (f32[4,3,256,128]{3,2,1,0:T(8,128)}, f32[4,3,256,128]{3,2,1,0:T(8,128)S(1)}, u32[]{:S(2)}, u32[]{:S(2)}) collective-permute-start(f32[4,3,256,128]{3,2,1,0:T(8,128)} %bitcast.29), channel_id=1, source_target_pairs={{0,4},{4,0},{8,12},{12,8},{16,20},{20,16},{24,28},{28,24},{32,36},... | collective-permute-start | bytes 4718600 | tf_op jit(solution)/shard_map/ppermute | solution.py:48
  170.8 3.1 %collective-permute-start.18 = (f32[32,1024]{1,0:T(8,128)S(1)}, f32[32,1024]{1,0:T(8,128)S(1)}, u32[]{:S(2)}, u32[]{:S(2)}) collective-permute-start(f32[32,1024]{1,0:T(8,128)S(1)} %add.25.refs_0_), channel_id=1, source_target_pairs={{0,128},{4,132},{8,136},{12,140},{16,144},{20,148},{24,152},{28,15... | collective-permute-start | bytes 393224 | tf_op jit(solution)/shard_map/ppermute | solution.py:48
  174.0 3.9 %collective-permute-done.18.refs_1_ = f32[32,1024]{1,0:T(8,128)S(1)} collective-permute-done((f32[32,1024]{1,0:T(8,128)S(1)}, f32[32,1024]{1,0:T(8,128)S(1)}, u32[]{:S(2)}, u32[]{:S(2)}) %collective-permute-start.18) | collective-permute-done | bytes 131104 | tf_op jit(solution)/shard_map/ppermute | solution.py:48
  180.2 4.4 %collective-permute-start.20 = (f32[32,512]{1,0:T(8,128)S(1)}, f32[32,512]{1,0:T(8,128)S(1)}, u32[]{:S(2)}, u32[]{:S(2)}) collective-permute-start(f32[32,512]{1,0:T(8,128)S(1)} %get-tuple-element.50.right), channel_id=1, source_target_pairs={{0,384},{4,388},{8,392},{12,396},{16,400},{20,404},{24,408},{28,41... | collective-permute-start | bytes 196616 | tf_op jit(solution)/shard_map/ppermute | solution.py:48
  186.5 3.5 %shard_map.99 = f32[32,2048]{1,0:T(8,128)S(1)} custom-call(s32[1]{0:T(128)} %bitcast.5.plane, f32[32,512]{1,0:T(8,128)S(1)} %get-tuple-element.50.right, f32[32,512]{1,0:T(8,128)S(1)} %collective-permute-done.20.right_far, f32[32,512]{1,0:T(8,128)S(1)} %copy-done.14, f32[32,512]{1,0:T(8,128)S(1)} %copy-done.16, f32[32,512]{1,0:T(8,128)S(1)} %get-tuple-element.53.z3, ...), custom_call_target="tpu_custom_call" | custom-call | tf_op jit(solution)/shard_map/pallas_call | solution.py:206
  190.1 3.3 %collective-permute-start.21 = (f32[32,2048]{1,0:T(8,128)S(1)}, f32[32,2048]{1,0:T(8,128)S(1)}, u32[]{:S(2)}, u32[]{:S(2)}) collective-permute-start(f32[32,2048]{1,0:T(8,128)S(1)} %shard_map.99), channel_id=1, source_target_pairs={{0,8},{4,12},{8,0},{12,4},{16,24},{20,28},{24,16},{28,20},{32,40},... | collective-permute-start | bytes 786440 | tf_op jit(solution)/shard_map/ppermute | solution.py:48
  193.4 4.6 %collective-permute-done.21 = f32[32,2048]{1,0:T(8,128)S(1)} collective-permute-done((f32[32,2048]{1,0:T(8,128)S(1)}, f32[32,2048]{1,0:T(8,128)S(1)}, u32[]{:S(2)}, u32[]{:S(2)}) %collective-permute-start.21) | collective-permute-done | bytes 262176 | tf_op jit(solution)/shard_map/ppermute | solution.py:48
  198.0 4.8 %collective-permute-start.22 = (f32[2,32,2048]{2,1,0:T(8,128)S(1)}, f32[2,32,2048]{2,1,0:T(8,128)S(1)}, u32[]{:S(2)}, u32[]{:S(2)}) collective-permute-start(f32[2,32,2048]{2,1,0:T(8,128)S(1)} %pad_maximum_fusion.1.near), channel_id=1, source_target_pairs={{0,4},{4,0},{8,12},{12,8},{16,20},{20,16},{24,28},{28,24},{32,36},... | collective-permute-start | bytes 1572872 | tf_op jit(solution)/shard_map/ppermute | solution.py:48
  204.3 4.7 %shard_map.100 = (f32[896,128]{1,0:T(8,128)}, f32[172,128]{1,0:T(8,128)}) custom-call(s32[5]{0:T(128)S(1)} %stack.71.where, s32[1,21]{1,0:T(1,128)S(1)} %copy-done.18, f32[896,128]{1,0:T(8,128)S(1)} %copy-done.10, f32[2,32,2048]{2,1,0:T(8,128)S(1)} %pad_maximum_fusion.1.near, f32[2,32,2048]{2,1,0:T(8,128)S(1)} %collective-permute-done.22.across_core, ...), custom_call_target="tpu_custom_call" | custom-call | tf_op jit(solution)/shard_map/pallas_call | solution.py:206
  (95 shorter events, 36.4 us)
Async XLA Ops:
  7.9 22.5 %collective-permute-start.1 = (f32[1,4,128]{2,1,0:T(4,128)S(1)}, f32[1,4,128]{2,1,0:T(4,128)S(1)}, u32[]{:S(2)}, u32[]{:S(2)}) collective-permute-start(f32[1,4,128]{2,1,0:T(4,128)S(1)} %slice_bitcast_fusion.6), channel_id=1, source_target_pairs={{0,384},{4,388},{8,392},{12,396},{16,400},{20,404},{24,408},{28,41... | collective-permute-start | bytes 6152 | tf_op jit(solution)/shard_map/ppermute | solution.py:48
  14.2 16.1 %collective-permute-start = (f32[2,128,128]{2,1,0:T(8,128)S(1)}, f32[2,128,128]{2,1,0:T(8,128)S(1)}, u32[]{:S(2)}, u32[]{:S(2)}) collective-permute-start(f32[2,128,128]{2,1,0:T(8,128)S(1)} %pad_maximum_fusion.6), channel_id=1, source_target_pairs={{0,8},{4,12},{8,0},{12,4},{16,24},{20,28},{24,16},{28,20},{32,40},... | collective-permute-start | bytes 393224 | tf_op jit(solution)/shard_map/ppermute | solution.py:48
  30.4 40.8 %all-to-all-start = ((f32[4,32,2048]{2,1,0:T(8,128)}), f32[4,32,2048]{2,1,0:T(8,128)S(1)}, u32[]{:S(2)}, u32[]{:S(2)}) async-start(f32[4,32,2048]{2,1,0:T(8,128)} %bitcast.11), calls=%async_computation | async-start | bytes 2097152 | tf_op jit(solution)/shard_map/all_to_all | solution.py:256
  37.0 19.3 %collective-permute-start.5 = (f32[3,8,128]{2,1,0:T(8,128)S(1)}, f32[3,8,128]{2,1,0:T(8,128)S(1)}, u32[]{:S(2)}, u32[]{:S(2)}) collective-permute-start(f32[3,8,128]{2,1,0:T(8,128)S(1)} %pad_maximum_fusion.13), channel_id=1, source_target_pairs={{0,128},{4,132},{8,136},{12,140},{16,144},{20,148},{24,152},{28,15... | collective-permute-start | bytes 36872 | tf_op jit(solution)/shard_map/ppermute | solution.py:48
  38.9 32.2 %collective-permute-start.4 = (f32[2,256,128]{2,1,0:T(8,128)S(1)}, f32[2,256,128]{2,1,0:T(8,128)S(1)}, u32[]{:S(2)}, u32[]{:S(2)}) collective-permute-start(f32[2,256,128]{2,1,0:T(8,128)S(1)} %pad_maximum_fusion.3), channel_id=1, source_target_pairs={{0,3},{1,2},{2,1},{3,0},{4,7},{5,6},{6,5},{7,4},{8,11},{9,10},{10,... | collective-permute-start | bytes 786440 | tf_op jit(solution)/shard_map/ppermute | solution.py:48
  42.8 28.3 %collective-permute-start.3 = (f32[2,256,128]{2,1,0:T(8,128)S(1)}, f32[2,256,128]{2,1,0:T(8,128)S(1)}, u32[]{:S(2)}, u32[]{:S(2)}) collective-permute-start(f32[2,256,128]{2,1,0:T(8,128)S(1)} %pad_maximum_fusion.3), channel_id=1, source_target_pairs={{0,2},{1,3},{2,0},{3,1},{4,6},{5,7},{6,4},{7,5},{8,10},{9,11},{10,... | collective-permute-start | bytes 786440 | tf_op jit(solution)/shard_map/ppermute | solution.py:48
  45.3 25.8 %collective-permute-start.2 = (f32[2,256,128]{2,1,0:T(8,128)S(1)}, f32[2,256,128]{2,1,0:T(8,128)S(1)}, u32[]{:S(2)}, u32[]{:S(2)}) collective-permute-start(f32[2,256,128]{2,1,0:T(8,128)S(1)} %pad_maximum_fusion.3), channel_id=1, source_target_pairs={{0,1},{1,0},{2,3},{3,2},{4,5},{5,4},{6,7},{7,6},{8,9},{9,8},{10,11... | collective-permute-start | bytes 786440 | tf_op jit(solution)/shard_map/ppermute | solution.py:48
  47.9 16.3 %collective-permute-start.7 = (f32[2,32,128]{2,1,0:T(8,128)S(1)}, f32[2,32,128]{2,1,0:T(8,128)S(1)}, u32[]{:S(2)}, u32[]{:S(2)}) collective-permute-start(f32[2,32,128]{2,1,0:T(8,128)S(1)} %pad_maximum_fusion.11), channel_id=1, source_target_pairs={{0,32},{4,36},{8,40},{12,44},{16,48},{20,52},{24,56},{28,60},{32,0... | collective-permute-start | bytes 98312 | tf_op jit(solution)/shard_map/ppermute | solution.py:48
  56.3 11.1 %collective-permute-start.6 = (f32[3,16,128]{2,1,0:T(8,128)S(1)}, f32[3,16,128]{2,1,0:T(8,128)S(1)}, u32[]{:S(2)}, u32[]{:S(2)}) collective-permute-start(f32[3,16,128]{2,1,0:T(8,128)S(1)} %pad_maximum_fusion.12), channel_id=1, source_target_pairs={{0,96},{4,100},{8,104},{12,108},{16,112},{20,116},{24,120},{28,124... | collective-permute-start | bytes 73736 | tf_op jit(solution)/shard_map/ppermute | solution.py:48
  64.2 6.2 %collective-permute-start.8 = (f32[2,64,128]{2,1,0:T(8,128)S(1)}, f32[2,64,128]{2,1,0:T(8,128)S(1)}, u32[]{:S(2)}, u32[]{:S(2)}) collective-permute-start(f32[2,64,128]{2,1,0:T(8,128)S(1)} %pad_maximum_fusion.9), channel_id=1, source_target_pairs={{0,16},{4,20},{8,24},{12,28},{16,0},{20,4},{24,8},{28,12},{32,48},... | collective-permute-start | bytes 196616 | tf_op jit(solution)/shard_map/ppermute | solution.py:48
  71.2 12.0 %collective-permute-start.9 = (f32[4,2,256,128]{3,2,1,0:T(8,128)S(1)}, f32[4,2,256,128]{3,2,1,0:T(8,128)S(1)}, u32[]{:S(2)}, u32[]{:S(2)}) collective-permute-start(f32[4,2,256,128]{3,2,1,0:T(8,128)S(1)} %pad_maximum_fusion.refs_1_.m1), channel_id=1, source_target_pairs={{0,4},{4,0},{8,12},{12,8},{16,20},{20,16},{24,28},{28,24},{32,36},... | collective-permute-start | bytes 3145736 | tf_op jit(solution)/shard_map/ppermute | solution.py:48
  75.5 12.0 %collective-permute-start.12 = (f32[3,32,128]{2,1,0:T(8,128)S(1)}, f32[3,32,128]{2,1,0:T(8,128)}, u32[]{:S(2)}, u32[]{:S(2)}) collective-permute-start(f32[3,32,128]{2,1,0:T(8,128)S(1)} %pad_maximum_fusion.10), channel_id=1, source_target_pairs={{0,32},{4,36},{8,40},{12,44},{16,48},{20,52},{24,56},{28,60},{32,0... | collective-permute-start | bytes 147464 | tf_op jit(solution)/shard_map/ppermute | solution.py:48
  79.5 8.8 %collective-permute-start.11 = (f32[2,128,128]{2,1,0:T(8,128)}, f32[2,128,128]{2,1,0:T(8,128)}, u32[]{:S(2)}, u32[]{:S(2)}) collective-permute-start(f32[2,128,128]{2,1,0:T(8,128)} %pad_maximum_fusion.7), channel_id=1, source_target_pairs={{0,8},{4,12},{8,0},{12,4},{16,24},{20,28},{24,16},{28,20},{32,40},... | collective-permute-start | bytes 393224 | tf_op jit(solution)/shard_map/ppermute | solution.py:48
  84.2 13.5 %collective-permute-start.10 = (f32[32,1536]{1,0:T(8,128)S(1)}, f32[32,1536]{1,0:T(8,128)S(1)}, u32[]{:S(2)}, u32[]{:S(2)}) collective-permute-start(f32[32,1536]{1,0:T(8,128)S(1)} %get-tuple-element.41), channel_id=1, source_target_pairs={{0,16},{4,20},{8,24},{12,28},{16,0},{20,4},{24,8},{28,12},{32,48},... | collective-permute-start | bytes 589832 | tf_op jit(solution)/shard_map/ppermute | solution.py:48
  88.3 22.6 %copy-start.19 = (f32[3,64,128]{2,1,0:T(8,128)}, f32[3,64,128]{2,1,0:T(8,128)S(1)}, u32[]{:S(2)}) copy-start(f32[3,64,128]{2,1,0:T(8,128)S(1)} %pad_maximum_fusion.8) | copy-start | bytes 294916
  98.8 39.1 %all-to-all-start.1 = ((f32[4,2,256,128]{3,2,1,0:T(8,128)}), f32[4,2,256,128]{3,2,1,0:T(8,128)S(1)}, u32[]{:S(2)}, u32[]{:S(2)}) async-start(f32[4,2,256,128]{3,2,1,0:T(8,128)} %broadcast_in_dim.14), calls=%async_computation.1 | async-start | bytes 2097152 | tf_op jit(solution)/shard_map/all_to_all | solution.py:233
  102.8 65.5 %all-gather.3.cloned.1.call-start = ((), (), s32[]{:S(2)}) async-start(), calls=%async_computation.2 | async-start | bytes 1966080 | tf_op jit(solution)/shard_map/all_gather | solution.py:277
  102.8 8.1 %collective-permute-start.13 = (f32[3,64,128]{2,1,0:T(8,128)S(1)}, f32[3,64,128]{2,1,0:T(8,128)S(1)}, u32[]{:S(2)}, u32[]{:S(2)}) collective-permute-start(f32[3,64,128]{2,1,0:T(8,128)S(1)} %pad_maximum_fusion.8), channel_id=1, source_target_pairs={{0,16},{4,20},{8,24},{12,28},{16,0},{20,4},{24,8},{28,12},{32,48},... | collective-permute-start | bytes 294920 | tf_op jit(solution)/shard_map/ppermute | solution.py:48
  110.9 8.5 %collective-permute-start.14 = (f32[3,128,128]{2,1,0:T(8,128)S(1)}, f32[3,128,128]{2,1,0:T(8,128)S(1)}, u32[]{:S(2)}, u32[]{:S(2)}) collective-permute-start(f32[3,128,128]{2,1,0:T(8,128)S(1)} %pad_maximum_fusion.5), channel_id=1, source_target_pairs={{0,8},{4,12},{8,0},{12,4},{16,24},{20,28},{24,16},{28,20},{32,40},... | collective-permute-start | bytes 589832 | tf_op jit(solution)/shard_map/ppermute | solution.py:48
  113.8 24.0 %collective-permute-start.15 = (f32[32,1536]{1,0:T(8,128)S(1)}, f32[32,1536]{1,0:T(8,128)S(1)}, u32[]{:S(2)}, u32[]{:S(2)}) collective-permute-start(f32[32,1536]{1,0:T(8,128)S(1)} %add.24.refs_0_), channel_id=1, source_target_pairs={{0,32},{4,36},{8,40},{12,44},{16,48},{20,52},{24,56},{28,60},{32,0... | collective-permute-start | bytes 589832 | tf_op jit(solution)/shard_map/ppermute | solution.py:48
  137.9 5.9 %collective-permute-start.16 = (f32[4,2,256,128]{3,2,1,0:T(8,128)S(1)}, f32[4,2,256,128]{3,2,1,0:T(8,128)S(1)}, u32[]{:S(2)}, u32[]{:S(2)}) collective-permute-start(f32[4,2,256,128]{3,2,1,0:T(8,128)S(1)} %all-to-all-done.1.refs_2_.m2), channel_id=1, source_target_pairs={{0,4},{4,0},{8,12},{12,8},{16,20},{20,16},{24,28},{28,24},{32,36},... | collective-permute-start | bytes 3145736 | tf_op jit(solution)/shard_map/ppermute | solution.py:48
  146.4 10.5 %collective-permute-start.17 = (f32[32,1024]{1,0:T(8,128)S(1)}, f32[32,1024]{1,0:T(8,128)S(1)}, u32[]{:S(2)}, u32[]{:S(2)}) collective-permute-start(f32[32,1024]{1,0:T(8,128)S(1)} %get-tuple-element.46), channel_id=1, source_target_pairs={{0,96},{4,100},{8,104},{12,108},{16,112},{20,116},{24,120},{28,124... | collective-permute-start | bytes 393224 | tf_op jit(solution)/shard_map/ppermute | solution.py:48
  156.8 29.6 %copy-start.14 = (f32[32,512]{1,0:T(8,128)S(1)}, f32[32,512]{1,0:T(8,128)}, u32[]{:S(2)}) copy-start(f32[32,512]{1,0:T(8,128)} %copy-done.13) | copy-start | bytes 196612
  156.8 29.6 %copy-start.16 = (f32[32,512]{1,0:T(8,128)S(1)}, f32[32,512]{1,0:T(8,128)}, u32[]{:S(2)}) copy-start(f32[32,512]{1,0:T(8,128)} %copy-done.15) | copy-start | bytes 196612
  168.3 9.6 %collective-permute-start.19 = (f32[4,3,256,128]{3,2,1,0:T(8,128)}, f32[4,3,256,128]{3,2,1,0:T(8,128)S(1)}, u32[]{:S(2)}, u32[]{:S(2)}) collective-permute-start(f32[4,3,256,128]{3,2,1,0:T(8,128)} %bitcast.29), channel_id=1, source_target_pairs={{0,4},{4,0},{8,12},{12,8},{16,20},{20,16},{24,28},{28,24},{32,36},... | collective-permute-start | bytes 4718600 | tf_op jit(solution)/shard_map/ppermute | solution.py:48
  170.8 7.0 %collective-permute-start.18 = (f32[32,1024]{1,0:T(8,128)S(1)}, f32[32,1024]{1,0:T(8,128)S(1)}, u32[]{:S(2)}, u32[]{:S(2)}) collective-permute-start(f32[32,1024]{1,0:T(8,128)S(1)} %add.25.refs_0_), channel_id=1, source_target_pairs={{0,128},{4,132},{8,136},{12,140},{16,144},{20,148},{24,152},{28,15... | collective-permute-start | bytes 393224 | tf_op jit(solution)/shard_map/ppermute | solution.py:48
  180.2 6.2 %collective-permute-start.20 = (f32[32,512]{1,0:T(8,128)S(1)}, f32[32,512]{1,0:T(8,128)S(1)}, u32[]{:S(2)}, u32[]{:S(2)}) collective-permute-start(f32[32,512]{1,0:T(8,128)S(1)} %get-tuple-element.50.right), channel_id=1, source_target_pairs={{0,384},{4,388},{8,392},{12,396},{16,400},{20,404},{24,408},{28,41... | collective-permute-start | bytes 196616 | tf_op jit(solution)/shard_map/ppermute | solution.py:48
  186.5 17.8 %copy-start.2 = (f32[21,128,128]{2,1,0:T(8,128)S(1)}, f32[21,128,128]{2,1,0:T(8,128)}, u32[]{:S(2)}) copy-start(f32[21,128,128]{2,1,0:T(8,128)} %blocks.3) | copy-start | bytes 4128772
  186.5 17.8 %copy-start.8 = (f32[7,128,128]{2,1,0:T(8,128)S(1)}, f32[7,128,128]{2,1,0:T(8,128)}, u32[]{:S(2)}) copy-start(f32[7,128,128]{2,1,0:T(8,128)} %inverse.3) | copy-start | bytes 1376260
  186.5 17.8 %copy-start.10 = (f32[896,128]{1,0:T(8,128)S(1)}, f32[896,128]{1,0:T(8,128)}, u32[]{:S(2)}) copy-start(f32[896,128]{1,0:T(8,128)} %copy-done.9) | copy-start | bytes 1376260
  190.1 7.9 %collective-permute-start.21 = (f32[32,2048]{1,0:T(8,128)S(1)}, f32[32,2048]{1,0:T(8,128)S(1)}, u32[]{:S(2)}, u32[]{:S(2)}) collective-permute-start(f32[32,2048]{1,0:T(8,128)S(1)} %shard_map.99), channel_id=1, source_target_pairs={{0,8},{4,12},{8,0},{12,4},{16,24},{20,28},{24,16},{28,20},{32,40},... | collective-permute-start | bytes 786440 | tf_op jit(solution)/shard_map/ppermute | solution.py:48
  198.0 6.3 %collective-permute-start.22 = (f32[2,32,2048]{2,1,0:T(8,128)S(1)}, f32[2,32,2048]{2,1,0:T(8,128)S(1)}, u32[]{:S(2)}, u32[]{:S(2)}) collective-permute-start(f32[2,32,2048]{2,1,0:T(8,128)S(1)} %pad_maximum_fusion.1.near), channel_id=1, source_target_pairs={{0,4},{4,0},{8,12},{12,8},{16,20},{20,16},{24,28},{28,24},{32,36},... | collective-permute-start | bytes 1572872 | tf_op jit(solution)/shard_map/ppermute | solution.py:48
  (16 other events, 81.7 us)
Sparse Core Ops, SparseCore 0:
  138.0 30.2 all-gather.2

commit v8 on v7

--- a/solution.py
+++ b/solution.py
@@ -163,11 +163,13 @@
 def level_kernel(index, turned, plane, *refs):
     mine, other, z_out, v_out = refs[-4:]
     mats = (mine, other)
-    total = summed(refs[:-4], z_out.shape[0])
+    count, width = z_out.shape
+    more = v_out.shape[1]
+    heads = [ref for ref in refs[:-4] if ref.shape[1] in (width, width + more)]
+    rests = [ref for ref in refs[:-4] if ref.shape[1] >= more and ref.shape[1] != width]
     places = spots(0, mine.shape[0], plane[0] if turned else None)
-    width = z_out.shape[1]
-    z_out[...] = total[:, :width]
-    v_out[...] = total[:, width:]
+    z_out[...] = summed(heads, count)[:, :width]
+    v_out[...] = summed(rests, count)[:, -more:]
     z = times_rows(z_out, places, mats, index)
     z_out[...] = jnp.concatenate(z, axis=1)
     for r, place in enumerate(places):
@@ -270,13 +272,18 @@
 
     second = planes(second)
     v = v + v_far
+    v, upper = v[:, :width], v[:, width:]
     v_far = across(v, halves_z)
-    far = grow(grow(far, 1 << Z2), 1 << Z1)
-    far, second, v, v_far = tie((far, second, v, v_far))
+    far = grow(far, 1 << Z2)
+    far, upper, v_far = tie((far, upper, v_far))
+
+    upper_far = across(upper, halves_z)
+    far = grow(far, 1 << Z1)
+    far, second = tie((far, second))
 
     third = lax.all_gather(far, "col", axis=0)
     second = (second, across(second, CORE_MASK))
-    z2, v = solve(0, False, 2, v, v_far, *second)
+    z2, v = solve(0, False, 2, v, v_far, upper, upper_far, *second)
     v = v + across(v, wrap_z)
     v, third = tie((v, third))
 

time: 217 us -> 211 us (0.972)
  waiting for transfers between devices: 68.4 us -> 56.2 us
  starting transfers between devices: 96.9 us -> 103 us
    all_gather x1, waiting for transfers between devices: 11.4 us -> 0.02 us  [shards(): third = lax.all_gather(far, 'col', axis=0)]
    ppermute x23 -> x24, starting transfers between devices: 87.6 us -> 93.8 us  [swap(): lax.ppermute(value, axis, [(i, i ^ mask) for i in range(lax.axis_size(axi...]
    ppermute x23 -> x24, waiting for transfers between devices: 57 us -> 56.1 us  [swap(): lax.ppermute(value, axis, [(i, i ^ mask) for i in range(lax.axis_size(axi...]
    unnamed x44 -> x32, local copies, waits for them, and re-layouts: 9.97 us -> 9.32 us
  transfers between devices with their start and end apart: 26 -> 27, of which waited for: 11 -> 10; matrix products, arithmetic and copies ran while one was open for 4% -> 4% of each run, Pallas kernels for 3% -> 3%
where the time goes in v8:
time: 211 us; the launch traced here: 210 us
  starting transfers between devices  103 us (49%)
  waiting for transfers between devices  56.2 us (27%)
  Pallas kernels  15.9 us (8%)
  between operations  14.5 us (7%)
  local copies, waits for them, and re-layouts  14.2 us (7%)
  other arithmetic  5.9 us (3%)
    ppermute x24, starting transfers between devices, swap(): lax.ppermute(value, axis, [(i, i ^ mask) for i in range(lax.axis_size(axi...  93.8 us
    ppermute x24, waiting for transfers between devices, swap(): lax.ppermute(value, axis, [(i, i ^ mask) for i in range(lax.axis_size(axi...  56.1 us
    pallas_call x6, Pallas kernels, call(): pl.pallas_call(kernel, out_shape=[jax.ShapeDtypeStruct(s, F32) for s in o...  15.9 us
    unnamed x32, local copies, waits for them, and re-layouts  9.32 us
    all_to_all x1, starting transfers between devices, shards(): t = lax.all_to_all(t, 'leaf', 0, 0, axis_index_groups=near, tiled=True)  5.19 us
    concatenate x10, other arithmetic, grow(): return jnp.concatenate([value, across(value, mask)], axis=1)  4.79 us
  transfers between devices with their start and end apart: 27, of which 10 were waited for; matrix products, arithmetic and copies ran while one was open for 4% of the time, Pallas kernels for 3%

profile of v8, /device:TPU:1, one launch (start us, length us, event | category | flops | bytes accessed | tf_op | source)
XLA Modules:
  0.0 209.7 jit_solution(2181944112665779932)
XLA Ops:
  7.9 5.5 %collective-permute-start.1 = (f32[1,4,128]{2,1,0:T(4,128)S(1)}, f32[1,4,128]{2,1,0:T(4,128)S(1)}, u32[]{:S(2)}, u32[]{:S(2)}) collective-permute-start(f32[1,4,128]{2,1,0:T(4,128)S(1)} %slice_bitcast_fusion.6), channel_id=1, source_target_pairs={{0,384},{4,388},{8,392},{12,396},{16,400},{20,404},{24,408},{28,41... | collective-permute-start | bytes 6152 | tf_op jit(solution)/shard_map/ppermute | solution.py:48
  14.2 3.5 %collective-permute-start = (f32[2,128,128]{2,1,0:T(8,128)S(1)}, f32[2,128,128]{2,1,0:T(8,128)S(1)}, u32[]{:S(2)}, u32[]{:S(2)}) collective-permute-start(f32[2,128,128]{2,1,0:T(8,128)S(1)} %pad_maximum_fusion.6), channel_id=1, source_target_pairs={{0,8},{4,12},{8,0},{12,4},{16,24},{20,28},{24,16},{28,20},{32,40},... | collective-permute-start | bytes 393224 | tf_op jit(solution)/shard_map/ppermute | solution.py:48
  24.8 4.8 %shard_map.95 = (f32[896,128]{1,0:T(8,128)S(1)}, f32[128,2048]{1,0:T(8,128)}) custom-call(s32[5]{0:T(128)S(1)} %stack.71.where, s32[1,21]{1,0:T(1,128)S(1)} %copy-done.13, f32[896,128]{1,0:T(8,128)S(1)} %copy-done.11, f32[7,128,128]{2,1,0:T(8,128)S(1)} %copy-done.7, f32[21,128,128]{2,1,0:T(8,128)S(1)} %copy-done.1, f32[512,512]{1,0:T(8,128)S(1)} %copy-done.3, ...), custom_call_target="tpu_custom_call" | custom-call | tf_op jit(solution)/shard_map/pallas_call | solution.py:208
  30.4 5.2 %all-to-all-start = ((f32[4,32,2048]{2,1,0:T(8,128)}), f32[4,32,2048]{2,1,0:T(8,128)S(1)}, u32[]{:S(2)}, u32[]{:S(2)}) async-start(f32[4,32,2048]{2,1,0:T(8,128)} %bitcast.11), calls=%async_computation | async-start | bytes 2097152 | tf_op jit(solution)/shard_map/all_to_all | solution.py:258
  38.9 3.9 %collective-permute-start.4 = (f32[2,256,128]{2,1,0:T(8,128)S(1)}, f32[2,256,128]{2,1,0:T(8,128)S(1)}, u32[]{:S(2)}, u32[]{:S(2)}) collective-permute-start(f32[2,256,128]{2,1,0:T(8,128)S(1)} %pad_maximum_fusion.3), channel_id=1, source_target_pairs={{0,3},{1,2},{2,1},{3,0},{4,7},{5,6},{6,5},{7,4},{8,11},{9,10},{10,... | collective-permute-start | bytes 786440 | tf_op jit(solution)/shard_map/ppermute | solution.py:48
  45.2 2.6 %collective-permute-start.2 = (f32[2,256,128]{2,1,0:T(8,128)S(1)}, f32[2,256,128]{2,1,0:T(8,128)S(1)}, u32[]{:S(2)}, u32[]{:S(2)}) collective-permute-start(f32[2,256,128]{2,1,0:T(8,128)S(1)} %pad_maximum_fusion.3), channel_id=1, source_target_pairs={{0,1},{1,0},{2,3},{3,2},{4,5},{5,4},{6,7},{7,6},{8,9},{9,8},{10,11... | collective-permute-start | bytes 786440 | tf_op jit(solution)/shard_map/ppermute | solution.py:48
  47.9 8.4 %collective-permute-start.7 = (f32[2,32,128]{2,1,0:T(8,128)S(1)}, f32[2,32,128]{2,1,0:T(8,128)S(1)}, u32[]{:S(2)}, u32[]{:S(2)}) collective-permute-start(f32[2,32,128]{2,1,0:T(8,128)S(1)} %pad_maximum_fusion.11), channel_id=1, source_target_pairs={{0,32},{4,36},{8,40},{12,44},{16,48},{20,52},{24,56},{28,60},{32,0... | collective-permute-start | bytes 98312 | tf_op jit(solution)/shard_map/ppermute | solution.py:48
  56.3 7.9 %collective-permute-start.6 = (f32[3,16,128]{2,1,0:T(8,128)S(1)}, f32[3,16,128]{2,1,0:T(8,128)S(1)}, u32[]{:S(2)}, u32[]{:S(2)}) collective-permute-start(f32[3,16,128]{2,1,0:T(8,128)S(1)} %pad_maximum_fusion.12), channel_id=1, source_target_pairs={{0,96},{4,100},{8,104},{12,108},{16,112},{20,116},{24,120},{28,124... | collective-permute-start | bytes 73736 | tf_op jit(solution)/shard_map/ppermute | solution.py:48
  64.2 3.1 %collective-permute-start.8 = (f32[2,64,128]{2,1,0:T(8,128)S(1)}, f32[2,64,128]{2,1,0:T(8,128)S(1)}, u32[]{:S(2)}, u32[]{:S(2)}) collective-permute-start(f32[2,64,128]{2,1,0:T(8,128)S(1)} %pad_maximum_fusion.9), channel_id=1, source_target_pairs={{0,16},{4,20},{8,24},{12,28},{16,0},{20,4},{24,8},{28,12},{32,48},... | collective-permute-start | bytes 196616 | tf_op jit(solution)/shard_map/ppermute | solution.py:48
  70.5 4.4 %collective-permute-start.9 = (f32[4,2,256,128]{3,2,1,0:T(8,128)S(1)}, f32[4,2,256,128]{3,2,1,0:T(8,128)S(1)}, u32[]{:S(2)}, u32[]{:S(2)}) collective-permute-start(f32[4,2,256,128]{3,2,1,0:T(8,128)S(1)} %pad_maximum_fusion.refs_1_.m1), channel_id=1, source_target_pairs={{0,4},{4,0},{8,12},{12,8},{16,20},{20,16},{24,28},{28,24},{32,36},... | collective-permute-start | bytes 3145736 | tf_op jit(solution)/shard_map/ppermute | solution.py:48
  74.9 4.0 %collective-permute-start.12 = (f32[3,32,128]{2,1,0:T(8,128)}, f32[3,32,128]{2,1,0:T(8,128)}, u32[]{:S(2)}, u32[]{:S(2)}) collective-permute-start(f32[3,32,128]{2,1,0:T(8,128)} %pad_maximum_fusion.10), channel_id=1, source_target_pairs={{0,32},{4,36},{8,40},{12,44},{16,48},{20,52},{24,56},{28,60},{32,0... | collective-permute-start | bytes 147464 | tf_op jit(solution)/shard_map/ppermute | solution.py:48
  78.9 3.6 %collective-permute-start.11 = (f32[2,128,128]{2,1,0:T(8,128)S(1)}, f32[2,128,128]{2,1,0:T(8,128)}, u32[]{:S(2)}, u32[]{:S(2)}) collective-permute-start(f32[2,128,128]{2,1,0:T(8,128)S(1)} %pad_maximum_fusion.7), channel_id=1, source_target_pairs={{0,8},{4,12},{8,0},{12,4},{16,24},{20,28},{24,16},{28,20},{32,40},... | collective-permute-start | bytes 393224 | tf_op jit(solution)/shard_map/ppermute | solution.py:48
  83.5 3.3 %collective-permute-start.10 = (f32[32,1536]{1,0:T(8,128)S(1)}, f32[32,1536]{1,0:T(8,128)S(1)}, u32[]{:S(2)}, u32[]{:S(2)}) collective-permute-start(f32[32,1536]{1,0:T(8,128)S(1)} %get-tuple-element.40), channel_id=1, source_target_pairs={{0,16},{4,20},{8,24},{12,28},{16,0},{20,4},{24,8},{28,12},{32,48},... | collective-permute-start | bytes 589832 | tf_op jit(solution)/shard_map/ppermute | solution.py:48
  89.3 7.5 %collective-permute-done.10 = f32[32,1536]{1,0:T(8,128)S(1)} collective-permute-done((f32[32,1536]{1,0:T(8,128)S(1)}, f32[32,1536]{1,0:T(8,128)S(1)}, u32[]{:S(2)}, u32[]{:S(2)}) %collective-permute-start.10) | collective-permute-done | bytes 196640 | tf_op jit(solution)/shard_map/ppermute | solution.py:48
  97.9 4.0 %all-to-all-start.1 = ((f32[4,2,256,128]{3,2,1,0:T(8,128)}), f32[4,2,256,128]{3,2,1,0:T(8,128)S(1)}, u32[]{:S(2)}, u32[]{:S(2)}) async-start(f32[4,2,256,128]{3,2,1,0:T(8,128)} %broadcast_in_dim.14), calls=%async_computation.1 | async-start | bytes 2097152 | tf_op jit(solution)/shard_map/all_to_all | solution.py:235
  104.8 5.4 %collective-permute-start.14 = (f32[32,512]{1,0:T(8,128)S(1)}, f32[32,512]{1,0:T(8,128)S(1)}, u32[]{:S(2)}, u32[]{:S(2)}) collective-permute-start(f32[32,512]{1,0:T(8,128)S(1)} %slice.36.refs_0_), channel_id=1, source_target_pairs={{0,32},{4,36},{8,40},{12,44},{16,48},{20,52},{24,56},{28,60},{32,0... | collective-permute-start | bytes 196616 | tf_op jit(solution)/shard_map/ppermute | solution.py:48
  111.2 2.5 %collective-permute-done.14.refs_1_ = f32[32,512]{1,0:T(8,128)S(1)} collective-permute-done((f32[32,512]{1,0:T(8,128)S(1)}, f32[32,512]{1,0:T(8,128)S(1)}, u32[]{:S(2)}, u32[]{:S(2)}) %collective-permute-start.14) | collective-permute-done | bytes 65568 | tf_op jit(solution)/shard_map/ppermute | solution.py:48
  113.8 3.7 %collective-permute-start.16 = (f32[3,128,128]{2,1,0:T(8,128)S(1)}, f32[3,128,128]{2,1,0:T(8,128)S(1)}, u32[]{:S(2)}, u32[]{:S(2)}) collective-permute-start(f32[3,128,128]{2,1,0:T(8,128)S(1)} %pad_maximum_fusion.5), channel_id=1, source_target_pairs={{0,8},{4,12},{8,0},{12,4},{16,24},{20,28},{24,16},{28,20},{32,40},... | collective-permute-start | bytes 589832 | tf_op jit(solution)/shard_map/ppermute | solution.py:48
  117.4 3.4 %collective-permute-done.16 = f32[3,128,128]{2,1,0:T(8,128)S(1)} collective-permute-done((f32[3,128,128]{2,1,0:T(8,128)S(1)}, f32[3,128,128]{2,1,0:T(8,128)S(1)}, u32[]{:S(2)}, u32[]{:S(2)}) %collective-permute-start.16) | collective-permute-done | bytes 196640 | tf_op jit(solution)/shard_map/ppermute | solution.py:48
  121.6 8.1 %collective-permute-start.17 = (f32[4,2,256,128]{3,2,1,0:T(8,128)S(1)}, f32[4,2,256,128]{3,2,1,0:T(8,128)S(1)}, u32[]{:S(2)}, u32[]{:S(2)}) collective-permute-start(f32[4,2,256,128]{3,2,1,0:T(8,128)S(1)} %all-to-all-done.1.refs_4_.m2), channel_id=1, source_target_pairs={{0,4},{4,0},{8,12},{12,8},{16,20},{20,16},{24,28},{28,24},{32,36},... | collective-permute-start | bytes 3145736 | tf_op jit(solution)/shard_map/ppermute | solution.py:48
  129.7 2.6 %collective-permute-start.15 = (f32[32,1024]{1,0:T(8,128)S(1)}, f32[32,1024]{1,0:T(8,128)S(1)}, u32[]{:S(2)}, u32[]{:S(2)}) collective-permute-start(f32[32,1024]{1,0:T(8,128)S(1)} %slice.37.refs_2_), channel_id=1, source_target_pairs={{0,32},{4,36},{8,40},{12,44},{16,48},{20,52},{24,56},{28,60},{32,0... | collective-permute-start | bytes 393224 | tf_op jit(solution)/shard_map/ppermute | solution.py:48
  132.3 16.5 %collective-permute-done.15.refs_3_ = f32[32,1024]{1,0:T(8,128)S(1)} collective-permute-done((f32[32,1024]{1,0:T(8,128)S(1)}, f32[32,1024]{1,0:T(8,128)S(1)}, u32[]{:S(2)}, u32[]{:S(2)}) %collective-permute-start.15) | collective-permute-done | bytes 131104 | tf_op jit(solution)/shard_map/ppermute | solution.py:48
  152.7 8.7 %collective-permute-done.18 = f32[32,1024]{1,0:T(8,128)S(1)} collective-permute-done((f32[32,1024]{1,0:T(8,128)S(1)}, f32[32,1024]{1,0:T(8,128)S(1)}, u32[]{:S(2)}, u32[]{:S(2)}) %collective-permute-start.18) | collective-permute-done | bytes 131104 | tf_op jit(solution)/shard_map/ppermute | solution.py:48
  161.5 3.0 %collective-permute-start.20 = (f32[4,3,256,128]{3,2,1,0:T(8,128)}, f32[4,3,256,128]{3,2,1,0:T(8,128)S(1)}, u32[]{:S(2)}, u32[]{:S(2)}) collective-permute-start(f32[4,3,256,128]{3,2,1,0:T(8,128)} %bitcast.29), channel_id=1, source_target_pairs={{0,4},{4,0},{8,12},{12,8},{16,20},{20,16},{24,28},{28,24},{32,36},... | collective-permute-start | bytes 4718600 | tf_op jit(solution)/shard_map/ppermute | solution.py:48
  164.5 3.5 %collective-permute-start.19 = (f32[32,1024]{1,0:T(8,128)S(1)}, f32[32,1024]{1,0:T(8,128)S(1)}, u32[]{:S(2)}, u32[]{:S(2)}) collective-permute-start(f32[32,1024]{1,0:T(8,128)S(1)} %add.25.refs_0_), channel_id=1, source_target_pairs={{0,128},{4,132},{8,136},{12,140},{16,144},{20,148},{24,152},{28,15... | collective-permute-start | bytes 393224 | tf_op jit(solution)/shard_map/ppermute | solution.py:48
  168.0 3.7 %collective-permute-done.19.refs_1_ = f32[32,1024]{1,0:T(8,128)S(1)} collective-permute-done((f32[32,1024]{1,0:T(8,128)S(1)}, f32[32,1024]{1,0:T(8,128)S(1)}, u32[]{:S(2)}, u32[]{:S(2)}) %collective-permute-start.19) | collective-permute-done | bytes 131104 | tf_op jit(solution)/shard_map/ppermute | solution.py:48
  174.1 2.4 %collective-permute-start.21 = (f32[32,512]{1,0:T(8,128)S(1)}, f32[32,512]{1,0:T(8,128)S(1)}, u32[]{:S(2)}, u32[]{:S(2)}) collective-permute-start(f32[32,512]{1,0:T(8,128)S(1)} %get-tuple-element.52.right), channel_id=1, source_target_pairs={{0,384},{4,388},{8,392},{12,396},{16,400},{20,404},{24,408},{28,41... | collective-permute-start | bytes 196616 | tf_op jit(solution)/shard_map/ppermute | solution.py:48
  176.6 3.8 %collective-permute-done.21.right_far = f32[32,512]{1,0:T(8,128)S(1)} collective-permute-done((f32[32,512]{1,0:T(8,128)S(1)}, f32[32,512]{1,0:T(8,128)S(1)}, u32[]{:S(2)}, u32[]{:S(2)}) %collective-permute-start.21) | collective-permute-done | bytes 65568 | tf_op jit(solution)/shard_map/ppermute | solution.py:48
  180.4 3.5 %shard_map.99 = f32[32,2048]{1,0:T(8,128)S(1)} custom-call(s32[1]{0:T(128)} %bitcast.5.plane, f32[32,512]{1,0:T(8,128)S(1)} %get-tuple-element.52.right, f32[32,512]{1,0:T(8,128)S(1)} %collective-permute-done.21.right_far, f32[32,512]{1,0:T(8,128)S(1)} %get-tuple-element.53.z1, f32[32,512]{1,0:T(8,128)S(1)} %get-tuple-element.54.z2, ...), custom_call_target="tpu_custom_call" | custom-call | tf_op jit(solution)/shard_map/pallas_call | solution.py:208
  186.0 5.9 %collective-permute-done.22 = f32[32,2048]{1,0:T(8,128)S(1)} collective-permute-done((f32[32,2048]{1,0:T(8,128)S(1)}, f32[32,2048]{1,0:T(8,128)S(1)}, u32[]{:S(2)}, u32[]{:S(2)}) %collective-permute-start.22) | collective-permute-done | bytes 262176 | tf_op jit(solution)/shard_map/ppermute | solution.py:48
  191.9 4.7 %collective-permute-start.23 = (f32[2,32,2048]{2,1,0:T(8,128)S(1)}, f32[2,32,2048]{2,1,0:T(8,128)S(1)}, u32[]{:S(2)}, u32[]{:S(2)}) collective-permute-start(f32[2,32,2048]{2,1,0:T(8,128)S(1)} %pad_maximum_fusion.1.near), channel_id=1, source_target_pairs={{0,4},{4,0},{8,12},{12,8},{16,20},{20,16},{24,28},{28,24},{32,36},... | collective-permute-start | bytes 1572872 | tf_op jit(solution)/shard_map/ppermute | solution.py:48
  198.2 4.6 %shard_map.100 = (f32[896,128]{1,0:T(8,128)}, f32[172,128]{1,0:T(8,128)}) custom-call(s32[5]{0:T(128)S(1)} %stack.71.where, s32[1,21]{1,0:T(1,128)S(1)} %copy-done.14, f32[896,128]{1,0:T(8,128)S(1)} %copy-done.10, f32[2,32,2048]{2,1,0:T(8,128)S(1)} %pad_maximum_fusion.1.near, f32[2,32,2048]{2,1,0:T(8,128)S(1)} %collective-permute-done.23.across_core, ...), custom_call_target="tpu_custom_call" | custom-call | tf_op jit(solution)/shard_map/pallas_call | solution.py:208
  (87 shorter events, 37.2 us)
Async XLA Ops:
  7.9 22.5 %collective-permute-start.1 = (f32[1,4,128]{2,1,0:T(4,128)S(1)}, f32[1,4,128]{2,1,0:T(4,128)S(1)}, u32[]{:S(2)}, u32[]{:S(2)}) collective-permute-start(f32[1,4,128]{2,1,0:T(4,128)S(1)} %slice_bitcast_fusion.6), channel_id=1, source_target_pairs={{0,384},{4,388},{8,392},{12,396},{16,400},{20,404},{24,408},{28,41... | collective-permute-start | bytes 6152 | tf_op jit(solution)/shard_map/ppermute | solution.py:48
  14.2 16.1 %collective-permute-start = (f32[2,128,128]{2,1,0:T(8,128)S(1)}, f32[2,128,128]{2,1,0:T(8,128)S(1)}, u32[]{:S(2)}, u32[]{:S(2)}) collective-permute-start(f32[2,128,128]{2,1,0:T(8,128)S(1)} %pad_maximum_fusion.6), channel_id=1, source_target_pairs={{0,8},{4,12},{8,0},{12,4},{16,24},{20,28},{24,16},{28,20},{32,40},... | collective-permute-start | bytes 393224 | tf_op jit(solution)/shard_map/ppermute | solution.py:48
  30.4 40.1 %all-to-all-start = ((f32[4,32,2048]{2,1,0:T(8,128)}), f32[4,32,2048]{2,1,0:T(8,128)S(1)}, u32[]{:S(2)}, u32[]{:S(2)}) async-start(f32[4,32,2048]{2,1,0:T(8,128)} %bitcast.11), calls=%async_computation | async-start | bytes 2097152 | tf_op jit(solution)/shard_map/all_to_all | solution.py:258
  37.0 19.3 %collective-permute-start.5 = (f32[3,8,128]{2,1,0:T(8,128)S(1)}, f32[3,8,128]{2,1,0:T(8,128)S(1)}, u32[]{:S(2)}, u32[]{:S(2)}) collective-permute-start(f32[3,8,128]{2,1,0:T(8,128)S(1)} %pad_maximum_fusion.13), channel_id=1, source_target_pairs={{0,128},{4,132},{8,136},{12,140},{16,144},{20,148},{24,152},{28,15... | collective-permute-start | bytes 36872 | tf_op jit(solution)/shard_map/ppermute | solution.py:48
  38.9 31.5 %collective-permute-start.4 = (f32[2,256,128]{2,1,0:T(8,128)S(1)}, f32[2,256,128]{2,1,0:T(8,128)S(1)}, u32[]{:S(2)}, u32[]{:S(2)}) collective-permute-start(f32[2,256,128]{2,1,0:T(8,128)S(1)} %pad_maximum_fusion.3), channel_id=1, source_target_pairs={{0,3},{1,2},{2,1},{3,0},{4,7},{5,6},{6,5},{7,4},{8,11},{9,10},{10,... | collective-permute-start | bytes 786440 | tf_op jit(solution)/shard_map/ppermute | solution.py:48
  42.8 27.6 %collective-permute-start.3 = (f32[2,256,128]{2,1,0:T(8,128)S(1)}, f32[2,256,128]{2,1,0:T(8,128)S(1)}, u32[]{:S(2)}, u32[]{:S(2)}) collective-permute-start(f32[2,256,128]{2,1,0:T(8,128)S(1)} %pad_maximum_fusion.3), channel_id=1, source_target_pairs={{0,2},{1,3},{2,0},{3,1},{4,6},{5,7},{6,4},{7,5},{8,10},{9,11},{10,... | collective-permute-start | bytes 786440 | tf_op jit(solution)/shard_map/ppermute | solution.py:48
  45.2 25.2 %collective-permute-start.2 = (f32[2,256,128]{2,1,0:T(8,128)S(1)}, f32[2,256,128]{2,1,0:T(8,128)S(1)}, u32[]{:S(2)}, u32[]{:S(2)}) collective-permute-start(f32[2,256,128]{2,1,0:T(8,128)S(1)} %pad_maximum_fusion.3), channel_id=1, source_target_pairs={{0,1},{1,0},{2,3},{3,2},{4,5},{5,4},{6,7},{7,6},{8,9},{9,8},{10,11... | collective-permute-start | bytes 786440 | tf_op jit(solution)/shard_map/ppermute | solution.py:48
  47.9 16.3 %collective-permute-start.7 = (f32[2,32,128]{2,1,0:T(8,128)S(1)}, f32[2,32,128]{2,1,0:T(8,128)S(1)}, u32[]{:S(2)}, u32[]{:S(2)}) collective-permute-start(f32[2,32,128]{2,1,0:T(8,128)S(1)} %pad_maximum_fusion.11), channel_id=1, source_target_pairs={{0,32},{4,36},{8,40},{12,44},{16,48},{20,52},{24,56},{28,60},{32,0... | collective-permute-start | bytes 98312 | tf_op jit(solution)/shard_map/ppermute | solution.py:48
  56.3 11.1 %collective-permute-start.6 = (f32[3,16,128]{2,1,0:T(8,128)S(1)}, f32[3,16,128]{2,1,0:T(8,128)S(1)}, u32[]{:S(2)}, u32[]{:S(2)}) collective-permute-start(f32[3,16,128]{2,1,0:T(8,128)S(1)} %pad_maximum_fusion.12), channel_id=1, source_target_pairs={{0,96},{4,100},{8,104},{12,108},{16,112},{20,116},{24,120},{28,124... | collective-permute-start | bytes 73736 | tf_op jit(solution)/shard_map/ppermute | solution.py:48
  64.2 6.2 %collective-permute-start.8 = (f32[2,64,128]{2,1,0:T(8,128)S(1)}, f32[2,64,128]{2,1,0:T(8,128)S(1)}, u32[]{:S(2)}, u32[]{:S(2)}) collective-permute-start(f32[2,64,128]{2,1,0:T(8,128)S(1)} %pad_maximum_fusion.9), channel_id=1, source_target_pairs={{0,16},{4,20},{8,24},{12,28},{16,0},{20,4},{24,8},{28,12},{32,48},... | collective-permute-start | bytes 196616 | tf_op jit(solution)/shard_map/ppermute | solution.py:48
  70.5 12.0 %collective-permute-start.9 = (f32[4,2,256,128]{3,2,1,0:T(8,128)S(1)}, f32[4,2,256,128]{3,2,1,0:T(8,128)S(1)}, u32[]{:S(2)}, u32[]{:S(2)}) collective-permute-start(f32[4,2,256,128]{3,2,1,0:T(8,128)S(1)} %pad_maximum_fusion.refs_1_.m1), channel_id=1, source_target_pairs={{0,4},{4,0},{8,12},{12,8},{16,20},{20,16},{24,28},{28,24},{32,36},... | collective-permute-start | bytes 3145736 | tf_op jit(solution)/shard_map/ppermute | solution.py:48
  74.9 11.9 %collective-permute-start.12 = (f32[3,32,128]{2,1,0:T(8,128)}, f32[3,32,128]{2,1,0:T(8,128)}, u32[]{:S(2)}, u32[]{:S(2)}) collective-permute-start(f32[3,32,128]{2,1,0:T(8,128)} %pad_maximum_fusion.10), channel_id=1, source_target_pairs={{0,32},{4,36},{8,40},{12,44},{16,48},{20,52},{24,56},{28,60},{32,0... | collective-permute-start | bytes 147464 | tf_op jit(solution)/shard_map/ppermute | solution.py:48
  78.9 9.4 %collective-permute-start.11 = (f32[2,128,128]{2,1,0:T(8,128)S(1)}, f32[2,128,128]{2,1,0:T(8,128)}, u32[]{:S(2)}, u32[]{:S(2)}) collective-permute-start(f32[2,128,128]{2,1,0:T(8,128)S(1)} %pad_maximum_fusion.7), channel_id=1, source_target_pairs={{0,8},{4,12},{8,0},{12,4},{16,24},{20,28},{24,16},{28,20},{32,40},... | collective-permute-start | bytes 393224 | tf_op jit(solution)/shard_map/ppermute | solution.py:48
  83.5 13.3 %collective-permute-start.10 = (f32[32,1536]{1,0:T(8,128)S(1)}, f32[32,1536]{1,0:T(8,128)S(1)}, u32[]{:S(2)}, u32[]{:S(2)}) collective-permute-start(f32[32,1536]{1,0:T(8,128)S(1)} %get-tuple-element.40), channel_id=1, source_target_pairs={{0,16},{4,20},{8,24},{12,28},{16,0},{20,4},{24,8},{28,12},{32,48},... | collective-permute-start | bytes 589832 | tf_op jit(solution)/shard_map/ppermute | solution.py:48
  97.9 23.7 %all-to-all-start.1 = ((f32[4,2,256,128]{3,2,1,0:T(8,128)}), f32[4,2,256,128]{3,2,1,0:T(8,128)S(1)}, u32[]{:S(2)}, u32[]{:S(2)}) async-start(f32[4,2,256,128]{3,2,1,0:T(8,128)} %broadcast_in_dim.14), calls=%async_computation.1 | async-start | bytes 2097152 | tf_op jit(solution)/shard_map/all_to_all | solution.py:235
  101.9 59.6 %all-gather.3.cloned.1.call-start = ((), (), s32[]{:S(2)}) async-start(), calls=%async_computation.2 | async-start | bytes 1966080 | tf_op jit(solution)/shard_map/all_gather | solution.py:284
  101.9 8.4 %collective-permute-start.13 = (f32[3,64,128]{2,1,0:T(8,128)}, f32[3,64,128]{2,1,0:T(8,128)S(1)}, u32[]{:S(2)}, u32[]{:S(2)}) collective-permute-start(f32[3,64,128]{2,1,0:T(8,128)} %pad_maximum_fusion.8), channel_id=1, source_target_pairs={{0,16},{4,20},{8,24},{12,28},{16,0},{20,4},{24,8},{28,12},{32,48},... | collective-permute-start | bytes 294920 | tf_op jit(solution)/shard_map/ppermute | solution.py:48
  104.8 8.9 %collective-permute-start.14 = (f32[32,512]{1,0:T(8,128)S(1)}, f32[32,512]{1,0:T(8,128)S(1)}, u32[]{:S(2)}, u32[]{:S(2)}) collective-permute-start(f32[32,512]{1,0:T(8,128)S(1)} %slice.36.refs_0_), channel_id=1, source_target_pairs={{0,32},{4,36},{8,40},{12,44},{16,48},{20,52},{24,56},{28,60},{32,0... | collective-permute-start | bytes 196616 | tf_op jit(solution)/shard_map/ppermute | solution.py:48
  113.8 7.1 %collective-permute-start.16 = (f32[3,128,128]{2,1,0:T(8,128)S(1)}, f32[3,128,128]{2,1,0:T(8,128)S(1)}, u32[]{:S(2)}, u32[]{:S(2)}) collective-permute-start(f32[3,128,128]{2,1,0:T(8,128)S(1)} %pad_maximum_fusion.5), channel_id=1, source_target_pairs={{0,8},{4,12},{8,0},{12,4},{16,24},{20,28},{24,16},{28,20},{32,40},... | collective-permute-start | bytes 589832 | tf_op jit(solution)/shard_map/ppermute | solution.py:48
  121.6 27.2 %collective-permute-start.17 = (f32[4,2,256,128]{3,2,1,0:T(8,128)S(1)}, f32[4,2,256,128]{3,2,1,0:T(8,128)S(1)}, u32[]{:S(2)}, u32[]{:S(2)}) collective-permute-start(f32[4,2,256,128]{3,2,1,0:T(8,128)S(1)} %all-to-all-done.1.refs_4_.m2), channel_id=1, source_target_pairs={{0,4},{4,0},{8,12},{12,8},{16,20},{20,16},{24,28},{28,24},{32,36},... | collective-permute-start | bytes 3145736 | tf_op jit(solution)/shard_map/ppermute | solution.py:48
  129.7 19.1 %collective-permute-start.15 = (f32[32,1024]{1,0:T(8,128)S(1)}, f32[32,1024]{1,0:T(8,128)S(1)}, u32[]{:S(2)}, u32[]{:S(2)}) collective-permute-start(f32[32,1024]{1,0:T(8,128)S(1)} %slice.37.refs_2_), channel_id=1, source_target_pairs={{0,32},{4,36},{8,40},{12,44},{16,48},{20,52},{24,56},{28,60},{32,0... | collective-permute-start | bytes 393224 | tf_op jit(solution)/shard_map/ppermute | solution.py:48
  150.8 10.7 %collective-permute-start.18 = (f32[32,1024]{1,0:T(8,128)S(1)}, f32[32,1024]{1,0:T(8,128)S(1)}, u32[]{:S(2)}, u32[]{:S(2)}) collective-permute-start(f32[32,1024]{1,0:T(8,128)S(1)} %get-tuple-element.48), channel_id=1, source_target_pairs={{0,96},{4,100},{8,104},{12,108},{16,112},{20,116},{24,120},{28,124... | collective-permute-start | bytes 393224 | tf_op jit(solution)/shard_map/ppermute | solution.py:48
  161.5 10.2 %collective-permute-start.20 = (f32[4,3,256,128]{3,2,1,0:T(8,128)}, f32[4,3,256,128]{3,2,1,0:T(8,128)S(1)}, u32[]{:S(2)}, u32[]{:S(2)}) collective-permute-start(f32[4,3,256,128]{3,2,1,0:T(8,128)} %bitcast.29), channel_id=1, source_target_pairs={{0,4},{4,0},{8,12},{12,8},{16,20},{20,16},{24,28},{28,24},{32,36},... | collective-permute-start | bytes 4718600 | tf_op jit(solution)/shard_map/ppermute | solution.py:48
  164.5 7.3 %collective-permute-start.19 = (f32[32,1024]{1,0:T(8,128)S(1)}, f32[32,1024]{1,0:T(8,128)S(1)}, u32[]{:S(2)}, u32[]{:S(2)}) collective-permute-start(f32[32,1024]{1,0:T(8,128)S(1)} %add.25.refs_0_), channel_id=1, source_target_pairs={{0,128},{4,132},{8,136},{12,140},{16,144},{20,148},{24,152},{28,15... | collective-permute-start | bytes 393224 | tf_op jit(solution)/shard_map/ppermute | solution.py:48
  174.1 6.2 %collective-permute-start.21 = (f32[32,512]{1,0:T(8,128)S(1)}, f32[32,512]{1,0:T(8,128)S(1)}, u32[]{:S(2)}, u32[]{:S(2)}) collective-permute-start(f32[32,512]{1,0:T(8,128)S(1)} %get-tuple-element.52.right), channel_id=1, source_target_pairs={{0,384},{4,388},{8,392},{12,396},{16,400},{20,404},{24,408},{28,41... | collective-permute-start | bytes 196616 | tf_op jit(solution)/shard_map/ppermute | solution.py:48
  180.3 17.8 %copy-start.2 = (f32[21,128,128]{2,1,0:T(8,128)S(1)}, f32[21,128,128]{2,1,0:T(8,128)}, u32[]{:S(2)}) copy-start(f32[21,128,128]{2,1,0:T(8,128)} %blocks.3) | copy-start | bytes 4128772
  180.3 17.8 %copy-start.8 = (f32[7,128,128]{2,1,0:T(8,128)S(1)}, f32[7,128,128]{2,1,0:T(8,128)}, u32[]{:S(2)}) copy-start(f32[7,128,128]{2,1,0:T(8,128)} %inverse.3) | copy-start | bytes 1376260
  180.4 17.8 %copy-start.10 = (f32[896,128]{1,0:T(8,128)S(1)}, f32[896,128]{1,0:T(8,128)}, u32[]{:S(2)}) copy-start(f32[896,128]{1,0:T(8,128)} %copy-done.9) | copy-start | bytes 1376260
  180.4 17.8 %copy-start.14 = (s32[1,21]{1,0:T(1,128)S(1)}, s32[1,21]{1,0:T(1,128)}, u32[]{:S(2)}) copy-start(s32[1,21]{1,0:T(1,128)} %pattern.3) | copy-start | bytes 256
  183.9 14.2 %copy-start.4 = (f32[512,512]{1,0:T(8,128)S(1)}, f32[512,512]{1,0:T(8,128)}, u32[]{:S(2)}) copy-start(f32[512,512]{1,0:T(8,128)} %coupling.3) | copy-start | bytes 3145732
  183.9 8.0 %collective-permute-start.22 = (f32[32,2048]{1,0:T(8,128)S(1)}, f32[32,2048]{1,0:T(8,128)S(1)}, u32[]{:S(2)}, u32[]{:S(2)}) collective-permute-start(f32[32,2048]{1,0:T(8,128)S(1)} %shard_map.99), channel_id=1, source_target_pairs={{0,8},{4,12},{8,0},{12,4},{16,24},{20,28},{24,16},{28,20},{32,40},... | collective-permute-start | bytes 786440 | tf_op jit(solution)/shard_map/ppermute | solution.py:48
  191.9 6.2 %collective-permute-start.23 = (f32[2,32,2048]{2,1,0:T(8,128)S(1)}, f32[2,32,2048]{2,1,0:T(8,128)S(1)}, u32[]{:S(2)}, u32[]{:S(2)}) collective-permute-start(f32[2,32,2048]{2,1,0:T(8,128)S(1)} %pad_maximum_fusion.1.near), channel_id=1, source_target_pairs={{0,4},{4,0},{8,12},{12,8},{16,20},{20,16},{24,28},{28,24},{32,36},... | collective-permute-start | bytes 1572872 | tf_op jit(solution)/shard_map/ppermute | solution.py:48
  (11 other events, 17.6 us)
Sparse Core Ops, SparseCore 0:
  121.8 34.8 all-gather.2

commit v9 on v8

--- a/solution.py
+++ b/solution.py
@@ -165,11 +165,12 @@
     mats = (mine, other)
     count, width = z_out.shape
     more = v_out.shape[1]
-    heads = [ref for ref in refs[:-4] if ref.shape[1] in (width, width + more)]
-    rests = [ref for ref in refs[:-4] if ref.shape[1] >= more and ref.shape[1] != width]
+    both = [ref for ref in refs[:-4] if ref.shape[1] >= width + more]
+    heads = [ref for ref in refs[:-4] if ref.shape[1] == width]
+    rests = [ref for ref in refs[:-4] if width < ref.shape[1] < width + more]
     places = spots(0, mine.shape[0], plane[0] if turned else None)
-    z_out[...] = summed(heads, count)[:, :width]
-    v_out[...] = summed(rests, count)[:, -more:]
+    z_out[...] = summed([ref[:, :width] for ref in both] + heads, count)
+    v_out[...] = summed([ref[:, width : width + more] for ref in both] + rests, count)
     z = times_rows(z_out, places, mats, index)
     z_out[...] = jnp.concatenate(z, axis=1)
     for r, place in enumerate(places):
@@ -263,21 +264,24 @@
     second = grow(second, 1 << Z2)
     t, first, far, second = tie((t, first, far, second))
 
+    upper = t[:, 2 * width :].reshape(4, columns // 4, 2 * width).sum(0)
+    upper_far = across(upper, 1 << Z2)
     first = (first, across(first, CORE_MASK))
     second = grow(second, 1 << Z1)
     far = grow(far, halves_z)
-    z1, v = solve(0, True, 3, t, *first)
+    upper, upper_far, far = tie((upper, upper_far, far))
+    upper = upper + upper_far
+    upper_far = across(upper, halves_z)
+    z1, v = solve(0, True, 1, t, *first)
     v_far = across(v, 1 << Z2)
-    v, v_far, second, far = tie((v, v_far, second, far))
+    v, v_far, second, far, upper, upper_far = tie((v, v_far, second, far, upper, upper_far))
 
     second = planes(second)
     v = v + v_far
-    v, upper = v[:, :width], v[:, width:]
     v_far = across(v, halves_z)
     far = grow(far, 1 << Z2)
-    far, upper, v_far = tie((far, upper, v_far))
-
-    upper_far = across(upper, halves_z)
+    far, v_far = tie((far, v_far))
+
     far = grow(far, 1 << Z1)
     far, second = tie((far, second))
 

time: 211 us -> 220 us (1.043)
  waiting for transfers between devices: 56.2 us -> 64.8 us
  local copies, waits for them, and re-layouts: 14.2 us -> 17.1 us
    all_gather x1, waiting for transfers between devices: 0.02 us -> 9.16 us  [shards(): third = lax.all_gather(far, 'col', axis=0)]
    ppermute x24 -> x25, starting transfers between devices: 93.8 us -> 91.3 us  [swap(): lax.ppermute(value, axis, [(i, i ^ mask) for i in range(lax.axis_size(axi...]
    unnamed x32 -> x42, local copies, waits for them, and re-layouts: 9.32 us -> 11.4 us
    ppermute x24 -> x25, waiting for transfers between devices: 56.1 us -> 55.6 us  [swap(): lax.ppermute(value, axis, [(i, i ^ mask) for i in range(lax.axis_size(axi...]
  transfers between devices with their start and end apart: 27 -> 28, of which waited for: 10 -> 13; matrix products, arithmetic and copies ran while one was open for 4% -> 5% of each run, Pallas kernels for 3% -> 3%
where the time goes in v9:
time: 220 us; the launch traced here: 219 us
  starting transfers between devices  101 us (46%)
  waiting for transfers between devices  64.8 us (29%)
  local copies, waits for them, and re-layouts  17.1 us (8%)
  Pallas kernels  15.9 us (7%)
  between operations  14.5 us (7%)
  other arithmetic  6.17 us (3%)
    ppermute x25, starting transfers between devices, swap(): lax.ppermute(value, axis, [(i, i ^ mask) for i in range(lax.axis_size(axi...  91.3 us
    ppermute x25, waiting for transfers between devices, swap(): lax.ppermute(value, axis, [(i, i ^ mask) for i in range(lax.axis_size(axi...  55.6 us
    pallas_call x6, Pallas kernels, call(): pl.pallas_call(kernel, out_shape=[jax.ShapeDtypeStruct(s, F32) for s in o...  15.9 us
    unnamed x42, local copies, waits for them, and re-layouts  11.4 us
    all_gather x1, waiting for transfers between devices, shards(): third = lax.all_gather(far, 'col', axis=0)  9.16 us
    all_to_all x1, starting transfers between devices, shards(): t = lax.all_to_all(t, 'leaf', 0, 0, axis_index_groups=near, tiled=True)  5.19 us
  transfers between devices with their start and end apart: 28, of which 13 were waited for; matrix products, arithmetic and copies ran while one was open for 5% of the time, Pallas kernels for 3%

profile of v9, /device:TPU:1, one launch (start us, length us, event | category | flops | bytes accessed | tf_op | source)
XLA Modules:
  0.0 218.9 jit_solution(1510617035104759200)
XLA Ops:
  7.9 5.5 %collective-permute-start.1 = (f32[1,4,128]{2,1,0:T(4,128)S(1)}, f32[1,4,128]{2,1,0:T(4,128)S(1)}, u32[]{:S(2)}, u32[]{:S(2)}) collective-permute-start(f32[1,4,128]{2,1,0:T(4,128)S(1)} %slice_bitcast_fusion.6), channel_id=1, source_target_pairs={{0,384},{4,388},{8,392},{12,396},{16,400},{20,404},{24,408},{28,41... | collective-permute-start | bytes 6152 | tf_op jit(solution)/shard_map/ppermute | solution.py:48
  14.2 3.5 %collective-permute-start = (f32[2,128,128]{2,1,0:T(8,128)S(1)}, f32[2,128,128]{2,1,0:T(8,128)S(1)}, u32[]{:S(2)}, u32[]{:S(2)}) collective-permute-start(f32[2,128,128]{2,1,0:T(8,128)S(1)} %pad_maximum_fusion.6), channel_id=1, source_target_pairs={{0,8},{4,12},{8,0},{12,4},{16,24},{20,28},{24,16},{28,20},{32,40},... | collective-permute-start | bytes 393224 | tf_op jit(solution)/shard_map/ppermute | solution.py:48
  24.8 4.8 %shard_map.95 = (f32[896,128]{1,0:T(8,128)S(1)}, f32[128,2048]{1,0:T(8,128)}) custom-call(s32[5]{0:T(128)S(1)} %stack.71.where, s32[1,21]{1,0:T(1,128)S(1)} %copy-done.18, f32[896,128]{1,0:T(8,128)S(1)} %copy-done.11, f32[7,128,128]{2,1,0:T(8,128)S(1)} %copy-done.7, f32[21,128,128]{2,1,0:T(8,128)S(1)} %copy-done.1, f32[512,512]{1,0:T(8,128)S(1)} %copy-done.3, ...), custom_call_target="tpu_custom_call" | custom-call | tf_op jit(solution)/shard_map/pallas_call | solution.py:209
  30.4 5.2 %all-to-all-start = ((f32[4,32,2048]{2,1,0:T(8,128)}), f32[4,32,2048]{2,1,0:T(8,128)S(1)}, u32[]{:S(2)}, u32[]{:S(2)}) async-start(f32[4,32,2048]{2,1,0:T(8,128)} %bitcast.11), calls=%async_computation | async-start | bytes 2097152 | tf_op jit(solution)/shard_map/all_to_all | solution.py:259
  38.9 3.9 %collective-permute-start.4 = (f32[2,256,128]{2,1,0:T(8,128)S(1)}, f32[2,256,128]{2,1,0:T(8,128)S(1)}, u32[]{:S(2)}, u32[]{:S(2)}) collective-permute-start(f32[2,256,128]{2,1,0:T(8,128)S(1)} %pad_maximum_fusion.3), channel_id=1, source_target_pairs={{0,3},{1,2},{2,1},{3,0},{4,7},{5,6},{6,5},{7,4},{8,11},{9,10},{10,... | collective-permute-start | bytes 786440 | tf_op jit(solution)/shard_map/ppermute | solution.py:48
  45.2 2.6 %collective-permute-start.2 = (f32[2,256,128]{2,1,0:T(8,128)S(1)}, f32[2,256,128]{2,1,0:T(8,128)S(1)}, u32[]{:S(2)}, u32[]{:S(2)}) collective-permute-start(f32[2,256,128]{2,1,0:T(8,128)S(1)} %pad_maximum_fusion.3), channel_id=1, source_target_pairs={{0,1},{1,0},{2,3},{3,2},{4,5},{5,4},{6,7},{7,6},{8,9},{9,8},{10,11... | collective-permute-start | bytes 786440 | tf_op jit(solution)/shard_map/ppermute | solution.py:48
  47.9 8.4 %collective-permute-start.7 = (f32[2,32,128]{2,1,0:T(8,128)S(1)}, f32[2,32,128]{2,1,0:T(8,128)S(1)}, u32[]{:S(2)}, u32[]{:S(2)}) collective-permute-start(f32[2,32,128]{2,1,0:T(8,128)S(1)} %pad_maximum_fusion.11), channel_id=1, source_target_pairs={{0,32},{4,36},{8,40},{12,44},{16,48},{20,52},{24,56},{28,60},{32,0... | collective-permute-start | bytes 98312 | tf_op jit(solution)/shard_map/ppermute | solution.py:48
  56.3 7.9 %collective-permute-start.6 = (f32[3,16,128]{2,1,0:T(8,128)S(1)}, f32[3,16,128]{2,1,0:T(8,128)S(1)}, u32[]{:S(2)}, u32[]{:S(2)}) collective-permute-start(f32[3,16,128]{2,1,0:T(8,128)S(1)} %pad_maximum_fusion.12), channel_id=1, source_target_pairs={{0,96},{4,100},{8,104},{12,108},{16,112},{20,116},{24,120},{28,124... | collective-permute-start | bytes 73736 | tf_op jit(solution)/shard_map/ppermute | solution.py:48
  64.2 3.1 %collective-permute-start.8 = (f32[2,64,128]{2,1,0:T(8,128)S(1)}, f32[2,64,128]{2,1,0:T(8,128)S(1)}, u32[]{:S(2)}, u32[]{:S(2)}) collective-permute-start(f32[2,64,128]{2,1,0:T(8,128)S(1)} %pad_maximum_fusion.9), channel_id=1, source_target_pairs={{0,16},{4,20},{8,24},{12,28},{16,0},{20,4},{24,8},{28,12},{32,48},... | collective-permute-start | bytes 196616 | tf_op jit(solution)/shard_map/ppermute | solution.py:48
  67.4 3.0 %collective-permute-done.8 = f32[2,64,128]{2,1,0:T(8,128)S(1)} collective-permute-done((f32[2,64,128]{2,1,0:T(8,128)S(1)}, f32[2,64,128]{2,1,0:T(8,128)S(1)}, u32[]{:S(2)}, u32[]{:S(2)}) %collective-permute-start.8) | collective-permute-done | bytes 65568 | tf_op jit(solution)/shard_map/ppermute | solution.py:48
  71.2 4.4 %collective-permute-start.9 = (f32[4,2,256,128]{3,2,1,0:T(8,128)S(1)}, f32[4,2,256,128]{3,2,1,0:T(8,128)S(1)}, u32[]{:S(2)}, u32[]{:S(2)}) collective-permute-start(f32[4,2,256,128]{3,2,1,0:T(8,128)S(1)} %pad_maximum_fusion.refs_1_.m1), channel_id=1, source_target_pairs={{0,4},{4,0},{8,12},{12,8},{16,20},{20,16},{24,28},{28,24},{32,36},... | collective-permute-start | bytes 3145736 | tf_op jit(solution)/shard_map/ppermute | solution.py:48
  75.5 4.0 %collective-permute-start.13 = (f32[3,32,128]{2,1,0:T(8,128)S(1)}, f32[3,32,128]{2,1,0:T(8,128)S(1)}, u32[]{:S(2)}, u32[]{:S(2)}) collective-permute-start(f32[3,32,128]{2,1,0:T(8,128)S(1)} %pad_maximum_fusion.10), channel_id=1, source_target_pairs={{0,32},{4,36},{8,40},{12,44},{16,48},{20,52},{24,56},{28,60},{32,0... | collective-permute-start | bytes 147464 | tf_op jit(solution)/shard_map/ppermute | solution.py:48
  81.5 3.1 %collective-permute-start.12 = (f32[32,1024]{1,0:T(8,128)S(1)}, f32[32,1024]{1,0:T(8,128)S(1)}, u32[]{:S(2)}, u32[]{:S(2)}) collective-permute-start(f32[32,1024]{1,0:T(8,128)S(1)} %reduce_sum.9), channel_id=1, source_target_pairs={{0,16},{4,20},{8,24},{12,28},{16,0},{20,4},{24,8},{28,12},{32,48},... | collective-permute-start | bytes 393224 | tf_op jit(solution)/shard_map/ppermute | solution.py:48
  84.6 3.8 %collective-permute-start.11 = (f32[2,128,128]{2,1,0:T(8,128)}, f32[2,128,128]{2,1,0:T(8,128)}, u32[]{:S(2)}, u32[]{:S(2)}) collective-permute-start(f32[2,128,128]{2,1,0:T(8,128)} %pad_maximum_fusion.7), channel_id=1, source_target_pairs={{0,8},{4,12},{8,0},{12,4},{16,24},{20,28},{24,16},{28,20},{32,40},... | collective-permute-start | bytes 393224 | tf_op jit(solution)/shard_map/ppermute | solution.py:48
  89.1 3.4 %collective-permute-done.12 = f32[32,1024]{1,0:T(8,128)S(1)} collective-permute-done((f32[32,1024]{1,0:T(8,128)S(1)}, f32[32,1024]{1,0:T(8,128)S(1)}, u32[]{:S(2)}, u32[]{:S(2)}) %collective-permute-start.12) | collective-permute-done | bytes 131104 | tf_op jit(solution)/shard_map/ppermute | solution.py:48
  92.5 4.5 %collective-permute-start.14 = (f32[32,1024]{1,0:T(8,128)S(1)}, f32[32,1024]{1,0:T(8,128)S(1)}, u32[]{:S(2)}, u32[]{:S(2)}) collective-permute-start(f32[32,1024]{1,0:T(8,128)S(1)} %add.27.refs_2_), channel_id=1, source_target_pairs={{0,32},{4,36},{8,40},{12,44},{16,48},{20,52},{24,56},{28,60},{32,0... | collective-permute-start | bytes 393224 | tf_op jit(solution)/shard_map/ppermute | solution.py:48
  101.0 10.0 %collective-permute-done.14.refs_3_ = f32[32,1024]{1,0:T(8,128)S(1)} collective-permute-done((f32[32,1024]{1,0:T(8,128)S(1)}, f32[32,1024]{1,0:T(8,128)S(1)}, u32[]{:S(2)}, u32[]{:S(2)}) %collective-permute-start.14) | collective-permute-done | bytes 131104 | tf_op jit(solution)/shard_map/ppermute | solution.py:48
  112.1 4.0 %all-to-all-start.1 = ((f32[4,2,256,128]{3,2,1,0:T(8,128)}), f32[4,2,256,128]{3,2,1,0:T(8,128)S(1)}, u32[]{:S(2)}, u32[]{:S(2)}) async-start(f32[4,2,256,128]{3,2,1,0:T(8,128)} %broadcast_in_dim.14), calls=%async_computation.1 | async-start | bytes 2097152 | tf_op jit(solution)/shard_map/all_to_all | solution.py:236
  120.8 3.3 %collective-permute-done.15 = f32[3,64,128]{2,1,0:T(8,128)S(1)} collective-permute-done((f32[3,64,128]{2,1,0:T(8,128)}, f32[3,64,128]{2,1,0:T(8,128)S(1)}, u32[]{:S(2)}, u32[]{:S(2)}) %collective-permute-start.15) | collective-permute-done | bytes 98336 | tf_op jit(solution)/shard_map/ppermute | solution.py:48
  125.0 6.2 %collective-permute-done.16.refs_1_ = f32[32,512]{1,0:T(8,128)S(1)} collective-permute-done((f32[32,512]{1,0:T(8,128)S(1)}, f32[32,512]{1,0:T(8,128)S(1)}, u32[]{:S(2)}, u32[]{:S(2)}) %collective-permute-start.16) | collective-permute-done | bytes 65568 | tf_op jit(solution)/shard_map/ppermute | solution.py:48
  133.7 4.8 %collective-permute-done.17 = f32[3,128,128]{2,1,0:T(8,128)S(1)} collective-permute-done((f32[3,128,128]{2,1,0:T(8,128)S(1)}, f32[3,128,128]{2,1,0:T(8,128)S(1)}, u32[]{:S(2)}, u32[]{:S(2)}) %collective-permute-start.17) | collective-permute-done | bytes 196640 | tf_op jit(solution)/shard_map/ppermute | solution.py:48
  139.3 4.4 %collective-permute-start.18 = (f32[4,2,256,128]{3,2,1,0:T(8,128)S(1)}, f32[4,2,256,128]{3,2,1,0:T(8,128)S(1)}, u32[]{:S(2)}, u32[]{:S(2)}) collective-permute-start(f32[4,2,256,128]{3,2,1,0:T(8,128)S(1)} %all-to-all-done.1.refs_4_.m2), channel_id=1, source_target_pairs={{0,4},{4,0},{8,12},{12,8},{16,20},{20,16},{24,28},{28,24},{32,36},... | collective-permute-start | bytes 3145736 | tf_op jit(solution)/shard_map/ppermute | solution.py:48
  151.4 10.8 %collective-permute-done.19 = f32[32,1024]{1,0:T(8,128)S(1)} collective-permute-done((f32[32,1024]{1,0:T(8,128)S(1)}, f32[32,1024]{1,0:T(8,128)S(1)}, u32[]{:S(2)}, u32[]{:S(2)}) %collective-permute-start.19) | collective-permute-done | bytes 131104 | tf_op jit(solution)/shard_map/ppermute | solution.py:48
  162.2 9.2 %all-gather.3.cloned.1.call-done = f32[12,256,128]{2,1,0:T(8,128)} async-done(((f32[3,256,128]{2,1,0:T(8,128)}), f32[12,256,128]{2,1,0:T(8,128)}) %all-gather.3.cloned.1.call-update) | async-done | bytes 1572880 | tf_op jit(solution)/shard_map/all_gather | solution.py:288
  174.0 3.1 %collective-permute-start.20 = (f32[32,1024]{1,0:T(8,128)S(1)}, f32[32,1024]{1,0:T(8,128)S(1)}, u32[]{:S(2)}, u32[]{:S(2)}) collective-permute-start(f32[32,1024]{1,0:T(8,128)S(1)} %add.29.refs_0_), channel_id=1, source_target_pairs={{0,128},{4,132},{8,136},{12,140},{16,144},{20,148},{24,152},{28,15... | collective-permute-start | bytes 393224 | tf_op jit(solution)/shard_map/ppermute | solution.py:48
  177.1 3.9 %collective-permute-done.20.refs_1_ = f32[32,1024]{1,0:T(8,128)S(1)} collective-permute-done((f32[32,1024]{1,0:T(8,128)S(1)}, f32[32,1024]{1,0:T(8,128)S(1)}, u32[]{:S(2)}, u32[]{:S(2)}) %collective-permute-start.20) | collective-permute-done | bytes 131104 | tf_op jit(solution)/shard_map/ppermute | solution.py:48
  183.4 4.4 %collective-permute-start.22 = (f32[32,512]{1,0:T(8,128)S(1)}, f32[32,512]{1,0:T(8,128)S(1)}, u32[]{:S(2)}, u32[]{:S(2)}) collective-permute-start(f32[32,512]{1,0:T(8,128)S(1)} %get-tuple-element.60.right), channel_id=1, source_target_pairs={{0,384},{4,388},{8,392},{12,396},{16,400},{20,404},{24,408},{28,41... | collective-permute-start | bytes 196616 | tf_op jit(solution)/shard_map/ppermute | solution.py:48
  189.6 3.5 %shard_map.99 = f32[32,2048]{1,0:T(8,128)S(1)} custom-call(s32[1]{0:T(128)} %bitcast.5.plane, f32[32,512]{1,0:T(8,128)S(1)} %get-tuple-element.60.right, f32[32,512]{1,0:T(8,128)S(1)} %collective-permute-done.22.right_far, f32[32,512]{1,0:T(8,128)S(1)} %get-tuple-element.61.z1, f32[32,512]{1,0:T(8,128)S(1)} %copy-done.14, ...), custom_call_target="tpu_custom_call" | custom-call | tf_op jit(solution)/shard_map/pallas_call | solution.py:209
  193.2 3.3 %collective-permute-start.23 = (f32[32,2048]{1,0:T(8,128)S(1)}, f32[32,2048]{1,0:T(8,128)S(1)}, u32[]{:S(2)}, u32[]{:S(2)}) collective-permute-start(f32[32,2048]{1,0:T(8,128)S(1)} %shard_map.99), channel_id=1, source_target_pairs={{0,8},{4,12},{8,0},{12,4},{16,24},{20,28},{24,16},{28,20},{32,40},... | collective-permute-start | bytes 786440 | tf_op jit(solution)/shard_map/ppermute | solution.py:48
  196.5 4.6 %collective-permute-done.23 = f32[32,2048]{1,0:T(8,128)S(1)} collective-permute-done((f32[32,2048]{1,0:T(8,128)S(1)}, f32[32,2048]{1,0:T(8,128)S(1)}, u32[]{:S(2)}, u32[]{:S(2)}) %collective-permute-start.23) | collective-permute-done | bytes 262176 | tf_op jit(solution)/shard_map/ppermute | solution.py:48
  201.1 4.8 %collective-permute-start.24 = (f32[2,32,2048]{2,1,0:T(8,128)S(1)}, f32[2,32,2048]{2,1,0:T(8,128)S(1)}, u32[]{:S(2)}, u32[]{:S(2)}) collective-permute-start(f32[2,32,2048]{2,1,0:T(8,128)S(1)} %pad_maximum_fusion.1.near), channel_id=1, source_target_pairs={{0,4},{4,0},{8,12},{12,8},{16,20},{20,16},{24,28},{28,24},{32,36},... | collective-permute-start | bytes 1572872 | tf_op jit(solution)/shard_map/ppermute | solution.py:48
  207.4 4.7 %shard_map.100 = (f32[896,128]{1,0:T(8,128)}, f32[172,128]{1,0:T(8,128)}) custom-call(s32[5]{0:T(128)S(1)} %stack.71.where, s32[1,21]{1,0:T(1,128)S(1)} %copy-done.19, f32[896,128]{1,0:T(8,128)S(1)} %copy-done.10, f32[2,32,2048]{2,1,0:T(8,128)S(1)} %pad_maximum_fusion.1.near, f32[2,32,2048]{2,1,0:T(8,128)S(1)} %collective-permute-done.24.across_core, ...), custom_call_target="tpu_custom_call" | custom-call | tf_op jit(solution)/shard_map/pallas_call | solution.py:209
  (100 shorter events, 48.5 us)
Async XLA Ops:
  7.9 22.5 %collective-permute-start.1 = (f32[1,4,128]{2,1,0:T(4,128)S(1)}, f32[1,4,128]{2,1,0:T(4,128)S(1)}, u32[]{:S(2)}, u32[]{:S(2)}) collective-permute-start(f32[1,4,128]{2,1,0:T(4,128)S(1)} %slice_bitcast_fusion.6), channel_id=1, source_target_pairs={{0,384},{4,388},{8,392},{12,396},{16,400},{20,404},{24,408},{28,41... | collective-permute-start | bytes 6152 | tf_op jit(solution)/shard_map/ppermute | solution.py:48
  14.2 16.1 %collective-permute-start = (f32[2,128,128]{2,1,0:T(8,128)S(1)}, f32[2,128,128]{2,1,0:T(8,128)S(1)}, u32[]{:S(2)}, u32[]{:S(2)}) collective-permute-start(f32[2,128,128]{2,1,0:T(8,128)S(1)} %pad_maximum_fusion.6), channel_id=1, source_target_pairs={{0,8},{4,12},{8,0},{12,4},{16,24},{20,28},{24,16},{28,20},{32,40},... | collective-permute-start | bytes 393224 | tf_op jit(solution)/shard_map/ppermute | solution.py:48
  30.4 40.8 %all-to-all-start = ((f32[4,32,2048]{2,1,0:T(8,128)}), f32[4,32,2048]{2,1,0:T(8,128)S(1)}, u32[]{:S(2)}, u32[]{:S(2)}) async-start(f32[4,32,2048]{2,1,0:T(8,128)} %bitcast.11), calls=%async_computation | async-start | bytes 2097152 | tf_op jit(solution)/shard_map/all_to_all | solution.py:259
  37.0 19.3 %collective-permute-start.5 = (f32[3,8,128]{2,1,0:T(8,128)S(1)}, f32[3,8,128]{2,1,0:T(8,128)S(1)}, u32[]{:S(2)}, u32[]{:S(2)}) collective-permute-start(f32[3,8,128]{2,1,0:T(8,128)S(1)} %pad_maximum_fusion.13), channel_id=1, source_target_pairs={{0,128},{4,132},{8,136},{12,140},{16,144},{20,148},{24,152},{28,15... | collective-permute-start | bytes 36872 | tf_op jit(solution)/shard_map/ppermute | solution.py:48
  38.9 32.2 %collective-permute-start.4 = (f32[2,256,128]{2,1,0:T(8,128)S(1)}, f32[2,256,128]{2,1,0:T(8,128)S(1)}, u32[]{:S(2)}, u32[]{:S(2)}) collective-permute-start(f32[2,256,128]{2,1,0:T(8,128)S(1)} %pad_maximum_fusion.3), channel_id=1, source_target_pairs={{0,3},{1,2},{2,1},{3,0},{4,7},{5,6},{6,5},{7,4},{8,11},{9,10},{10,... | collective-permute-start | bytes 786440 | tf_op jit(solution)/shard_map/ppermute | solution.py:48
  42.8 28.3 %collective-permute-start.3 = (f32[2,256,128]{2,1,0:T(8,128)S(1)}, f32[2,256,128]{2,1,0:T(8,128)S(1)}, u32[]{:S(2)}, u32[]{:S(2)}) collective-permute-start(f32[2,256,128]{2,1,0:T(8,128)S(1)} %pad_maximum_fusion.3), channel_id=1, source_target_pairs={{0,2},{1,3},{2,0},{3,1},{4,6},{5,7},{6,4},{7,5},{8,10},{9,11},{10,... | collective-permute-start | bytes 786440 | tf_op jit(solution)/shard_map/ppermute | solution.py:48
  45.2 25.8 %collective-permute-start.2 = (f32[2,256,128]{2,1,0:T(8,128)S(1)}, f32[2,256,128]{2,1,0:T(8,128)S(1)}, u32[]{:S(2)}, u32[]{:S(2)}) collective-permute-start(f32[2,256,128]{2,1,0:T(8,128)S(1)} %pad_maximum_fusion.3), channel_id=1, source_target_pairs={{0,1},{1,0},{2,3},{3,2},{4,5},{5,4},{6,7},{7,6},{8,9},{9,8},{10,11... | collective-permute-start | bytes 786440 | tf_op jit(solution)/shard_map/ppermute | solution.py:48
  47.9 16.3 %collective-permute-start.7 = (f32[2,32,128]{2,1,0:T(8,128)S(1)}, f32[2,32,128]{2,1,0:T(8,128)S(1)}, u32[]{:S(2)}, u32[]{:S(2)}) collective-permute-start(f32[2,32,128]{2,1,0:T(8,128)S(1)} %pad_maximum_fusion.11), channel_id=1, source_target_pairs={{0,32},{4,36},{8,40},{12,44},{16,48},{20,52},{24,56},{28,60},{32,0... | collective-permute-start | bytes 98312 | tf_op jit(solution)/shard_map/ppermute | solution.py:48
  56.3 11.1 %collective-permute-start.6 = (f32[3,16,128]{2,1,0:T(8,128)S(1)}, f32[3,16,128]{2,1,0:T(8,128)S(1)}, u32[]{:S(2)}, u32[]{:S(2)}) collective-permute-start(f32[3,16,128]{2,1,0:T(8,128)S(1)} %pad_maximum_fusion.12), channel_id=1, source_target_pairs={{0,96},{4,100},{8,104},{12,108},{16,112},{20,116},{24,120},{28,124... | collective-permute-start | bytes 73736 | tf_op jit(solution)/shard_map/ppermute | solution.py:48
  64.2 6.2 %collective-permute-start.8 = (f32[2,64,128]{2,1,0:T(8,128)S(1)}, f32[2,64,128]{2,1,0:T(8,128)S(1)}, u32[]{:S(2)}, u32[]{:S(2)}) collective-permute-start(f32[2,64,128]{2,1,0:T(8,128)S(1)} %pad_maximum_fusion.9), channel_id=1, source_target_pairs={{0,16},{4,20},{8,24},{12,28},{16,0},{20,4},{24,8},{28,12},{32,48},... | collective-permute-start | bytes 196616 | tf_op jit(solution)/shard_map/ppermute | solution.py:48
  71.2 25.9 %collective-permute-start.9 = (f32[4,2,256,128]{3,2,1,0:T(8,128)S(1)}, f32[4,2,256,128]{3,2,1,0:T(8,128)S(1)}, u32[]{:S(2)}, u32[]{:S(2)}) collective-permute-start(f32[4,2,256,128]{3,2,1,0:T(8,128)S(1)} %pad_maximum_fusion.refs_1_.m1), channel_id=1, source_target_pairs={{0,4},{4,0},{8,12},{12,8},{16,20},{20,16},{24,28},{28,24},{32,36},... | collective-permute-start | bytes 3145736 | tf_op jit(solution)/shard_map/ppermute | solution.py:48
  75.5 12.9 %collective-permute-start.13 = (f32[3,32,128]{2,1,0:T(8,128)S(1)}, f32[3,32,128]{2,1,0:T(8,128)S(1)}, u32[]{:S(2)}, u32[]{:S(2)}) collective-permute-start(f32[3,32,128]{2,1,0:T(8,128)S(1)} %pad_maximum_fusion.10), channel_id=1, source_target_pairs={{0,32},{4,36},{8,40},{12,44},{16,48},{20,52},{24,56},{28,60},{32,0... | collective-permute-start | bytes 147464 | tf_op jit(solution)/shard_map/ppermute | solution.py:48
  81.5 11.0 %collective-permute-start.12 = (f32[32,1024]{1,0:T(8,128)S(1)}, f32[32,1024]{1,0:T(8,128)S(1)}, u32[]{:S(2)}, u32[]{:S(2)}) collective-permute-start(f32[32,1024]{1,0:T(8,128)S(1)} %reduce_sum.9), channel_id=1, source_target_pairs={{0,16},{4,20},{8,24},{12,28},{16,0},{20,4},{24,8},{28,12},{32,48},... | collective-permute-start | bytes 393224 | tf_op jit(solution)/shard_map/ppermute | solution.py:48
  84.6 15.4 %collective-permute-start.11 = (f32[2,128,128]{2,1,0:T(8,128)}, f32[2,128,128]{2,1,0:T(8,128)}, u32[]{:S(2)}, u32[]{:S(2)}) collective-permute-start(f32[2,128,128]{2,1,0:T(8,128)} %pad_maximum_fusion.7), channel_id=1, source_target_pairs={{0,8},{4,12},{8,0},{12,4},{16,24},{20,28},{24,16},{28,20},{32,40},... | collective-permute-start | bytes 393224 | tf_op jit(solution)/shard_map/ppermute | solution.py:48
  92.5 18.5 %collective-permute-start.14 = (f32[32,1024]{1,0:T(8,128)S(1)}, f32[32,1024]{1,0:T(8,128)S(1)}, u32[]{:S(2)}, u32[]{:S(2)}) collective-permute-start(f32[32,1024]{1,0:T(8,128)S(1)} %add.27.refs_2_), channel_id=1, source_target_pairs={{0,32},{4,36},{8,40},{12,44},{16,48},{20,52},{24,56},{28,60},{32,0... | collective-permute-start | bytes 393224 | tf_op jit(solution)/shard_map/ppermute | solution.py:48
  98.1 13.0 %collective-permute-start.10 = (f32[32,512]{1,0:T(8,128)S(1)}, f32[32,512]{1,0:T(8,128)S(1)}, u32[]{:S(2)}, u32[]{:S(2)}) collective-permute-start(f32[32,512]{1,0:T(8,128)S(1)} %get-tuple-element.47), channel_id=1, source_target_pairs={{0,16},{4,20},{8,24},{12,28},{16,0},{20,4},{24,8},{28,12},{32,48},... | collective-permute-start | bytes 196616 | tf_op jit(solution)/shard_map/ppermute | solution.py:48
  112.1 27.2 %all-to-all-start.1 = ((f32[4,2,256,128]{3,2,1,0:T(8,128)}), f32[4,2,256,128]{3,2,1,0:T(8,128)S(1)}, u32[]{:S(2)}, u32[]{:S(2)}) async-start(f32[4,2,256,128]{3,2,1,0:T(8,128)} %broadcast_in_dim.14), calls=%async_computation.1 | async-start | bytes 2097152 | tf_op jit(solution)/shard_map/all_to_all | solution.py:236
  116.1 55.3 %all-gather.3.cloned.1.call-start = ((), (), s32[]{:S(2)}) async-start(), calls=%async_computation.2 | async-start | bytes 1966080 | tf_op jit(solution)/shard_map/all_gather | solution.py:288
  116.1 8.0 %collective-permute-start.15 = (f32[3,64,128]{2,1,0:T(8,128)}, f32[3,64,128]{2,1,0:T(8,128)S(1)}, u32[]{:S(2)}, u32[]{:S(2)}) collective-permute-start(f32[3,64,128]{2,1,0:T(8,128)} %pad_maximum_fusion.8), channel_id=1, source_target_pairs={{0,16},{4,20},{8,24},{12,28},{16,0},{20,4},{24,8},{28,12},{32,48},... | collective-permute-start | bytes 294920 | tf_op jit(solution)/shard_map/ppermute | solution.py:48
  118.9 12.3 %collective-permute-start.16 = (f32[32,512]{1,0:T(8,128)S(1)}, f32[32,512]{1,0:T(8,128)S(1)}, u32[]{:S(2)}, u32[]{:S(2)}) collective-permute-start(f32[32,512]{1,0:T(8,128)S(1)} %add.28.refs_0_), channel_id=1, source_target_pairs={{0,32},{4,36},{8,40},{12,44},{16,48},{20,52},{24,56},{28,60},{32,0... | collective-permute-start | bytes 196616 | tf_op jit(solution)/shard_map/ppermute | solution.py:48
  131.8 6.7 %collective-permute-start.17 = (f32[3,128,128]{2,1,0:T(8,128)S(1)}, f32[3,128,128]{2,1,0:T(8,128)S(1)}, u32[]{:S(2)}, u32[]{:S(2)}) collective-permute-start(f32[3,128,128]{2,1,0:T(8,128)S(1)} %pad_maximum_fusion.5), channel_id=1, source_target_pairs={{0,8},{4,12},{8,0},{12,4},{16,24},{20,28},{24,16},{28,20},{32,40},... | collective-permute-start | bytes 589832 | tf_op jit(solution)/shard_map/ppermute | solution.py:48
  139.3 6.7 %collective-permute-start.18 = (f32[4,2,256,128]{3,2,1,0:T(8,128)S(1)}, f32[4,2,256,128]{3,2,1,0:T(8,128)S(1)}, u32[]{:S(2)}, u32[]{:S(2)}) collective-permute-start(f32[4,2,256,128]{3,2,1,0:T(8,128)S(1)} %all-to-all-done.1.refs_4_.m2), channel_id=1, source_target_pairs={{0,4},{4,0},{8,12},{12,8},{16,20},{20,16},{24,28},{28,24},{32,36},... | collective-permute-start | bytes 3145736 | tf_op jit(solution)/shard_map/ppermute | solution.py:48
  149.4 12.8 %collective-permute-start.19 = (f32[32,1024]{1,0:T(8,128)S(1)}, f32[32,1024]{1,0:T(8,128)S(1)}, u32[]{:S(2)}, u32[]{:S(2)}) collective-permute-start(f32[32,1024]{1,0:T(8,128)S(1)} %get-tuple-element.56), channel_id=1, source_target_pairs={{0,96},{4,100},{8,104},{12,108},{16,112},{20,116},{24,120},{28,124... | collective-permute-start | bytes 393224 | tf_op jit(solution)/shard_map/ppermute | solution.py:48
  162.2 27.4 %copy-start.14 = (f32[32,512]{1,0:T(8,128)S(1)}, f32[32,512]{1,0:T(8,128)}, u32[]{:S(2)}) copy-start(f32[32,512]{1,0:T(8,128)} %copy-done.13) | copy-start | bytes 196612
  171.4 9.6 %collective-permute-start.21 = (f32[4,3,256,128]{3,2,1,0:T(8,128)}, f32[4,3,256,128]{3,2,1,0:T(8,128)S(1)}, u32[]{:S(2)}, u32[]{:S(2)}) collective-permute-start(f32[4,3,256,128]{3,2,1,0:T(8,128)} %bitcast.32), channel_id=1, source_target_pairs={{0,4},{4,0},{8,12},{12,8},{16,20},{20,16},{24,28},{28,24},{32,36},... | collective-permute-start | bytes 4718600 | tf_op jit(solution)/shard_map/ppermute | solution.py:48
  174.0 7.0 %collective-permute-start.20 = (f32[32,1024]{1,0:T(8,128)S(1)}, f32[32,1024]{1,0:T(8,128)S(1)}, u32[]{:S(2)}, u32[]{:S(2)}) collective-permute-start(f32[32,1024]{1,0:T(8,128)S(1)} %add.29.refs_0_), channel_id=1, source_target_pairs={{0,128},{4,132},{8,136},{12,140},{16,144},{20,148},{24,152},{28,15... | collective-permute-start | bytes 393224 | tf_op jit(solution)/shard_map/ppermute | solution.py:48
  183.4 6.2 %collective-permute-start.22 = (f32[32,512]{1,0:T(8,128)S(1)}, f32[32,512]{1,0:T(8,128)S(1)}, u32[]{:S(2)}, u32[]{:S(2)}) collective-permute-start(f32[32,512]{1,0:T(8,128)S(1)} %get-tuple-element.60.right), channel_id=1, source_target_pairs={{0,384},{4,388},{8,392},{12,396},{16,400},{20,404},{24,408},{28,41... | collective-permute-start | bytes 196616 | tf_op jit(solution)/shard_map/ppermute | solution.py:48
  189.6 17.8 %copy-start.2 = (f32[21,128,128]{2,1,0:T(8,128)S(1)}, f32[21,128,128]{2,1,0:T(8,128)}, u32[]{:S(2)}) copy-start(f32[21,128,128]{2,1,0:T(8,128)} %blocks.3) | copy-start | bytes 4128772
  189.6 17.8 %copy-start.8 = (f32[7,128,128]{2,1,0:T(8,128)S(1)}, f32[7,128,128]{2,1,0:T(8,128)}, u32[]{:S(2)}) copy-start(f32[7,128,128]{2,1,0:T(8,128)} %inverse.3) | copy-start | bytes 1376260
  189.6 17.8 %copy-start.10 = (f32[896,128]{1,0:T(8,128)S(1)}, f32[896,128]{1,0:T(8,128)}, u32[]{:S(2)}) copy-start(f32[896,128]{1,0:T(8,128)} %copy-done.9) | copy-start | bytes 1376260
  193.2 7.9 %collective-permute-start.23 = (f32[32,2048]{1,0:T(8,128)S(1)}, f32[32,2048]{1,0:T(8,128)S(1)}, u32[]{:S(2)}, u32[]{:S(2)}) collective-permute-start(f32[32,2048]{1,0:T(8,128)S(1)} %shard_map.99), channel_id=1, source_target_pairs={{0,8},{4,12},{8,0},{12,4},{16,24},{20,28},{24,16},{28,20},{32,40},... | collective-permute-start | bytes 786440 | tf_op jit(solution)/shard_map/ppermute | solution.py:48
  201.1 6.3 %collective-permute-start.24 = (f32[2,32,2048]{2,1,0:T(8,128)S(1)}, f32[2,32,2048]{2,1,0:T(8,128)S(1)}, u32[]{:S(2)}, u32[]{:S(2)}) collective-permute-start(f32[2,32,2048]{2,1,0:T(8,128)S(1)} %pad_maximum_fusion.1.near), channel_id=1, source_target_pairs={{0,4},{4,0},{8,12},{12,8},{16,20},{20,16},{24,28},{28,24},{32,36},... | collective-permute-start | bytes 1572872 | tf_op jit(solution)/shard_map/ppermute | solution.py:48
  (17 other events, 64.7 us)
Sparse Core Ops, SparseCore 0:
  139.4 31.9 all-gather.2

commit v10 on v9

--- a/solution.py
+++ b/solution.py
@@ -126,10 +126,8 @@
             pending[earlier] = pending[earlier] - weight * mm(blocks[pair], solved, TN)
 
 
-def spots(start, count, turn=None):
-    if turn is None:
-        return [slice(start + r * 128, start + (r + 1) * 128) for r in range(count)]
-    return [pl.ds(pl.multiple_of(start + (turn ^ r) * 128, 128), 128) for r in range(count)]
+def spots(start, count):
+    return [slice(start + r * 128, start + (r + 1) * 128) for r in range(count)]
 
 
 def times_rows(value, places, mats, index):
@@ -160,7 +158,7 @@
     return total
 
 
-def level_kernel(index, turned, plane, *refs):
+def level_kernel(index, *refs):
     mine, other, z_out, v_out = refs[-4:]
     mats = (mine, other)
     count, width = z_out.shape
@@ -168,7 +166,7 @@
     both = [ref for ref in refs[:-4] if ref.shape[1] >= width + more]
     heads = [ref for ref in refs[:-4] if ref.shape[1] == width]
     rests = [ref for ref in refs[:-4] if width < ref.shape[1] < width + more]
-    places = spots(0, mine.shape[0], plane[0] if turned else None)
+    places = spots(0, mine.shape[0])
     z_out[...] = summed([ref[:, :width] for ref in both] + heads, count)
     v_out[...] = summed([ref[:, width : width + more] for ref in both] + rests, count)
     z = times_rows(z_out, places, mats, index)
@@ -177,21 +175,21 @@
         v_out[:, place] = v_out[:, place] - times_matrix(z, mats, index + 1, r)
 
 
-def top_kernel(plane, right, right_far, z1, z2, z3, m1, o1, m2, o2, m3, o3, x_out):
+def top_kernel(right, right_far, z1, z2, z3, m1, o1, m2, o2, m3, o3, x_out):
     width = right.shape[1]
     count = m3.shape[0]
     top = (m3, o3)
     z = times_rows(right[...] + right_far[...], spots(0, count), top, 0)
-    order = [(z3, top, 1, None), (z2, (m2, o2), 0, None), (z1, (m1, o1), 0, plane[0])]
-    mats, index, turn = top, 0, None
+    order = [(z3, top, 1), (z2, (m2, o2), 0), (z1, (m1, o1), 0)]
+    mats, index = top, 0
     level = 3
     while True:
-        for r, place in enumerate(spots(level * width, count, turn)):
+        for r, place in enumerate(spots(level * width, count)):
             x_out[:, place] = times_matrix(z, mats, index, r)
         if not order:
             break
-        held, mats, index, turn = order.pop(0)
-        moved = times_rows(x_out, spots(level * width, count, turn), mats, index + 1)
+        held, mats, index = order.pop(0)
+        moved = times_rows(x_out, spots(level * width, count), mats, index + 1)
         half = held.shape[1] // 2
         z = [held[:, :half] - moved[0], held[:, half:] - moved[1]]
         level -= 1
@@ -238,63 +236,50 @@
     tie = lax.optimization_barrier
     halves_z, wrap_z, wrap_y = 1 << Z4, (1 << Z8) | (1 << Z4), (1 << Y2) | (1 << Y1)
     near = [[g * 4 + m for m in range(4)] for g in range(leaves // 4)]
-    plane = lax.axis_index("col").astype(jnp.int32)[None]
-
-    def turned_planes(value):
-        return jnp.stack([value] + [swap(value, "col", r) for r in range(1, lax.axis_size("col"))])
-
-    def solve(index, turned, depth, *arrays):
+    def solve(index, depth, *arrays):
         outs = [(columns // 4, width), (columns // 4, depth * width)]
-        return call(functools.partial(level_kernel, index, turned), outs, plane, *arrays)
+        return call(functools.partial(level_kernel, index), outs, *arrays)
 
     first = grow(both(0), 1 << Z1)
     far = grow(rows(sep_inverse, 3)[None], wrap_y)
+    first = lax.all_gather(first, "col", axis=0)
     y, t = call(
         functools.partial(forward_kernel, sizes),
         [leaf_rhs.shape, (columns, LEVELS * width)],
         where, leaf_pattern, leaf_rhs, leaf_inverse, leaf_blocks, leaf_coupling, sep_rhs,
     )
-    t, first, far, second = tie((t, first, far, both(1)))
+    t, far, second = tie((t, far, both(1)))
 
     t = lax.all_to_all(t, "leaf", 0, 0, axis_index_groups=near, tiled=True)
     far = grow(jnp.concatenate([far, both(2)], 0), 1 << Y1)
     second = grow(second, halves_z)
-    first = turned_planes(first)
     far = grow(far, wrap_z)
     second = grow(second, 1 << Z2)
     t, first, far, second = tie((t, first, far, second))
 
-    upper = t[:, 2 * width :].reshape(4, columns // 4, 2 * width).sum(0)
-    upper_far = across(upper, 1 << Z2)
     first = (first, across(first, CORE_MASK))
     second = grow(second, 1 << Z1)
-    far = grow(far, halves_z)
-    upper, upper_far, far = tie((upper, upper_far, far))
-    upper = upper + upper_far
-    upper_far = across(upper, halves_z)
-    z1, v = solve(0, True, 1, t, *first)
+    far = grow(grow(far, halves_z), 1 << Z2)
+    z1, v = solve(0, 3, t, *first)
     v_far = across(v, 1 << Z2)
-    v, v_far, second, far, upper, upper_far = tie((v, v_far, second, far, upper, upper_far))
+    v, v_far, second, far = tie((v, v_far, second, far))
 
     second = planes(second)
     v = v + v_far
     v_far = across(v, halves_z)
-    far = grow(far, 1 << Z2)
-    far, v_far = tie((far, v_far))
-
     far = grow(far, 1 << Z1)
-    far, second = tie((far, second))
+    far, v_far, second = tie((far, v_far, second))
 
     third = lax.all_gather(far, "col", axis=0)
     second = (second, across(second, CORE_MASK))
-    z2, v = solve(0, False, 2, v, v_far, upper, upper_far, *second)
+    z2, v = solve(0, 2, v, v_far, *second)
     v = v + across(v, wrap_z)
     v, third = tie((v, third))
 
     third = (third, across(third, CORE_MASK))
-    z3, v = solve(1, False, 1, v, across(v, 1 << Y1), *third)
+    z3, v = solve(1, 1, v, across(v, 1 << Y1), *third)
     (x,) = call(
-        top_kernel, [(columns // 4, LEVELS * width)], plane, v, across(v, wrap_y), z1, z2, z3, *first, *second, *third
+        top_kernel, [(columns // 4, LEVELS * width)], v, across(v, wrap_y), z1, z2, z3, *first, *second, *third
     )
     x = jnp.stack([x, across(x, 1 << Z1)])
     return call(

time: 220 us -> 230 us (1.045)
  waiting for transfers between devices: 64.8 us -> 83.6 us
  other arithmetic: 6.17 us -> 1.68 us
  local copies, waits for them, and re-layouts: 17.1 us -> 12.8 us
    ppermute x25 -> x20, waiting for transfers between devices: 55.6 us -> 62.8 us  [swap(): lax.ppermute(value, axis, [(i, i ^ mask) for i in range(lax.axis_size(axi...]
    all_gather x0 -> x1, waiting for transfers between devices: none -> 6.29 us  [shards(): first = lax.all_gather(first, 'col', axis=0)]
    all_gather x1, waiting for transfers between devices: 9.16 us -> 14.5 us  [shards(): third = lax.all_gather(far, 'col', axis=0)]
    concatenate x10, other arithmetic: 4.04 us -> 1.58 us  [grow(): return jnp.concatenate([value, across(value, mask)], axis=1)]
    ppermute x25 -> x20, starting transfers between devices: 91.3 us -> 90 us  [swap(): lax.ppermute(value, axis, [(i, i ^ mask) for i in range(lax.axis_size(axi...]
    unnamed x42 -> x44, local copies, waits for them, and re-layouts: 11.4 us -> 10.2 us
  transfers between devices with their start and end apart: 28 -> 24, of which waited for: 13 -> 12; matrix products, arithmetic and copies ran while one was open for 5% -> 1% of each run, Pallas kernels for 3% -> 3%
where the time goes in v10:
time: 230 us; the launch traced here: 229 us
  starting transfers between devices  101 us (44%)
  waiting for transfers between devices  83.6 us (36%)
  Pallas kernels  15.7 us (7%)
  between operations  14.5 us (6%)
  local copies, waits for them, and re-layouts  12.8 us (6%)
    ppermute x20, starting transfers between devices, swap(): lax.ppermute(value, axis, [(i, i ^ mask) for i in range(lax.axis_size(axi...  90 us
    ppermute x20, waiting for transfers between devices, swap(): lax.ppermute(value, axis, [(i, i ^ mask) for i in range(lax.axis_size(axi...  62.8 us
    pallas_call x6, Pallas kernels, call(): pl.pallas_call(kernel, out_shape=[jax.ShapeDtypeStruct(s, F32) for s in o...  15.7 us
    all_gather x1, waiting for transfers between devices, shards(): third = lax.all_gather(far, 'col', axis=0)  14.5 us
    unnamed x44, local copies, waits for them, and re-layouts  10.2 us
    all_to_all x1, starting transfers between devices, shards(): t = lax.all_to_all(t, 'leaf', 0, 0, axis_index_groups=near, tiled=True)  6.95 us
    all_gather x1, waiting for transfers between devices, shards(): first = lax.all_gather(first, 'col', axis=0)  6.29 us
  transfers between devices with their start and end apart: 24, of which 12 were waited for; matrix products, arithmetic and copies ran while one was open for 1% of the time, Pallas kernels for 3%

profile of v10, /device:TPU:1, one launch (start us, length us, event | category | flops | bytes accessed | tf_op | source)
XLA Modules:
  0.0 228.8 jit_solution(7223983778331728204)
XLA Ops:
  7.9 5.5 %collective-permute-start = (f32[1,4,128]{2,1,0:T(4,128)S(1)}, f32[1,4,128]{2,1,0:T(4,128)S(1)}, u32[]{:S(2)}, u32[]{:S(2)}) collective-permute-start(f32[1,4,128]{2,1,0:T(4,128)S(1)} %slice_bitcast_fusion.6), channel_id=1, source_target_pairs={{0,384},{4,388},{8,392},{12,396},{16,400},{20,404},{24,408},{28,41... | collective-permute-start | bytes 6152 | tf_op jit(solution)/shard_map/ppermute | solution.py:48
  20.3 4.8 %shard_map.95 = (f32[896,128]{1,0:T(8,128)S(1)}, f32[128,2048]{1,0:T(8,128)}) custom-call(s32[5]{0:T(128)S(1)} %stack.56.where, s32[1,21]{1,0:T(1,128)S(1)} %copy-done.18, f32[896,128]{1,0:T(8,128)S(1)} %copy-done.12, f32[7,128,128]{2,1,0:T(8,128)S(1)} %copy-done.8, f32[21,128,128]{2,1,0:T(8,128)S(1)} %copy-done.2, f32[512,512]{1,0:T(8,128)S(1)} %copy-done.6, ...), custom_call_target="tpu_custom_call" | custom-call | tf_op jit(solution)/shard_map/pallas_call | solution.py:207
  25.9 7.0 %all-to-all-start = ((f32[4,32,2048]{2,1,0:T(8,128)}), f32[4,32,2048]{2,1,0:T(8,128)S(1)}, u32[]{:S(2)}, u32[]{:S(2)}) async-start(f32[4,32,2048]{2,1,0:T(8,128)} %bitcast.8), calls=%async_computation | async-start | bytes 2097152 | tf_op jit(solution)/shard_map/all_to_all | solution.py:253
  32.9 3.3 %collective-permute-start.1 = (f32[2,128,128]{2,1,0:T(8,128)S(1)}, f32[2,128,128]{2,1,0:T(8,128)S(1)}, u32[]{:S(2)}, u32[]{:S(2)}) collective-permute-start(f32[2,128,128]{2,1,0:T(8,128)S(1)} %pad_maximum_fusion.5), channel_id=1, source_target_pairs={{0,8},{4,12},{8,0},{12,4},{16,24},{20,28},{24,16},{28,20},{32,40},... | collective-permute-start | bytes 393224 | tf_op jit(solution)/shard_map/ppermute | solution.py:48
  36.2 13.0 %collective-permute-done.1 = f32[2,128,128]{2,1,0:T(8,128)S(1)} collective-permute-done((f32[2,128,128]{2,1,0:T(8,128)S(1)}, f32[2,128,128]{2,1,0:T(8,128)S(1)}, u32[]{:S(2)}, u32[]{:S(2)}) %collective-permute-start.1) | collective-permute-done | bytes 131104 | tf_op jit(solution)/shard_map/ppermute | solution.py:48
  52.0 6.4 %collective-permute-start.4 = (f32[2,32,128]{2,1,0:T(8,128)S(1)}, f32[2,32,128]{2,1,0:T(8,128)S(1)}, u32[]{:S(2)}, u32[]{:S(2)}) collective-permute-start(f32[2,32,128]{2,1,0:T(8,128)S(1)} %pad_maximum_fusion.10), channel_id=1, source_target_pairs={{0,32},{4,36},{8,40},{12,44},{16,48},{20,52},{24,56},{28,60},{32,0... | collective-permute-start | bytes 98312 | tf_op jit(solution)/shard_map/ppermute | solution.py:48
  58.5 8.8 %collective-permute-start.3 = (f32[3,16,128]{2,1,0:T(8,128)S(1)}, f32[3,16,128]{2,1,0:T(8,128)S(1)}, u32[]{:S(2)}, u32[]{:S(2)}) collective-permute-start(f32[3,16,128]{2,1,0:T(8,128)S(1)} %pad_maximum_fusion.11), channel_id=1, source_target_pairs={{0,96},{4,100},{8,104},{12,108},{16,112},{20,116},{24,120},{28,124... | collective-permute-start | bytes 73736 | tf_op jit(solution)/shard_map/ppermute | solution.py:48
  67.3 3.1 %collective-permute-start.5 = (f32[2,64,128]{2,1,0:T(8,128)S(1)}, f32[2,64,128]{2,1,0:T(8,128)S(1)}, u32[]{:S(2)}, u32[]{:S(2)}) collective-permute-start(f32[2,64,128]{2,1,0:T(8,128)S(1)} %pad_maximum_fusion.8), channel_id=1, source_target_pairs={{0,16},{4,20},{8,24},{12,28},{16,0},{20,4},{24,8},{28,12},{32,48},... | collective-permute-start | bytes 196616 | tf_op jit(solution)/shard_map/ppermute | solution.py:48
  70.5 3.9 %collective-permute-done.5 = f32[2,64,128]{2,1,0:T(8,128)S(1)} collective-permute-done((f32[2,64,128]{2,1,0:T(8,128)S(1)}, f32[2,64,128]{2,1,0:T(8,128)S(1)}, u32[]{:S(2)}, u32[]{:S(2)}) %collective-permute-start.5) | collective-permute-done | bytes 65568 | tf_op jit(solution)/shard_map/ppermute | solution.py:48
  74.3 6.3 %all-gather.5.cloned.1.call-done = f32[8,256,128]{2,1,0:T(8,128)} async-done(((f32[2,256,128]{2,1,0:T(8,128)}), f32[8,256,128]{2,1,0:T(8,128)}) %all-gather.5.cloned.1.call-update) | async-done | bytes 1048592 | tf_op jit(solution)/shard_map/all_gather | solution.py:245
  80.6 3.5 %collective-permute-start.6 = (f32[4,2,256,128]{3,2,1,0:T(8,128)}, f32[4,2,256,128]{3,2,1,0:T(8,128)S(1)}, u32[]{:S(2)}, u32[]{:S(2)}) collective-permute-start(f32[4,2,256,128]{3,2,1,0:T(8,128)} %bitcast.28), channel_id=1, source_target_pairs={{0,4},{4,0},{8,12},{12,8},{16,20},{20,16},{24,28},{28,24},{32,36},... | collective-permute-start | bytes 3145736 | tf_op jit(solution)/shard_map/ppermute | solution.py:48
  84.1 7.4 %collective-permute-start.9 = (f32[3,32,128]{2,1,0:T(8,128)S(1)}, f32[3,32,128]{2,1,0:T(8,128)S(1)}, u32[]{:S(2)}, u32[]{:S(2)}) collective-permute-start(f32[3,32,128]{2,1,0:T(8,128)S(1)} %pad_maximum_fusion.9), channel_id=1, source_target_pairs={{0,32},{4,36},{8,40},{12,44},{16,48},{20,52},{24,56},{28,60},{32,0... | collective-permute-start | bytes 147464 | tf_op jit(solution)/shard_map/ppermute | solution.py:48
  91.5 3.2 %collective-permute-start.8 = (f32[2,128,128]{2,1,0:T(8,128)S(1)}, f32[2,128,128]{2,1,0:T(8,128)S(1)}, u32[]{:S(2)}, u32[]{:S(2)}) collective-permute-start(f32[2,128,128]{2,1,0:T(8,128)S(1)} %pad_maximum_fusion.6), channel_id=1, source_target_pairs={{0,8},{4,12},{8,0},{12,4},{16,24},{20,28},{24,16},{28,20},{32,40},... | collective-permute-start | bytes 393224 | tf_op jit(solution)/shard_map/ppermute | solution.py:48
  94.7 4.4 %collective-permute-start.10 = (f32[3,64,128]{2,1,0:T(8,128)S(1)}, f32[3,64,128]{2,1,0:T(8,128)S(1)}, u32[]{:S(2)}, u32[]{:S(2)}) collective-permute-start(f32[3,64,128]{2,1,0:T(8,128)S(1)} %pad_maximum_fusion.7), channel_id=1, source_target_pairs={{0,16},{4,20},{8,24},{12,28},{16,0},{20,4},{24,8},{28,12},{32,48},... | collective-permute-start | bytes 294920 | tf_op jit(solution)/shard_map/ppermute | solution.py:48
  103.3 10.7 %collective-permute-done.7 = f32[32,1536]{1,0:T(8,128)S(1)} collective-permute-done((f32[32,1536]{1,0:T(8,128)S(1)}, f32[32,1536]{1,0:T(8,128)S(1)}, u32[]{:S(2)}, u32[]{:S(2)}) %collective-permute-start.7) | collective-permute-done | bytes 196640 | tf_op jit(solution)/shard_map/ppermute | solution.py:48
  115.1 3.5 %all-to-all-start.1 = ((f32[4,2,256,128]{3,2,1,0:T(8,128)}), f32[4,2,256,128]{3,2,1,0:T(8,128)S(1)}, u32[]{:S(2)}, u32[]{:S(2)}) async-start(f32[4,2,256,128]{3,2,1,0:T(8,128)} %broadcast_in_dim.10), calls=%async_computation.1 | async-start | bytes 2097152 | tf_op jit(solution)/shard_map/all_to_all | solution.py:234
  120.6 8.0 %collective-permute-start.12 = (f32[32,1536]{1,0:T(8,128)S(1)}, f32[32,1536]{1,0:T(8,128)S(1)}, u32[]{:S(2)}, u32[]{:S(2)}) collective-permute-start(f32[32,1536]{1,0:T(8,128)S(1)} %add.24.refs_0_), channel_id=1, source_target_pairs={{0,32},{4,36},{8,40},{12,44},{16,48},{20,52},{24,56},{28,60},{32,0... | collective-permute-start | bytes 589832 | tf_op jit(solution)/shard_map/ppermute | solution.py:48
  129.4 12.8 %collective-permute-done.12.refs_1_ = f32[32,1536]{1,0:T(8,128)S(1)} collective-permute-done((f32[32,1536]{1,0:T(8,128)S(1)}, f32[32,1536]{1,0:T(8,128)S(1)}, u32[]{:S(2)}, u32[]{:S(2)}) %collective-permute-start.12) | collective-permute-done | bytes 196640 | tf_op jit(solution)/shard_map/ppermute | solution.py:48
  142.3 6.8 %collective-permute-start.13 = (f32[4,2,256,128]{3,2,1,0:T(8,128)S(1)}, f32[4,2,256,128]{3,2,1,0:T(8,128)S(1)}, u32[]{:S(2)}, u32[]{:S(2)}) collective-permute-start(f32[4,2,256,128]{3,2,1,0:T(8,128)S(1)} %all-to-all-done.1.refs_2_.m2), channel_id=1, source_target_pairs={{0,4},{4,0},{8,12},{12,8},{16,20},{20,16},{24,28},{28,24},{32,36},... | collective-permute-start | bytes 3145736 | tf_op jit(solution)/shard_map/ppermute | solution.py:48
  149.1 2.3 collective-permute-done.13.refs_3_.o2
  152.9 5.8 %collective-permute-start.14 = (f32[32,1024]{1,0:T(8,128)S(1)}, f32[32,1024]{1,0:T(8,128)S(1)}, u32[]{:S(2)}, u32[]{:S(2)}) collective-permute-start(f32[32,1024]{1,0:T(8,128)S(1)} %get-tuple-element.42), channel_id=1, source_target_pairs={{0,96},{4,100},{8,104},{12,108},{16,112},{20,116},{24,120},{28,124... | collective-permute-start | bytes 393224 | tf_op jit(solution)/shard_map/ppermute | solution.py:48
  158.7 8.2 %collective-permute-done.14 = f32[32,1024]{1,0:T(8,128)S(1)} collective-permute-done((f32[32,1024]{1,0:T(8,128)S(1)}, f32[32,1024]{1,0:T(8,128)S(1)}, u32[]{:S(2)}, u32[]{:S(2)}) %collective-permute-start.14) | collective-permute-done | bytes 131104 | tf_op jit(solution)/shard_map/ppermute | solution.py:48
  167.0 14.5 %all-gather.7.cloned.1.call-done = f32[12,256,128]{2,1,0:T(8,128)} async-done(((f32[3,256,128]{2,1,0:T(8,128)}), f32[12,256,128]{2,1,0:T(8,128)}) %all-gather.7.cloned.1.call-update) | async-done | bytes 1572880 | tf_op jit(solution)/shard_map/all_gather | solution.py:273
  181.4 2.6 %collective-permute-start.16 = (f32[4,3,256,128]{3,2,1,0:T(8,128)}, f32[4,3,256,128]{3,2,1,0:T(8,128)S(1)}, u32[]{:S(2)}, u32[]{:S(2)}) collective-permute-start(f32[4,3,256,128]{3,2,1,0:T(8,128)} %bitcast.25), channel_id=1, source_target_pairs={{0,4},{4,0},{8,12},{12,8},{16,20},{20,16},{24,28},{28,24},{32,36},... | collective-permute-start | bytes 4718600 | tf_op jit(solution)/shard_map/ppermute | solution.py:48
  184.0 3.1 %collective-permute-start.15 = (f32[32,1024]{1,0:T(8,128)S(1)}, f32[32,1024]{1,0:T(8,128)S(1)}, u32[]{:S(2)}, u32[]{:S(2)}) collective-permute-start(f32[32,1024]{1,0:T(8,128)S(1)} %add.25.refs_0_), channel_id=1, source_target_pairs={{0,128},{4,132},{8,136},{12,140},{16,144},{20,148},{24,152},{28,15... | collective-permute-start | bytes 393224 | tf_op jit(solution)/shard_map/ppermute | solution.py:48
  187.1 3.9 %collective-permute-done.15.refs_1_ = f32[32,1024]{1,0:T(8,128)S(1)} collective-permute-done((f32[32,1024]{1,0:T(8,128)S(1)}, f32[32,1024]{1,0:T(8,128)S(1)}, u32[]{:S(2)}, u32[]{:S(2)}) %collective-permute-start.15) | collective-permute-done | bytes 131104 | tf_op jit(solution)/shard_map/ppermute | solution.py:48
  193.4 4.4 %collective-permute-start.17 = (f32[32,512]{1,0:T(8,128)S(1)}, f32[32,512]{1,0:T(8,128)S(1)}, u32[]{:S(2)}, u32[]{:S(2)}) collective-permute-start(f32[32,512]{1,0:T(8,128)S(1)} %get-tuple-element.46.right), channel_id=1, source_target_pairs={{0,384},{4,388},{8,392},{12,396},{16,400},{20,404},{24,408},{28,41... | collective-permute-start | bytes 196616 | tf_op jit(solution)/shard_map/ppermute | solution.py:48
  199.7 3.4 %shard_map.99 = f32[32,2048]{1,0:T(8,128)S(1)} custom-call(f32[32,512]{1,0:T(8,128)S(1)} %get-tuple-element.46.right, f32[32,512]{1,0:T(8,128)S(1)} %collective-permute-done.17.right_far, f32[32,512]{1,0:T(8,128)S(1)} %copy-done.15, f32[32,512]{1,0:T(8,128)S(1)} %copy-done.17, f32[32,512]{1,0:T(8,128)S(1)} %get-tuple-element.49.z3, ...), custom_call_target="tpu_custom_call" | custom-call | tf_op jit(solution)/shard_map/pallas_call | solution.py:207
  203.1 3.3 %collective-permute-start.18 = (f32[32,2048]{1,0:T(8,128)S(1)}, f32[32,2048]{1,0:T(8,128)S(1)}, u32[]{:S(2)}, u32[]{:S(2)}) collective-permute-start(f32[32,2048]{1,0:T(8,128)S(1)} %shard_map.99), channel_id=1, source_target_pairs={{0,8},{4,12},{8,0},{12,4},{16,24},{20,28},{24,16},{28,20},{32,40},... | collective-permute-start | bytes 786440 | tf_op jit(solution)/shard_map/ppermute | solution.py:48
  206.4 4.6 %collective-permute-done.18 = f32[32,2048]{1,0:T(8,128)S(1)} collective-permute-done((f32[32,2048]{1,0:T(8,128)S(1)}, f32[32,2048]{1,0:T(8,128)S(1)}, u32[]{:S(2)}, u32[]{:S(2)}) %collective-permute-start.18) | collective-permute-done | bytes 262176 | tf_op jit(solution)/shard_map/ppermute | solution.py:48
  211.0 4.8 %collective-permute-start.19 = (f32[2,32,2048]{2,1,0:T(8,128)S(1)}, f32[2,32,2048]{2,1,0:T(8,128)S(1)}, u32[]{:S(2)}, u32[]{:S(2)}) collective-permute-start(f32[2,32,2048]{2,1,0:T(8,128)S(1)} %pad_maximum_fusion.near), channel_id=1, source_target_pairs={{0,4},{4,0},{8,12},{12,8},{16,20},{20,16},{24,28},{28,24},{32,36},... | collective-permute-start | bytes 1572872 | tf_op jit(solution)/shard_map/ppermute | solution.py:48
  217.3 4.6 %shard_map.100 = (f32[896,128]{1,0:T(8,128)}, f32[172,128]{1,0:T(8,128)}) custom-call(s32[5]{0:T(128)S(1)} %stack.56.where, s32[1,21]{1,0:T(1,128)S(1)} %copy-done.19, f32[896,128]{1,0:T(8,128)S(1)} %copy-done.11, f32[2,32,2048]{2,1,0:T(8,128)S(1)} %pad_maximum_fusion.near, f32[2,32,2048]{2,1,0:T(8,128)S(1)} %collective-permute-done.19.across_core, ...), custom_call_target="tpu_custom_call" | custom-call | tf_op jit(solution)/shard_map/pallas_call | solution.py:207
  (92 shorter events, 26.6 us)
Async XLA Ops:
  7.9 18.1 %collective-permute-start = (f32[1,4,128]{2,1,0:T(4,128)S(1)}, f32[1,4,128]{2,1,0:T(4,128)S(1)}, u32[]{:S(2)}, u32[]{:S(2)}) collective-permute-start(f32[1,4,128]{2,1,0:T(4,128)S(1)} %slice_bitcast_fusion.6), channel_id=1, source_target_pairs={{0,384},{4,388},{8,392},{12,396},{16,400},{20,404},{24,408},{28,41... | collective-permute-start | bytes 6152 | tf_op jit(solution)/shard_map/ppermute | solution.py:48
  25.9 54.7 %all-to-all-start = ((f32[4,32,2048]{2,1,0:T(8,128)}), f32[4,32,2048]{2,1,0:T(8,128)S(1)}, u32[]{:S(2)}, u32[]{:S(2)}) async-start(f32[4,32,2048]{2,1,0:T(8,128)} %bitcast.8), calls=%async_computation | async-start | bytes 2097152 | tf_op jit(solution)/shard_map/all_to_all | solution.py:253
  32.9 47.8 %all-gather.5.cloned.1.call-start = ((), (), s32[]{:S(2)}) async-start(), calls=%async_computation.2 | async-start | bytes 1310720 | tf_op jit(solution)/shard_map/all_gather | solution.py:245
  32.9 16.3 %collective-permute-start.1 = (f32[2,128,128]{2,1,0:T(8,128)S(1)}, f32[2,128,128]{2,1,0:T(8,128)S(1)}, u32[]{:S(2)}, u32[]{:S(2)}) collective-permute-start(f32[2,128,128]{2,1,0:T(8,128)S(1)} %pad_maximum_fusion.5), channel_id=1, source_target_pairs={{0,8},{4,12},{8,0},{12,4},{16,24},{20,28},{24,16},{28,20},{32,40},... | collective-permute-start | bytes 393224 | tf_op jit(solution)/shard_map/ppermute | solution.py:48
  50.1 8.4 %collective-permute-start.2 = (f32[3,8,128]{2,1,0:T(8,128)S(1)}, f32[3,8,128]{2,1,0:T(8,128)S(1)}, u32[]{:S(2)}, u32[]{:S(2)}) collective-permute-start(f32[3,8,128]{2,1,0:T(8,128)S(1)} %pad_maximum_fusion.12), channel_id=1, source_target_pairs={{0,128},{4,132},{8,136},{12,140},{16,144},{20,148},{24,152},{28,15... | collective-permute-start | bytes 36872 | tf_op jit(solution)/shard_map/ppermute | solution.py:48
  52.0 15.3 %collective-permute-start.4 = (f32[2,32,128]{2,1,0:T(8,128)S(1)}, f32[2,32,128]{2,1,0:T(8,128)S(1)}, u32[]{:S(2)}, u32[]{:S(2)}) collective-permute-start(f32[2,32,128]{2,1,0:T(8,128)S(1)} %pad_maximum_fusion.10), channel_id=1, source_target_pairs={{0,32},{4,36},{8,40},{12,44},{16,48},{20,52},{24,56},{28,60},{32,0... | collective-permute-start | bytes 98312 | tf_op jit(solution)/shard_map/ppermute | solution.py:48
  58.5 12.0 %collective-permute-start.3 = (f32[3,16,128]{2,1,0:T(8,128)S(1)}, f32[3,16,128]{2,1,0:T(8,128)S(1)}, u32[]{:S(2)}, u32[]{:S(2)}) collective-permute-start(f32[3,16,128]{2,1,0:T(8,128)S(1)} %pad_maximum_fusion.11), channel_id=1, source_target_pairs={{0,96},{4,100},{8,104},{12,108},{16,112},{20,116},{24,120},{28,124... | collective-permute-start | bytes 73736 | tf_op jit(solution)/shard_map/ppermute | solution.py:48
  67.3 7.0 %collective-permute-start.5 = (f32[2,64,128]{2,1,0:T(8,128)S(1)}, f32[2,64,128]{2,1,0:T(8,128)S(1)}, u32[]{:S(2)}, u32[]{:S(2)}) collective-permute-start(f32[2,64,128]{2,1,0:T(8,128)S(1)} %pad_maximum_fusion.8), channel_id=1, source_target_pairs={{0,16},{4,20},{8,24},{12,28},{16,0},{20,4},{24,8},{28,12},{32,48},... | collective-permute-start | bytes 196616 | tf_op jit(solution)/shard_map/ppermute | solution.py:48
  80.6 18.5 %collective-permute-start.6 = (f32[4,2,256,128]{3,2,1,0:T(8,128)}, f32[4,2,256,128]{3,2,1,0:T(8,128)S(1)}, u32[]{:S(2)}, u32[]{:S(2)}) collective-permute-start(f32[4,2,256,128]{3,2,1,0:T(8,128)} %bitcast.28), channel_id=1, source_target_pairs={{0,4},{4,0},{8,12},{12,8},{16,20},{20,16},{24,28},{28,24},{32,36},... | collective-permute-start | bytes 3145736 | tf_op jit(solution)/shard_map/ppermute | solution.py:48
  84.1 10.6 %collective-permute-start.9 = (f32[3,32,128]{2,1,0:T(8,128)S(1)}, f32[3,32,128]{2,1,0:T(8,128)S(1)}, u32[]{:S(2)}, u32[]{:S(2)}) collective-permute-start(f32[3,32,128]{2,1,0:T(8,128)S(1)} %pad_maximum_fusion.9), channel_id=1, source_target_pairs={{0,32},{4,36},{8,40},{12,44},{16,48},{20,52},{24,56},{28,60},{32,0... | collective-permute-start | bytes 147464 | tf_op jit(solution)/shard_map/ppermute | solution.py:48
  91.5 11.8 %collective-permute-start.8 = (f32[2,128,128]{2,1,0:T(8,128)S(1)}, f32[2,128,128]{2,1,0:T(8,128)S(1)}, u32[]{:S(2)}, u32[]{:S(2)}) collective-permute-start(f32[2,128,128]{2,1,0:T(8,128)S(1)} %pad_maximum_fusion.6), channel_id=1, source_target_pairs={{0,8},{4,12},{8,0},{12,4},{16,24},{20,28},{24,16},{28,20},{32,40},... | collective-permute-start | bytes 393224 | tf_op jit(solution)/shard_map/ppermute | solution.py:48
  94.7 8.6 %collective-permute-start.10 = (f32[3,64,128]{2,1,0:T(8,128)S(1)}, f32[3,64,128]{2,1,0:T(8,128)S(1)}, u32[]{:S(2)}, u32[]{:S(2)}) collective-permute-start(f32[3,64,128]{2,1,0:T(8,128)S(1)} %pad_maximum_fusion.7), channel_id=1, source_target_pairs={{0,16},{4,20},{8,24},{12,28},{16,0},{20,4},{24,8},{28,12},{32,48},... | collective-permute-start | bytes 294920 | tf_op jit(solution)/shard_map/ppermute | solution.py:48
  101.3 12.7 %copy-start.14 = (f32[32,512]{1,0:T(8,128)}, f32[32,512]{1,0:T(8,128)S(1)}, u32[]{:S(2)}) copy-start(f32[32,512]{1,0:T(8,128)S(1)} %get-tuple-element.47.z1) | copy-start | bytes 196612
  101.3 12.7 %collective-permute-start.7 = (f32[32,1536]{1,0:T(8,128)S(1)}, f32[32,1536]{1,0:T(8,128)S(1)}, u32[]{:S(2)}, u32[]{:S(2)}) collective-permute-start(f32[32,1536]{1,0:T(8,128)S(1)} %get-tuple-element.36), channel_id=1, source_target_pairs={{0,16},{4,20},{8,24},{12,28},{16,0},{20,4},{24,8},{28,12},{32,48},... | collective-permute-start | bytes 589832 | tf_op jit(solution)/shard_map/ppermute | solution.py:48
  115.1 27.2 %all-to-all-start.1 = ((f32[4,2,256,128]{3,2,1,0:T(8,128)}), f32[4,2,256,128]{3,2,1,0:T(8,128)S(1)}, u32[]{:S(2)}, u32[]{:S(2)}) async-start(f32[4,2,256,128]{3,2,1,0:T(8,128)} %broadcast_in_dim.10), calls=%async_computation.1 | async-start | bytes 2097152 | tf_op jit(solution)/shard_map/all_to_all | solution.py:234
  118.6 62.8 %all-gather.7.cloned.1.call-start = ((), (), s32[]{:S(2)}) async-start(), calls=%async_computation.3 | async-start | bytes 1966080 | tf_op jit(solution)/shard_map/all_gather | solution.py:273
  118.7 10.0 %collective-permute-start.11 = (f32[3,128,128]{2,1,0:T(8,128)S(1)}, f32[3,128,128]{2,1,0:T(8,128)S(1)}, u32[]{:S(2)}, u32[]{:S(2)}) collective-permute-start(f32[3,128,128]{2,1,0:T(8,128)S(1)} %pad_maximum_fusion.4), channel_id=1, source_target_pairs={{0,8},{4,12},{8,0},{12,4},{16,24},{20,28},{24,16},{28,20},{32,40},... | collective-permute-start | bytes 589832 | tf_op jit(solution)/shard_map/ppermute | solution.py:48
  120.6 21.6 %collective-permute-start.12 = (f32[32,1536]{1,0:T(8,128)S(1)}, f32[32,1536]{1,0:T(8,128)S(1)}, u32[]{:S(2)}, u32[]{:S(2)}) collective-permute-start(f32[32,1536]{1,0:T(8,128)S(1)} %add.24.refs_0_), channel_id=1, source_target_pairs={{0,32},{4,36},{8,40},{12,44},{16,48},{20,52},{24,56},{28,60},{32,0... | collective-permute-start | bytes 589832 | tf_op jit(solution)/shard_map/ppermute | solution.py:48
  142.3 9.0 %collective-permute-start.13 = (f32[4,2,256,128]{3,2,1,0:T(8,128)S(1)}, f32[4,2,256,128]{3,2,1,0:T(8,128)S(1)}, u32[]{:S(2)}, u32[]{:S(2)}) collective-permute-start(f32[4,2,256,128]{3,2,1,0:T(8,128)S(1)} %all-to-all-done.1.refs_2_.m2), channel_id=1, source_target_pairs={{0,4},{4,0},{8,12},{12,8},{16,20},{20,16},{24,28},{28,24},{32,36},... | collective-permute-start | bytes 3145736 | tf_op jit(solution)/shard_map/ppermute | solution.py:48
  152.9 14.0 %collective-permute-start.14 = (f32[32,1024]{1,0:T(8,128)S(1)}, f32[32,1024]{1,0:T(8,128)S(1)}, u32[]{:S(2)}, u32[]{:S(2)}) collective-permute-start(f32[32,1024]{1,0:T(8,128)S(1)} %get-tuple-element.42), channel_id=1, source_target_pairs={{0,96},{4,100},{8,104},{12,108},{16,112},{20,116},{24,120},{28,124... | collective-permute-start | bytes 393224 | tf_op jit(solution)/shard_map/ppermute | solution.py:48
  166.9 32.7 %copy-start.15 = (f32[32,512]{1,0:T(8,128)S(1)}, f32[32,512]{1,0:T(8,128)}, u32[]{:S(2)}) copy-start(f32[32,512]{1,0:T(8,128)} %copy-done.14) | copy-start | bytes 196612
  166.9 32.7 %copy-start.17 = (f32[32,512]{1,0:T(8,128)S(1)}, f32[32,512]{1,0:T(8,128)}, u32[]{:S(2)}) copy-start(f32[32,512]{1,0:T(8,128)} %copy-done.16) | copy-start | bytes 196612
  181.4 9.6 %collective-permute-start.16 = (f32[4,3,256,128]{3,2,1,0:T(8,128)}, f32[4,3,256,128]{3,2,1,0:T(8,128)S(1)}, u32[]{:S(2)}, u32[]{:S(2)}) collective-permute-start(f32[4,3,256,128]{3,2,1,0:T(8,128)} %bitcast.25), channel_id=1, source_target_pairs={{0,4},{4,0},{8,12},{12,8},{16,20},{20,16},{24,28},{28,24},{32,36},... | collective-permute-start | bytes 4718600 | tf_op jit(solution)/shard_map/ppermute | solution.py:48
  184.0 7.0 %collective-permute-start.15 = (f32[32,1024]{1,0:T(8,128)S(1)}, f32[32,1024]{1,0:T(8,128)S(1)}, u32[]{:S(2)}, u32[]{:S(2)}) collective-permute-start(f32[32,1024]{1,0:T(8,128)S(1)} %add.25.refs_0_), channel_id=1, source_target_pairs={{0,128},{4,132},{8,136},{12,140},{16,144},{20,148},{24,152},{28,15... | collective-permute-start | bytes 393224 | tf_op jit(solution)/shard_map/ppermute | solution.py:48
  193.4 6.2 %collective-permute-start.17 = (f32[32,512]{1,0:T(8,128)S(1)}, f32[32,512]{1,0:T(8,128)S(1)}, u32[]{:S(2)}, u32[]{:S(2)}) collective-permute-start(f32[32,512]{1,0:T(8,128)S(1)} %get-tuple-element.46.right), channel_id=1, source_target_pairs={{0,384},{4,388},{8,392},{12,396},{16,400},{20,404},{24,408},{28,41... | collective-permute-start | bytes 196616 | tf_op jit(solution)/shard_map/ppermute | solution.py:48
  199.6 17.7 %copy-start.3 = (f32[21,128,128]{2,1,0:T(8,128)S(1)}, f32[21,128,128]{2,1,0:T(8,128)}, u32[]{:S(2)}) copy-start(f32[21,128,128]{2,1,0:T(8,128)} %blocks.3) | copy-start | bytes 4128772
  199.6 17.7 %copy-start.9 = (f32[7,128,128]{2,1,0:T(8,128)S(1)}, f32[7,128,128]{2,1,0:T(8,128)}, u32[]{:S(2)}) copy-start(f32[7,128,128]{2,1,0:T(8,128)} %inverse.3) | copy-start | bytes 1376260
  199.7 17.7 %copy-start.11 = (f32[896,128]{1,0:T(8,128)S(1)}, f32[896,128]{1,0:T(8,128)}, u32[]{:S(2)}) copy-start(f32[896,128]{1,0:T(8,128)} %copy-done.10) | copy-start | bytes 1376260
  199.7 17.7 %copy-start.19 = (s32[1,21]{1,0:T(1,128)S(1)}, s32[1,21]{1,0:T(1,128)}, u32[]{:S(2)}) copy-start(s32[1,21]{1,0:T(1,128)} %pattern.3) | copy-start | bytes 256
  203.1 14.2 %copy-start.7 = (f32[512,512]{1,0:T(8,128)S(1)}, f32[512,512]{1,0:T(8,128)}, u32[]{:S(2)}) copy-start(f32[512,512]{1,0:T(8,128)} %coupling.3) | copy-start | bytes 3145732
  203.1 7.9 %collective-permute-start.18 = (f32[32,2048]{1,0:T(8,128)S(1)}, f32[32,2048]{1,0:T(8,128)S(1)}, u32[]{:S(2)}, u32[]{:S(2)}) collective-permute-start(f32[32,2048]{1,0:T(8,128)S(1)} %shard_map.99), channel_id=1, source_target_pairs={{0,8},{4,12},{8,0},{12,4},{16,24},{20,28},{24,16},{28,20},{32,40},... | collective-permute-start | bytes 786440 | tf_op jit(solution)/shard_map/ppermute | solution.py:48
  211.0 6.3 %collective-permute-start.19 = (f32[2,32,2048]{2,1,0:T(8,128)S(1)}, f32[2,32,2048]{2,1,0:T(8,128)S(1)}, u32[]{:S(2)}, u32[]{:S(2)}) collective-permute-start(f32[2,32,2048]{2,1,0:T(8,128)S(1)} %pad_maximum_fusion.near), channel_id=1, source_target_pairs={{0,4},{4,0},{8,12},{12,8},{16,20},{20,16},{24,28},{28,24},{32,36},... | collective-permute-start | bytes 1572872 | tf_op jit(solution)/shard_map/ppermute | solution.py:48
  (14 other events, 38.5 us)
Sparse Core Ops, SparseCore 0:
  50.1 30.4 all-gather.4
  142.4 38.9 all-gather.6

commit v11 on v9

--- a/solution.py
+++ b/solution.py
@@ -254,38 +254,34 @@
         [leaf_rhs.shape, (columns, LEVELS * width)],
         where, leaf_pattern, leaf_rhs, leaf_inverse, leaf_blocks, leaf_coupling, sep_rhs,
     )
-    t, first, far, second = tie((t, first, far, both(1)))
+    t, first, far = tie((t, first, far))
 
     t = lax.all_to_all(t, "leaf", 0, 0, axis_index_groups=near, tiled=True)
+    first = turned_planes(first)
     far = grow(jnp.concatenate([far, both(2)], 0), 1 << Y1)
-    second = grow(second, halves_z)
-    first = turned_planes(first)
     far = grow(far, wrap_z)
-    second = grow(second, 1 << Z2)
-    t, first, far, second = tie((t, first, far, second))
-
+    t, first, far = tie((t, first, far))
+
+    first = (first, across(first, CORE_MASK))
     upper = t[:, 2 * width :].reshape(4, columns // 4, 2 * width).sum(0)
     upper_far = across(upper, 1 << Z2)
-    first = (first, across(first, CORE_MASK))
-    second = grow(second, 1 << Z1)
-    far = grow(far, halves_z)
-    upper, upper_far, far = tie((upper, upper_far, far))
+    far = grow(jnp.concatenate([far, both(1)], 0), halves_z)
+    z1, v = solve(0, True, 1, t, *first)
+    v, far, upper, upper_far = tie((v, far, upper, upper_far))
+
     upper = upper + upper_far
+    v_far = across(v, 1 << Z2)
     upper_far = across(upper, halves_z)
-    z1, v = solve(0, True, 1, t, *first)
-    v_far = across(v, 1 << Z2)
-    v, v_far, second, far, upper, upper_far = tie((v, v_far, second, far, upper, upper_far))
-
+    far = grow(grow(far, 1 << Z2), 1 << Z1)
+    v = v + v_far
+    far, v, upper, upper_far = tie((far, v, upper, upper_far))
+
+    second, third = far[3:], far[:3]
     second = planes(second)
-    v = v + v_far
     v_far = across(v, halves_z)
-    far = grow(far, 1 << Z2)
-    far, v_far = tie((far, v_far))
-
-    far = grow(far, 1 << Z1)
-    far, second = tie((far, second))
-
-    third = lax.all_gather(far, "col", axis=0)
+    second, third, v_far = tie((second, third, v_far))
+
+    third = lax.all_gather(third, "col", axis=0)
     second = (second, across(second, CORE_MASK))
     z2, v = solve(0, False, 2, v, v_far, upper, upper_far, *second)
     v = v + across(v, wrap_z)

time: 220 us -> 221 us (level)
  waiting for transfers between devices: 64.8 us -> 75.1 us
  starting transfers between devices: 101 us -> 92.4 us
  other arithmetic: 6.17 us -> 2.93 us
    ppermute x25 -> x22, starting transfers between devices: 91.3 us -> 83.2 us  [swap(): lax.ppermute(value, axis, [(i, i ^ mask) for i in range(lax.axis_size(axi...]
    ppermute x25 -> x22, waiting for transfers between devices: 55.6 us -> 62.2 us  [swap(): lax.ppermute(value, axis, [(i, i ^ mask) for i in range(lax.axis_size(axi...]
    all_to_all x1, waiting for transfers between devices: 0.01 us -> 5.37 us  [planes(): lax.all_to_all(jnp.broadcast_to(value[None], (count, *value.shape)), 'col...]
    concatenate x10 -> x7, other arithmetic: 4.04 us -> 0.12 us  [grow(): return jnp.concatenate([value, across(value, mask)], axis=1)]
    unnamed x42 -> x36, local copies, waits for them, and re-layouts: 11.4 us -> 9.94 us
  transfers between devices with their start and end apart: 28 -> 25, of which waited for: 13 -> 15; matrix products, arithmetic and copies ran while one was open for 5% -> 4% of each run, Pallas kernels for 3% -> 3%
where the time goes in v11:
time: 221 us; the launch traced here: 220 us
  starting transfers between devices  92.4 us (42%)
  waiting for transfers between devices  75.1 us (34%)
  local copies, waits for them, and re-layouts  18.1 us (8%)
  Pallas kernels  16.7 us (8%)
  between operations  14.5 us (7%)
  other arithmetic  2.93 us (1%)
    ppermute x22, starting transfers between devices, swap(): lax.ppermute(value, axis, [(i, i ^ mask) for i in range(lax.axis_size(axi...  83.2 us
    ppermute x22, waiting for transfers between devices, swap(): lax.ppermute(value, axis, [(i, i ^ mask) for i in range(lax.axis_size(axi...  62.2 us
    pallas_call x6, Pallas kernels, call(): pl.pallas_call(kernel, out_shape=[jax.ShapeDtypeStruct(s, F32) for s in o...  16.7 us
    unnamed x36, local copies, waits for them, and re-layouts  9.94 us
    all_gather x1, waiting for transfers between devices, shards(): third = lax.all_gather(third, 'col', axis=0)  7.41 us
    all_to_all x1, waiting for transfers between devices, planes(): lax.all_to_all(jnp.broadcast_to(value[None], (count, *value.shape)), 'col...  5.37 us
    all_to_all x1, starting transfers between devices, shards(): t = lax.all_to_all(t, 'leaf', 0, 0, axis_index_groups=near, tiled=True)  5.19 us
  transfers between devices with their start and end apart: 25, of which 15 were waited for; matrix products, arithmetic and copies ran while one was open for 4% of the time, Pallas kernels for 3%

profile of v11, /device:TPU:1, one launch (start us, length us, event | category | flops | bytes accessed | tf_op | source)
XLA Modules:
  0.0 219.7 jit_solution(16420735439790632689)
XLA Ops:
  8.1 4.4 %collective-permute-start = (f32[2,128,128]{2,1,0:T(8,128)S(1)}, f32[2,128,128]{2,1,0:T(8,128)S(1)}, u32[]{:S(2)}, u32[]{:S(2)}) collective-permute-start(f32[2,128,128]{2,1,0:T(8,128)S(1)} %pad_maximum_fusion.6), channel_id=1, source_target_pairs={{0,8},{4,12},{8,0},{12,4},{16,24},{20,28},{24,16},{28,20},{32,40},... | collective-permute-start | bytes 393224 | tf_op jit(solution)/shard_map/ppermute | solution.py:48
  13.1 4.6 %collective-permute-start.1 = (f32[1,4,128]{2,1,0:T(4,128)S(1)}, f32[1,4,128]{2,1,0:T(4,128)S(1)}, u32[]{:S(2)}, u32[]{:S(2)}) collective-permute-start(f32[1,4,128]{2,1,0:T(4,128)S(1)} %slice_bitcast_fusion.6), channel_id=1, source_target_pairs={{0,384},{4,388},{8,392},{12,396},{16,400},{20,404},{24,408},{28,41... | collective-permute-start | bytes 6152 | tf_op jit(solution)/shard_map/ppermute | solution.py:48
  24.1 4.8 %shard_map.95 = (f32[896,128]{1,0:T(8,128)S(1)}, f32[128,2048]{1,0:T(8,128)}) custom-call(s32[5]{0:T(128)S(1)} %stack.68.where, s32[1,21]{1,0:T(1,128)S(1)} %copy-done.15, f32[896,128]{1,0:T(8,128)S(1)} %copy-done.11, f32[7,128,128]{2,1,0:T(8,128)S(1)} %copy-done.7, f32[21,128,128]{2,1,0:T(8,128)S(1)} %copy-done.1, f32[512,512]{1,0:T(8,128)S(1)} %copy-done.3, ...), custom_call_target="tpu_custom_call" | custom-call | tf_op jit(solution)/shard_map/pallas_call | solution.py:209
  29.7 5.2 %all-to-all-start = ((f32[4,32,2048]{2,1,0:T(8,128)}), f32[4,32,2048]{2,1,0:T(8,128)S(1)}, u32[]{:S(2)}, u32[]{:S(2)}) async-start(f32[4,32,2048]{2,1,0:T(8,128)} %bitcast.9), calls=%async_computation | async-start | bytes 2097152 | tf_op jit(solution)/shard_map/all_to_all | solution.py:259
  38.2 3.9 %collective-permute-start.4 = (f32[2,256,128]{2,1,0:T(8,128)S(1)}, f32[2,256,128]{2,1,0:T(8,128)S(1)}, u32[]{:S(2)}, u32[]{:S(2)}) collective-permute-start(f32[2,256,128]{2,1,0:T(8,128)S(1)} %pad_maximum_fusion.4), channel_id=1, source_target_pairs={{0,3},{1,2},{2,1},{3,0},{4,7},{5,6},{6,5},{7,4},{8,11},{9,10},{10,... | collective-permute-start | bytes 786440 | tf_op jit(solution)/shard_map/ppermute | solution.py:48
  42.1 2.4 %collective-permute-start.3 = (f32[2,256,128]{2,1,0:T(8,128)S(1)}, f32[2,256,128]{2,1,0:T(8,128)S(1)}, u32[]{:S(2)}, u32[]{:S(2)}) collective-permute-start(f32[2,256,128]{2,1,0:T(8,128)S(1)} %pad_maximum_fusion.4), channel_id=1, source_target_pairs={{0,2},{1,3},{2,0},{3,1},{4,6},{5,7},{6,4},{7,5},{8,10},{9,11},{10,... | collective-permute-start | bytes 786440 | tf_op jit(solution)/shard_map/ppermute | solution.py:48
  44.6 2.6 %collective-permute-start.2 = (f32[2,256,128]{2,1,0:T(8,128)S(1)}, f32[2,256,128]{2,1,0:T(8,128)S(1)}, u32[]{:S(2)}, u32[]{:S(2)}) collective-permute-start(f32[2,256,128]{2,1,0:T(8,128)S(1)} %pad_maximum_fusion.4), channel_id=1, source_target_pairs={{0,1},{1,0},{2,3},{3,2},{4,5},{5,4},{6,7},{7,6},{8,9},{9,8},{10,11... | collective-permute-start | bytes 786440 | tf_op jit(solution)/shard_map/ppermute | solution.py:48
  47.2 11.1 %collective-permute-start.6 = (f32[3,16,128]{2,1,0:T(8,128)S(1)}, f32[3,16,128]{2,1,0:T(8,128)S(1)}, u32[]{:S(2)}, u32[]{:S(2)}) collective-permute-start(f32[3,16,128]{2,1,0:T(8,128)S(1)} %pad_maximum_fusion.9), channel_id=1, source_target_pairs={{0,96},{4,100},{8,104},{12,108},{16,112},{20,116},{24,120},{28,124... | collective-permute-start | bytes 73736 | tf_op jit(solution)/shard_map/ppermute | solution.py:48
  59.6 3.8 %collective-permute-start.7 = (f32[4,2,256,128]{3,2,1,0:T(8,128)S(1)}, f32[4,2,256,128]{3,2,1,0:T(8,128)S(1)}, u32[]{:S(2)}, u32[]{:S(2)}) collective-permute-start(f32[4,2,256,128]{3,2,1,0:T(8,128)S(1)} %pad_maximum_fusion.refs_1_.m1), channel_id=1, source_target_pairs={{0,4},{4,0},{8,12},{12,8},{16,20},{20,16},{24,28},{28,24},{32,36},... | collective-permute-start | bytes 3145736 | tf_op jit(solution)/shard_map/ppermute | solution.py:48
  65.5 5.3 %collective-permute-start.8 = (f32[5,32,128]{2,1,0:T(8,128)}, f32[5,32,128]{2,1,0:T(8,128)S(1)}, u32[]{:S(2)}, u32[]{:S(2)}) collective-permute-start(f32[5,32,128]{2,1,0:T(8,128)} %pad_maximum_fusion.7), channel_id=1, source_target_pairs={{0,32},{4,36},{8,40},{12,44},{16,48},{20,52},{24,56},{28,60},{32,0... | collective-permute-start | bytes 245768 | tf_op jit(solution)/shard_map/ppermute | solution.py:48
  72.8 4.7 %collective-permute-start.9 = (f32[32,1024]{1,0:T(8,128)S(1)}, f32[32,1024]{1,0:T(8,128)}, u32[]{:S(2)}, u32[]{:S(2)}) collective-permute-start(f32[32,1024]{1,0:T(8,128)S(1)} %reduce_sum.9), channel_id=1, source_target_pairs={{0,16},{4,20},{8,24},{12,28},{16,0},{20,4},{24,8},{28,12},{32,48},... | collective-permute-start | bytes 393224 | tf_op jit(solution)/shard_map/ppermute | solution.py:48
  77.4 2.8 %collective-permute-done.8 = f32[5,32,128]{2,1,0:T(8,128)S(1)} collective-permute-done((f32[5,32,128]{2,1,0:T(8,128)}, f32[5,32,128]{2,1,0:T(8,128)S(1)}, u32[]{:S(2)}, u32[]{:S(2)}) %collective-permute-start.8) | collective-permute-done | bytes 81952 | tf_op jit(solution)/shard_map/ppermute | solution.py:48
  81.2 5.0 %collective-permute-done.9 = f32[32,1024]{1,0:T(8,128)} collective-permute-done((f32[32,1024]{1,0:T(8,128)S(1)}, f32[32,1024]{1,0:T(8,128)}, u32[]{:S(2)}, u32[]{:S(2)}) %collective-permute-start.9) | collective-permute-done | bytes 131104 | tf_op jit(solution)/shard_map/ppermute | solution.py:48
  88.1 9.5 %collective-permute-done.10 = f32[5,64,128]{2,1,0:T(8,128)S(1)} collective-permute-done((f32[5,64,128]{2,1,0:T(8,128)S(1)}, f32[5,64,128]{2,1,0:T(8,128)S(1)}, u32[]{:S(2)}, u32[]{:S(2)}) %collective-permute-start.10) | collective-permute-done | bytes 163872 | tf_op jit(solution)/shard_map/ppermute | solution.py:48
  99.6 4.1 %collective-permute-start.12 = (f32[32,512]{1,0:T(8,128)S(1)}, f32[32,512]{1,0:T(8,128)S(1)}, u32[]{:S(2)}, u32[]{:S(2)}) collective-permute-start(f32[32,512]{1,0:T(8,128)S(1)} %get-tuple-element.39), channel_id=1, source_target_pairs={{0,16},{4,20},{8,24},{12,28},{16,0},{20,4},{24,8},{28,12},{32,48},... | collective-permute-start | bytes 196616 | tf_op jit(solution)/shard_map/ppermute | solution.py:48
  104.6 5.0 %collective-permute-start.13 = (f32[32,1024]{1,0:T(8,128)S(1)}, f32[32,1024]{1,0:T(8,128)S(1)}, u32[]{:S(2)}, u32[]{:S(2)}) collective-permute-start(f32[32,1024]{1,0:T(8,128)S(1)} %add.28.refs_2_), channel_id=1, source_target_pairs={{0,32},{4,36},{8,40},{12,44},{16,48},{20,52},{24,56},{28,60},{32,0... | collective-permute-start | bytes 393224 | tf_op jit(solution)/shard_map/ppermute | solution.py:48
  109.8 14.2 %collective-permute-done.13.refs_3_ = f32[32,1024]{1,0:T(8,128)S(1)} collective-permute-done((f32[32,1024]{1,0:T(8,128)S(1)}, f32[32,1024]{1,0:T(8,128)S(1)}, u32[]{:S(2)}, u32[]{:S(2)}) %collective-permute-start.13) | collective-permute-done | bytes 131104 | tf_op jit(solution)/shard_map/ppermute | solution.py:48
  125.1 4.0 %all-to-all-start.1 = ((f32[4,2,256,128]{3,2,1,0:T(8,128)}), f32[4,2,256,128]{3,2,1,0:T(8,128)S(1)}, u32[]{:S(2)}, u32[]{:S(2)}) async-start(f32[4,2,256,128]{3,2,1,0:T(8,128)} %broadcast_in_dim.14), calls=%async_computation.1 | async-start | bytes 2097152 | tf_op jit(solution)/shard_map/all_to_all | solution.py:236
  132.8 5.3 %collective-permute-done.14.refs_1_ = f32[32,512]{1,0:T(8,128)} collective-permute-done((f32[32,512]{1,0:T(8,128)S(1)}, f32[32,512]{1,0:T(8,128)}, u32[]{:S(2)}, u32[]{:S(2)}) %collective-permute-start.14) | collective-permute-done | bytes 65568 | tf_op jit(solution)/shard_map/ppermute | solution.py:48
  138.1 5.4 %all-to-all-done.1.refs_4_.m2 = f32[4,2,256,128]{3,2,1,0:T(8,128)S(1)} async-done(((f32[4,2,256,128]{3,2,1,0:T(8,128)}), f32[4,2,256,128]{3,2,1,0:T(8,128)S(1)}, u32[]{:S(2)}, u32[]{:S(2)}) %all-to-all-start.1) | async-done | bytes 1048608 | tf_op jit(solution)/shard_map/all_to_all | solution.py:236
  143.5 3.6 %collective-permute-start.15 = (f32[4,2,256,128]{3,2,1,0:T(8,128)S(1)}, f32[4,2,256,128]{3,2,1,0:T(8,128)S(1)}, u32[]{:S(2)}, u32[]{:S(2)}) collective-permute-start(f32[4,2,256,128]{3,2,1,0:T(8,128)S(1)} %all-to-all-done.1.refs_4_.m2), channel_id=1, source_target_pairs={{0,4},{4,0},{8,12},{12,8},{16,20},{20,16},{24,28},{28,24},{32,36},... | collective-permute-start | bytes 3145736 | tf_op jit(solution)/shard_map/ppermute | solution.py:48
  154.6 10.1 %collective-permute-done.16 = f32[32,1024]{1,0:T(8,128)S(1)} collective-permute-done((f32[32,1024]{1,0:T(8,128)S(1)}, f32[32,1024]{1,0:T(8,128)S(1)}, u32[]{:S(2)}, u32[]{:S(2)}) %collective-permute-start.16) | collective-permute-done | bytes 131104 | tf_op jit(solution)/shard_map/ppermute | solution.py:48
  164.7 7.4 %all-gather.3.cloned.1.call-done = f32[12,256,128]{2,1,0:T(8,128)} async-done(((f32[3,256,128]{2,1,0:T(8,128)}), f32[12,256,128]{2,1,0:T(8,128)}) %all-gather.3.cloned.1.call-update) | async-done | bytes 1572880 | tf_op jit(solution)/shard_map/all_gather | solution.py:284
  172.1 2.6 %collective-permute-start.18 = (f32[4,3,256,128]{3,2,1,0:T(8,128)}, f32[4,3,256,128]{3,2,1,0:T(8,128)S(1)}, u32[]{:S(2)}, u32[]{:S(2)}) collective-permute-start(f32[4,3,256,128]{3,2,1,0:T(8,128)} %bitcast.32), channel_id=1, source_target_pairs={{0,4},{4,0},{8,12},{12,8},{16,20},{20,16},{24,28},{28,24},{32,36},... | collective-permute-start | bytes 4718600 | tf_op jit(solution)/shard_map/ppermute | solution.py:48
  174.7 3.1 %collective-permute-start.17 = (f32[32,1024]{1,0:T(8,128)S(1)}, f32[32,1024]{1,0:T(8,128)S(1)}, u32[]{:S(2)}, u32[]{:S(2)}) collective-permute-start(f32[32,1024]{1,0:T(8,128)S(1)} %add.29.refs_0_), channel_id=1, source_target_pairs={{0,128},{4,132},{8,136},{12,140},{16,144},{20,148},{24,152},{28,15... | collective-permute-start | bytes 393224 | tf_op jit(solution)/shard_map/ppermute | solution.py:48
  177.8 3.9 %collective-permute-done.17.refs_1_ = f32[32,1024]{1,0:T(8,128)S(1)} collective-permute-done((f32[32,1024]{1,0:T(8,128)S(1)}, f32[32,1024]{1,0:T(8,128)S(1)}, u32[]{:S(2)}, u32[]{:S(2)}) %collective-permute-start.17) | collective-permute-done | bytes 131104 | tf_op jit(solution)/shard_map/ppermute | solution.py:48
  184.1 4.4 %collective-permute-start.19 = (f32[32,512]{1,0:T(8,128)S(1)}, f32[32,512]{1,0:T(8,128)S(1)}, u32[]{:S(2)}, u32[]{:S(2)}) collective-permute-start(f32[32,512]{1,0:T(8,128)S(1)} %get-tuple-element.52.right), channel_id=1, source_target_pairs={{0,384},{4,388},{8,392},{12,396},{16,400},{20,404},{24,408},{28,41... | collective-permute-start | bytes 196616 | tf_op jit(solution)/shard_map/ppermute | solution.py:48
  190.4 3.6 %shard_map.99 = f32[32,2048]{1,0:T(8,128)S(1)} custom-call(s32[1]{0:T(128)} %bitcast.5.plane, f32[32,512]{1,0:T(8,128)S(1)} %get-tuple-element.52.right, f32[32,512]{1,0:T(8,128)S(1)} %collective-permute-done.19.right_far, f32[32,512]{1,0:T(8,128)S(1)} %get-tuple-element.53.z1, f32[32,512]{1,0:T(8,128)S(1)} %copy-done.14, ...), custom_call_target="tpu_custom_call" | custom-call | tf_op jit(solution)/shard_map/pallas_call | solution.py:209
  193.9 3.3 %collective-permute-start.20 = (f32[32,2048]{1,0:T(8,128)S(1)}, f32[32,2048]{1,0:T(8,128)S(1)}, u32[]{:S(2)}, u32[]{:S(2)}) collective-permute-start(f32[32,2048]{1,0:T(8,128)S(1)} %shard_map.99), channel_id=1, source_target_pairs={{0,8},{4,12},{8,0},{12,4},{16,24},{20,28},{24,16},{28,20},{32,40},... | collective-permute-start | bytes 786440 | tf_op jit(solution)/shard_map/ppermute | solution.py:48
  197.3 4.6 %collective-permute-done.20 = f32[32,2048]{1,0:T(8,128)S(1)} collective-permute-done((f32[32,2048]{1,0:T(8,128)S(1)}, f32[32,2048]{1,0:T(8,128)S(1)}, u32[]{:S(2)}, u32[]{:S(2)}) %collective-permute-start.20) | collective-permute-done | bytes 262176 | tf_op jit(solution)/shard_map/ppermute | solution.py:48
  201.9 4.8 %collective-permute-start.21 = (f32[2,32,2048]{2,1,0:T(8,128)S(1)}, f32[2,32,2048]{2,1,0:T(8,128)S(1)}, u32[]{:S(2)}, u32[]{:S(2)}) collective-permute-start(f32[2,32,2048]{2,1,0:T(8,128)S(1)} %pad_maximum_fusion.2.near), channel_id=1, source_target_pairs={{0,4},{4,0},{8,12},{12,8},{16,20},{20,16},{24,28},{28,24},{32,36},... | collective-permute-start | bytes 1572872 | tf_op jit(solution)/shard_map/ppermute | solution.py:48
  208.2 4.7 %shard_map.100 = (f32[896,128]{1,0:T(8,128)}, f32[172,128]{1,0:T(8,128)}) custom-call(s32[5]{0:T(128)S(1)} %stack.68.where, s32[1,21]{1,0:T(1,128)S(1)} %copy-done.16, f32[896,128]{1,0:T(8,128)S(1)} %copy-done.10, f32[2,32,2048]{2,1,0:T(8,128)S(1)} %pad_maximum_fusion.2.near, f32[2,32,2048]{2,1,0:T(8,128)S(1)} %collective-permute-done.21.across_core, ...), custom_call_target="tpu_custom_call" | custom-call | tf_op jit(solution)/shard_map/pallas_call | solution.py:209
  (88 shorter events, 41.3 us)
Async XLA Ops:
  8.1 21.6 %collective-permute-start = (f32[2,128,128]{2,1,0:T(8,128)S(1)}, f32[2,128,128]{2,1,0:T(8,128)S(1)}, u32[]{:S(2)}, u32[]{:S(2)}) collective-permute-start(f32[2,128,128]{2,1,0:T(8,128)S(1)} %pad_maximum_fusion.6), channel_id=1, source_target_pairs={{0,8},{4,12},{8,0},{12,4},{16,24},{20,28},{24,16},{28,20},{32,40},... | collective-permute-start | bytes 393224 | tf_op jit(solution)/shard_map/ppermute | solution.py:48
  13.1 16.5 %collective-permute-start.1 = (f32[1,4,128]{2,1,0:T(4,128)S(1)}, f32[1,4,128]{2,1,0:T(4,128)S(1)}, u32[]{:S(2)}, u32[]{:S(2)}) collective-permute-start(f32[1,4,128]{2,1,0:T(4,128)S(1)} %slice_bitcast_fusion.6), channel_id=1, source_target_pairs={{0,384},{4,388},{8,392},{12,396},{16,400},{20,404},{24,408},{28,41... | collective-permute-start | bytes 6152 | tf_op jit(solution)/shard_map/ppermute | solution.py:48
  29.7 29.9 %all-to-all-start = ((f32[4,32,2048]{2,1,0:T(8,128)}), f32[4,32,2048]{2,1,0:T(8,128)S(1)}, u32[]{:S(2)}, u32[]{:S(2)}) async-start(f32[4,32,2048]{2,1,0:T(8,128)} %bitcast.9), calls=%async_computation | async-start | bytes 2097152 | tf_op jit(solution)/shard_map/all_to_all | solution.py:259
  36.3 10.9 %collective-permute-start.5 = (f32[3,8,128]{2,1,0:T(8,128)S(1)}, f32[3,8,128]{2,1,0:T(8,128)S(1)}, u32[]{:S(2)}, u32[]{:S(2)}) collective-permute-start(f32[3,8,128]{2,1,0:T(8,128)S(1)} %pad_maximum_fusion.10), channel_id=1, source_target_pairs={{0,128},{4,132},{8,136},{12,140},{16,144},{20,148},{24,152},{28,15... | collective-permute-start | bytes 36872 | tf_op jit(solution)/shard_map/ppermute | solution.py:48
  38.2 21.3 %collective-permute-start.4 = (f32[2,256,128]{2,1,0:T(8,128)S(1)}, f32[2,256,128]{2,1,0:T(8,128)S(1)}, u32[]{:S(2)}, u32[]{:S(2)}) collective-permute-start(f32[2,256,128]{2,1,0:T(8,128)S(1)} %pad_maximum_fusion.4), channel_id=1, source_target_pairs={{0,3},{1,2},{2,1},{3,0},{4,7},{5,6},{6,5},{7,4},{8,11},{9,10},{10,... | collective-permute-start | bytes 786440 | tf_op jit(solution)/shard_map/ppermute | solution.py:48
  42.1 17.4 %collective-permute-start.3 = (f32[2,256,128]{2,1,0:T(8,128)S(1)}, f32[2,256,128]{2,1,0:T(8,128)S(1)}, u32[]{:S(2)}, u32[]{:S(2)}) collective-permute-start(f32[2,256,128]{2,1,0:T(8,128)S(1)} %pad_maximum_fusion.4), channel_id=1, source_target_pairs={{0,2},{1,3},{2,0},{3,1},{4,6},{5,7},{6,4},{7,5},{8,10},{9,11},{10,... | collective-permute-start | bytes 786440 | tf_op jit(solution)/shard_map/ppermute | solution.py:48
  44.6 15.0 %collective-permute-start.2 = (f32[2,256,128]{2,1,0:T(8,128)S(1)}, f32[2,256,128]{2,1,0:T(8,128)S(1)}, u32[]{:S(2)}, u32[]{:S(2)}) collective-permute-start(f32[2,256,128]{2,1,0:T(8,128)S(1)} %pad_maximum_fusion.4), channel_id=1, source_target_pairs={{0,1},{1,0},{2,3},{3,2},{4,5},{5,4},{6,7},{7,6},{8,9},{9,8},{10,11... | collective-permute-start | bytes 786440 | tf_op jit(solution)/shard_map/ppermute | solution.py:48
  47.2 12.3 %collective-permute-start.6 = (f32[3,16,128]{2,1,0:T(8,128)S(1)}, f32[3,16,128]{2,1,0:T(8,128)S(1)}, u32[]{:S(2)}, u32[]{:S(2)}) collective-permute-start(f32[3,16,128]{2,1,0:T(8,128)S(1)} %pad_maximum_fusion.9), channel_id=1, source_target_pairs={{0,96},{4,100},{8,104},{12,108},{16,112},{20,116},{24,120},{28,124... | collective-permute-start | bytes 73736 | tf_op jit(solution)/shard_map/ppermute | solution.py:48
  59.6 20.6 %collective-permute-start.7 = (f32[4,2,256,128]{3,2,1,0:T(8,128)S(1)}, f32[4,2,256,128]{3,2,1,0:T(8,128)S(1)}, u32[]{:S(2)}, u32[]{:S(2)}) collective-permute-start(f32[4,2,256,128]{3,2,1,0:T(8,128)S(1)} %pad_maximum_fusion.refs_1_.m1), channel_id=1, source_target_pairs={{0,4},{4,0},{8,12},{12,8},{16,20},{20,16},{24,28},{28,24},{32,36},... | collective-permute-start | bytes 3145736 | tf_op jit(solution)/shard_map/ppermute | solution.py:48
  65.5 14.7 %collective-permute-start.8 = (f32[5,32,128]{2,1,0:T(8,128)}, f32[5,32,128]{2,1,0:T(8,128)S(1)}, u32[]{:S(2)}, u32[]{:S(2)}) collective-permute-start(f32[5,32,128]{2,1,0:T(8,128)} %pad_maximum_fusion.7), channel_id=1, source_target_pairs={{0,32},{4,36},{8,40},{12,44},{16,48},{20,52},{24,56},{28,60},{32,0... | collective-permute-start | bytes 245768 | tf_op jit(solution)/shard_map/ppermute | solution.py:48
  72.8 13.4 %collective-permute-start.9 = (f32[32,1024]{1,0:T(8,128)S(1)}, f32[32,1024]{1,0:T(8,128)}, u32[]{:S(2)}, u32[]{:S(2)}) collective-permute-start(f32[32,1024]{1,0:T(8,128)S(1)} %reduce_sum.9), channel_id=1, source_target_pairs={{0,16},{4,20},{8,24},{12,28},{16,0},{20,4},{24,8},{28,12},{32,48},... | collective-permute-start | bytes 393224 | tf_op jit(solution)/shard_map/ppermute | solution.py:48
  86.2 11.5 %collective-permute-start.10 = (f32[5,64,128]{2,1,0:T(8,128)S(1)}, f32[5,64,128]{2,1,0:T(8,128)S(1)}, u32[]{:S(2)}, u32[]{:S(2)}) collective-permute-start(f32[5,64,128]{2,1,0:T(8,128)S(1)} %pad_maximum_fusion.5), channel_id=1, source_target_pairs={{0,16},{4,20},{8,24},{12,28},{16,0},{20,4},{24,8},{28,12},{32,48},... | collective-permute-start | bytes 491528 | tf_op jit(solution)/shard_map/ppermute | solution.py:48
  97.7 12.1 %collective-permute-start.11 = (f32[5,128,128]{2,1,0:T(8,128)S(1)}, f32[5,128,128]{2,1,0:T(8,128)S(1)}, u32[]{:S(2)}, u32[]{:S(2)}) collective-permute-start(f32[5,128,128]{2,1,0:T(8,128)S(1)} %pad_maximum_fusion.3), channel_id=1, source_target_pairs={{0,8},{4,12},{8,0},{12,4},{16,24},{20,28},{24,16},{28,20},{32,40},... | collective-permute-start | bytes 983048 | tf_op jit(solution)/shard_map/ppermute | solution.py:48
  99.6 10.0 %collective-permute-start.12 = (f32[32,512]{1,0:T(8,128)S(1)}, f32[32,512]{1,0:T(8,128)S(1)}, u32[]{:S(2)}, u32[]{:S(2)}) collective-permute-start(f32[32,512]{1,0:T(8,128)S(1)} %get-tuple-element.39), channel_id=1, source_target_pairs={{0,16},{4,20},{8,24},{12,28},{16,0},{20,4},{24,8},{28,12},{32,48},... | collective-permute-start | bytes 196616 | tf_op jit(solution)/shard_map/ppermute | solution.py:48
  104.6 19.4 %collective-permute-start.13 = (f32[32,1024]{1,0:T(8,128)S(1)}, f32[32,1024]{1,0:T(8,128)S(1)}, u32[]{:S(2)}, u32[]{:S(2)}) collective-permute-start(f32[32,1024]{1,0:T(8,128)S(1)} %add.28.refs_2_), channel_id=1, source_target_pairs={{0,32},{4,36},{8,40},{12,44},{16,48},{20,52},{24,56},{28,60},{32,0... | collective-permute-start | bytes 393224 | tf_op jit(solution)/shard_map/ppermute | solution.py:48
  109.8 15.3 %copy-start.17 = (f32[5,256,128]{2,1,0:T(8,128)}, f32[5,256,128]{2,1,0:T(8,128)S(1)}, u32[]{:S(2)}) copy-start(f32[5,256,128]{2,1,0:T(8,128)S(1)} %pad_maximum_fusion.1) | copy-start | bytes 1966084
  125.1 18.4 %all-to-all-start.1 = ((f32[4,2,256,128]{3,2,1,0:T(8,128)}), f32[4,2,256,128]{3,2,1,0:T(8,128)S(1)}, u32[]{:S(2)}, u32[]{:S(2)}) async-start(f32[4,2,256,128]{3,2,1,0:T(8,128)} %broadcast_in_dim.14), calls=%async_computation.1 | async-start | bytes 2097152 | tf_op jit(solution)/shard_map/all_to_all | solution.py:236
  129.1 43.1 %all-gather.3.cloned.1.call-start = ((), (), s32[]{:S(2)}) async-start(), calls=%async_computation.2 | async-start | bytes 1966080 | tf_op jit(solution)/shard_map/all_gather | solution.py:284
  129.1 9.0 %collective-permute-start.14 = (f32[32,512]{1,0:T(8,128)S(1)}, f32[32,512]{1,0:T(8,128)}, u32[]{:S(2)}, u32[]{:S(2)}) collective-permute-start(f32[32,512]{1,0:T(8,128)S(1)} %add.27.refs_0_), channel_id=1, source_target_pairs={{0,32},{4,36},{8,40},{12,44},{16,48},{20,52},{24,56},{28,60},{32,0... | collective-permute-start | bytes 196616 | tf_op jit(solution)/shard_map/ppermute | solution.py:48
  143.5 5.8 %collective-permute-start.15 = (f32[4,2,256,128]{3,2,1,0:T(8,128)S(1)}, f32[4,2,256,128]{3,2,1,0:T(8,128)S(1)}, u32[]{:S(2)}, u32[]{:S(2)}) collective-permute-start(f32[4,2,256,128]{3,2,1,0:T(8,128)S(1)} %all-to-all-done.1.refs_4_.m2), channel_id=1, source_target_pairs={{0,4},{4,0},{8,12},{12,8},{16,20},{20,16},{24,28},{28,24},{32,36},... | collective-permute-start | bytes 3145736 | tf_op jit(solution)/shard_map/ppermute | solution.py:48
  152.7 12.0 %collective-permute-start.16 = (f32[32,1024]{1,0:T(8,128)S(1)}, f32[32,1024]{1,0:T(8,128)S(1)}, u32[]{:S(2)}, u32[]{:S(2)}) collective-permute-start(f32[32,1024]{1,0:T(8,128)S(1)} %get-tuple-element.48), channel_id=1, source_target_pairs={{0,96},{4,100},{8,104},{12,108},{16,112},{20,116},{24,120},{28,124... | collective-permute-start | bytes 393224 | tf_op jit(solution)/shard_map/ppermute | solution.py:48
  164.7 25.6 %copy-start.14 = (f32[32,512]{1,0:T(8,128)S(1)}, f32[32,512]{1,0:T(8,128)}, u32[]{:S(2)}) copy-start(f32[32,512]{1,0:T(8,128)} %copy-done.13) | copy-start | bytes 196612
  172.1 9.6 %collective-permute-start.18 = (f32[4,3,256,128]{3,2,1,0:T(8,128)}, f32[4,3,256,128]{3,2,1,0:T(8,128)S(1)}, u32[]{:S(2)}, u32[]{:S(2)}) collective-permute-start(f32[4,3,256,128]{3,2,1,0:T(8,128)} %bitcast.32), channel_id=1, source_target_pairs={{0,4},{4,0},{8,12},{12,8},{16,20},{20,16},{24,28},{28,24},{32,36},... | collective-permute-start | bytes 4718600 | tf_op jit(solution)/shard_map/ppermute | solution.py:48
  174.7 7.0 %collective-permute-start.17 = (f32[32,1024]{1,0:T(8,128)S(1)}, f32[32,1024]{1,0:T(8,128)S(1)}, u32[]{:S(2)}, u32[]{:S(2)}) collective-permute-start(f32[32,1024]{1,0:T(8,128)S(1)} %add.29.refs_0_), channel_id=1, source_target_pairs={{0,128},{4,132},{8,136},{12,140},{16,144},{20,148},{24,152},{28,15... | collective-permute-start | bytes 393224 | tf_op jit(solution)/shard_map/ppermute | solution.py:48
  184.1 6.2 %collective-permute-start.19 = (f32[32,512]{1,0:T(8,128)S(1)}, f32[32,512]{1,0:T(8,128)S(1)}, u32[]{:S(2)}, u32[]{:S(2)}) collective-permute-start(f32[32,512]{1,0:T(8,128)S(1)} %get-tuple-element.52.right), channel_id=1, source_target_pairs={{0,384},{4,388},{8,392},{12,396},{16,400},{20,404},{24,408},{28,41... | collective-permute-start | bytes 196616 | tf_op jit(solution)/shard_map/ppermute | solution.py:48
  190.3 17.8 %copy-start.2 = (f32[21,128,128]{2,1,0:T(8,128)S(1)}, f32[21,128,128]{2,1,0:T(8,128)}, u32[]{:S(2)}) copy-start(f32[21,128,128]{2,1,0:T(8,128)} %blocks.3) | copy-start | bytes 4128772
  190.3 17.8 %copy-start.8 = (f32[7,128,128]{2,1,0:T(8,128)S(1)}, f32[7,128,128]{2,1,0:T(8,128)}, u32[]{:S(2)}) copy-start(f32[7,128,128]{2,1,0:T(8,128)} %inverse.3) | copy-start | bytes 1376260
  190.3 17.8 %copy-start.10 = (f32[896,128]{1,0:T(8,128)S(1)}, f32[896,128]{1,0:T(8,128)}, u32[]{:S(2)}) copy-start(f32[896,128]{1,0:T(8,128)} %copy-done.9) | copy-start | bytes 1376260
  190.4 17.8 %copy-start.16 = (s32[1,21]{1,0:T(1,128)S(1)}, s32[1,21]{1,0:T(1,128)}, u32[]{:S(2)}) copy-start(s32[1,21]{1,0:T(1,128)} %pattern.3) | copy-start | bytes 256
  193.9 14.2 %copy-start.4 = (f32[512,512]{1,0:T(8,128)S(1)}, f32[512,512]{1,0:T(8,128)}, u32[]{:S(2)}) copy-start(f32[512,512]{1,0:T(8,128)} %coupling.3) | copy-start | bytes 3145732
  193.9 7.9 %collective-permute-start.20 = (f32[32,2048]{1,0:T(8,128)S(1)}, f32[32,2048]{1,0:T(8,128)S(1)}, u32[]{:S(2)}, u32[]{:S(2)}) collective-permute-start(f32[32,2048]{1,0:T(8,128)S(1)} %shard_map.99), channel_id=1, source_target_pairs={{0,8},{4,12},{8,0},{12,4},{16,24},{20,28},{24,16},{28,20},{32,40},... | collective-permute-start | bytes 786440 | tf_op jit(solution)/shard_map/ppermute | solution.py:48
  201.9 6.3 %collective-permute-start.21 = (f32[2,32,2048]{2,1,0:T(8,128)S(1)}, f32[2,32,2048]{2,1,0:T(8,128)S(1)}, u32[]{:S(2)}, u32[]{:S(2)}) collective-permute-start(f32[2,32,2048]{2,1,0:T(8,128)S(1)} %pad_maximum_fusion.2.near), channel_id=1, source_target_pairs={{0,4},{4,0},{8,12},{12,8},{16,20},{20,16},{24,28},{28,24},{32,36},... | collective-permute-start | bytes 1572872 | tf_op jit(solution)/shard_map/ppermute | solution.py:48
  (11 other events, 17.1 us)
Sparse Core Ops, SparseCore 0:
  143.6 28.5 all-gather.2

commit v12 on v6

--- a/solution.py
+++ b/solution.py
@@ -233,7 +233,7 @@
         return lax.all_to_all(jnp.broadcast_to(value[None], (count, *value.shape)), "col", 0, 0, tiled=True)
 
     tie = lax.optimization_barrier
-    halves_z, wrap_z, wrap_y = 1 << Z4, (1 << Z8) | (1 << Z4) | (1 << Z2), (1 << Y2) | (1 << Y1)
+    halves_z, wrap_z, wrap_y = 1 << Z4, (1 << Z8) | (1 << Z4), (1 << Y2) | (1 << Y1)
     near = [[g * 4 + m for m in range(4)] for g in range(leaves // 4)]
     plane = lax.axis_index("col").astype(jnp.int32)[None]
 
@@ -277,9 +277,9 @@
 
     second = (second, across(second, CORE_MASK))
     z2, v = solve(0, False, 2, v, v_far, *second)
+    v, third = tie((v, third))
+
     v = v + across(v, wrap_z)
-    v, third = tie((v, third))
-
     third = (third, across(third, CORE_MASK))
     z3, v = solve(1, False, 1, v, across(v, 1 << Y1), *third)
     (x,) = call(

time: 208 us -> 212 us (1.019)
  waiting for transfers between devices: 43.6 us -> 77.9 us
  starting transfers between devices: 117 us -> 84 us
    ppermute x20, waiting for transfers between devices: 42.6 us -> 77.9 us  [swap(): lax.ppermute(value, axis, [(i, i ^ mask) for i in range(lax.axis_size(axi...]
    ppermute x20, starting transfers between devices: 107 us -> 74.8 us  [swap(): lax.ppermute(value, axis, [(i, i ^ mask) for i in range(lax.axis_size(axi...]
    unnamed x38 -> x40, local copies, waits for them, and re-layouts: 9.95 us -> 10.6 us
  transfers between devices with their start and end apart: 23 -> 23, of which waited for: 12 -> 12; matrix products, arithmetic and copies ran while one was open for 2% -> 3% of each run, Pallas kernels for 3% -> 3%
where the time goes in v12:
time: 212 us; the launch traced here: 210 us
  starting transfers between devices  84 us (40%)
  waiting for transfers between devices  77.9 us (37%)
  local copies, waits for them, and re-layouts  16.9 us (8%)
  Pallas kernels  15.9 us (8%)
  between operations  14.5 us (7%)
    ppermute x20, waiting for transfers between devices, swap(): lax.ppermute(value, axis, [(i, i ^ mask) for i in range(lax.axis_size(axi...  77.9 us
    ppermute x20, starting transfers between devices, swap(): lax.ppermute(value, axis, [(i, i ^ mask) for i in range(lax.axis_size(axi...  74.8 us
    pallas_call x6, Pallas kernels, call(): pl.pallas_call(kernel, out_shape=[jax.ShapeDtypeStruct(s, F32) for s in o...  15.9 us
    unnamed x40, local copies, waits for them, and re-layouts  10.6 us
    all_to_all x1, starting transfers between devices, shards(): t = lax.all_to_all(t, 'leaf', 0, 0, axis_index_groups=near, tiled=True)  5.19 us
  transfers between devices with their start and end apart: 23, of which 12 were waited for; matrix products, arithmetic and copies ran while one was open for 3% of the time, Pallas kernels for 3%

profile of v12, /device:TPU:1, one launch (start us, length us, event | category | flops | bytes accessed | tf_op | source)
XLA Modules:
  0.0 210.4 jit_solution(7643042996822717032)
XLA Ops:
  8.1 4.4 %collective-permute-start = (f32[2,128,128]{2,1,0:T(8,128)S(1)}, f32[2,128,128]{2,1,0:T(8,128)S(1)}, u32[]{:S(2)}, u32[]{:S(2)}) collective-permute-start(f32[2,128,128]{2,1,0:T(8,128)S(1)} %pad_maximum_fusion.6), channel_id=1, source_target_pairs={{0,8},{4,12},{8,0},{12,4},{16,24},{20,28},{24,16},{28,20},{32,40},... | collective-permute-start | bytes 393224 | tf_op jit(solution)/shard_map/ppermute | solution.py:48
  13.1 4.6 %collective-permute-start.1 = (f32[1,4,128]{2,1,0:T(4,128)S(1)}, f32[1,4,128]{2,1,0:T(4,128)S(1)}, u32[]{:S(2)}, u32[]{:S(2)}) collective-permute-start(f32[1,4,128]{2,1,0:T(4,128)S(1)} %slice_bitcast_fusion.6), channel_id=1, source_target_pairs={{0,384},{4,388},{8,392},{12,396},{16,400},{20,404},{24,408},{28,41... | collective-permute-start | bytes 6152 | tf_op jit(solution)/shard_map/ppermute | solution.py:48
  24.1 4.8 %shard_map.95 = (f32[896,128]{1,0:T(8,128)S(1)}, f32[128,2048]{1,0:T(8,128)}) custom-call(s32[5]{0:T(128)S(1)} %stack.68.where, s32[1,21]{1,0:T(1,128)S(1)} %copy-done.18, f32[896,128]{1,0:T(8,128)S(1)} %copy-done.11, f32[7,128,128]{2,1,0:T(8,128)S(1)} %copy-done.7, f32[21,128,128]{2,1,0:T(8,128)S(1)} %copy-done.1, f32[512,512]{1,0:T(8,128)S(1)} %copy-done.3, ...), custom_call_target="tpu_custom_call" | custom-call | tf_op jit(solution)/shard_map/pallas_call | solution.py:206
  29.7 5.2 %all-to-all-start = ((f32[4,32,2048]{2,1,0:T(8,128)}), f32[4,32,2048]{2,1,0:T(8,128)S(1)}, u32[]{:S(2)}, u32[]{:S(2)}) async-start(f32[4,32,2048]{2,1,0:T(8,128)} %bitcast.9), calls=%async_computation | async-start | bytes 2097152 | tf_op jit(solution)/shard_map/all_to_all | solution.py:256
  38.2 3.9 %collective-permute-start.4 = (f32[2,256,128]{2,1,0:T(8,128)S(1)}, f32[2,256,128]{2,1,0:T(8,128)S(1)}, u32[]{:S(2)}, u32[]{:S(2)}) collective-permute-start(f32[2,256,128]{2,1,0:T(8,128)S(1)} %pad_maximum_fusion.4), channel_id=1, source_target_pairs={{0,3},{1,2},{2,1},{3,0},{4,7},{5,6},{6,5},{7,4},{8,11},{9,10},{10,... | collective-permute-start | bytes 786440 | tf_op jit(solution)/shard_map/ppermute | solution.py:48
  42.1 2.4 %collective-permute-start.3 = (f32[2,256,128]{2,1,0:T(8,128)S(1)}, f32[2,256,128]{2,1,0:T(8,128)S(1)}, u32[]{:S(2)}, u32[]{:S(2)}) collective-permute-start(f32[2,256,128]{2,1,0:T(8,128)S(1)} %pad_maximum_fusion.4), channel_id=1, source_target_pairs={{0,2},{1,3},{2,0},{3,1},{4,6},{5,7},{6,4},{7,5},{8,10},{9,11},{10,... | collective-permute-start | bytes 786440 | tf_op jit(solution)/shard_map/ppermute | solution.py:48
  44.5 2.6 %collective-permute-start.2 = (f32[2,256,128]{2,1,0:T(8,128)S(1)}, f32[2,256,128]{2,1,0:T(8,128)S(1)}, u32[]{:S(2)}, u32[]{:S(2)}) collective-permute-start(f32[2,256,128]{2,1,0:T(8,128)S(1)} %pad_maximum_fusion.4), channel_id=1, source_target_pairs={{0,1},{1,0},{2,3},{3,2},{4,5},{5,4},{6,7},{7,6},{8,9},{9,8},{10,11... | collective-permute-start | bytes 786440 | tf_op jit(solution)/shard_map/ppermute | solution.py:48
  47.2 11.1 %collective-permute-start.6 = (f32[3,16,128]{2,1,0:T(8,128)S(1)}, f32[3,16,128]{2,1,0:T(8,128)S(1)}, u32[]{:S(2)}, u32[]{:S(2)}) collective-permute-start(f32[3,16,128]{2,1,0:T(8,128)S(1)} %pad_maximum_fusion.9), channel_id=1, source_target_pairs={{0,96},{4,100},{8,104},{12,108},{16,112},{20,116},{24,120},{28,124... | collective-permute-start | bytes 73736 | tf_op jit(solution)/shard_map/ppermute | solution.py:48
  59.6 3.8 %collective-permute-start.7 = (f32[4,2,256,128]{3,2,1,0:T(8,128)S(1)}, f32[4,2,256,128]{3,2,1,0:T(8,128)S(1)}, u32[]{:S(2)}, u32[]{:S(2)}) collective-permute-start(f32[4,2,256,128]{3,2,1,0:T(8,128)S(1)} %pad_maximum_fusion.refs_1_.m1), channel_id=1, source_target_pairs={{0,4},{4,0},{8,12},{12,8},{16,20},{20,16},{24,28},{28,24},{32,36},... | collective-permute-start | bytes 3145736 | tf_op jit(solution)/shard_map/ppermute | solution.py:48
  64.9 5.3 %collective-permute-start.8 = (f32[5,32,128]{2,1,0:T(8,128)S(1)}, f32[5,32,128]{2,1,0:T(8,128)S(1)}, u32[]{:S(2)}, u32[]{:S(2)}) collective-permute-start(f32[5,32,128]{2,1,0:T(8,128)S(1)} %pad_maximum_fusion.7), channel_id=1, source_target_pairs={{0,32},{4,36},{8,40},{12,44},{16,48},{20,52},{24,56},{28,60},{32,0... | collective-permute-start | bytes 245768 | tf_op jit(solution)/shard_map/ppermute | solution.py:48
  70.2 9.8 %collective-permute-done.8 = f32[5,32,128]{2,1,0:T(8,128)S(1)} collective-permute-done((f32[5,32,128]{2,1,0:T(8,128)S(1)}, f32[5,32,128]{2,1,0:T(8,128)S(1)}, u32[]{:S(2)}, u32[]{:S(2)}) %collective-permute-start.8) | collective-permute-done | bytes 81952 | tf_op jit(solution)/shard_map/ppermute | solution.py:48
  81.1 1.9 collective-permute-start.9
  83.0 10.2 %collective-permute-done.9 = f32[5,64,128]{2,1,0:T(8,128)S(1)} collective-permute-done((f32[5,64,128]{2,1,0:T(8,128)S(1)}, f32[5,64,128]{2,1,0:T(8,128)S(1)}, u32[]{:S(2)}, u32[]{:S(2)}) %collective-permute-start.9) | collective-permute-done | bytes 163872 | tf_op jit(solution)/shard_map/ppermute | solution.py:48
  93.2 1.9 collective-permute-start.10
  95.2 2.8 %collective-permute-start.11 = (f32[32,1536]{1,0:T(8,128)S(1)}, f32[32,1536]{1,0:T(8,128)S(1)}, u32[]{:S(2)}, u32[]{:S(2)}) collective-permute-start(f32[32,1536]{1,0:T(8,128)S(1)} %get-tuple-element.35), channel_id=1, source_target_pairs={{0,16},{4,20},{8,24},{12,28},{16,0},{20,4},{24,8},{28,12},{32,48},... | collective-permute-start | bytes 589832 | tf_op jit(solution)/shard_map/ppermute | solution.py:48
  98.0 8.3 %collective-permute-done.11 = f32[32,1536]{1,0:T(8,128)S(1)} collective-permute-done((f32[32,1536]{1,0:T(8,128)S(1)}, f32[32,1536]{1,0:T(8,128)S(1)}, u32[]{:S(2)}, u32[]{:S(2)}) %collective-permute-start.11) | collective-permute-done | bytes 196640 | tf_op jit(solution)/shard_map/ppermute | solution.py:48
  109.3 4.0 %all-to-all-start.1 = ((f32[4,2,256,128]{3,2,1,0:T(8,128)}), f32[4,2,256,128]{3,2,1,0:T(8,128)S(1)}, u32[]{:S(2)}, u32[]{:S(2)}) async-start(f32[4,2,256,128]{3,2,1,0:T(8,128)} %broadcast_in_dim.14), calls=%async_computation.1 | async-start | bytes 2097152 | tf_op jit(solution)/shard_map/all_to_all | solution.py:233
  113.3 3.6 %collective-permute-start.12 = (f32[32,1536]{1,0:T(8,128)S(1)}, f32[32,1536]{1,0:T(8,128)S(1)}, u32[]{:S(2)}, u32[]{:S(2)}) collective-permute-start(f32[32,1536]{1,0:T(8,128)S(1)} %add.24.refs_0_), channel_id=1, source_target_pairs={{0,32},{4,36},{8,40},{12,44},{16,48},{20,52},{24,56},{28,60},{32,0... | collective-permute-start | bytes 589832 | tf_op jit(solution)/shard_map/ppermute | solution.py:48
  116.9 21.6 %collective-permute-done.12.refs_1_ = f32[32,1536]{1,0:T(8,128)S(1)} collective-permute-done((f32[32,1536]{1,0:T(8,128)S(1)}, f32[32,1536]{1,0:T(8,128)S(1)}, u32[]{:S(2)}, u32[]{:S(2)}) %collective-permute-start.12) | collective-permute-done | bytes 196640 | tf_op jit(solution)/shard_map/ppermute | solution.py:48
  138.5 2.4 %collective-permute-start.13 = (f32[4,2,256,128]{3,2,1,0:T(8,128)S(1)}, f32[4,2,256,128]{3,2,1,0:T(8,128)S(1)}, u32[]{:S(2)}, u32[]{:S(2)}) collective-permute-start(f32[4,2,256,128]{3,2,1,0:T(8,128)S(1)} %all-to-all-done.1.refs_2_.m2), channel_id=1, source_target_pairs={{0,4},{4,0},{8,12},{12,8},{16,20},{20,16},{24,28},{28,24},{32,36},... | collective-permute-start | bytes 3145736 | tf_op jit(solution)/shard_map/ppermute | solution.py:48
  140.9 2.3 %collective-permute-done.13.refs_3_.o2 = f32[4,2,256,128]{3,2,1,0:T(8,128)S(1)} collective-permute-done((f32[4,2,256,128]{3,2,1,0:T(8,128)S(1)}, f32[4,2,256,128]{3,2,1,0:T(8,128)S(1)}, u32[]{:S(2)}, u32[]{:S(2)}) %collective-permute-start.13) | collective-permute-done | bytes 1048608 | tf_op jit(solution)/shard_map/ppermute | solution.py:48
  146.4 2.3 %collective-permute-start.16 = (f32[4,3,256,128]{3,2,1,0:T(8,128)}, f32[4,3,256,128]{3,2,1,0:T(8,128)S(1)}, u32[]{:S(2)}, u32[]{:S(2)}) collective-permute-start(f32[4,3,256,128]{3,2,1,0:T(8,128)} %bitcast.29), channel_id=1, source_target_pairs={{0,4},{4,0},{8,12},{12,8},{16,20},{20,16},{24,28},{28,24},{32,36},... | collective-permute-start | bytes 4718600 | tf_op jit(solution)/shard_map/ppermute | solution.py:48
  148.7 4.3 %collective-permute-start.14 = (f32[32,1024]{1,0:T(8,128)}, f32[32,1024]{1,0:T(8,128)S(1)}, u32[]{:S(2)}, u32[]{:S(2)}) collective-permute-start(f32[32,1024]{1,0:T(8,128)} %copy-done.12), channel_id=1, source_target_pairs={{0,96},{4,100},{8,104},{12,108},{16,112},{20,116},{24,120},{28,124... | collective-permute-start | bytes 393224 | tf_op jit(solution)/shard_map/ppermute | solution.py:48
  153.0 11.8 %collective-permute-done.14 = f32[32,1024]{1,0:T(8,128)S(1)} collective-permute-done((f32[32,1024]{1,0:T(8,128)}, f32[32,1024]{1,0:T(8,128)S(1)}, u32[]{:S(2)}, u32[]{:S(2)}) %collective-permute-start.14) | collective-permute-done | bytes 131104 | tf_op jit(solution)/shard_map/ppermute | solution.py:48
  165.8 3.3 %collective-permute-start.15 = (f32[32,1024]{1,0:T(8,128)S(1)}, f32[32,1024]{1,0:T(8,128)S(1)}, u32[]{:S(2)}, u32[]{:S(2)}) collective-permute-start(f32[32,1024]{1,0:T(8,128)S(1)} %add.25.refs_0_), channel_id=1, source_target_pairs={{0,128},{4,132},{8,136},{12,140},{16,144},{20,148},{24,152},{28,15... | collective-permute-start | bytes 393224 | tf_op jit(solution)/shard_map/ppermute | solution.py:48
  169.1 3.0 %collective-permute-done.15.refs_1_ = f32[32,1024]{1,0:T(8,128)S(1)} collective-permute-done((f32[32,1024]{1,0:T(8,128)S(1)}, f32[32,1024]{1,0:T(8,128)S(1)}, u32[]{:S(2)}, u32[]{:S(2)}) %collective-permute-start.15) | collective-permute-done | bytes 131104 | tf_op jit(solution)/shard_map/ppermute | solution.py:48
  174.5 4.4 %collective-permute-start.17 = (f32[32,512]{1,0:T(8,128)S(1)}, f32[32,512]{1,0:T(8,128)S(1)}, u32[]{:S(2)}, u32[]{:S(2)}) collective-permute-start(f32[32,512]{1,0:T(8,128)S(1)} %get-tuple-element.44.right), channel_id=1, source_target_pairs={{0,384},{4,388},{8,392},{12,396},{16,400},{20,404},{24,408},{28,41... | collective-permute-start | bytes 196616 | tf_op jit(solution)/shard_map/ppermute | solution.py:48
  180.8 3.6 %shard_map.99 = f32[32,2048]{1,0:T(8,128)S(1)} custom-call(s32[1]{0:T(128)} %bitcast.5.plane, f32[32,512]{1,0:T(8,128)S(1)} %get-tuple-element.44.right, f32[32,512]{1,0:T(8,128)S(1)} %collective-permute-done.17.right_far, f32[32,512]{1,0:T(8,128)S(1)} %copy-done.15, f32[32,512]{1,0:T(8,128)S(1)} %copy-done.17, f32[32,512]{1,0:T(8,128)S(1)} %get-tuple-element.47.z3, ...), custom_call_target="tpu_custom_call" | custom-call | tf_op jit(solution)/shard_map/pallas_call | solution.py:206
  184.4 2.1 collective-permute-start.18
  186.4 5.2 %collective-permute-done.18 = f32[32,2048]{1,0:T(8,128)S(1)} collective-permute-done((f32[32,2048]{1,0:T(8,128)S(1)}, f32[32,2048]{1,0:T(8,128)S(1)}, u32[]{:S(2)}, u32[]{:S(2)}) %collective-permute-start.18) | collective-permute-done | bytes 262176 | tf_op jit(solution)/shard_map/ppermute | solution.py:48
  191.7 5.7 %collective-permute-start.19 = (f32[2,32,2048]{2,1,0:T(8,128)S(1)}, f32[2,32,2048]{2,1,0:T(8,128)S(1)}, u32[]{:S(2)}, u32[]{:S(2)}) collective-permute-start(f32[2,32,2048]{2,1,0:T(8,128)S(1)} %pad_maximum_fusion.2.near), channel_id=1, source_target_pairs={{0,4},{4,0},{8,12},{12,8},{16,20},{20,16},{24,28},{28,24},{32,36},... | collective-permute-start | bytes 1572872 | tf_op jit(solution)/shard_map/ppermute | solution.py:48
  198.9 4.7 %shard_map.100 = (f32[896,128]{1,0:T(8,128)}, f32[172,128]{1,0:T(8,128)}) custom-call(s32[5]{0:T(128)S(1)} %stack.68.where, s32[1,21]{1,0:T(1,128)S(1)} %copy-done.19, f32[896,128]{1,0:T(8,128)S(1)} %copy-done.10, f32[2,32,2048]{2,1,0:T(8,128)S(1)} %pad_maximum_fusion.2.near, f32[2,32,2048]{2,1,0:T(8,128)S(1)} %collective-permute-done.19.across_core, ...), custom_call_target="tpu_custom_call" | custom-call | tf_op jit(solution)/shard_map/pallas_call | solution.py:206
  (85 shorter events, 28.6 us)
Async XLA Ops:
  8.1 21.6 %collective-permute-start = (f32[2,128,128]{2,1,0:T(8,128)S(1)}, f32[2,128,128]{2,1,0:T(8,128)S(1)}, u32[]{:S(2)}, u32[]{:S(2)}) collective-permute-start(f32[2,128,128]{2,1,0:T(8,128)S(1)} %pad_maximum_fusion.6), channel_id=1, source_target_pairs={{0,8},{4,12},{8,0},{12,4},{16,24},{20,28},{24,16},{28,20},{32,40},... | collective-permute-start | bytes 393224 | tf_op jit(solution)/shard_map/ppermute | solution.py:48
  13.1 16.5 %collective-permute-start.1 = (f32[1,4,128]{2,1,0:T(4,128)S(1)}, f32[1,4,128]{2,1,0:T(4,128)S(1)}, u32[]{:S(2)}, u32[]{:S(2)}) collective-permute-start(f32[1,4,128]{2,1,0:T(4,128)S(1)} %slice_bitcast_fusion.6), channel_id=1, source_target_pairs={{0,384},{4,388},{8,392},{12,396},{16,400},{20,404},{24,408},{28,41... | collective-permute-start | bytes 6152 | tf_op jit(solution)/shard_map/ppermute | solution.py:48
  29.7 29.9 %all-to-all-start = ((f32[4,32,2048]{2,1,0:T(8,128)}), f32[4,32,2048]{2,1,0:T(8,128)S(1)}, u32[]{:S(2)}, u32[]{:S(2)}) async-start(f32[4,32,2048]{2,1,0:T(8,128)} %bitcast.9), calls=%async_computation | async-start | bytes 2097152 | tf_op jit(solution)/shard_map/all_to_all | solution.py:256
  34.9 111.5 %all-gather.3.cloned.1.call-start = ((), (), s32[]{:S(2)}) async-start(), calls=%async_computation.2 | async-start | bytes 1966080 | tf_op jit(solution)/shard_map/all_gather | solution.py:275
  36.2 10.9 %collective-permute-start.5 = (f32[3,8,128]{2,1,0:T(8,128)S(1)}, f32[3,8,128]{2,1,0:T(8,128)S(1)}, u32[]{:S(2)}, u32[]{:S(2)}) collective-permute-start(f32[3,8,128]{2,1,0:T(8,128)S(1)} %pad_maximum_fusion.10), channel_id=1, source_target_pairs={{0,128},{4,132},{8,136},{12,140},{16,144},{20,148},{24,152},{28,15... | collective-permute-start | bytes 36872 | tf_op jit(solution)/shard_map/ppermute | solution.py:48
  38.2 21.3 %collective-permute-start.4 = (f32[2,256,128]{2,1,0:T(8,128)S(1)}, f32[2,256,128]{2,1,0:T(8,128)S(1)}, u32[]{:S(2)}, u32[]{:S(2)}) collective-permute-start(f32[2,256,128]{2,1,0:T(8,128)S(1)} %pad_maximum_fusion.4), channel_id=1, source_target_pairs={{0,3},{1,2},{2,1},{3,0},{4,7},{5,6},{6,5},{7,4},{8,11},{9,10},{10,... | collective-permute-start | bytes 786440 | tf_op jit(solution)/shard_map/ppermute | solution.py:48
  42.1 17.4 %collective-permute-start.3 = (f32[2,256,128]{2,1,0:T(8,128)S(1)}, f32[2,256,128]{2,1,0:T(8,128)S(1)}, u32[]{:S(2)}, u32[]{:S(2)}) collective-permute-start(f32[2,256,128]{2,1,0:T(8,128)S(1)} %pad_maximum_fusion.4), channel_id=1, source_target_pairs={{0,2},{1,3},{2,0},{3,1},{4,6},{5,7},{6,4},{7,5},{8,10},{9,11},{10,... | collective-permute-start | bytes 786440 | tf_op jit(solution)/shard_map/ppermute | solution.py:48
  44.5 15.0 %collective-permute-start.2 = (f32[2,256,128]{2,1,0:T(8,128)S(1)}, f32[2,256,128]{2,1,0:T(8,128)S(1)}, u32[]{:S(2)}, u32[]{:S(2)}) collective-permute-start(f32[2,256,128]{2,1,0:T(8,128)S(1)} %pad_maximum_fusion.4), channel_id=1, source_target_pairs={{0,1},{1,0},{2,3},{3,2},{4,5},{5,4},{6,7},{7,6},{8,9},{9,8},{10,11... | collective-permute-start | bytes 786440 | tf_op jit(solution)/shard_map/ppermute | solution.py:48
  47.2 12.3 %collective-permute-start.6 = (f32[3,16,128]{2,1,0:T(8,128)S(1)}, f32[3,16,128]{2,1,0:T(8,128)S(1)}, u32[]{:S(2)}, u32[]{:S(2)}) collective-permute-start(f32[3,16,128]{2,1,0:T(8,128)S(1)} %pad_maximum_fusion.9), channel_id=1, source_target_pairs={{0,96},{4,100},{8,104},{12,108},{16,112},{20,116},{24,120},{28,124... | collective-permute-start | bytes 73736 | tf_op jit(solution)/shard_map/ppermute | solution.py:48
  59.6 20.4 %collective-permute-start.7 = (f32[4,2,256,128]{3,2,1,0:T(8,128)S(1)}, f32[4,2,256,128]{3,2,1,0:T(8,128)S(1)}, u32[]{:S(2)}, u32[]{:S(2)}) collective-permute-start(f32[4,2,256,128]{3,2,1,0:T(8,128)S(1)} %pad_maximum_fusion.refs_1_.m1), channel_id=1, source_target_pairs={{0,4},{4,0},{8,12},{12,8},{16,20},{20,16},{24,28},{28,24},{32,36},... | collective-permute-start | bytes 3145736 | tf_op jit(solution)/shard_map/ppermute | solution.py:48
  64.9 15.1 %collective-permute-start.8 = (f32[5,32,128]{2,1,0:T(8,128)S(1)}, f32[5,32,128]{2,1,0:T(8,128)S(1)}, u32[]{:S(2)}, u32[]{:S(2)}) collective-permute-start(f32[5,32,128]{2,1,0:T(8,128)S(1)} %pad_maximum_fusion.7), channel_id=1, source_target_pairs={{0,32},{4,36},{8,40},{12,44},{16,48},{20,52},{24,56},{28,60},{32,0... | collective-permute-start | bytes 245768 | tf_op jit(solution)/shard_map/ppermute | solution.py:48
  81.0 25.2 %copy-start.14 = (f32[32,512]{1,0:T(8,128)}, f32[32,512]{1,0:T(8,128)S(1)}, u32[]{:S(2)}) copy-start(f32[32,512]{1,0:T(8,128)S(1)} %get-tuple-element.45.z1) | copy-start | bytes 196612
  81.1 12.2 %collective-permute-start.9 = (f32[5,64,128]{2,1,0:T(8,128)S(1)}, f32[5,64,128]{2,1,0:T(8,128)S(1)}, u32[]{:S(2)}, u32[]{:S(2)}) collective-permute-start(f32[5,64,128]{2,1,0:T(8,128)S(1)} %pad_maximum_fusion.5), channel_id=1, source_target_pairs={{0,16},{4,20},{8,24},{12,28},{16,0},{20,4},{24,8},{28,12},{32,48},... | collective-permute-start | bytes 491528 | tf_op jit(solution)/shard_map/ppermute | solution.py:48
  93.2 14.1 %collective-permute-start.10 = (f32[5,128,128]{2,1,0:T(8,128)S(1)}, f32[5,128,128]{2,1,0:T(8,128)S(1)}, u32[]{:S(2)}, u32[]{:S(2)}) collective-permute-start(f32[5,128,128]{2,1,0:T(8,128)S(1)} %pad_maximum_fusion.3), channel_id=1, source_target_pairs={{0,8},{4,12},{8,0},{12,4},{16,24},{20,28},{24,16},{28,20},{32,40},... | collective-permute-start | bytes 983048 | tf_op jit(solution)/shard_map/ppermute | solution.py:48
  95.2 11.1 %collective-permute-start.11 = (f32[32,1536]{1,0:T(8,128)S(1)}, f32[32,1536]{1,0:T(8,128)S(1)}, u32[]{:S(2)}, u32[]{:S(2)}) collective-permute-start(f32[32,1536]{1,0:T(8,128)S(1)} %get-tuple-element.35), channel_id=1, source_target_pairs={{0,16},{4,20},{8,24},{12,28},{16,0},{20,4},{24,8},{28,12},{32,48},... | collective-permute-start | bytes 589832 | tf_op jit(solution)/shard_map/ppermute | solution.py:48
  109.3 29.2 %all-to-all-start.1 = ((f32[4,2,256,128]{3,2,1,0:T(8,128)}), f32[4,2,256,128]{3,2,1,0:T(8,128)S(1)}, u32[]{:S(2)}, u32[]{:S(2)}) async-start(f32[4,2,256,128]{3,2,1,0:T(8,128)} %broadcast_in_dim.14), calls=%async_computation.1 | async-start | bytes 2097152 | tf_op jit(solution)/shard_map/all_to_all | solution.py:233
  113.3 25.2 %collective-permute-start.12 = (f32[32,1536]{1,0:T(8,128)S(1)}, f32[32,1536]{1,0:T(8,128)S(1)}, u32[]{:S(2)}, u32[]{:S(2)}) collective-permute-start(f32[32,1536]{1,0:T(8,128)S(1)} %add.24.refs_0_), channel_id=1, source_target_pairs={{0,32},{4,36},{8,40},{12,44},{16,48},{20,52},{24,56},{28,60},{32,0... | collective-permute-start | bytes 589832 | tf_op jit(solution)/shard_map/ppermute | solution.py:48
  138.5 4.7 %collective-permute-start.13 = (f32[4,2,256,128]{3,2,1,0:T(8,128)S(1)}, f32[4,2,256,128]{3,2,1,0:T(8,128)S(1)}, u32[]{:S(2)}, u32[]{:S(2)}) collective-permute-start(f32[4,2,256,128]{3,2,1,0:T(8,128)S(1)} %all-to-all-done.1.refs_2_.m2), channel_id=1, source_target_pairs={{0,4},{4,0},{8,12},{12,8},{16,20},{20,16},{24,28},{28,24},{32,36},... | collective-permute-start | bytes 3145736 | tf_op jit(solution)/shard_map/ppermute | solution.py:48
  146.4 25.8 %collective-permute-start.16 = (f32[4,3,256,128]{3,2,1,0:T(8,128)}, f32[4,3,256,128]{3,2,1,0:T(8,128)S(1)}, u32[]{:S(2)}, u32[]{:S(2)}) collective-permute-start(f32[4,3,256,128]{3,2,1,0:T(8,128)} %bitcast.29), channel_id=1, source_target_pairs={{0,4},{4,0},{8,12},{12,8},{16,20},{20,16},{24,28},{28,24},{32,36},... | collective-permute-start | bytes 4718600 | tf_op jit(solution)/shard_map/ppermute | solution.py:48
  148.7 16.1 %collective-permute-start.14 = (f32[32,1024]{1,0:T(8,128)}, f32[32,1024]{1,0:T(8,128)S(1)}, u32[]{:S(2)}, u32[]{:S(2)}) collective-permute-start(f32[32,1024]{1,0:T(8,128)} %copy-done.12), channel_id=1, source_target_pairs={{0,96},{4,100},{8,104},{12,108},{16,112},{20,116},{24,120},{28,124... | collective-permute-start | bytes 393224 | tf_op jit(solution)/shard_map/ppermute | solution.py:48
  164.8 15.9 %copy-start.15 = (f32[32,512]{1,0:T(8,128)S(1)}, f32[32,512]{1,0:T(8,128)}, u32[]{:S(2)}) copy-start(f32[32,512]{1,0:T(8,128)} %copy-done.14) | copy-start | bytes 196612
  164.8 15.9 %copy-start.17 = (f32[32,512]{1,0:T(8,128)S(1)}, f32[32,512]{1,0:T(8,128)}, u32[]{:S(2)}) copy-start(f32[32,512]{1,0:T(8,128)} %copy-done.16) | copy-start | bytes 196612
  165.8 6.4 %collective-permute-start.15 = (f32[32,1024]{1,0:T(8,128)S(1)}, f32[32,1024]{1,0:T(8,128)S(1)}, u32[]{:S(2)}, u32[]{:S(2)}) collective-permute-start(f32[32,1024]{1,0:T(8,128)S(1)} %add.25.refs_0_), channel_id=1, source_target_pairs={{0,128},{4,132},{8,136},{12,140},{16,144},{20,148},{24,152},{28,15... | collective-permute-start | bytes 393224 | tf_op jit(solution)/shard_map/ppermute | solution.py:48
  173.6 7.2 %copy-start.6 = (f32[4,2,256,128]{3,2,1,0:T(8,128)S(1)}, f32[4,2,256,128]{3,2,1,0:T(8,128)}, u32[]{:S(2)}) copy-start(f32[4,2,256,128]{3,2,1,0:T(8,128)} %copy-done.5) | copy-start | bytes 3145732
  174.5 6.2 %collective-permute-start.17 = (f32[32,512]{1,0:T(8,128)S(1)}, f32[32,512]{1,0:T(8,128)S(1)}, u32[]{:S(2)}, u32[]{:S(2)}) collective-permute-start(f32[32,512]{1,0:T(8,128)S(1)} %get-tuple-element.44.right), channel_id=1, source_target_pairs={{0,384},{4,388},{8,392},{12,396},{16,400},{20,404},{24,408},{28,41... | collective-permute-start | bytes 196616 | tf_op jit(solution)/shard_map/ppermute | solution.py:48
  180.8 18.1 %copy-start.2 = (f32[21,128,128]{2,1,0:T(8,128)S(1)}, f32[21,128,128]{2,1,0:T(8,128)}, u32[]{:S(2)}) copy-start(f32[21,128,128]{2,1,0:T(8,128)} %blocks.3) | copy-start | bytes 4128772
  180.8 18.1 %copy-start.8 = (f32[7,128,128]{2,1,0:T(8,128)S(1)}, f32[7,128,128]{2,1,0:T(8,128)}, u32[]{:S(2)}) copy-start(f32[7,128,128]{2,1,0:T(8,128)} %inverse.3) | copy-start | bytes 1376260
  180.8 18.1 %copy-start.10 = (f32[896,128]{1,0:T(8,128)S(1)}, f32[896,128]{1,0:T(8,128)}, u32[]{:S(2)}) copy-start(f32[896,128]{1,0:T(8,128)} %copy-done.9) | copy-start | bytes 1376260
  180.8 18.1 %copy-start.19 = (s32[1,21]{1,0:T(1,128)S(1)}, s32[1,21]{1,0:T(1,128)}, u32[]{:S(2)}) copy-start(s32[1,21]{1,0:T(1,128)} %pattern.3) | copy-start | bytes 256
  184.4 14.5 %copy-start.4 = (f32[512,512]{1,0:T(8,128)S(1)}, f32[512,512]{1,0:T(8,128)}, u32[]{:S(2)}) copy-start(f32[512,512]{1,0:T(8,128)} %coupling.3) | copy-start | bytes 3145732
  184.4 7.2 %collective-permute-start.18 = (f32[32,2048]{1,0:T(8,128)S(1)}, f32[32,2048]{1,0:T(8,128)S(1)}, u32[]{:S(2)}, u32[]{:S(2)}) collective-permute-start(f32[32,2048]{1,0:T(8,128)S(1)} %shard_map.99), channel_id=1, source_target_pairs={{0,8},{4,12},{8,0},{12,4},{16,24},{20,28},{24,16},{28,20},{32,40},... | collective-permute-start | bytes 786440 | tf_op jit(solution)/shard_map/ppermute | solution.py:48
  191.7 7.2 %collective-permute-start.19 = (f32[2,32,2048]{2,1,0:T(8,128)S(1)}, f32[2,32,2048]{2,1,0:T(8,128)S(1)}, u32[]{:S(2)}, u32[]{:S(2)}) collective-permute-start(f32[2,32,2048]{2,1,0:T(8,128)S(1)} %pad_maximum_fusion.2.near), channel_id=1, source_target_pairs={{0,4},{4,0},{8,12},{12,8},{16,20},{20,16},{24,28},{28,24},{32,36},... | collective-permute-start | bytes 1572872 | tf_op jit(solution)/shard_map/ppermute | solution.py:48
  (11 other events, 10.6 us)
Sparse Core Ops, SparseCore 0:
  108.3 33.9 all-gather.2

commit v13 on v12

--- a/solution.py
+++ b/solution.py
@@ -71,13 +71,29 @@
     return jnp.where(inside & (row - offset == column - start), 1.0, 0.0).astype(BF16)
 
 
-def forward_kernel(sizes, where, pattern, rhs, inverse, blocks, coupling, sep_rhs, y_out, t_out):
+def forward_kernel(
+    sizes, where, pattern, rhs_far, inverse_far, blocks_far, coupling_far, sep_rhs, y_out, t_out, rhs, inverse, blocks, coupling, sems
+):
     count, size = inverse.shape[0], inverse.shape[1]
     starts = pair_starts(count)
+    copies = [
+        pltpu.make_async_copy(rhs_far, rhs, sems.at[0]),
+        pltpu.make_async_copy(inverse_far, inverse, sems.at[1]),
+        pltpu.make_async_copy(coupling_far, coupling, sems.at[2]),
+    ]
+    for column in range(count - 1):
+        part = pl.ds(starts[column], count - 1 - column)
+        copies.append(pltpu.make_async_copy(blocks_far.at[part], blocks.at[part], sems.at[3 + column]))
+    for copy in copies[:2] + copies[3:] + copies[2:3]:
+        copy.start()
+    copies[0].wait()
+    copies[1].wait()
     pending = [rhs[i * size : (i + 1) * size, :] for i in range(count)]
     for column in range(count):
         solved = mm(inverse[column], pending[column], NN)
         y_out[column * size : (column + 1) * size, :] = solved
+        if column < count - 1:
+            copies[3 + column].wait()
         for later in range(column + 1, count):
             pair = starts[column] + later - column - 1
             weight = pattern[0, pair].astype(F32)
@@ -85,6 +101,7 @@
     last = y_out[(count - 1) * size :, :]
     right = sep_rhs[...]
     width = coupling.shape[1]
+    copies[2].wait()
     offset = 0
     for level, rows in enumerate(sizes):
         spread = placement(right.shape[0], offset, rows, where[level], width)
@@ -246,11 +263,18 @@
 
     first = grow(both(0), 1 << Z1)
     far = grow(rows(sep_inverse, 3)[None], wrap_y)
-    y, t = call(
+    y, t = pl.pallas_call(
         functools.partial(forward_kernel, sizes),
-        [leaf_rhs.shape, (columns, LEVELS * width)],
-        where, leaf_pattern, leaf_rhs, leaf_inverse, leaf_blocks, leaf_coupling, sep_rhs,
-    )
+        out_shape=[
+            jax.ShapeDtypeStruct(leaf_rhs.shape, F32),
+            jax.ShapeDtypeStruct((columns, LEVELS * width), F32),
+        ],
+        in_specs=[SMEM, SMEM] + [pl.BlockSpec(memory_space=pl.ANY)] * 4 + [VMEM],
+        out_specs=[VMEM, VMEM],
+        scratch_shapes=[pltpu.VMEM(v.shape, F32) for v in (leaf_rhs, leaf_inverse, leaf_blocks, leaf_coupling)]
+        + [pltpu.SemaphoreType.DMA((2 + leaf_inverse.shape[0],))],
+        compiler_params=pltpu.CompilerParams(vmem_limit_bytes=58 * 1024 * 1024),
+    )(where, leaf_pattern, leaf_rhs, leaf_inverse, leaf_blocks, leaf_coupling, sep_rhs)
     t, first, far = tie((t, first, far))
 
     t = lax.all_to_all(t, "leaf", 0, 0, axis_index_groups=near, tiled=True)
@@ -277,9 +301,9 @@
 
     second = (second, across(second, CORE_MASK))
     z2, v = solve(0, False, 2, v, v_far, *second)
+    v = v + across(v, wrap_z)
     v, third = tie((v, third))
 
-    v = v + across(v, wrap_z)
     third = (third, across(third, CORE_MASK))
     z3, v = solve(1, False, 1, v, across(v, 1 << Y1), *third)
     (x,) = call(

time: 212 us -> 202 us (0.953)
  local copies, waits for them, and re-layouts: 16.9 us -> 9.88 us
  starting transfers between devices: 84 us -> 81.5 us
    unnamed x40 -> x26, local copies, waits for them, and re-layouts: 10.6 us -> 3.05 us
    pallas_call x0 -> x1, Pallas kernels: none -> 6.58 us  [shards(): pl.pallas_call(functools.partial(forward_kernel, sizes), out_shape=[jax.S...]
    pallas_call x6 -> x5, Pallas kernels: 15.9 us -> 11 us  [call(): pl.pallas_call(kernel, out_shape=[jax.ShapeDtypeStruct(s, F32) for s in o...]
    ppermute x20, starting transfers between devices: 74.8 us -> 72.3 us  [swap(): lax.ppermute(value, axis, [(i, i ^ mask) for i in range(lax.axis_size(axi...]
  transfers between devices with their start and end apart: 23 -> 23, of which waited for: 12 -> 12; matrix products, arithmetic and copies ran while one was open for 3% -> 3% of each run, Pallas kernels for 3% -> 4%
where the time goes in v13:
time: 202 us; the launch traced here: 201 us
  starting transfers between devices  81.5 us (40%)
  waiting for transfers between devices  76.9 us (38%)
  Pallas kernels  17.6 us (9%)
  between operations  14.5 us (7%)
  local copies, waits for them, and re-layouts  9.88 us (5%)
    ppermute x20, waiting for transfers between devices, swap(): lax.ppermute(value, axis, [(i, i ^ mask) for i in range(lax.axis_size(axi...  76.8 us
    ppermute x20, starting transfers between devices, swap(): lax.ppermute(value, axis, [(i, i ^ mask) for i in range(lax.axis_size(axi...  72.3 us
    pallas_call x5, Pallas kernels, call(): pl.pallas_call(kernel, out_shape=[jax.ShapeDtypeStruct(s, F32) for s in o...  11 us
    pallas_call x1, Pallas kernels, shards(): pl.pallas_call(functools.partial(forward_kernel, sizes), out_shape=[jax.S...  6.58 us
    all_to_all x1, starting transfers between devices, shards(): t = lax.all_to_all(t, 'leaf', 0, 0, axis_index_groups=near, tiled=True)  5.19 us
  transfers between devices with their start and end apart: 23, of which 12 were waited for; matrix products, arithmetic and copies ran while one was open for 3% of the time, Pallas kernels for 4%

profile of v13, /device:TPU:1, one launch (start us, length us, event | category | flops | bytes accessed | tf_op | source)
XLA Modules:
  0.0 200.6 jit_solution(934395163148645887)
XLA Ops:
  8.1 4.4 %collective-permute-start = (f32[2,128,128]{2,1,0:T(8,128)S(1)}, f32[2,128,128]{2,1,0:T(8,128)S(1)}, u32[]{:S(2)}, u32[]{:S(2)}) collective-permute-start(f32[2,128,128]{2,1,0:T(8,128)S(1)} %pad_maximum_fusion.6), channel_id=1, source_target_pairs={{0,8},{4,12},{8,0},{12,4},{16,24},{20,28},{24,16},{28,20},{32,40},... | collective-permute-start | bytes 393224 | tf_op jit(solution)/shard_map/ppermute | solution.py:48
  13.1 4.6 %collective-permute-start.1 = (f32[1,4,128]{2,1,0:T(4,128)S(1)}, f32[1,4,128]{2,1,0:T(4,128)S(1)}, u32[]{:S(2)}, u32[]{:S(2)}) collective-permute-start(f32[1,4,128]{2,1,0:T(4,128)S(1)} %slice_bitcast_fusion.6), channel_id=1, source_target_pairs={{0,384},{4,388},{8,392},{12,396},{16,400},{20,404},{24,408},{28,41... | collective-permute-start | bytes 6152 | tf_op jit(solution)/shard_map/ppermute | solution.py:48
  18.4 6.6 %shard_map.95 = (f32[896,128]{1,0:T(8,128)}, f32[128,2048]{1,0:T(8,128)}) custom-call(s32[5]{0:T(128)} %stack.68.where, s32[1,21]{1,0:T(1,128)} %pattern.3, f32[896,128]{1,0:T(8,128)} %rhs_far.1, f32[7,128,128]{2,1,0:T(8,128)} %inverse.1, f32[21,128,128]{2,1,0:T(8,128)} %blocks.1, f32[512,512]{1,0:T(8,128)} %coupling.1, f32[172,128]{1,0:T(8,128)} %sep_rhs.1), custom_call_target="tpu_custom_call" | custom-call | tf_op jit(solution)/shard_map/pallas_call | solution.py:266
  25.1 5.2 %all-to-all-start = ((f32[4,32,2048]{2,1,0:T(8,128)}), f32[4,32,2048]{2,1,0:T(8,128)S(1)}, u32[]{:S(2)}, u32[]{:S(2)}) async-start(f32[4,32,2048]{2,1,0:T(8,128)} %bitcast.34), calls=%async_computation | async-start | bytes 2097152 | tf_op jit(solution)/shard_map/all_to_all | solution.py:280
  33.6 3.9 %collective-permute-start.4 = (f32[2,256,128]{2,1,0:T(8,128)S(1)}, f32[2,256,128]{2,1,0:T(8,128)S(1)}, u32[]{:S(2)}, u32[]{:S(2)}) collective-permute-start(f32[2,256,128]{2,1,0:T(8,128)S(1)} %pad_maximum_fusion.4), channel_id=1, source_target_pairs={{0,3},{1,2},{2,1},{3,0},{4,7},{5,6},{6,5},{7,4},{8,11},{9,10},{10,... | collective-permute-start | bytes 786440 | tf_op jit(solution)/shard_map/ppermute | solution.py:48
  37.5 2.4 %collective-permute-start.3 = (f32[2,256,128]{2,1,0:T(8,128)S(1)}, f32[2,256,128]{2,1,0:T(8,128)S(1)}, u32[]{:S(2)}, u32[]{:S(2)}) collective-permute-start(f32[2,256,128]{2,1,0:T(8,128)S(1)} %pad_maximum_fusion.4), channel_id=1, source_target_pairs={{0,2},{1,3},{2,0},{3,1},{4,6},{5,7},{6,4},{7,5},{8,10},{9,11},{10,... | collective-permute-start | bytes 786440 | tf_op jit(solution)/shard_map/ppermute | solution.py:48
  39.9 2.6 %collective-permute-start.2 = (f32[2,256,128]{2,1,0:T(8,128)S(1)}, f32[2,256,128]{2,1,0:T(8,128)S(1)}, u32[]{:S(2)}, u32[]{:S(2)}) collective-permute-start(f32[2,256,128]{2,1,0:T(8,128)S(1)} %pad_maximum_fusion.4), channel_id=1, source_target_pairs={{0,1},{1,0},{2,3},{3,2},{4,5},{5,4},{6,7},{7,6},{8,9},{9,8},{10,11... | collective-permute-start | bytes 786440 | tf_op jit(solution)/shard_map/ppermute | solution.py:48
  42.6 11.1 %collective-permute-start.6 = (f32[3,16,128]{2,1,0:T(8,128)S(1)}, f32[3,16,128]{2,1,0:T(8,128)S(1)}, u32[]{:S(2)}, u32[]{:S(2)}) collective-permute-start(f32[3,16,128]{2,1,0:T(8,128)S(1)} %pad_maximum_fusion.9), channel_id=1, source_target_pairs={{0,96},{4,100},{8,104},{12,108},{16,112},{20,116},{24,120},{28,124... | collective-permute-start | bytes 73736 | tf_op jit(solution)/shard_map/ppermute | solution.py:48
  55.0 3.8 %collective-permute-start.7 = (f32[4,2,256,128]{3,2,1,0:T(8,128)S(1)}, f32[4,2,256,128]{3,2,1,0:T(8,128)S(1)}, u32[]{:S(2)}, u32[]{:S(2)}) collective-permute-start(f32[4,2,256,128]{3,2,1,0:T(8,128)S(1)} %pad_maximum_fusion.refs_1_.m1), channel_id=1, source_target_pairs={{0,4},{4,0},{8,12},{12,8},{16,20},{20,16},{24,28},{28,24},{32,36},... | collective-permute-start | bytes 3145736 | tf_op jit(solution)/shard_map/ppermute | solution.py:48
  60.3 5.3 %collective-permute-start.8 = (f32[5,32,128]{2,1,0:T(8,128)S(1)}, f32[5,32,128]{2,1,0:T(8,128)S(1)}, u32[]{:S(2)}, u32[]{:S(2)}) collective-permute-start(f32[5,32,128]{2,1,0:T(8,128)S(1)} %pad_maximum_fusion.7), channel_id=1, source_target_pairs={{0,32},{4,36},{8,40},{12,44},{16,48},{20,52},{24,56},{28,60},{32,0... | collective-permute-start | bytes 245768 | tf_op jit(solution)/shard_map/ppermute | solution.py:48
  65.6 9.8 %collective-permute-done.8 = f32[5,32,128]{2,1,0:T(8,128)S(1)} collective-permute-done((f32[5,32,128]{2,1,0:T(8,128)S(1)}, f32[5,32,128]{2,1,0:T(8,128)S(1)}, u32[]{:S(2)}, u32[]{:S(2)}) %collective-permute-start.8) | collective-permute-done | bytes 81952 | tf_op jit(solution)/shard_map/ppermute | solution.py:48
  76.4 1.9 collective-permute-start.9
  78.4 10.2 %collective-permute-done.9 = f32[5,64,128]{2,1,0:T(8,128)S(1)} collective-permute-done((f32[5,64,128]{2,1,0:T(8,128)S(1)}, f32[5,64,128]{2,1,0:T(8,128)S(1)}, u32[]{:S(2)}, u32[]{:S(2)}) %collective-permute-start.9) | collective-permute-done | bytes 163872 | tf_op jit(solution)/shard_map/ppermute | solution.py:48
  90.6 2.8 %collective-permute-start.11 = (f32[32,1536]{1,0:T(8,128)S(1)}, f32[32,1536]{1,0:T(8,128)S(1)}, u32[]{:S(2)}, u32[]{:S(2)}) collective-permute-start(f32[32,1536]{1,0:T(8,128)S(1)} %get-tuple-element.35), channel_id=1, source_target_pairs={{0,16},{4,20},{8,24},{12,28},{16,0},{20,4},{24,8},{28,12},{32,48},... | collective-permute-start | bytes 589832 | tf_op jit(solution)/shard_map/ppermute | solution.py:48
  93.4 8.3 %collective-permute-done.11 = f32[32,1536]{1,0:T(8,128)S(1)} collective-permute-done((f32[32,1536]{1,0:T(8,128)S(1)}, f32[32,1536]{1,0:T(8,128)S(1)}, u32[]{:S(2)}, u32[]{:S(2)}) %collective-permute-start.11) | collective-permute-done | bytes 196640 | tf_op jit(solution)/shard_map/ppermute | solution.py:48
  104.7 4.0 %all-to-all-start.1 = ((f32[4,2,256,128]{3,2,1,0:T(8,128)}), f32[4,2,256,128]{3,2,1,0:T(8,128)S(1)}, u32[]{:S(2)}, u32[]{:S(2)}) async-start(f32[4,2,256,128]{3,2,1,0:T(8,128)} %broadcast_in_dim.14), calls=%async_computation.1 | async-start | bytes 2097152 | tf_op jit(solution)/shard_map/all_to_all | solution.py:250
  108.7 3.6 %collective-permute-start.12 = (f32[32,1536]{1,0:T(8,128)S(1)}, f32[32,1536]{1,0:T(8,128)S(1)}, u32[]{:S(2)}, u32[]{:S(2)}) collective-permute-start(f32[32,1536]{1,0:T(8,128)S(1)} %add.24.refs_0_), channel_id=1, source_target_pairs={{0,32},{4,36},{8,40},{12,44},{16,48},{20,52},{24,56},{28,60},{32,0... | collective-permute-start | bytes 589832 | tf_op jit(solution)/shard_map/ppermute | solution.py:48
  112.3 21.6 %collective-permute-done.12.refs_1_ = f32[32,1536]{1,0:T(8,128)S(1)} collective-permute-done((f32[32,1536]{1,0:T(8,128)S(1)}, f32[32,1536]{1,0:T(8,128)S(1)}, u32[]{:S(2)}, u32[]{:S(2)}) %collective-permute-start.12) | collective-permute-done | bytes 196640 | tf_op jit(solution)/shard_map/ppermute | solution.py:48
  133.9 2.5 %collective-permute-start.13 = (f32[4,2,256,128]{3,2,1,0:T(8,128)S(1)}, f32[4,2,256,128]{3,2,1,0:T(8,128)S(1)}, u32[]{:S(2)}, u32[]{:S(2)}) collective-permute-start(f32[4,2,256,128]{3,2,1,0:T(8,128)S(1)} %all-to-all-done.1.refs_2_.m2), channel_id=1, source_target_pairs={{0,4},{4,0},{8,12},{12,8},{16,20},{20,16},{24,28},{28,24},{32,36},... | collective-permute-start | bytes 3145736 | tf_op jit(solution)/shard_map/ppermute | solution.py:48
  136.3 2.3 %collective-permute-done.13.refs_3_.o2 = f32[4,2,256,128]{3,2,1,0:T(8,128)S(1)} collective-permute-done((f32[4,2,256,128]{3,2,1,0:T(8,128)S(1)}, f32[4,2,256,128]{3,2,1,0:T(8,128)S(1)}, u32[]{:S(2)}, u32[]{:S(2)}) %collective-permute-start.13) | collective-permute-done | bytes 1048608 | tf_op jit(solution)/shard_map/ppermute | solution.py:48
  141.1 4.1 %collective-permute-start.14 = (f32[32,1024]{1,0:T(8,128)S(1)}, f32[32,1024]{1,0:T(8,128)S(1)}, u32[]{:S(2)}, u32[]{:S(2)}) collective-permute-start(f32[32,1024]{1,0:T(8,128)S(1)} %get-tuple-element.41), channel_id=1, source_target_pairs={{0,96},{4,100},{8,104},{12,108},{16,112},{20,116},{24,120},{28,124... | collective-permute-start | bytes 393224 | tf_op jit(solution)/shard_map/ppermute | solution.py:48
  145.3 7.7 %collective-permute-done.14 = f32[32,1024]{1,0:T(8,128)S(1)} collective-permute-done((f32[32,1024]{1,0:T(8,128)S(1)}, f32[32,1024]{1,0:T(8,128)S(1)}, u32[]{:S(2)}, u32[]{:S(2)}) %collective-permute-start.14) | collective-permute-done | bytes 131104 | tf_op jit(solution)/shard_map/ppermute | solution.py:48
  153.1 2.6 %collective-permute-start.16 = (f32[4,3,256,128]{3,2,1,0:T(8,128)}, f32[4,3,256,128]{3,2,1,0:T(8,128)S(1)}, u32[]{:S(2)}, u32[]{:S(2)}) collective-permute-start(f32[4,3,256,128]{3,2,1,0:T(8,128)} %bitcast.29), channel_id=1, source_target_pairs={{0,4},{4,0},{8,12},{12,8},{16,20},{20,16},{24,28},{28,24},{32,36},... | collective-permute-start | bytes 4718600 | tf_op jit(solution)/shard_map/ppermute | solution.py:48
  155.6 3.4 %collective-permute-start.15 = (f32[32,1024]{1,0:T(8,128)S(1)}, f32[32,1024]{1,0:T(8,128)S(1)}, u32[]{:S(2)}, u32[]{:S(2)}) collective-permute-start(f32[32,1024]{1,0:T(8,128)S(1)} %add.25.refs_0_), channel_id=1, source_target_pairs={{0,128},{4,132},{8,136},{12,140},{16,144},{20,148},{24,152},{28,15... | collective-permute-start | bytes 393224 | tf_op jit(solution)/shard_map/ppermute | solution.py:48
  159.0 3.7 %collective-permute-done.15.refs_1_ = f32[32,1024]{1,0:T(8,128)S(1)} collective-permute-done((f32[32,1024]{1,0:T(8,128)S(1)}, f32[32,1024]{1,0:T(8,128)S(1)}, u32[]{:S(2)}, u32[]{:S(2)}) %collective-permute-start.15) | collective-permute-done | bytes 131104 | tf_op jit(solution)/shard_map/ppermute | solution.py:48
  165.0 2.5 %collective-permute-start.17 = (f32[32,512]{1,0:T(8,128)S(1)}, f32[32,512]{1,0:T(8,128)S(1)}, u32[]{:S(2)}, u32[]{:S(2)}) collective-permute-start(f32[32,512]{1,0:T(8,128)S(1)} %get-tuple-element.44.right), channel_id=1, source_target_pairs={{0,384},{4,388},{8,392},{12,396},{16,400},{20,404},{24,408},{28,41... | collective-permute-start | bytes 196616 | tf_op jit(solution)/shard_map/ppermute | solution.py:48
  167.6 3.7 %collective-permute-done.17.right_far = f32[32,512]{1,0:T(8,128)S(1)} collective-permute-done((f32[32,512]{1,0:T(8,128)S(1)}, f32[32,512]{1,0:T(8,128)S(1)}, u32[]{:S(2)}, u32[]{:S(2)}) %collective-permute-start.17) | collective-permute-done | bytes 65568 | tf_op jit(solution)/shard_map/ppermute | solution.py:48
  171.3 3.5 %shard_map.99 = f32[32,2048]{1,0:T(8,128)S(1)} custom-call(s32[1]{0:T(128)} %bitcast.5.plane, f32[32,512]{1,0:T(8,128)S(1)} %get-tuple-element.44.right, f32[32,512]{1,0:T(8,128)S(1)} %collective-permute-done.17.right_far, f32[32,512]{1,0:T(8,128)S(1)} %copy-done.8, f32[32,512]{1,0:T(8,128)S(1)} %copy-done.10, f32[32,512]{1,0:T(8,128)S(1)} %get-tuple-element.47.z3, ...), custom_call_target="tpu_custom_call" | custom-call | tf_op jit(solution)/shard_map/pallas_call | solution.py:223
  174.9 2.1 %collective-permute-start.18 = (f32[32,2048]{1,0:T(8,128)S(1)}, f32[32,2048]{1,0:T(8,128)S(1)}, u32[]{:S(2)}, u32[]{:S(2)}) collective-permute-start(f32[32,2048]{1,0:T(8,128)S(1)} %shard_map.99), channel_id=1, source_target_pairs={{0,8},{4,12},{8,0},{12,4},{16,24},{20,28},{24,16},{28,20},{32,40},... | collective-permute-start | bytes 786440 | tf_op jit(solution)/shard_map/ppermute | solution.py:48
  176.9 5.8 %collective-permute-done.18 = f32[32,2048]{1,0:T(8,128)S(1)} collective-permute-done((f32[32,2048]{1,0:T(8,128)S(1)}, f32[32,2048]{1,0:T(8,128)S(1)}, u32[]{:S(2)}, u32[]{:S(2)}) %collective-permute-start.18) | collective-permute-done | bytes 262176 | tf_op jit(solution)/shard_map/ppermute | solution.py:48
  182.8 4.8 %collective-permute-start.19 = (f32[2,32,2048]{2,1,0:T(8,128)S(1)}, f32[2,32,2048]{2,1,0:T(8,128)S(1)}, u32[]{:S(2)}, u32[]{:S(2)}) collective-permute-start(f32[2,32,2048]{2,1,0:T(8,128)S(1)} %pad_maximum_fusion.2.near), channel_id=1, source_target_pairs={{0,4},{4,0},{8,12},{12,8},{16,20},{20,16},{24,28},{28,24},{32,36},... | collective-permute-start | bytes 1572872 | tf_op jit(solution)/shard_map/ppermute | solution.py:48
  189.1 4.6 %shard_map.100 = (f32[896,128]{1,0:T(8,128)}, f32[172,128]{1,0:T(8,128)}) custom-call(s32[5]{0:T(128)S(1)} %copy-done.11, s32[1,21]{1,0:T(1,128)S(1)} %copy-done.12, f32[896,128]{1,0:T(8,128)S(1)} %copy-done.6, f32[2,32,2048]{2,1,0:T(8,128)S(1)} %pad_maximum_fusion.2.near, f32[2,32,2048]{2,1,0:T(8,128)S(1)} %collective-permute-done.19.across_core, ...), custom_call_target="tpu_custom_call" | custom-call | tf_op jit(solution)/shard_map/pallas_call | solution.py:223
  (71 shorter events, 20.7 us)
Async XLA Ops:
  8.1 17.0 %collective-permute-start = (f32[2,128,128]{2,1,0:T(8,128)S(1)}, f32[2,128,128]{2,1,0:T(8,128)S(1)}, u32[]{:S(2)}, u32[]{:S(2)}) collective-permute-start(f32[2,128,128]{2,1,0:T(8,128)S(1)} %pad_maximum_fusion.6), channel_id=1, source_target_pairs={{0,8},{4,12},{8,0},{12,4},{16,24},{20,28},{24,16},{28,20},{32,40},... | collective-permute-start | bytes 393224 | tf_op jit(solution)/shard_map/ppermute | solution.py:48
  13.1 11.9 %collective-permute-start.1 = (f32[1,4,128]{2,1,0:T(4,128)S(1)}, f32[1,4,128]{2,1,0:T(4,128)S(1)}, u32[]{:S(2)}, u32[]{:S(2)}) collective-permute-start(f32[1,4,128]{2,1,0:T(4,128)S(1)} %slice_bitcast_fusion.6), channel_id=1, source_target_pairs={{0,384},{4,388},{8,392},{12,396},{16,400},{20,404},{24,408},{28,41... | collective-permute-start | bytes 6152 | tf_op jit(solution)/shard_map/ppermute | solution.py:48
  25.1 29.9 %all-to-all-start = ((f32[4,32,2048]{2,1,0:T(8,128)}), f32[4,32,2048]{2,1,0:T(8,128)S(1)}, u32[]{:S(2)}, u32[]{:S(2)}) async-start(f32[4,32,2048]{2,1,0:T(8,128)} %bitcast.34), calls=%async_computation | async-start | bytes 2097152 | tf_op jit(solution)/shard_map/all_to_all | solution.py:280
  30.3 122.8 %all-gather.3.cloned.1.call-start = ((), (), s32[]{:S(2)}) async-start(), calls=%async_computation.2 | async-start | bytes 1966080 | tf_op jit(solution)/shard_map/all_gather | solution.py:299
  31.7 10.9 %collective-permute-start.5 = (f32[3,8,128]{2,1,0:T(8,128)S(1)}, f32[3,8,128]{2,1,0:T(8,128)S(1)}, u32[]{:S(2)}, u32[]{:S(2)}) collective-permute-start(f32[3,8,128]{2,1,0:T(8,128)S(1)} %pad_maximum_fusion.10), channel_id=1, source_target_pairs={{0,128},{4,132},{8,136},{12,140},{16,144},{20,148},{24,152},{28,15... | collective-permute-start | bytes 36872 | tf_op jit(solution)/shard_map/ppermute | solution.py:48
  33.6 21.3 %collective-permute-start.4 = (f32[2,256,128]{2,1,0:T(8,128)S(1)}, f32[2,256,128]{2,1,0:T(8,128)S(1)}, u32[]{:S(2)}, u32[]{:S(2)}) collective-permute-start(f32[2,256,128]{2,1,0:T(8,128)S(1)} %pad_maximum_fusion.4), channel_id=1, source_target_pairs={{0,3},{1,2},{2,1},{3,0},{4,7},{5,6},{6,5},{7,4},{8,11},{9,10},{10,... | collective-permute-start | bytes 786440 | tf_op jit(solution)/shard_map/ppermute | solution.py:48
  37.5 17.4 %collective-permute-start.3 = (f32[2,256,128]{2,1,0:T(8,128)S(1)}, f32[2,256,128]{2,1,0:T(8,128)S(1)}, u32[]{:S(2)}, u32[]{:S(2)}) collective-permute-start(f32[2,256,128]{2,1,0:T(8,128)S(1)} %pad_maximum_fusion.4), channel_id=1, source_target_pairs={{0,2},{1,3},{2,0},{3,1},{4,6},{5,7},{6,4},{7,5},{8,10},{9,11},{10,... | collective-permute-start | bytes 786440 | tf_op jit(solution)/shard_map/ppermute | solution.py:48
  39.9 15.0 %collective-permute-start.2 = (f32[2,256,128]{2,1,0:T(8,128)S(1)}, f32[2,256,128]{2,1,0:T(8,128)S(1)}, u32[]{:S(2)}, u32[]{:S(2)}) collective-permute-start(f32[2,256,128]{2,1,0:T(8,128)S(1)} %pad_maximum_fusion.4), channel_id=1, source_target_pairs={{0,1},{1,0},{2,3},{3,2},{4,5},{5,4},{6,7},{7,6},{8,9},{9,8},{10,11... | collective-permute-start | bytes 786440 | tf_op jit(solution)/shard_map/ppermute | solution.py:48
  42.6 12.3 %collective-permute-start.6 = (f32[3,16,128]{2,1,0:T(8,128)S(1)}, f32[3,16,128]{2,1,0:T(8,128)S(1)}, u32[]{:S(2)}, u32[]{:S(2)}) collective-permute-start(f32[3,16,128]{2,1,0:T(8,128)S(1)} %pad_maximum_fusion.9), channel_id=1, source_target_pairs={{0,96},{4,100},{8,104},{12,108},{16,112},{20,116},{24,120},{28,124... | collective-permute-start | bytes 73736 | tf_op jit(solution)/shard_map/ppermute | solution.py:48
  55.0 20.4 %collective-permute-start.7 = (f32[4,2,256,128]{3,2,1,0:T(8,128)S(1)}, f32[4,2,256,128]{3,2,1,0:T(8,128)S(1)}, u32[]{:S(2)}, u32[]{:S(2)}) collective-permute-start(f32[4,2,256,128]{3,2,1,0:T(8,128)S(1)} %pad_maximum_fusion.refs_1_.m1), channel_id=1, source_target_pairs={{0,4},{4,0},{8,12},{12,8},{16,20},{20,16},{24,28},{28,24},{32,36},... | collective-permute-start | bytes 3145736 | tf_op jit(solution)/shard_map/ppermute | solution.py:48
  60.3 15.1 %collective-permute-start.8 = (f32[5,32,128]{2,1,0:T(8,128)S(1)}, f32[5,32,128]{2,1,0:T(8,128)S(1)}, u32[]{:S(2)}, u32[]{:S(2)}) collective-permute-start(f32[5,32,128]{2,1,0:T(8,128)S(1)} %pad_maximum_fusion.7), channel_id=1, source_target_pairs={{0,32},{4,36},{8,40},{12,44},{16,48},{20,52},{24,56},{28,60},{32,0... | collective-permute-start | bytes 245768 | tf_op jit(solution)/shard_map/ppermute | solution.py:48
  76.4 25.3 %copy-start.7 = (f32[32,512]{1,0:T(8,128)}, f32[32,512]{1,0:T(8,128)S(1)}, u32[]{:S(2)}) copy-start(f32[32,512]{1,0:T(8,128)S(1)} %get-tuple-element.45.z1) | copy-start | bytes 196612
  76.4 12.2 %collective-permute-start.9 = (f32[5,64,128]{2,1,0:T(8,128)S(1)}, f32[5,64,128]{2,1,0:T(8,128)S(1)}, u32[]{:S(2)}, u32[]{:S(2)}) collective-permute-start(f32[5,64,128]{2,1,0:T(8,128)S(1)} %pad_maximum_fusion.5), channel_id=1, source_target_pairs={{0,16},{4,20},{8,24},{12,28},{16,0},{20,4},{24,8},{28,12},{32,48},... | collective-permute-start | bytes 491528 | tf_op jit(solution)/shard_map/ppermute | solution.py:48
  88.6 14.1 %collective-permute-start.10 = (f32[5,128,128]{2,1,0:T(8,128)S(1)}, f32[5,128,128]{2,1,0:T(8,128)S(1)}, u32[]{:S(2)}, u32[]{:S(2)}) collective-permute-start(f32[5,128,128]{2,1,0:T(8,128)S(1)} %pad_maximum_fusion.3), channel_id=1, source_target_pairs={{0,8},{4,12},{8,0},{12,4},{16,24},{20,28},{24,16},{28,20},{32,40},... | collective-permute-start | bytes 983048 | tf_op jit(solution)/shard_map/ppermute | solution.py:48
  90.6 11.1 %collective-permute-start.11 = (f32[32,1536]{1,0:T(8,128)S(1)}, f32[32,1536]{1,0:T(8,128)S(1)}, u32[]{:S(2)}, u32[]{:S(2)}) collective-permute-start(f32[32,1536]{1,0:T(8,128)S(1)} %get-tuple-element.35), channel_id=1, source_target_pairs={{0,16},{4,20},{8,24},{12,28},{16,0},{20,4},{24,8},{28,12},{32,48},... | collective-permute-start | bytes 589832 | tf_op jit(solution)/shard_map/ppermute | solution.py:48
  104.7 29.2 %all-to-all-start.1 = ((f32[4,2,256,128]{3,2,1,0:T(8,128)}), f32[4,2,256,128]{3,2,1,0:T(8,128)S(1)}, u32[]{:S(2)}, u32[]{:S(2)}) async-start(f32[4,2,256,128]{3,2,1,0:T(8,128)} %broadcast_in_dim.14), calls=%async_computation.1 | async-start | bytes 2097152 | tf_op jit(solution)/shard_map/all_to_all | solution.py:250
  108.7 25.2 %collective-permute-start.12 = (f32[32,1536]{1,0:T(8,128)S(1)}, f32[32,1536]{1,0:T(8,128)S(1)}, u32[]{:S(2)}, u32[]{:S(2)}) collective-permute-start(f32[32,1536]{1,0:T(8,128)S(1)} %add.24.refs_0_), channel_id=1, source_target_pairs={{0,32},{4,36},{8,40},{12,44},{16,48},{20,52},{24,56},{28,60},{32,0... | collective-permute-start | bytes 589832 | tf_op jit(solution)/shard_map/ppermute | solution.py:48
  133.9 4.7 %collective-permute-start.13 = (f32[4,2,256,128]{3,2,1,0:T(8,128)S(1)}, f32[4,2,256,128]{3,2,1,0:T(8,128)S(1)}, u32[]{:S(2)}, u32[]{:S(2)}) collective-permute-start(f32[4,2,256,128]{3,2,1,0:T(8,128)S(1)} %all-to-all-done.1.refs_2_.m2), channel_id=1, source_target_pairs={{0,4},{4,0},{8,12},{12,8},{16,20},{20,16},{24,28},{28,24},{32,36},... | collective-permute-start | bytes 3145736 | tf_op jit(solution)/shard_map/ppermute | solution.py:48
  141.1 11.9 %collective-permute-start.14 = (f32[32,1024]{1,0:T(8,128)S(1)}, f32[32,1024]{1,0:T(8,128)S(1)}, u32[]{:S(2)}, u32[]{:S(2)}) collective-permute-start(f32[32,1024]{1,0:T(8,128)S(1)} %get-tuple-element.41), channel_id=1, source_target_pairs={{0,96},{4,100},{8,104},{12,108},{16,112},{20,116},{24,120},{28,124... | collective-permute-start | bytes 393224 | tf_op jit(solution)/shard_map/ppermute | solution.py:48
  153.0 18.3 %copy-start.8 = (f32[32,512]{1,0:T(8,128)S(1)}, f32[32,512]{1,0:T(8,128)}, u32[]{:S(2)}) copy-start(f32[32,512]{1,0:T(8,128)} %copy-done.7) | copy-start | bytes 196612
  153.0 18.3 %copy-start.10 = (f32[32,512]{1,0:T(8,128)S(1)}, f32[32,512]{1,0:T(8,128)}, u32[]{:S(2)}) copy-start(f32[32,512]{1,0:T(8,128)} %copy-done.9) | copy-start | bytes 196612
  153.1 9.6 %collective-permute-start.16 = (f32[4,3,256,128]{3,2,1,0:T(8,128)}, f32[4,3,256,128]{3,2,1,0:T(8,128)S(1)}, u32[]{:S(2)}, u32[]{:S(2)}) collective-permute-start(f32[4,3,256,128]{3,2,1,0:T(8,128)} %bitcast.29), channel_id=1, source_target_pairs={{0,4},{4,0},{8,12},{12,8},{16,20},{20,16},{24,28},{28,24},{32,36},... | collective-permute-start | bytes 4718600 | tf_op jit(solution)/shard_map/ppermute | solution.py:48
  155.6 7.0 %collective-permute-start.15 = (f32[32,1024]{1,0:T(8,128)S(1)}, f32[32,1024]{1,0:T(8,128)S(1)}, u32[]{:S(2)}, u32[]{:S(2)}) collective-permute-start(f32[32,1024]{1,0:T(8,128)S(1)} %add.25.refs_0_), channel_id=1, source_target_pairs={{0,128},{4,132},{8,136},{12,140},{16,144},{20,148},{24,152},{28,15... | collective-permute-start | bytes 393224 | tf_op jit(solution)/shard_map/ppermute | solution.py:48
  165.0 6.2 %collective-permute-start.17 = (f32[32,512]{1,0:T(8,128)S(1)}, f32[32,512]{1,0:T(8,128)S(1)}, u32[]{:S(2)}, u32[]{:S(2)}) collective-permute-start(f32[32,512]{1,0:T(8,128)S(1)} %get-tuple-element.44.right), channel_id=1, source_target_pairs={{0,384},{4,388},{8,392},{12,396},{16,400},{20,404},{24,408},{28,41... | collective-permute-start | bytes 196616 | tf_op jit(solution)/shard_map/ppermute | solution.py:48
  171.3 17.8 %copy-start.1 = (f32[21,128,128]{2,1,0:T(8,128)S(1)}, f32[21,128,128]{2,1,0:T(8,128)}, u32[]{:S(2)}) copy-start(f32[21,128,128]{2,1,0:T(8,128)} %blocks.1) | copy-start | bytes 4128772
  171.3 17.8 %copy-start.5 = (f32[7,128,128]{2,1,0:T(8,128)S(1)}, f32[7,128,128]{2,1,0:T(8,128)}, u32[]{:S(2)}) copy-start(f32[7,128,128]{2,1,0:T(8,128)} %inverse.1) | copy-start | bytes 1376260
  171.3 17.8 %copy-start.6 = (f32[896,128]{1,0:T(8,128)S(1)}, f32[896,128]{1,0:T(8,128)}, u32[]{:S(2)}) copy-start(f32[896,128]{1,0:T(8,128)} %get-tuple-element.25.y) | copy-start | bytes 1376260
  171.3 17.8 %copy-start.11 = (s32[5]{0:T(128)S(1)}, s32[5]{0:T(128)}, u32[]{:S(2)}) copy-start(s32[5]{0:T(128)} %stack.68.where) | copy-start | bytes 64
  171.3 17.8 %copy-start.12 = (s32[1,21]{1,0:T(1,128)S(1)}, s32[1,21]{1,0:T(1,128)}, u32[]{:S(2)}) copy-start(s32[1,21]{1,0:T(1,128)} %pattern.3) | copy-start | bytes 256
  174.9 14.3 %copy-start.2 = (f32[512,512]{1,0:T(8,128)S(1)}, f32[512,512]{1,0:T(8,128)}, u32[]{:S(2)}) copy-start(f32[512,512]{1,0:T(8,128)} %coupling.1) | copy-start | bytes 3145732
  174.9 7.9 %collective-permute-start.18 = (f32[32,2048]{1,0:T(8,128)S(1)}, f32[32,2048]{1,0:T(8,128)S(1)}, u32[]{:S(2)}, u32[]{:S(2)}) collective-permute-start(f32[32,2048]{1,0:T(8,128)S(1)} %shard_map.99), channel_id=1, source_target_pairs={{0,8},{4,12},{8,0},{12,4},{16,24},{20,28},{24,16},{28,20},{32,40},... | collective-permute-start | bytes 786440 | tf_op jit(solution)/shard_map/ppermute | solution.py:48
  182.8 6.3 %collective-permute-start.19 = (f32[2,32,2048]{2,1,0:T(8,128)S(1)}, f32[2,32,2048]{2,1,0:T(8,128)S(1)}, u32[]{:S(2)}, u32[]{:S(2)}) collective-permute-start(f32[2,32,2048]{2,1,0:T(8,128)S(1)} %pad_maximum_fusion.2.near), channel_id=1, source_target_pairs={{0,4},{4,0},{8,12},{12,8},{16,20},{20,16},{24,28},{28,24},{32,36},... | collective-permute-start | bytes 1572872 | tf_op jit(solution)/shard_map/ppermute | solution.py:48
  (4 other events, 10.2 us)
Sparse Core Ops, SparseCore 0:
  103.7 33.8 all-gather.2

commit v14 on v13

--- a/solution.py
+++ b/solution.py
@@ -286,13 +286,12 @@
     first = (first, across(first, CORE_MASK))
     far = grow(jnp.concatenate([far, both(1)], 0), halves_z)
     z1, v = solve(0, True, 3, t, *first)
-    v, far = tie((v, far))
     v_far = across(v, 1 << Z2)
-
-    far = grow(far, 1 << Z2)
+    v, v_far, far = tie((v, v_far, far))
+
     v = v + v_far
     v_far = across(v, halves_z)
-    far = grow(far, 1 << Z1)
+    far = grow(grow(far, 1 << Z2), 1 << Z1)
     far, v = tie((far, v))
 
     second = planes(far[3:])

time: 202 us -> 203 us (level)
  waiting for transfers between devices: 76.9 us -> 79.7 us
    ppermute x20, waiting for transfers between devices: 76.8 us -> 79.7 us  [swap(): lax.ppermute(value, axis, [(i, i ^ mask) for i in range(lax.axis_size(axi...]
where the time goes in v14:
time: 203 us; the launch traced here: 202 us
  starting transfers between devices  80 us (39%)
  waiting for transfers between devices  79.7 us (39%)
  Pallas kernels  17.6 us (9%)
  between operations  14.5 us (7%)
  local copies, waits for them, and re-layouts  9.88 us (5%)
    ppermute x20, waiting for transfers between devices, swap(): lax.ppermute(value, axis, [(i, i ^ mask) for i in range(lax.axis_size(axi...  79.7 us
    ppermute x20, starting transfers between devices, swap(): lax.ppermute(value, axis, [(i, i ^ mask) for i in range(lax.axis_size(axi...  70.8 us
    pallas_call x5, Pallas kernels, call(): pl.pallas_call(kernel, out_shape=[jax.ShapeDtypeStruct(s, F32) for s in o...  11 us
    pallas_call x1, Pallas kernels, shards(): pl.pallas_call(functools.partial(forward_kernel, sizes), out_shape=[jax.S...  6.58 us
    all_to_all x1, starting transfers between devices, shards(): t = lax.all_to_all(t, 'leaf', 0, 0, axis_index_groups=near, tiled=True)  5.19 us
  transfers between devices with their start and end apart: 23, of which 12 were waited for; matrix products, arithmetic and copies ran while one was open for 3% of the time, Pallas kernels for 4%

profile of v14, /device:TPU:1, one launch (start us, length us, event | category | flops | bytes accessed | tf_op | source)
XLA Modules:
  0.0 202.0 jit_solution(12789537432351456819)
XLA Ops:
  8.1 4.4 %collective-permute-start = (f32[2,128,128]{2,1,0:T(8,128)S(1)}, f32[2,128,128]{2,1,0:T(8,128)S(1)}, u32[]{:S(2)}, u32[]{:S(2)}) collective-permute-start(f32[2,128,128]{2,1,0:T(8,128)S(1)} %pad_maximum_fusion.6), channel_id=1, source_target_pairs={{0,8},{4,12},{8,0},{12,4},{16,24},{20,28},{24,16},{28,20},{32,40},... | collective-permute-start | bytes 393224 | tf_op jit(solution)/shard_map/ppermute | solution.py:48
  13.1 4.6 %collective-permute-start.1 = (f32[1,4,128]{2,1,0:T(4,128)S(1)}, f32[1,4,128]{2,1,0:T(4,128)S(1)}, u32[]{:S(2)}, u32[]{:S(2)}) collective-permute-start(f32[1,4,128]{2,1,0:T(4,128)S(1)} %slice_bitcast_fusion.6), channel_id=1, source_target_pairs={{0,384},{4,388},{8,392},{12,396},{16,400},{20,404},{24,408},{28,41... | collective-permute-start | bytes 6152 | tf_op jit(solution)/shard_map/ppermute | solution.py:48
  18.4 6.6 %shard_map.95 = (f32[896,128]{1,0:T(8,128)}, f32[128,2048]{1,0:T(8,128)}) custom-call(s32[5]{0:T(128)} %stack.68.where, s32[1,21]{1,0:T(1,128)} %pattern.3, f32[896,128]{1,0:T(8,128)} %rhs_far.1, f32[7,128,128]{2,1,0:T(8,128)} %inverse.1, f32[21,128,128]{2,1,0:T(8,128)} %blocks.1, f32[512,512]{1,0:T(8,128)} %coupling.1, f32[172,128]{1,0:T(8,128)} %sep_rhs.1), custom_call_target="tpu_custom_call" | custom-call | tf_op jit(solution)/shard_map/pallas_call | solution.py:266
  25.1 5.2 %all-to-all-start = ((f32[4,32,2048]{2,1,0:T(8,128)}), f32[4,32,2048]{2,1,0:T(8,128)S(1)}, u32[]{:S(2)}, u32[]{:S(2)}) async-start(f32[4,32,2048]{2,1,0:T(8,128)} %bitcast.34), calls=%async_computation | async-start | bytes 2097152 | tf_op jit(solution)/shard_map/all_to_all | solution.py:280
  33.6 3.9 %collective-permute-start.4 = (f32[2,256,128]{2,1,0:T(8,128)S(1)}, f32[2,256,128]{2,1,0:T(8,128)S(1)}, u32[]{:S(2)}, u32[]{:S(2)}) collective-permute-start(f32[2,256,128]{2,1,0:T(8,128)S(1)} %pad_maximum_fusion.4), channel_id=1, source_target_pairs={{0,3},{1,2},{2,1},{3,0},{4,7},{5,6},{6,5},{7,4},{8,11},{9,10},{10,... | collective-permute-start | bytes 786440 | tf_op jit(solution)/shard_map/ppermute | solution.py:48
  37.5 2.4 %collective-permute-start.3 = (f32[2,256,128]{2,1,0:T(8,128)S(1)}, f32[2,256,128]{2,1,0:T(8,128)S(1)}, u32[]{:S(2)}, u32[]{:S(2)}) collective-permute-start(f32[2,256,128]{2,1,0:T(8,128)S(1)} %pad_maximum_fusion.4), channel_id=1, source_target_pairs={{0,2},{1,3},{2,0},{3,1},{4,6},{5,7},{6,4},{7,5},{8,10},{9,11},{10,... | collective-permute-start | bytes 786440 | tf_op jit(solution)/shard_map/ppermute | solution.py:48
  39.9 2.6 %collective-permute-start.2 = (f32[2,256,128]{2,1,0:T(8,128)S(1)}, f32[2,256,128]{2,1,0:T(8,128)S(1)}, u32[]{:S(2)}, u32[]{:S(2)}) collective-permute-start(f32[2,256,128]{2,1,0:T(8,128)S(1)} %pad_maximum_fusion.4), channel_id=1, source_target_pairs={{0,1},{1,0},{2,3},{3,2},{4,5},{5,4},{6,7},{7,6},{8,9},{9,8},{10,11... | collective-permute-start | bytes 786440 | tf_op jit(solution)/shard_map/ppermute | solution.py:48
  42.6 11.1 %collective-permute-start.6 = (f32[3,16,128]{2,1,0:T(8,128)S(1)}, f32[3,16,128]{2,1,0:T(8,128)S(1)}, u32[]{:S(2)}, u32[]{:S(2)}) collective-permute-start(f32[3,16,128]{2,1,0:T(8,128)S(1)} %pad_maximum_fusion.9), channel_id=1, source_target_pairs={{0,96},{4,100},{8,104},{12,108},{16,112},{20,116},{24,120},{28,124... | collective-permute-start | bytes 73736 | tf_op jit(solution)/shard_map/ppermute | solution.py:48
  55.0 3.8 %collective-permute-start.7 = (f32[4,2,256,128]{3,2,1,0:T(8,128)S(1)}, f32[4,2,256,128]{3,2,1,0:T(8,128)S(1)}, u32[]{:S(2)}, u32[]{:S(2)}) collective-permute-start(f32[4,2,256,128]{3,2,1,0:T(8,128)S(1)} %pad_maximum_fusion.refs_1_.m1), channel_id=1, source_target_pairs={{0,4},{4,0},{8,12},{12,8},{16,20},{20,16},{24,28},{28,24},{32,36},... | collective-permute-start | bytes 3145736 | tf_op jit(solution)/shard_map/ppermute | solution.py:48
  60.3 5.3 %collective-permute-start.9 = (f32[5,32,128]{2,1,0:T(8,128)S(1)}, f32[5,32,128]{2,1,0:T(8,128)S(1)}, u32[]{:S(2)}, u32[]{:S(2)}) collective-permute-start(f32[5,32,128]{2,1,0:T(8,128)S(1)} %pad_maximum_fusion.7), channel_id=1, source_target_pairs={{0,32},{4,36},{8,40},{12,44},{16,48},{20,52},{24,56},{28,60},{32,0... | collective-permute-start | bytes 245768 | tf_op jit(solution)/shard_map/ppermute | solution.py:48
  66.6 4.6 %collective-permute-start.8 = (f32[32,1536]{1,0:T(8,128)S(1)}, f32[32,1536]{1,0:T(8,128)S(1)}, u32[]{:S(2)}, u32[]{:S(2)}) collective-permute-start(f32[32,1536]{1,0:T(8,128)S(1)} %get-tuple-element.36), channel_id=1, source_target_pairs={{0,16},{4,20},{8,24},{12,28},{16,0},{20,4},{24,8},{28,12},{32,48},... | collective-permute-start | bytes 589832 | tf_op jit(solution)/shard_map/ppermute | solution.py:48
  71.3 2.8 %collective-permute-done.9 = f32[5,32,128]{2,1,0:T(8,128)S(1)} collective-permute-done((f32[5,32,128]{2,1,0:T(8,128)S(1)}, f32[5,32,128]{2,1,0:T(8,128)S(1)}, u32[]{:S(2)}, u32[]{:S(2)}) %collective-permute-start.9) | collective-permute-done | bytes 81952 | tf_op jit(solution)/shard_map/ppermute | solution.py:48
  74.0 8.7 %collective-permute-done.8 = f32[32,1536]{1,0:T(8,128)S(1)} collective-permute-done((f32[32,1536]{1,0:T(8,128)S(1)}, f32[32,1536]{1,0:T(8,128)S(1)}, u32[]{:S(2)}, u32[]{:S(2)}) %collective-permute-start.8) | collective-permute-done | bytes 196640 | tf_op jit(solution)/shard_map/ppermute | solution.py:48
  84.7 9.5 %collective-permute-done.10 = f32[5,64,128]{2,1,0:T(8,128)S(1)} collective-permute-done((f32[5,64,128]{2,1,0:T(8,128)S(1)}, f32[5,64,128]{2,1,0:T(8,128)S(1)}, u32[]{:S(2)}, u32[]{:S(2)}) %collective-permute-start.10) | collective-permute-done | bytes 163872 | tf_op jit(solution)/shard_map/ppermute | solution.py:48
  94.2 1.9 collective-permute-start.11
  96.2 8.7 %collective-permute-done.11 = f32[5,128,128]{2,1,0:T(8,128)S(1)} collective-permute-done((f32[5,128,128]{2,1,0:T(8,128)S(1)}, f32[5,128,128]{2,1,0:T(8,128)S(1)}, u32[]{:S(2)}, u32[]{:S(2)}) %collective-permute-start.11) | collective-permute-done | bytes 327712 | tf_op jit(solution)/shard_map/ppermute | solution.py:48
  106.8 4.0 %all-to-all-start.1 = ((f32[4,2,256,128]{3,2,1,0:T(8,128)}), f32[4,2,256,128]{3,2,1,0:T(8,128)S(1)}, u32[]{:S(2)}, u32[]{:S(2)}) async-start(f32[4,2,256,128]{3,2,1,0:T(8,128)} %broadcast_in_dim.14), calls=%async_computation.1 | async-start | bytes 2097152 | tf_op jit(solution)/shard_map/all_to_all | solution.py:250
  112.7 23.3 %collective-permute-done.12.refs_1_ = f32[32,1536]{1,0:T(8,128)S(1)} collective-permute-done((f32[32,1536]{1,0:T(8,128)S(1)}, f32[32,1536]{1,0:T(8,128)S(1)}, u32[]{:S(2)}, u32[]{:S(2)}) %collective-permute-start.12) | collective-permute-done | bytes 196640 | tf_op jit(solution)/shard_map/ppermute | solution.py:48
  136.0 2.4 %collective-permute-start.13 = (f32[4,2,256,128]{3,2,1,0:T(8,128)S(1)}, f32[4,2,256,128]{3,2,1,0:T(8,128)S(1)}, u32[]{:S(2)}, u32[]{:S(2)}) collective-permute-start(f32[4,2,256,128]{3,2,1,0:T(8,128)S(1)} %all-to-all-done.1.refs_2_.m2), channel_id=1, source_target_pairs={{0,4},{4,0},{8,12},{12,8},{16,20},{20,16},{24,28},{28,24},{32,36},... | collective-permute-start | bytes 3145736 | tf_op jit(solution)/shard_map/ppermute | solution.py:48
  138.5 2.3 %collective-permute-done.13.refs_3_.o2 = f32[4,2,256,128]{3,2,1,0:T(8,128)S(1)} collective-permute-done((f32[4,2,256,128]{3,2,1,0:T(8,128)S(1)}, f32[4,2,256,128]{3,2,1,0:T(8,128)S(1)}, u32[]{:S(2)}, u32[]{:S(2)}) %collective-permute-start.13) | collective-permute-done | bytes 1048608 | tf_op jit(solution)/shard_map/ppermute | solution.py:48
  143.3 2.0 collective-permute-start.14
  145.2 8.5 %collective-permute-done.14 = f32[32,1024]{1,0:T(8,128)S(1)} collective-permute-done((f32[32,1024]{1,0:T(8,128)S(1)}, f32[32,1024]{1,0:T(8,128)S(1)}, u32[]{:S(2)}, u32[]{:S(2)}) %collective-permute-start.14) | collective-permute-done | bytes 131104 | tf_op jit(solution)/shard_map/ppermute | solution.py:48
  153.8 3.2 %collective-permute-start.16 = (f32[4,3,256,128]{3,2,1,0:T(8,128)}, f32[4,3,256,128]{3,2,1,0:T(8,128)S(1)}, u32[]{:S(2)}, u32[]{:S(2)}) collective-permute-start(f32[4,3,256,128]{3,2,1,0:T(8,128)} %bitcast.29), channel_id=1, source_target_pairs={{0,4},{4,0},{8,12},{12,8},{16,20},{20,16},{24,28},{28,24},{32,36},... | collective-permute-start | bytes 4718600 | tf_op jit(solution)/shard_map/ppermute | solution.py:48
  157.0 3.4 %collective-permute-start.15 = (f32[32,1024]{1,0:T(8,128)S(1)}, f32[32,1024]{1,0:T(8,128)S(1)}, u32[]{:S(2)}, u32[]{:S(2)}) collective-permute-start(f32[32,1024]{1,0:T(8,128)S(1)} %add.25.refs_0_), channel_id=1, source_target_pairs={{0,128},{4,132},{8,136},{12,140},{16,144},{20,148},{24,152},{28,15... | collective-permute-start | bytes 393224 | tf_op jit(solution)/shard_map/ppermute | solution.py:48
  160.4 3.7 %collective-permute-done.15.refs_1_ = f32[32,1024]{1,0:T(8,128)S(1)} collective-permute-done((f32[32,1024]{1,0:T(8,128)S(1)}, f32[32,1024]{1,0:T(8,128)S(1)}, u32[]{:S(2)}, u32[]{:S(2)}) %collective-permute-start.15) | collective-permute-done | bytes 131104 | tf_op jit(solution)/shard_map/ppermute | solution.py:48
  166.5 2.5 %collective-permute-start.17 = (f32[32,512]{1,0:T(8,128)S(1)}, f32[32,512]{1,0:T(8,128)S(1)}, u32[]{:S(2)}, u32[]{:S(2)}) collective-permute-start(f32[32,512]{1,0:T(8,128)S(1)} %get-tuple-element.46.right), channel_id=1, source_target_pairs={{0,384},{4,388},{8,392},{12,396},{16,400},{20,404},{24,408},{28,41... | collective-permute-start | bytes 196616 | tf_op jit(solution)/shard_map/ppermute | solution.py:48
  169.0 3.7 %collective-permute-done.17.right_far = f32[32,512]{1,0:T(8,128)S(1)} collective-permute-done((f32[32,512]{1,0:T(8,128)S(1)}, f32[32,512]{1,0:T(8,128)S(1)}, u32[]{:S(2)}, u32[]{:S(2)}) %collective-permute-start.17) | collective-permute-done | bytes 65568 | tf_op jit(solution)/shard_map/ppermute | solution.py:48
  172.8 3.5 %shard_map.99 = f32[32,2048]{1,0:T(8,128)S(1)} custom-call(s32[1]{0:T(128)} %bitcast.5.plane, f32[32,512]{1,0:T(8,128)S(1)} %get-tuple-element.46.right, f32[32,512]{1,0:T(8,128)S(1)} %collective-permute-done.17.right_far, f32[32,512]{1,0:T(8,128)S(1)} %copy-done.8, f32[32,512]{1,0:T(8,128)S(1)} %copy-done.10, f32[32,512]{1,0:T(8,128)S(1)} %get-tuple-element.49.z3, ...), custom_call_target="tpu_custom_call" | custom-call | tf_op jit(solution)/shard_map/pallas_call | solution.py:223
  176.3 2.1 %collective-permute-start.18 = (f32[32,2048]{1,0:T(8,128)S(1)}, f32[32,2048]{1,0:T(8,128)S(1)}, u32[]{:S(2)}, u32[]{:S(2)}) collective-permute-start(f32[32,2048]{1,0:T(8,128)S(1)} %shard_map.99), channel_id=1, source_target_pairs={{0,8},{4,12},{8,0},{12,4},{16,24},{20,28},{24,16},{28,20},{32,40},... | collective-permute-start | bytes 786440 | tf_op jit(solution)/shard_map/ppermute | solution.py:48
  178.4 5.8 %collective-permute-done.18 = f32[32,2048]{1,0:T(8,128)S(1)} collective-permute-done((f32[32,2048]{1,0:T(8,128)S(1)}, f32[32,2048]{1,0:T(8,128)S(1)}, u32[]{:S(2)}, u32[]{:S(2)}) %collective-permute-start.18) | collective-permute-done | bytes 262176 | tf_op jit(solution)/shard_map/ppermute | solution.py:48
  184.2 4.8 %collective-permute-start.19 = (f32[2,32,2048]{2,1,0:T(8,128)S(1)}, f32[2,32,2048]{2,1,0:T(8,128)S(1)}, u32[]{:S(2)}, u32[]{:S(2)}) collective-permute-start(f32[2,32,2048]{2,1,0:T(8,128)S(1)} %pad_maximum_fusion.2.near), channel_id=1, source_target_pairs={{0,4},{4,0},{8,12},{12,8},{16,20},{20,16},{24,28},{28,24},{32,36},... | collective-permute-start | bytes 1572872 | tf_op jit(solution)/shard_map/ppermute | solution.py:48
  190.5 4.6 %shard_map.100 = (f32[896,128]{1,0:T(8,128)}, f32[172,128]{1,0:T(8,128)}) custom-call(s32[5]{0:T(128)S(1)} %copy-done.11, s32[1,21]{1,0:T(1,128)S(1)} %copy-done.12, f32[896,128]{1,0:T(8,128)S(1)} %copy-done.6, f32[2,32,2048]{2,1,0:T(8,128)S(1)} %pad_maximum_fusion.2.near, f32[2,32,2048]{2,1,0:T(8,128)S(1)} %collective-permute-done.19.across_core, ...), custom_call_target="tpu_custom_call" | custom-call | tf_op jit(solution)/shard_map/pallas_call | solution.py:223
  (71 shorter events, 21.5 us)
Async XLA Ops:
  8.1 17.0 %collective-permute-start = (f32[2,128,128]{2,1,0:T(8,128)S(1)}, f32[2,128,128]{2,1,0:T(8,128)S(1)}, u32[]{:S(2)}, u32[]{:S(2)}) collective-permute-start(f32[2,128,128]{2,1,0:T(8,128)S(1)} %pad_maximum_fusion.6), channel_id=1, source_target_pairs={{0,8},{4,12},{8,0},{12,4},{16,24},{20,28},{24,16},{28,20},{32,40},... | collective-permute-start | bytes 393224 | tf_op jit(solution)/shard_map/ppermute | solution.py:48
  13.1 11.9 %collective-permute-start.1 = (f32[1,4,128]{2,1,0:T(4,128)S(1)}, f32[1,4,128]{2,1,0:T(4,128)S(1)}, u32[]{:S(2)}, u32[]{:S(2)}) collective-permute-start(f32[1,4,128]{2,1,0:T(4,128)S(1)} %slice_bitcast_fusion.6), channel_id=1, source_target_pairs={{0,384},{4,388},{8,392},{12,396},{16,400},{20,404},{24,408},{28,41... | collective-permute-start | bytes 6152 | tf_op jit(solution)/shard_map/ppermute | solution.py:48
  25.1 29.9 %all-to-all-start = ((f32[4,32,2048]{2,1,0:T(8,128)}), f32[4,32,2048]{2,1,0:T(8,128)S(1)}, u32[]{:S(2)}, u32[]{:S(2)}) async-start(f32[4,32,2048]{2,1,0:T(8,128)} %bitcast.34), calls=%async_computation | async-start | bytes 2097152 | tf_op jit(solution)/shard_map/all_to_all | solution.py:280
  30.3 123.5 %all-gather.3.cloned.1.call-start = ((), (), s32[]{:S(2)}) async-start(), calls=%async_computation.2 | async-start | bytes 1966080 | tf_op jit(solution)/shard_map/all_gather | solution.py:298
  31.7 10.9 %collective-permute-start.5 = (f32[3,8,128]{2,1,0:T(8,128)S(1)}, f32[3,8,128]{2,1,0:T(8,128)S(1)}, u32[]{:S(2)}, u32[]{:S(2)}) collective-permute-start(f32[3,8,128]{2,1,0:T(8,128)S(1)} %pad_maximum_fusion.10), channel_id=1, source_target_pairs={{0,128},{4,132},{8,136},{12,140},{16,144},{20,148},{24,152},{28,15... | collective-permute-start | bytes 36872 | tf_op jit(solution)/shard_map/ppermute | solution.py:48
  33.6 21.3 %collective-permute-start.4 = (f32[2,256,128]{2,1,0:T(8,128)S(1)}, f32[2,256,128]{2,1,0:T(8,128)S(1)}, u32[]{:S(2)}, u32[]{:S(2)}) collective-permute-start(f32[2,256,128]{2,1,0:T(8,128)S(1)} %pad_maximum_fusion.4), channel_id=1, source_target_pairs={{0,3},{1,2},{2,1},{3,0},{4,7},{5,6},{6,5},{7,4},{8,11},{9,10},{10,... | collective-permute-start | bytes 786440 | tf_op jit(solution)/shard_map/ppermute | solution.py:48
  37.5 17.4 %collective-permute-start.3 = (f32[2,256,128]{2,1,0:T(8,128)S(1)}, f32[2,256,128]{2,1,0:T(8,128)S(1)}, u32[]{:S(2)}, u32[]{:S(2)}) collective-permute-start(f32[2,256,128]{2,1,0:T(8,128)S(1)} %pad_maximum_fusion.4), channel_id=1, source_target_pairs={{0,2},{1,3},{2,0},{3,1},{4,6},{5,7},{6,4},{7,5},{8,10},{9,11},{10,... | collective-permute-start | bytes 786440 | tf_op jit(solution)/shard_map/ppermute | solution.py:48
  39.9 15.0 %collective-permute-start.2 = (f32[2,256,128]{2,1,0:T(8,128)S(1)}, f32[2,256,128]{2,1,0:T(8,128)S(1)}, u32[]{:S(2)}, u32[]{:S(2)}) collective-permute-start(f32[2,256,128]{2,1,0:T(8,128)S(1)} %pad_maximum_fusion.4), channel_id=1, source_target_pairs={{0,1},{1,0},{2,3},{3,2},{4,5},{5,4},{6,7},{7,6},{8,9},{9,8},{10,11... | collective-permute-start | bytes 786440 | tf_op jit(solution)/shard_map/ppermute | solution.py:48
  42.6 12.3 %collective-permute-start.6 = (f32[3,16,128]{2,1,0:T(8,128)S(1)}, f32[3,16,128]{2,1,0:T(8,128)S(1)}, u32[]{:S(2)}, u32[]{:S(2)}) collective-permute-start(f32[3,16,128]{2,1,0:T(8,128)S(1)} %pad_maximum_fusion.9), channel_id=1, source_target_pairs={{0,96},{4,100},{8,104},{12,108},{16,112},{20,116},{24,120},{28,124... | collective-permute-start | bytes 73736 | tf_op jit(solution)/shard_map/ppermute | solution.py:48
  55.0 10.6 %collective-permute-start.7 = (f32[4,2,256,128]{3,2,1,0:T(8,128)S(1)}, f32[4,2,256,128]{3,2,1,0:T(8,128)S(1)}, u32[]{:S(2)}, u32[]{:S(2)}) collective-permute-start(f32[4,2,256,128]{3,2,1,0:T(8,128)S(1)} %pad_maximum_fusion.refs_1_.m1), channel_id=1, source_target_pairs={{0,4},{4,0},{8,12},{12,8},{16,20},{20,16},{24,28},{28,24},{32,36},... | collective-permute-start | bytes 3145736 | tf_op jit(solution)/shard_map/ppermute | solution.py:48
  60.3 13.7 %collective-permute-start.9 = (f32[5,32,128]{2,1,0:T(8,128)S(1)}, f32[5,32,128]{2,1,0:T(8,128)S(1)}, u32[]{:S(2)}, u32[]{:S(2)}) collective-permute-start(f32[5,32,128]{2,1,0:T(8,128)S(1)} %pad_maximum_fusion.7), channel_id=1, source_target_pairs={{0,32},{4,36},{8,40},{12,44},{16,48},{20,52},{24,56},{28,60},{32,0... | collective-permute-start | bytes 245768 | tf_op jit(solution)/shard_map/ppermute | solution.py:48
  66.6 29.5 %copy-start.7 = (f32[32,512]{1,0:T(8,128)}, f32[32,512]{1,0:T(8,128)S(1)}, u32[]{:S(2)}) copy-start(f32[32,512]{1,0:T(8,128)S(1)} %get-tuple-element.47.z1) | copy-start | bytes 196612
  66.6 16.1 %collective-permute-start.8 = (f32[32,1536]{1,0:T(8,128)S(1)}, f32[32,1536]{1,0:T(8,128)S(1)}, u32[]{:S(2)}, u32[]{:S(2)}) collective-permute-start(f32[32,1536]{1,0:T(8,128)S(1)} %get-tuple-element.36), channel_id=1, source_target_pairs={{0,16},{4,20},{8,24},{12,28},{16,0},{20,4},{24,8},{28,12},{32,48},... | collective-permute-start | bytes 589832 | tf_op jit(solution)/shard_map/ppermute | solution.py:48
  82.8 11.4 %collective-permute-start.10 = (f32[5,64,128]{2,1,0:T(8,128)S(1)}, f32[5,64,128]{2,1,0:T(8,128)S(1)}, u32[]{:S(2)}, u32[]{:S(2)}) collective-permute-start(f32[5,64,128]{2,1,0:T(8,128)S(1)} %pad_maximum_fusion.5), channel_id=1, source_target_pairs={{0,16},{4,20},{8,24},{12,28},{16,0},{20,4},{24,8},{28,12},{32,48},... | collective-permute-start | bytes 491528 | tf_op jit(solution)/shard_map/ppermute | solution.py:48
  94.2 10.7 %collective-permute-start.11 = (f32[5,128,128]{2,1,0:T(8,128)S(1)}, f32[5,128,128]{2,1,0:T(8,128)S(1)}, u32[]{:S(2)}, u32[]{:S(2)}) collective-permute-start(f32[5,128,128]{2,1,0:T(8,128)S(1)} %pad_maximum_fusion.3), channel_id=1, source_target_pairs={{0,8},{4,12},{8,0},{12,4},{16,24},{20,28},{24,16},{28,20},{32,40},... | collective-permute-start | bytes 983048 | tf_op jit(solution)/shard_map/ppermute | solution.py:48
  106.8 29.2 %all-to-all-start.1 = ((f32[4,2,256,128]{3,2,1,0:T(8,128)}), f32[4,2,256,128]{3,2,1,0:T(8,128)S(1)}, u32[]{:S(2)}, u32[]{:S(2)}) async-start(f32[4,2,256,128]{3,2,1,0:T(8,128)} %broadcast_in_dim.14), calls=%async_computation.1 | async-start | bytes 2097152 | tf_op jit(solution)/shard_map/all_to_all | solution.py:250
  110.8 25.2 %collective-permute-start.12 = (f32[32,1536]{1,0:T(8,128)S(1)}, f32[32,1536]{1,0:T(8,128)S(1)}, u32[]{:S(2)}, u32[]{:S(2)}) collective-permute-start(f32[32,1536]{1,0:T(8,128)S(1)} %add.24.refs_0_), channel_id=1, source_target_pairs={{0,32},{4,36},{8,40},{12,44},{16,48},{20,52},{24,56},{28,60},{32,0... | collective-permute-start | bytes 589832 | tf_op jit(solution)/shard_map/ppermute | solution.py:48
  136.0 4.7 %collective-permute-start.13 = (f32[4,2,256,128]{3,2,1,0:T(8,128)S(1)}, f32[4,2,256,128]{3,2,1,0:T(8,128)S(1)}, u32[]{:S(2)}, u32[]{:S(2)}) collective-permute-start(f32[4,2,256,128]{3,2,1,0:T(8,128)S(1)} %all-to-all-done.1.refs_2_.m2), channel_id=1, source_target_pairs={{0,4},{4,0},{8,12},{12,8},{16,20},{20,16},{24,28},{28,24},{32,36},... | collective-permute-start | bytes 3145736 | tf_op jit(solution)/shard_map/ppermute | solution.py:48
  143.3 10.5 %collective-permute-start.14 = (f32[32,1024]{1,0:T(8,128)S(1)}, f32[32,1024]{1,0:T(8,128)S(1)}, u32[]{:S(2)}, u32[]{:S(2)}) collective-permute-start(f32[32,1024]{1,0:T(8,128)S(1)} %get-tuple-element.43), channel_id=1, source_target_pairs={{0,96},{4,100},{8,104},{12,108},{16,112},{20,116},{24,120},{28,124... | collective-permute-start | bytes 393224 | tf_op jit(solution)/shard_map/ppermute | solution.py:48
  153.8 18.9 %copy-start.8 = (f32[32,512]{1,0:T(8,128)S(1)}, f32[32,512]{1,0:T(8,128)}, u32[]{:S(2)}) copy-start(f32[32,512]{1,0:T(8,128)} %copy-done.7) | copy-start | bytes 196612
  153.8 18.9 %copy-start.10 = (f32[32,512]{1,0:T(8,128)S(1)}, f32[32,512]{1,0:T(8,128)}, u32[]{:S(2)}) copy-start(f32[32,512]{1,0:T(8,128)} %copy-done.9) | copy-start | bytes 196612
  153.8 10.3 %collective-permute-start.16 = (f32[4,3,256,128]{3,2,1,0:T(8,128)}, f32[4,3,256,128]{3,2,1,0:T(8,128)S(1)}, u32[]{:S(2)}, u32[]{:S(2)}) collective-permute-start(f32[4,3,256,128]{3,2,1,0:T(8,128)} %bitcast.29), channel_id=1, source_target_pairs={{0,4},{4,0},{8,12},{12,8},{16,20},{20,16},{24,28},{28,24},{32,36},... | collective-permute-start | bytes 4718600 | tf_op jit(solution)/shard_map/ppermute | solution.py:48
  157.0 7.0 %collective-permute-start.15 = (f32[32,1024]{1,0:T(8,128)S(1)}, f32[32,1024]{1,0:T(8,128)S(1)}, u32[]{:S(2)}, u32[]{:S(2)}) collective-permute-start(f32[32,1024]{1,0:T(8,128)S(1)} %add.25.refs_0_), channel_id=1, source_target_pairs={{0,128},{4,132},{8,136},{12,140},{16,144},{20,148},{24,152},{28,15... | collective-permute-start | bytes 393224 | tf_op jit(solution)/shard_map/ppermute | solution.py:48
  166.5 6.2 %collective-permute-start.17 = (f32[32,512]{1,0:T(8,128)S(1)}, f32[32,512]{1,0:T(8,128)S(1)}, u32[]{:S(2)}, u32[]{:S(2)}) collective-permute-start(f32[32,512]{1,0:T(8,128)S(1)} %get-tuple-element.46.right), channel_id=1, source_target_pairs={{0,384},{4,388},{8,392},{12,396},{16,400},{20,404},{24,408},{28,41... | collective-permute-start | bytes 196616 | tf_op jit(solution)/shard_map/ppermute | solution.py:48
  172.7 17.8 %copy-start.1 = (f32[21,128,128]{2,1,0:T(8,128)S(1)}, f32[21,128,128]{2,1,0:T(8,128)}, u32[]{:S(2)}) copy-start(f32[21,128,128]{2,1,0:T(8,128)} %blocks.1) | copy-start | bytes 4128772
  172.7 17.8 %copy-start.5 = (f32[7,128,128]{2,1,0:T(8,128)S(1)}, f32[7,128,128]{2,1,0:T(8,128)}, u32[]{:S(2)}) copy-start(f32[7,128,128]{2,1,0:T(8,128)} %inverse.1) | copy-start | bytes 1376260
  172.7 17.8 %copy-start.6 = (f32[896,128]{1,0:T(8,128)S(1)}, f32[896,128]{1,0:T(8,128)}, u32[]{:S(2)}) copy-start(f32[896,128]{1,0:T(8,128)} %get-tuple-element.26.y) | copy-start | bytes 1376260
  172.7 17.8 %copy-start.11 = (s32[5]{0:T(128)S(1)}, s32[5]{0:T(128)}, u32[]{:S(2)}) copy-start(s32[5]{0:T(128)} %stack.68.where) | copy-start | bytes 64
  172.7 17.8 %copy-start.12 = (s32[1,21]{1,0:T(1,128)S(1)}, s32[1,21]{1,0:T(1,128)}, u32[]{:S(2)}) copy-start(s32[1,21]{1,0:T(1,128)} %pattern.3) | copy-start | bytes 256
  176.3 14.3 %copy-start.2 = (f32[512,512]{1,0:T(8,128)S(1)}, f32[512,512]{1,0:T(8,128)}, u32[]{:S(2)}) copy-start(f32[512,512]{1,0:T(8,128)} %coupling.1) | copy-start | bytes 3145732
  176.3 7.9 %collective-permute-start.18 = (f32[32,2048]{1,0:T(8,128)S(1)}, f32[32,2048]{1,0:T(8,128)S(1)}, u32[]{:S(2)}, u32[]{:S(2)}) collective-permute-start(f32[32,2048]{1,0:T(8,128)S(1)} %shard_map.99), channel_id=1, source_target_pairs={{0,8},{4,12},{8,0},{12,4},{16,24},{20,28},{24,16},{28,20},{32,40},... | collective-permute-start | bytes 786440 | tf_op jit(solution)/shard_map/ppermute | solution.py:48
  184.2 6.3 %collective-permute-start.19 = (f32[2,32,2048]{2,1,0:T(8,128)S(1)}, f32[2,32,2048]{2,1,0:T(8,128)S(1)}, u32[]{:S(2)}, u32[]{:S(2)}) collective-permute-start(f32[2,32,2048]{2,1,0:T(8,128)S(1)} %pad_maximum_fusion.2.near), channel_id=1, source_target_pairs={{0,4},{4,0},{8,12},{12,8},{16,20},{20,16},{24,28},{28,24},{32,36},... | collective-permute-start | bytes 1572872 | tf_op jit(solution)/shard_map/ppermute | solution.py:48
  (4 other events, 10.2 us)
Sparse Core Ops, SparseCore 0:
  105.8 33.5 all-gather.2

commit v15 on v14

--- a/solution.py
+++ b/solution.py
@@ -72,7 +72,8 @@
 
 
 def forward_kernel(
-    sizes, where, pattern, rhs_far, inverse_far, blocks_far, coupling_far, sep_rhs, y_out, t_out, rhs, inverse, blocks, coupling, sems
+    sizes, where, pattern, rhs_far, inverse_far, blocks_far, coupling_far, sep_rhs, sep_inverse, sep_coupling,
+    y_out, t_out, second_out, third_out, rhs, inverse, blocks, coupling, sems,
 ):
     count, size = inverse.shape[0], inverse.shape[1]
     starts = pair_starts(count)
@@ -86,6 +87,11 @@
         copies.append(pltpu.make_async_copy(blocks_far.at[part], blocks.at[part], sems.at[3 + column]))
     for copy in copies[:2] + copies[3:] + copies[2:3]:
         copy.start()
+    offset = sizes[0]
+    for pack in (second_out, third_out):
+        for place, source in enumerate((sep_inverse, sep_coupling)):
+            pack[place] = source[offset : offset + pack.shape[1], :]
+        offset += pack.shape[1]
     copies[0].wait()
     copies[1].wait()
     pending = [rhs[i * size : (i + 1) * size, :] for i in range(count)]
@@ -216,7 +222,7 @@
 
 
 def params():
-    return pltpu.CompilerParams(vmem_limit_bytes=40 * 1024 * 1024)
+    return pltpu.CompilerParams(vmem_limit_bytes=20 * 1024 * 1024)
 
 
 def call(kernel, outs, *arrays):
@@ -263,28 +269,30 @@
 
     first = grow(both(0), 1 << Z1)
     far = grow(rows(sep_inverse, 3)[None], wrap_y)
-    y, t = pl.pallas_call(
+    y, t, second, third = pl.pallas_call(
         functools.partial(forward_kernel, sizes),
         out_shape=[
             jax.ShapeDtypeStruct(leaf_rhs.shape, F32),
             jax.ShapeDtypeStruct((columns, LEVELS * width), F32),
+            jax.ShapeDtypeStruct((2, sizes[1], 128), F32),
+            jax.ShapeDtypeStruct((2, sizes[2], 128), F32),
         ],
-        in_specs=[SMEM, SMEM] + [pl.BlockSpec(memory_space=pl.ANY)] * 4 + [VMEM],
-        out_specs=[VMEM, VMEM],
+        in_specs=[SMEM, SMEM] + [pl.BlockSpec(memory_space=pl.ANY)] * 4 + [VMEM] * 3,
+        out_specs=[VMEM] * 4,
         scratch_shapes=[pltpu.VMEM(v.shape, F32) for v in (leaf_rhs, leaf_inverse, leaf_blocks, leaf_coupling)]
         + [pltpu.SemaphoreType.DMA((2 + leaf_inverse.shape[0],))],
         compiler_params=pltpu.CompilerParams(vmem_limit_bytes=58 * 1024 * 1024),
-    )(where, leaf_pattern, leaf_rhs, leaf_inverse, leaf_blocks, leaf_coupling, sep_rhs)
+    )(where, leaf_pattern, leaf_rhs, leaf_inverse, leaf_blocks, leaf_coupling, sep_rhs, sep_inverse, sep_coupling)
     t, first, far = tie((t, first, far))
 
     t = lax.all_to_all(t, "leaf", 0, 0, axis_index_groups=near, tiled=True)
     first = turned_planes(first)
-    far = grow(jnp.concatenate([far, both(2)], 0), 1 << Y1)
+    far = grow(jnp.concatenate([far, third], 0), 1 << Y1)
     far = grow(far, wrap_z)
     t, first, far = tie((t, first, far))
 
     first = (first, across(first, CORE_MASK))
-    far = grow(jnp.concatenate([far, both(1)], 0), halves_z)
+    far = grow(jnp.concatenate([far, second], 0), halves_z)
     z1, v = solve(0, True, 3, t, *first)
     v_far = across(v, 1 << Z2)
     v, v_far, far = tie((v, v_far, far))

time: 203 us -> 200 us (0.985)
  local copies, waits for them, and re-layouts: 9.88 us -> 7.09 us
    another operation x5 -> x1, local copies, waits for them, and re-layouts: 3.7 us -> 0.88 us  [both(): return jnp.stack([rows(sep_inverse, level), rows(sep_coupling, level)])]
  transfers between devices with their start and end apart: 23 -> 23, of which waited for: 12 -> 12; matrix products, arithmetic and copies ran while one was open for 3% -> 1% of each run, Pallas kernels for 4% -> 4%
where the time goes in v15:
time: 200 us; the launch traced here: 199 us
  starting transfers between devices  80 us (40%)
  waiting for transfers between devices  79.8 us (40%)
  Pallas kernels  17.7 us (9%)
  between operations  14.6 us (7%)
  local copies, waits for them, and re-layouts  7.09 us (4%)
    ppermute x20, waiting for transfers between devices, swap(): lax.ppermute(value, axis, [(i, i ^ mask) for i in range(lax.axis_size(axi...  79.7 us
    ppermute x20, starting transfers between devices, swap(): lax.ppermute(value, axis, [(i, i ^ mask) for i in range(lax.axis_size(axi...  70.8 us
    pallas_call x5, Pallas kernels, call(): pl.pallas_call(kernel, out_shape=[jax.ShapeDtypeStruct(s, F32) for s in o...  11 us
    pallas_call x1, Pallas kernels, shards(): pl.pallas_call(functools.partial(forward_kernel, sizes), out_shape=[jax.S...  6.69 us
    all_to_all x1, starting transfers between devices, shards(): t = lax.all_to_all(t, 'leaf', 0, 0, axis_index_groups=near, tiled=True)  5.19 us
    all_to_all x1, starting transfers between devices, planes(): lax.all_to_all(jnp.broadcast_to(value[None], (count, *value.shape)), 'col...  4.01 us
  transfers between devices with their start and end apart: 23, of which 12 were waited for; matrix products, arithmetic and copies ran while one was open for 1% of the time, Pallas kernels for 4%

profile of v15, /device:TPU:1, one launch (start us, length us, event | category | flops | bytes accessed | tf_op | source)
XLA Modules:
  0.0 199.4 jit_solution(5507126394355972455)
XLA Ops:
  8.1 4.4 %collective-permute-start = (f32[2,128,128]{2,1,0:T(8,128)S(1)}, f32[2,128,128]{2,1,0:T(8,128)S(1)}, u32[]{:S(2)}, u32[]{:S(2)}) collective-permute-start(f32[2,128,128]{2,1,0:T(8,128)S(1)} %pad_maximum_fusion.6), channel_id=1, source_target_pairs={{0,8},{4,12},{8,0},{12,4},{16,24},{20,28},{24,16},{28,20},{32,40},... | collective-permute-start | bytes 393224 | tf_op jit(solution)/shard_map/ppermute | solution.py:48
  13.1 4.6 %collective-permute-start.1 = (f32[1,4,128]{2,1,0:T(4,128)S(1)}, f32[1,4,128]{2,1,0:T(4,128)S(1)}, u32[]{:S(2)}, u32[]{:S(2)}) collective-permute-start(f32[1,4,128]{2,1,0:T(4,128)S(1)} %slice_bitcast_fusion.2), channel_id=1, source_target_pairs={{0,384},{4,388},{8,392},{12,396},{16,400},{20,404},{24,408},{28,41... | collective-permute-start | bytes 6152 | tf_op jit(solution)/shard_map/ppermute | solution.py:48
  18.4 6.7 %shard_map.95 = (f32[896,128]{1,0:T(8,128)}, f32[128,2048]{1,0:T(8,128)}, f32[2,32,128]{2,1,0:T(8,128)}, f32[2,8,128]{2,1,0:T(8,128)}) custom-call(s32[5]{0:T(128)} %stack.56.where, s32[1,21]{1,0:T(1,128)} %pattern.3, f32[896,128]{1,0:T(8,128)} %rhs_far.1, f32[7,128,128]{2,1,0:T(8,128)} %inverse.1, f32[21,128,128]{2,1,0:T(8,128)} %blocks.1, ...), custom_call_target="tpu_custom_call" | custom-call | tf_op jit(solution)/shard_map/pallas_call | solution.py:272
  25.2 5.2 %all-to-all-start = ((f32[4,32,2048]{2,1,0:T(8,128)}), f32[4,32,2048]{2,1,0:T(8,128)S(1)}, u32[]{:S(2)}, u32[]{:S(2)}) async-start(f32[4,32,2048]{2,1,0:T(8,128)} %bitcast.26), calls=%async_computation | async-start | bytes 2097152 | tf_op jit(solution)/shard_map/all_to_all | solution.py:288
  32.3 3.9 %collective-permute-start.4 = (f32[2,256,128]{2,1,0:T(8,128)S(1)}, f32[2,256,128]{2,1,0:T(8,128)S(1)}, u32[]{:S(2)}, u32[]{:S(2)}) collective-permute-start(f32[2,256,128]{2,1,0:T(8,128)S(1)} %pad_maximum_fusion.4), channel_id=1, source_target_pairs={{0,3},{1,2},{2,1},{3,0},{4,7},{5,6},{6,5},{7,4},{8,11},{9,10},{10,... | collective-permute-start | bytes 786440 | tf_op jit(solution)/shard_map/ppermute | solution.py:48
  36.3 2.4 %collective-permute-start.3 = (f32[2,256,128]{2,1,0:T(8,128)S(1)}, f32[2,256,128]{2,1,0:T(8,128)S(1)}, u32[]{:S(2)}, u32[]{:S(2)}) collective-permute-start(f32[2,256,128]{2,1,0:T(8,128)S(1)} %pad_maximum_fusion.4), channel_id=1, source_target_pairs={{0,2},{1,3},{2,0},{3,1},{4,6},{5,7},{6,4},{7,5},{8,10},{9,11},{10,... | collective-permute-start | bytes 786440 | tf_op jit(solution)/shard_map/ppermute | solution.py:48
  38.7 2.7 %collective-permute-start.2 = (f32[2,256,128]{2,1,0:T(8,128)S(1)}, f32[2,256,128]{2,1,0:T(8,128)S(1)}, u32[]{:S(2)}, u32[]{:S(2)}) collective-permute-start(f32[2,256,128]{2,1,0:T(8,128)S(1)} %pad_maximum_fusion.4), channel_id=1, source_target_pairs={{0,1},{1,0},{2,3},{3,2},{4,5},{5,4},{6,7},{7,6},{8,9},{9,8},{10,11... | collective-permute-start | bytes 786440 | tf_op jit(solution)/shard_map/ppermute | solution.py:48
  41.4 11.1 %collective-permute-start.6 = (f32[3,16,128]{2,1,0:T(8,128)S(1)}, f32[3,16,128]{2,1,0:T(8,128)S(1)}, u32[]{:S(2)}, u32[]{:S(2)}) collective-permute-start(f32[3,16,128]{2,1,0:T(8,128)S(1)} %pad_maximum_fusion.8), channel_id=1, source_target_pairs={{0,96},{4,100},{8,104},{12,108},{16,112},{20,116},{24,120},{28,124... | collective-permute-start | bytes 73736 | tf_op jit(solution)/shard_map/ppermute | solution.py:48
  53.8 3.9 %collective-permute-start.7 = (f32[4,2,256,128]{3,2,1,0:T(8,128)S(1)}, f32[4,2,256,128]{3,2,1,0:T(8,128)S(1)}, u32[]{:S(2)}, u32[]{:S(2)}) collective-permute-start(f32[4,2,256,128]{3,2,1,0:T(8,128)S(1)} %pad_maximum_fusion.refs_1_.m1), channel_id=1, source_target_pairs={{0,4},{4,0},{8,12},{12,8},{16,20},{20,16},{24,28},{28,24},{32,36},... | collective-permute-start | bytes 3145736 | tf_op jit(solution)/shard_map/ppermute | solution.py:48
  57.7 5.3 %collective-permute-start.9 = (f32[5,32,128]{2,1,0:T(8,128)S(1)}, f32[5,32,128]{2,1,0:T(8,128)S(1)}, u32[]{:S(2)}, u32[]{:S(2)}) collective-permute-start(f32[5,32,128]{2,1,0:T(8,128)S(1)} %constant_dynamic-update-slice_fusion.2), channel_id=1, source_target_pairs={{0,32},{4,36},{8,40},{12,44},{16,48},{20,52},{24,56},{28,60},{32,0... | collective-permute-start | bytes 245768 | tf_op jit(solution)/shard_map/ppermute | solution.py:48
  64.0 4.6 %collective-permute-start.8 = (f32[32,1536]{1,0:T(8,128)S(1)}, f32[32,1536]{1,0:T(8,128)S(1)}, u32[]{:S(2)}, u32[]{:S(2)}) collective-permute-start(f32[32,1536]{1,0:T(8,128)S(1)} %get-tuple-element.40), channel_id=1, source_target_pairs={{0,16},{4,20},{8,24},{12,28},{16,0},{20,4},{24,8},{28,12},{32,48},... | collective-permute-start | bytes 589832 | tf_op jit(solution)/shard_map/ppermute | solution.py:48
  68.6 2.8 %collective-permute-done.9 = f32[5,32,128]{2,1,0:T(8,128)S(1)} collective-permute-done((f32[5,32,128]{2,1,0:T(8,128)S(1)}, f32[5,32,128]{2,1,0:T(8,128)S(1)}, u32[]{:S(2)}, u32[]{:S(2)}) %collective-permute-start.9) | collective-permute-done | bytes 81952 | tf_op jit(solution)/shard_map/ppermute | solution.py:48
  71.5 8.7 %collective-permute-done.8 = f32[32,1536]{1,0:T(8,128)S(1)} collective-permute-done((f32[32,1536]{1,0:T(8,128)S(1)}, f32[32,1536]{1,0:T(8,128)S(1)}, u32[]{:S(2)}, u32[]{:S(2)}) %collective-permute-start.8) | collective-permute-done | bytes 196640 | tf_op jit(solution)/shard_map/ppermute | solution.py:48
  82.1 9.5 %collective-permute-done.10 = f32[5,64,128]{2,1,0:T(8,128)S(1)} collective-permute-done((f32[5,64,128]{2,1,0:T(8,128)S(1)}, f32[5,64,128]{2,1,0:T(8,128)S(1)}, u32[]{:S(2)}, u32[]{:S(2)}) %collective-permute-start.10) | collective-permute-done | bytes 163872 | tf_op jit(solution)/shard_map/ppermute | solution.py:48
  91.6 1.9 collective-permute-start.11
  93.5 8.7 %collective-permute-done.11 = f32[5,128,128]{2,1,0:T(8,128)S(1)} collective-permute-done((f32[5,128,128]{2,1,0:T(8,128)S(1)}, f32[5,128,128]{2,1,0:T(8,128)S(1)}, u32[]{:S(2)}, u32[]{:S(2)}) %collective-permute-start.11) | collective-permute-done | bytes 327712 | tf_op jit(solution)/shard_map/ppermute | solution.py:48
  104.2 4.0 %all-to-all-start.1 = ((f32[4,2,256,128]{3,2,1,0:T(8,128)}), f32[4,2,256,128]{3,2,1,0:T(8,128)S(1)}, u32[]{:S(2)}, u32[]{:S(2)}) async-start(f32[4,2,256,128]{3,2,1,0:T(8,128)} %broadcast_in_dim.14), calls=%async_computation.1 | async-start | bytes 2097152 | tf_op jit(solution)/shard_map/all_to_all | solution.py:256
  110.1 23.3 %collective-permute-done.12.refs_1_ = f32[32,1536]{1,0:T(8,128)S(1)} collective-permute-done((f32[32,1536]{1,0:T(8,128)S(1)}, f32[32,1536]{1,0:T(8,128)S(1)}, u32[]{:S(2)}, u32[]{:S(2)}) %collective-permute-start.12) | collective-permute-done | bytes 196640 | tf_op jit(solution)/shard_map/ppermute | solution.py:48
  133.4 2.4 %collective-permute-start.13 = (f32[4,2,256,128]{3,2,1,0:T(8,128)S(1)}, f32[4,2,256,128]{3,2,1,0:T(8,128)S(1)}, u32[]{:S(2)}, u32[]{:S(2)}) collective-permute-start(f32[4,2,256,128]{3,2,1,0:T(8,128)S(1)} %all-to-all-done.1.refs_2_.m2), channel_id=1, source_target_pairs={{0,4},{4,0},{8,12},{12,8},{16,20},{20,16},{24,28},{28,24},{32,36},... | collective-permute-start | bytes 3145736 | tf_op jit(solution)/shard_map/ppermute | solution.py:48
  135.8 2.3 %collective-permute-done.13.refs_3_.o2 = f32[4,2,256,128]{3,2,1,0:T(8,128)S(1)} collective-permute-done((f32[4,2,256,128]{3,2,1,0:T(8,128)S(1)}, f32[4,2,256,128]{3,2,1,0:T(8,128)S(1)}, u32[]{:S(2)}, u32[]{:S(2)}) %collective-permute-start.13) | collective-permute-done | bytes 1048608 | tf_op jit(solution)/shard_map/ppermute | solution.py:48
  140.6 2.0 collective-permute-start.14
  142.6 8.5 %collective-permute-done.14 = f32[32,1024]{1,0:T(8,128)S(1)} collective-permute-done((f32[32,1024]{1,0:T(8,128)S(1)}, f32[32,1024]{1,0:T(8,128)S(1)}, u32[]{:S(2)}, u32[]{:S(2)}) %collective-permute-start.14) | collective-permute-done | bytes 131104 | tf_op jit(solution)/shard_map/ppermute | solution.py:48
  151.2 3.2 %collective-permute-start.16 = (f32[4,3,256,128]{3,2,1,0:T(8,128)}, f32[4,3,256,128]{3,2,1,0:T(8,128)S(1)}, u32[]{:S(2)}, u32[]{:S(2)}) collective-permute-start(f32[4,3,256,128]{3,2,1,0:T(8,128)} %bitcast.21), channel_id=1, source_target_pairs={{0,4},{4,0},{8,12},{12,8},{16,20},{20,16},{24,28},{28,24},{32,36},... | collective-permute-start | bytes 4718600 | tf_op jit(solution)/shard_map/ppermute | solution.py:48
  154.4 3.4 %collective-permute-start.15 = (f32[32,1024]{1,0:T(8,128)S(1)}, f32[32,1024]{1,0:T(8,128)S(1)}, u32[]{:S(2)}, u32[]{:S(2)}) collective-permute-start(f32[32,1024]{1,0:T(8,128)S(1)} %add.25.refs_0_), channel_id=1, source_target_pairs={{0,128},{4,132},{8,136},{12,140},{16,144},{20,148},{24,152},{28,15... | collective-permute-start | bytes 393224 | tf_op jit(solution)/shard_map/ppermute | solution.py:48
  157.8 3.7 %collective-permute-done.15.refs_1_ = f32[32,1024]{1,0:T(8,128)S(1)} collective-permute-done((f32[32,1024]{1,0:T(8,128)S(1)}, f32[32,1024]{1,0:T(8,128)S(1)}, u32[]{:S(2)}, u32[]{:S(2)}) %collective-permute-start.15) | collective-permute-done | bytes 131104 | tf_op jit(solution)/shard_map/ppermute | solution.py:48
  163.9 2.5 %collective-permute-start.17 = (f32[32,512]{1,0:T(8,128)S(1)}, f32[32,512]{1,0:T(8,128)S(1)}, u32[]{:S(2)}, u32[]{:S(2)}) collective-permute-start(f32[32,512]{1,0:T(8,128)S(1)} %get-tuple-element.50.right), channel_id=1, source_target_pairs={{0,384},{4,388},{8,392},{12,396},{16,400},{20,404},{24,408},{28,41... | collective-permute-start | bytes 196616 | tf_op jit(solution)/shard_map/ppermute | solution.py:48
  166.4 3.7 %collective-permute-done.17.right_far = f32[32,512]{1,0:T(8,128)S(1)} collective-permute-done((f32[32,512]{1,0:T(8,128)S(1)}, f32[32,512]{1,0:T(8,128)S(1)}, u32[]{:S(2)}, u32[]{:S(2)}) %collective-permute-start.17) | collective-permute-done | bytes 65568 | tf_op jit(solution)/shard_map/ppermute | solution.py:48
  170.2 3.5 %shard_map.99 = f32[32,2048]{1,0:T(8,128)S(1)} custom-call(s32[1]{0:T(128)} %bitcast.5.plane, f32[32,512]{1,0:T(8,128)S(1)} %get-tuple-element.50.right, f32[32,512]{1,0:T(8,128)S(1)} %collective-permute-done.17.right_far, f32[32,512]{1,0:T(8,128)S(1)} %copy-done.8, f32[32,512]{1,0:T(8,128)S(1)} %copy-done.10, f32[32,512]{1,0:T(8,128)S(1)} %get-tuple-element.53.z3, ...), custom_call_target="tpu_custom_call" | custom-call | tf_op jit(solution)/shard_map/pallas_call | solution.py:229
  173.7 2.1 %collective-permute-start.18 = (f32[32,2048]{1,0:T(8,128)S(1)}, f32[32,2048]{1,0:T(8,128)S(1)}, u32[]{:S(2)}, u32[]{:S(2)}) collective-permute-start(f32[32,2048]{1,0:T(8,128)S(1)} %shard_map.99), channel_id=1, source_target_pairs={{0,8},{4,12},{8,0},{12,4},{16,24},{20,28},{24,16},{28,20},{32,40},... | collective-permute-start | bytes 786440 | tf_op jit(solution)/shard_map/ppermute | solution.py:48
  175.8 5.9 %collective-permute-done.18 = f32[32,2048]{1,0:T(8,128)S(1)} collective-permute-done((f32[32,2048]{1,0:T(8,128)S(1)}, f32[32,2048]{1,0:T(8,128)S(1)}, u32[]{:S(2)}, u32[]{:S(2)}) %collective-permute-start.18) | collective-permute-done | bytes 262176 | tf_op jit(solution)/shard_map/ppermute | solution.py:48
  181.7 4.7 %collective-permute-start.19 = (f32[2,32,2048]{2,1,0:T(8,128)S(1)}, f32[2,32,2048]{2,1,0:T(8,128)S(1)}, u32[]{:S(2)}, u32[]{:S(2)}) collective-permute-start(f32[2,32,2048]{2,1,0:T(8,128)S(1)} %pad_maximum_fusion.2.near), channel_id=1, source_target_pairs={{0,4},{4,0},{8,12},{12,8},{16,20},{20,16},{24,28},{28,24},{32,36},... | collective-permute-start | bytes 1572872 | tf_op jit(solution)/shard_map/ppermute | solution.py:48
  188.0 4.6 %shard_map.100 = (f32[896,128]{1,0:T(8,128)}, f32[172,128]{1,0:T(8,128)}) custom-call(s32[5]{0:T(128)S(1)} %copy-done.11, s32[1,21]{1,0:T(1,128)S(1)} %copy-done.12, f32[896,128]{1,0:T(8,128)S(1)} %copy-done.6, f32[2,32,2048]{2,1,0:T(8,128)S(1)} %pad_maximum_fusion.2.near, f32[2,32,2048]{2,1,0:T(8,128)S(1)} %collective-permute-done.19.across_core, ...), custom_call_target="tpu_custom_call" | custom-call | tf_op jit(solution)/shard_map/pallas_call | solution.py:229
  (73 shorter events, 18.8 us)
Async XLA Ops:
  8.1 17.1 %collective-permute-start = (f32[2,128,128]{2,1,0:T(8,128)S(1)}, f32[2,128,128]{2,1,0:T(8,128)S(1)}, u32[]{:S(2)}, u32[]{:S(2)}) collective-permute-start(f32[2,128,128]{2,1,0:T(8,128)S(1)} %pad_maximum_fusion.6), channel_id=1, source_target_pairs={{0,8},{4,12},{8,0},{12,4},{16,24},{20,28},{24,16},{28,20},{32,40},... | collective-permute-start | bytes 393224 | tf_op jit(solution)/shard_map/ppermute | solution.py:48
  13.1 12.0 %collective-permute-start.1 = (f32[1,4,128]{2,1,0:T(4,128)S(1)}, f32[1,4,128]{2,1,0:T(4,128)S(1)}, u32[]{:S(2)}, u32[]{:S(2)}) collective-permute-start(f32[1,4,128]{2,1,0:T(4,128)S(1)} %slice_bitcast_fusion.2), channel_id=1, source_target_pairs={{0,384},{4,388},{8,392},{12,396},{16,400},{20,404},{24,408},{28,41... | collective-permute-start | bytes 6152 | tf_op jit(solution)/shard_map/ppermute | solution.py:48
  25.2 28.6 %all-to-all-start = ((f32[4,32,2048]{2,1,0:T(8,128)}), f32[4,32,2048]{2,1,0:T(8,128)S(1)}, u32[]{:S(2)}, u32[]{:S(2)}) async-start(f32[4,32,2048]{2,1,0:T(8,128)} %bitcast.26), calls=%async_computation | async-start | bytes 2097152 | tf_op jit(solution)/shard_map/all_to_all | solution.py:288
  30.4 27.3 %copy-start.13 = (f32[2,32,128]{2,1,0:T(8,128)S(1)}, f32[2,32,128]{2,1,0:T(8,128)}, u32[]{:S(2)}) copy-start(f32[2,32,128]{2,1,0:T(8,128)} %get-tuple-element.38) | copy-start | bytes 98308
  30.4 120.8 %all-gather.3.cloned.1.call-start = ((), (), s32[]{:S(2)}) async-start(), calls=%async_computation.2 | async-start | bytes 1966080 | tf_op jit(solution)/shard_map/all_gather | solution.py:306
  30.4 11.0 %collective-permute-start.5 = (f32[3,8,128]{2,1,0:T(8,128)S(1)}, f32[3,8,128]{2,1,0:T(8,128)S(1)}, u32[]{:S(2)}, u32[]{:S(2)}) collective-permute-start(f32[3,8,128]{2,1,0:T(8,128)S(1)} %constant_dynamic-update-slice_fusion), channel_id=1, source_target_pairs={{0,128},{4,132},{8,136},{12,140},{16,144},{20,148},{24,152},{28,15... | collective-permute-start | bytes 36872 | tf_op jit(solution)/shard_map/ppermute | solution.py:48
  32.3 21.3 %collective-permute-start.4 = (f32[2,256,128]{2,1,0:T(8,128)S(1)}, f32[2,256,128]{2,1,0:T(8,128)S(1)}, u32[]{:S(2)}, u32[]{:S(2)}) collective-permute-start(f32[2,256,128]{2,1,0:T(8,128)S(1)} %pad_maximum_fusion.4), channel_id=1, source_target_pairs={{0,3},{1,2},{2,1},{3,0},{4,7},{5,6},{6,5},{7,4},{8,11},{9,10},{10,... | collective-permute-start | bytes 786440 | tf_op jit(solution)/shard_map/ppermute | solution.py:48
  36.3 17.4 %collective-permute-start.3 = (f32[2,256,128]{2,1,0:T(8,128)S(1)}, f32[2,256,128]{2,1,0:T(8,128)S(1)}, u32[]{:S(2)}, u32[]{:S(2)}) collective-permute-start(f32[2,256,128]{2,1,0:T(8,128)S(1)} %pad_maximum_fusion.4), channel_id=1, source_target_pairs={{0,2},{1,3},{2,0},{3,1},{4,6},{5,7},{6,4},{7,5},{8,10},{9,11},{10,... | collective-permute-start | bytes 786440 | tf_op jit(solution)/shard_map/ppermute | solution.py:48
  38.7 15.0 %collective-permute-start.2 = (f32[2,256,128]{2,1,0:T(8,128)S(1)}, f32[2,256,128]{2,1,0:T(8,128)S(1)}, u32[]{:S(2)}, u32[]{:S(2)}) collective-permute-start(f32[2,256,128]{2,1,0:T(8,128)S(1)} %pad_maximum_fusion.4), channel_id=1, source_target_pairs={{0,1},{1,0},{2,3},{3,2},{4,5},{5,4},{6,7},{7,6},{8,9},{9,8},{10,11... | collective-permute-start | bytes 786440 | tf_op jit(solution)/shard_map/ppermute | solution.py:48
  41.4 12.3 %collective-permute-start.6 = (f32[3,16,128]{2,1,0:T(8,128)S(1)}, f32[3,16,128]{2,1,0:T(8,128)S(1)}, u32[]{:S(2)}, u32[]{:S(2)}) collective-permute-start(f32[3,16,128]{2,1,0:T(8,128)S(1)} %pad_maximum_fusion.8), channel_id=1, source_target_pairs={{0,96},{4,100},{8,104},{12,108},{16,112},{20,116},{24,120},{28,124... | collective-permute-start | bytes 73736 | tf_op jit(solution)/shard_map/ppermute | solution.py:48
  53.8 9.2 %collective-permute-start.7 = (f32[4,2,256,128]{3,2,1,0:T(8,128)S(1)}, f32[4,2,256,128]{3,2,1,0:T(8,128)S(1)}, u32[]{:S(2)}, u32[]{:S(2)}) collective-permute-start(f32[4,2,256,128]{3,2,1,0:T(8,128)S(1)} %pad_maximum_fusion.refs_1_.m1), channel_id=1, source_target_pairs={{0,4},{4,0},{8,12},{12,8},{16,20},{20,16},{24,28},{28,24},{32,36},... | collective-permute-start | bytes 3145736 | tf_op jit(solution)/shard_map/ppermute | solution.py:48
  57.7 13.7 %collective-permute-start.9 = (f32[5,32,128]{2,1,0:T(8,128)S(1)}, f32[5,32,128]{2,1,0:T(8,128)S(1)}, u32[]{:S(2)}, u32[]{:S(2)}) collective-permute-start(f32[5,32,128]{2,1,0:T(8,128)S(1)} %constant_dynamic-update-slice_fusion.2), channel_id=1, source_target_pairs={{0,32},{4,36},{8,40},{12,44},{16,48},{20,52},{24,56},{28,60},{32,0... | collective-permute-start | bytes 245768 | tf_op jit(solution)/shard_map/ppermute | solution.py:48
  64.0 29.5 %copy-start.7 = (f32[32,512]{1,0:T(8,128)}, f32[32,512]{1,0:T(8,128)S(1)}, u32[]{:S(2)}) copy-start(f32[32,512]{1,0:T(8,128)S(1)} %get-tuple-element.51.z1) | copy-start | bytes 196612
  64.0 16.1 %collective-permute-start.8 = (f32[32,1536]{1,0:T(8,128)S(1)}, f32[32,1536]{1,0:T(8,128)S(1)}, u32[]{:S(2)}, u32[]{:S(2)}) collective-permute-start(f32[32,1536]{1,0:T(8,128)S(1)} %get-tuple-element.40), channel_id=1, source_target_pairs={{0,16},{4,20},{8,24},{12,28},{16,0},{20,4},{24,8},{28,12},{32,48},... | collective-permute-start | bytes 589832 | tf_op jit(solution)/shard_map/ppermute | solution.py:48
  80.1 11.4 %collective-permute-start.10 = (f32[5,64,128]{2,1,0:T(8,128)S(1)}, f32[5,64,128]{2,1,0:T(8,128)S(1)}, u32[]{:S(2)}, u32[]{:S(2)}) collective-permute-start(f32[5,64,128]{2,1,0:T(8,128)S(1)} %pad_maximum_fusion.5), channel_id=1, source_target_pairs={{0,16},{4,20},{8,24},{12,28},{16,0},{20,4},{24,8},{28,12},{32,48},... | collective-permute-start | bytes 491528 | tf_op jit(solution)/shard_map/ppermute | solution.py:48
  91.6 10.7 %collective-permute-start.11 = (f32[5,128,128]{2,1,0:T(8,128)S(1)}, f32[5,128,128]{2,1,0:T(8,128)S(1)}, u32[]{:S(2)}, u32[]{:S(2)}) collective-permute-start(f32[5,128,128]{2,1,0:T(8,128)S(1)} %pad_maximum_fusion.3), channel_id=1, source_target_pairs={{0,8},{4,12},{8,0},{12,4},{16,24},{20,28},{24,16},{28,20},{32,40},... | collective-permute-start | bytes 983048 | tf_op jit(solution)/shard_map/ppermute | solution.py:48
  104.2 29.2 %all-to-all-start.1 = ((f32[4,2,256,128]{3,2,1,0:T(8,128)}), f32[4,2,256,128]{3,2,1,0:T(8,128)S(1)}, u32[]{:S(2)}, u32[]{:S(2)}) async-start(f32[4,2,256,128]{3,2,1,0:T(8,128)} %broadcast_in_dim.14), calls=%async_computation.1 | async-start | bytes 2097152 | tf_op jit(solution)/shard_map/all_to_all | solution.py:256
  108.2 25.2 %collective-permute-start.12 = (f32[32,1536]{1,0:T(8,128)S(1)}, f32[32,1536]{1,0:T(8,128)S(1)}, u32[]{:S(2)}, u32[]{:S(2)}) collective-permute-start(f32[32,1536]{1,0:T(8,128)S(1)} %add.24.refs_0_), channel_id=1, source_target_pairs={{0,32},{4,36},{8,40},{12,44},{16,48},{20,52},{24,56},{28,60},{32,0... | collective-permute-start | bytes 589832 | tf_op jit(solution)/shard_map/ppermute | solution.py:48
  133.4 4.7 %collective-permute-start.13 = (f32[4,2,256,128]{3,2,1,0:T(8,128)S(1)}, f32[4,2,256,128]{3,2,1,0:T(8,128)S(1)}, u32[]{:S(2)}, u32[]{:S(2)}) collective-permute-start(f32[4,2,256,128]{3,2,1,0:T(8,128)S(1)} %all-to-all-done.1.refs_2_.m2), channel_id=1, source_target_pairs={{0,4},{4,0},{8,12},{12,8},{16,20},{20,16},{24,28},{28,24},{32,36},... | collective-permute-start | bytes 3145736 | tf_op jit(solution)/shard_map/ppermute | solution.py:48
  140.6 10.5 %collective-permute-start.14 = (f32[32,1024]{1,0:T(8,128)S(1)}, f32[32,1024]{1,0:T(8,128)S(1)}, u32[]{:S(2)}, u32[]{:S(2)}) collective-permute-start(f32[32,1024]{1,0:T(8,128)S(1)} %get-tuple-element.47), channel_id=1, source_target_pairs={{0,96},{4,100},{8,104},{12,108},{16,112},{20,116},{24,120},{28,124... | collective-permute-start | bytes 393224 | tf_op jit(solution)/shard_map/ppermute | solution.py:48
  151.1 19.0 %copy-start.8 = (f32[32,512]{1,0:T(8,128)S(1)}, f32[32,512]{1,0:T(8,128)}, u32[]{:S(2)}) copy-start(f32[32,512]{1,0:T(8,128)} %copy-done.7) | copy-start | bytes 196612
  151.1 19.0 %copy-start.10 = (f32[32,512]{1,0:T(8,128)S(1)}, f32[32,512]{1,0:T(8,128)}, u32[]{:S(2)}) copy-start(f32[32,512]{1,0:T(8,128)} %copy-done.9) | copy-start | bytes 196612
  151.2 10.3 %collective-permute-start.16 = (f32[4,3,256,128]{3,2,1,0:T(8,128)}, f32[4,3,256,128]{3,2,1,0:T(8,128)S(1)}, u32[]{:S(2)}, u32[]{:S(2)}) collective-permute-start(f32[4,3,256,128]{3,2,1,0:T(8,128)} %bitcast.21), channel_id=1, source_target_pairs={{0,4},{4,0},{8,12},{12,8},{16,20},{20,16},{24,28},{28,24},{32,36},... | collective-permute-start | bytes 4718600 | tf_op jit(solution)/shard_map/ppermute | solution.py:48
  154.4 7.1 %collective-permute-start.15 = (f32[32,1024]{1,0:T(8,128)S(1)}, f32[32,1024]{1,0:T(8,128)S(1)}, u32[]{:S(2)}, u32[]{:S(2)}) collective-permute-start(f32[32,1024]{1,0:T(8,128)S(1)} %add.25.refs_0_), channel_id=1, source_target_pairs={{0,128},{4,132},{8,136},{12,140},{16,144},{20,148},{24,152},{28,15... | collective-permute-start | bytes 393224 | tf_op jit(solution)/shard_map/ppermute | solution.py:48
  163.9 6.2 %collective-permute-start.17 = (f32[32,512]{1,0:T(8,128)S(1)}, f32[32,512]{1,0:T(8,128)S(1)}, u32[]{:S(2)}, u32[]{:S(2)}) collective-permute-start(f32[32,512]{1,0:T(8,128)S(1)} %get-tuple-element.50.right), channel_id=1, source_target_pairs={{0,384},{4,388},{8,392},{12,396},{16,400},{20,404},{24,408},{28,41... | collective-permute-start | bytes 196616 | tf_op jit(solution)/shard_map/ppermute | solution.py:48
  170.1 17.8 %copy-start.1 = (f32[21,128,128]{2,1,0:T(8,128)S(1)}, f32[21,128,128]{2,1,0:T(8,128)}, u32[]{:S(2)}) copy-start(f32[21,128,128]{2,1,0:T(8,128)} %blocks.1) | copy-start | bytes 4128772
  170.1 17.8 %copy-start.5 = (f32[7,128,128]{2,1,0:T(8,128)S(1)}, f32[7,128,128]{2,1,0:T(8,128)}, u32[]{:S(2)}) copy-start(f32[7,128,128]{2,1,0:T(8,128)} %inverse.1) | copy-start | bytes 1376260
  170.1 17.8 %copy-start.6 = (f32[896,128]{1,0:T(8,128)S(1)}, f32[896,128]{1,0:T(8,128)}, u32[]{:S(2)}) copy-start(f32[896,128]{1,0:T(8,128)} %get-tuple-element.28.y) | copy-start | bytes 1376260
  170.1 17.8 %copy-start.11 = (s32[5]{0:T(128)S(1)}, s32[5]{0:T(128)}, u32[]{:S(2)}) copy-start(s32[5]{0:T(128)} %stack.56.where) | copy-start | bytes 64
  170.2 17.8 %copy-start.12 = (s32[1,21]{1,0:T(1,128)S(1)}, s32[1,21]{1,0:T(1,128)}, u32[]{:S(2)}) copy-start(s32[1,21]{1,0:T(1,128)} %pattern.3) | copy-start | bytes 256
  173.7 7.9 %collective-permute-start.18 = (f32[32,2048]{1,0:T(8,128)S(1)}, f32[32,2048]{1,0:T(8,128)S(1)}, u32[]{:S(2)}, u32[]{:S(2)}) collective-permute-start(f32[32,2048]{1,0:T(8,128)S(1)} %shard_map.99), channel_id=1, source_target_pairs={{0,8},{4,12},{8,0},{12,4},{16,24},{20,28},{24,16},{28,20},{32,40},... | collective-permute-start | bytes 786440 | tf_op jit(solution)/shard_map/ppermute | solution.py:48
  181.7 6.3 %collective-permute-start.19 = (f32[2,32,2048]{2,1,0:T(8,128)S(1)}, f32[2,32,2048]{2,1,0:T(8,128)S(1)}, u32[]{:S(2)}, u32[]{:S(2)}) collective-permute-start(f32[2,32,2048]{2,1,0:T(8,128)S(1)} %pad_maximum_fusion.2.near), channel_id=1, source_target_pairs={{0,4},{4,0},{8,12},{12,8},{16,20},{20,16},{24,28},{28,24},{32,36},... | collective-permute-start | bytes 1572872 | tf_op jit(solution)/shard_map/ppermute | solution.py:48
  (6 other events, 29.7 us)
Sparse Core Ops, SparseCore 0:
  103.2 33.5 all-gather.2

commit v16 on v15

--- a/solution.py
+++ b/solution.py
@@ -268,7 +268,8 @@
         return call(functools.partial(level_kernel, index, turned), outs, plane, *arrays)
 
     first = grow(both(0), 1 << Z1)
-    far = grow(rows(sep_inverse, 3)[None], wrap_y)
+    own = jnp.concatenate([rows(sep_inverse, 2), rows(sep_coupling, 2), rows(sep_inverse, 3)], 0)
+    far = (own, across(own, wrap_z))
     y, t, second, third = pl.pallas_call(
         functools.partial(forward_kernel, sizes),
         out_shape=[
@@ -287,8 +288,9 @@
 
     t = lax.all_to_all(t, "leaf", 0, 0, axis_index_groups=near, tiled=True)
     first = turned_planes(first)
-    far = grow(jnp.concatenate([far, third], 0), 1 << Y1)
-    far = grow(far, wrap_z)
+    top = jnp.concatenate([part[2 * sizes[2] :] for part in far], 0)[None]
+    third = jnp.stack([part[: 2 * sizes[2]].reshape(2, sizes[2], 128) for part in far], 1).reshape(2, -1, 128)
+    far = grow(jnp.concatenate([grow(top, wrap_y), third], 0), 1 << Y1)
     t, first, far = tie((t, first, far))
 
     first = (first, across(first, CORE_MASK))

time: 200 us -> 204 us (1.020)
  waiting for transfers between devices: 79.8 us -> 81.9 us
    ppermute x20, waiting for transfers between devices: 79.7 us -> 81.9 us  [swap(): lax.ppermute(value, axis, [(i, i ^ mask) for i in range(lax.axis_size(axi...]
    slice x0 -> x5, local copies, waits for them, and re-layouts: none -> 2.07 us  [the longest x3 2.07 us: rows(): return array[offsets[level]:offsets[level] + sizes[level]]]
  transfers between devices with their start and end apart: 23 -> 23, of which waited for: 12 -> 13; matrix products, arithmetic and copies ran while one was open for 1% -> 2% of each run, Pallas kernels for 4% -> 4%
where the time goes in v16:
time: 204 us; the launch traced here: 203 us
  waiting for transfers between devices  81.9 us (40%)
  starting transfers between devices  79.8 us (39%)
  Pallas kernels  17.7 us (9%)
  between operations  14.6 us (7%)
  local copies, waits for them, and re-layouts  8.54 us (4%)
    ppermute x20, waiting for transfers between devices, swap(): lax.ppermute(value, axis, [(i, i ^ mask) for i in range(lax.axis_size(axi...  81.9 us
    ppermute x20, starting transfers between devices, swap(): lax.ppermute(value, axis, [(i, i ^ mask) for i in range(lax.axis_size(axi...  71 us
    pallas_call x5, Pallas kernels, call(): pl.pallas_call(kernel, out_shape=[jax.ShapeDtypeStruct(s, F32) for s in o...  11 us
    pallas_call x1, Pallas kernels, shards(): pl.pallas_call(functools.partial(forward_kernel, sizes), out_shape=[jax.S...  6.67 us
    all_to_all x1, starting transfers between devices, shards(): t = lax.all_to_all(t, 'leaf', 0, 0, axis_index_groups=near, tiled=True)  4.73 us
  transfers between devices with their start and end apart: 23, of which 13 were waited for; matrix products, arithmetic and copies ran while one was open for 2% of the time, Pallas kernels for 4%

profile of v16, /device:TPU:1, one launch (start us, length us, event | category | flops | bytes accessed | tf_op | source)
XLA Modules:
  0.0 202.8 jit_solution(3869595742936220105)
XLA Ops:
  8.1 4.4 %collective-permute-start = (f32[2,128,128]{2,1,0:T(8,128)S(1)}, f32[2,128,128]{2,1,0:T(8,128)S(1)}, u32[]{:S(2)}, u32[]{:S(2)}) collective-permute-start(f32[2,128,128]{2,1,0:T(8,128)S(1)} %pad_maximum_fusion.6), channel_id=1, source_target_pairs={{0,8},{4,12},{8,0},{12,4},{16,24},{20,28},{24,16},{28,20},{32,40},... | collective-permute-start | bytes 393224 | tf_op jit(solution)/shard_map/ppermute | solution.py:48
  14.5 11.5 %collective-permute-start.1 = (f32[20,128]{1,0:T(8,128)S(1)}, f32[20,128]{1,0:T(8,128)S(1)}, u32[]{:S(2)}, u32[]{:S(2)}) collective-permute-start(f32[20,128]{1,0:T(8,128)S(1)} %pad_maximum_fusion.9), channel_id=1, source_target_pairs={{0,96},{4,100},{8,104},{12,108},{16,112},{20,116},{24,120},{28,124... | collective-permute-start | bytes 30728 | tf_op jit(solution)/shard_map/ppermute | solution.py:48
  26.8 6.7 %shard_map.95 = (f32[896,128]{1,0:T(8,128)}, f32[128,2048]{1,0:T(8,128)}, f32[2,32,128]{2,1,0:T(8,128)}, f32[2,8,128]{2,1,0:T(8,128)}) custom-call(s32[5]{0:T(128)} %stack.59.where, s32[1,21]{1,0:T(1,128)} %pattern.3, f32[896,128]{1,0:T(8,128)} %rhs_far.1, f32[7,128,128]{2,1,0:T(8,128)} %inverse.1, f32[21,128,128]{2,1,0:T(8,128)} %blocks.1, ...), custom_call_target="tpu_custom_call" | custom-call | tf_op jit(solution)/shard_map/pallas_call | solution.py:273
  33.5 4.7 %all-to-all-start = ((f32[4,32,2048]{2,1,0:T(8,128)}), f32[4,32,2048]{2,1,0:T(8,128)S(1)}, u32[]{:S(2)}, u32[]{:S(2)}) async-start(f32[4,32,2048]{2,1,0:T(8,128)} %bitcast.36), calls=%async_computation | async-start | bytes 2097152 | tf_op jit(solution)/shard_map/all_to_all | solution.py:289
  38.3 4.5 %collective-permute-start.4 = (f32[2,256,128]{2,1,0:T(8,128)S(1)}, f32[2,256,128]{2,1,0:T(8,128)S(1)}, u32[]{:S(2)}, u32[]{:S(2)}) collective-permute-start(f32[2,256,128]{2,1,0:T(8,128)S(1)} %pad_maximum_fusion.4), channel_id=1, source_target_pairs={{0,3},{1,2},{2,1},{3,0},{4,7},{5,6},{6,5},{7,4},{8,11},{9,10},{10,... | collective-permute-start | bytes 786440 | tf_op jit(solution)/shard_map/ppermute | solution.py:48
  42.8 2.4 %collective-permute-start.3 = (f32[2,256,128]{2,1,0:T(8,128)S(1)}, f32[2,256,128]{2,1,0:T(8,128)S(1)}, u32[]{:S(2)}, u32[]{:S(2)}) collective-permute-start(f32[2,256,128]{2,1,0:T(8,128)S(1)} %pad_maximum_fusion.4), channel_id=1, source_target_pairs={{0,2},{1,3},{2,0},{3,1},{4,6},{5,7},{6,4},{7,5},{8,10},{9,11},{10,... | collective-permute-start | bytes 786440 | tf_op jit(solution)/shard_map/ppermute | solution.py:48
  45.2 2.2 %collective-permute-start.2 = (f32[2,256,128]{2,1,0:T(8,128)S(1)}, f32[2,256,128]{2,1,0:T(8,128)S(1)}, u32[]{:S(2)}, u32[]{:S(2)}) collective-permute-start(f32[2,256,128]{2,1,0:T(8,128)S(1)} %pad_maximum_fusion.4), channel_id=1, source_target_pairs={{0,1},{1,0},{2,3},{3,2},{4,5},{5,4},{6,7},{7,6},{8,9},{9,8},{10,11... | collective-permute-start | bytes 786440 | tf_op jit(solution)/shard_map/ppermute | solution.py:48
  47.4 4.6 %collective-permute-start.5 = (f32[1,8,128]{2,1,0:T(8,128)S(1)}, f32[1,8,128]{2,1,0:T(8,128)S(1)}, u32[]{:S(2)}, u32[]{:S(2)}) collective-permute-start(f32[1,8,128]{2,1,0:T(8,128)S(1)} %maximum_bitcast_fusion.1), channel_id=1, source_target_pairs={{0,384},{4,388},{8,392},{12,396},{16,400},{20,404},{24,408},{28,41... | collective-permute-start | bytes 12296 | tf_op jit(solution)/shard_map/ppermute | solution.py:48
  53.4 1.9 collective-permute-start.6
  55.3 2.7 %collective-permute-done.6 = f32[3,16,128]{2,1,0:T(8,128)S(1)} collective-permute-done((f32[3,16,128]{2,1,0:T(8,128)S(1)}, f32[3,16,128]{2,1,0:T(8,128)S(1)}, u32[]{:S(2)}, u32[]{:S(2)}) %collective-permute-start.6) | collective-permute-done | bytes 24608 | tf_op jit(solution)/shard_map/ppermute | solution.py:48
  58.1 4.6 %collective-permute-start.7 = (f32[4,2,256,128]{3,2,1,0:T(8,128)S(1)}, f32[4,2,256,128]{3,2,1,0:T(8,128)S(1)}, u32[]{:S(2)}, u32[]{:S(2)}) collective-permute-start(f32[4,2,256,128]{3,2,1,0:T(8,128)S(1)} %pad_maximum_fusion.refs_1_.m1), channel_id=1, source_target_pairs={{0,4},{4,0},{8,12},{12,8},{16,20},{20,16},{24,28},{28,24},{32,36},... | collective-permute-start | bytes 3145736 | tf_op jit(solution)/shard_map/ppermute | solution.py:48
  62.7 5.2 %collective-permute-start.9 = (f32[5,32,128]{2,1,0:T(8,128)S(1)}, f32[5,32,128]{2,1,0:T(8,128)S(1)}, u32[]{:S(2)}, u32[]{:S(2)}) collective-permute-start(f32[5,32,128]{2,1,0:T(8,128)S(1)} %constant_dynamic-update-slice_fusion), channel_id=1, source_target_pairs={{0,32},{4,36},{8,40},{12,44},{16,48},{20,52},{24,56},{28,60},{32,0... | collective-permute-start | bytes 245768 | tf_op jit(solution)/shard_map/ppermute | solution.py:48
  68.9 3.1 %collective-permute-start.8 = (f32[32,1536]{1,0:T(8,128)S(1)}, f32[32,1536]{1,0:T(8,128)S(1)}, u32[]{:S(2)}, u32[]{:S(2)}) collective-permute-start(f32[32,1536]{1,0:T(8,128)S(1)} %get-tuple-element.40), channel_id=1, source_target_pairs={{0,16},{4,20},{8,24},{12,28},{16,0},{20,4},{24,8},{28,12},{32,48},... | collective-permute-start | bytes 589832 | tf_op jit(solution)/shard_map/ppermute | solution.py:48
  72.0 4.6 %collective-permute-done.9 = f32[5,32,128]{2,1,0:T(8,128)S(1)} collective-permute-done((f32[5,32,128]{2,1,0:T(8,128)S(1)}, f32[5,32,128]{2,1,0:T(8,128)S(1)}, u32[]{:S(2)}, u32[]{:S(2)}) %collective-permute-start.9) | collective-permute-done | bytes 81952 | tf_op jit(solution)/shard_map/ppermute | solution.py:48
  76.7 7.9 %collective-permute-done.8 = f32[32,1536]{1,0:T(8,128)S(1)} collective-permute-done((f32[32,1536]{1,0:T(8,128)S(1)}, f32[32,1536]{1,0:T(8,128)S(1)}, u32[]{:S(2)}, u32[]{:S(2)}) %collective-permute-start.8) | collective-permute-done | bytes 196640 | tf_op jit(solution)/shard_map/ppermute | solution.py:48
  86.5 8.5 %collective-permute-done.10 = f32[5,64,128]{2,1,0:T(8,128)S(1)} collective-permute-done((f32[5,64,128]{2,1,0:T(8,128)S(1)}, f32[5,64,128]{2,1,0:T(8,128)S(1)}, u32[]{:S(2)}, u32[]{:S(2)}) %collective-permute-start.10) | collective-permute-done | bytes 163872 | tf_op jit(solution)/shard_map/ppermute | solution.py:48
  95.0 1.9 collective-permute-start.11
  96.9 8.7 %collective-permute-done.11 = f32[5,128,128]{2,1,0:T(8,128)S(1)} collective-permute-done((f32[5,128,128]{2,1,0:T(8,128)S(1)}, f32[5,128,128]{2,1,0:T(8,128)S(1)}, u32[]{:S(2)}, u32[]{:S(2)}) %collective-permute-start.11) | collective-permute-done | bytes 327712 | tf_op jit(solution)/shard_map/ppermute | solution.py:48
  107.6 4.0 %all-to-all-start.1 = ((f32[4,2,256,128]{3,2,1,0:T(8,128)}), f32[4,2,256,128]{3,2,1,0:T(8,128)S(1)}, u32[]{:S(2)}, u32[]{:S(2)}) async-start(f32[4,2,256,128]{3,2,1,0:T(8,128)} %broadcast_in_dim.14), calls=%async_computation.1 | async-start | bytes 2097152 | tf_op jit(solution)/shard_map/all_to_all | solution.py:256
  113.5 23.3 %collective-permute-done.12.refs_1_ = f32[32,1536]{1,0:T(8,128)S(1)} collective-permute-done((f32[32,1536]{1,0:T(8,128)S(1)}, f32[32,1536]{1,0:T(8,128)S(1)}, u32[]{:S(2)}, u32[]{:S(2)}) %collective-permute-start.12) | collective-permute-done | bytes 196640 | tf_op jit(solution)/shard_map/ppermute | solution.py:48
  136.8 2.4 %collective-permute-start.13 = (f32[4,2,256,128]{3,2,1,0:T(8,128)S(1)}, f32[4,2,256,128]{3,2,1,0:T(8,128)S(1)}, u32[]{:S(2)}, u32[]{:S(2)}) collective-permute-start(f32[4,2,256,128]{3,2,1,0:T(8,128)S(1)} %all-to-all-done.1.refs_2_.m2), channel_id=1, source_target_pairs={{0,4},{4,0},{8,12},{12,8},{16,20},{20,16},{24,28},{28,24},{32,36},... | collective-permute-start | bytes 3145736 | tf_op jit(solution)/shard_map/ppermute | solution.py:48
  139.2 2.3 %collective-permute-done.13.refs_3_.o2 = f32[4,2,256,128]{3,2,1,0:T(8,128)S(1)} collective-permute-done((f32[4,2,256,128]{3,2,1,0:T(8,128)S(1)}, f32[4,2,256,128]{3,2,1,0:T(8,128)S(1)}, u32[]{:S(2)}, u32[]{:S(2)}) %collective-permute-start.13) | collective-permute-done | bytes 1048608 | tf_op jit(solution)/shard_map/ppermute | solution.py:48
  146.0 8.6 %collective-permute-done.14 = f32[32,1024]{1,0:T(8,128)S(1)} collective-permute-done((f32[32,1024]{1,0:T(8,128)S(1)}, f32[32,1024]{1,0:T(8,128)S(1)}, u32[]{:S(2)}, u32[]{:S(2)}) %collective-permute-start.14) | collective-permute-done | bytes 131104 | tf_op jit(solution)/shard_map/ppermute | solution.py:48
  154.6 3.2 %collective-permute-start.16 = (f32[4,3,256,128]{3,2,1,0:T(8,128)}, f32[4,3,256,128]{3,2,1,0:T(8,128)S(1)}, u32[]{:S(2)}, u32[]{:S(2)}) collective-permute-start(f32[4,3,256,128]{3,2,1,0:T(8,128)} %bitcast.31), channel_id=1, source_target_pairs={{0,4},{4,0},{8,12},{12,8},{16,20},{20,16},{24,28},{28,24},{32,36},... | collective-permute-start | bytes 4718600 | tf_op jit(solution)/shard_map/ppermute | solution.py:48
  157.8 1.9 collective-permute-start.15
  159.7 5.1 %collective-permute-done.15.refs_1_ = f32[32,1024]{1,0:T(8,128)S(1)} collective-permute-done((f32[32,1024]{1,0:T(8,128)S(1)}, f32[32,1024]{1,0:T(8,128)S(1)}, u32[]{:S(2)}, u32[]{:S(2)}) %collective-permute-start.15) | collective-permute-done | bytes 131104 | tf_op jit(solution)/shard_map/ppermute | solution.py:48
  167.2 4.5 %collective-permute-start.17 = (f32[32,512]{1,0:T(8,128)S(1)}, f32[32,512]{1,0:T(8,128)S(1)}, u32[]{:S(2)}, u32[]{:S(2)}) collective-permute-start(f32[32,512]{1,0:T(8,128)S(1)} %get-tuple-element.50.right), channel_id=1, source_target_pairs={{0,384},{4,388},{8,392},{12,396},{16,400},{20,404},{24,408},{28,41... | collective-permute-start | bytes 196616 | tf_op jit(solution)/shard_map/ppermute | solution.py:48
  173.5 3.5 %shard_map.99 = f32[32,2048]{1,0:T(8,128)S(1)} custom-call(s32[1]{0:T(128)} %bitcast.5.plane, f32[32,512]{1,0:T(8,128)S(1)} %get-tuple-element.50.right, f32[32,512]{1,0:T(8,128)S(1)} %collective-permute-done.17.right_far, f32[32,512]{1,0:T(8,128)S(1)} %copy-done.8, f32[32,512]{1,0:T(8,128)S(1)} %copy-done.10, f32[32,512]{1,0:T(8,128)S(1)} %get-tuple-element.53.z3, ...), custom_call_target="tpu_custom_call" | custom-call | tf_op jit(solution)/shard_map/pallas_call | solution.py:229
  177.0 2.1 %collective-permute-start.18 = (f32[32,2048]{1,0:T(8,128)S(1)}, f32[32,2048]{1,0:T(8,128)S(1)}, u32[]{:S(2)}, u32[]{:S(2)}) collective-permute-start(f32[32,2048]{1,0:T(8,128)S(1)} %shard_map.99), channel_id=1, source_target_pairs={{0,8},{4,12},{8,0},{12,4},{16,24},{20,28},{24,16},{28,20},{32,40},... | collective-permute-start | bytes 786440 | tf_op jit(solution)/shard_map/ppermute | solution.py:48
  179.1 5.8 %collective-permute-done.18 = f32[32,2048]{1,0:T(8,128)S(1)} collective-permute-done((f32[32,2048]{1,0:T(8,128)S(1)}, f32[32,2048]{1,0:T(8,128)S(1)}, u32[]{:S(2)}, u32[]{:S(2)}) %collective-permute-start.18) | collective-permute-done | bytes 262176 | tf_op jit(solution)/shard_map/ppermute | solution.py:48
  184.9 4.8 %collective-permute-start.19 = (f32[2,32,2048]{2,1,0:T(8,128)S(1)}, f32[2,32,2048]{2,1,0:T(8,128)S(1)}, u32[]{:S(2)}, u32[]{:S(2)}) collective-permute-start(f32[2,32,2048]{2,1,0:T(8,128)S(1)} %pad_maximum_fusion.2.near), channel_id=1, source_target_pairs={{0,4},{4,0},{8,12},{12,8},{16,20},{20,16},{24,28},{28,24},{32,36},... | collective-permute-start | bytes 1572872 | tf_op jit(solution)/shard_map/ppermute | solution.py:48
  191.3 4.6 %shard_map.100 = (f32[896,128]{1,0:T(8,128)}, f32[172,128]{1,0:T(8,128)}) custom-call(s32[5]{0:T(128)S(1)} %copy-done.11, s32[1,21]{1,0:T(1,128)S(1)} %copy-done.12, f32[896,128]{1,0:T(8,128)S(1)} %copy-done.6, f32[2,32,2048]{2,1,0:T(8,128)S(1)} %pad_maximum_fusion.2.near, f32[2,32,2048]{2,1,0:T(8,128)S(1)} %collective-permute-done.19.across_core, ...), custom_call_target="tpu_custom_call" | custom-call | tf_op jit(solution)/shard_map/pallas_call | solution.py:229
  (77 shorter events, 21.9 us)
Async XLA Ops:
  8.1 25.4 %collective-permute-start = (f32[2,128,128]{2,1,0:T(8,128)S(1)}, f32[2,128,128]{2,1,0:T(8,128)S(1)}, u32[]{:S(2)}, u32[]{:S(2)}) collective-permute-start(f32[2,128,128]{2,1,0:T(8,128)S(1)} %pad_maximum_fusion.6), channel_id=1, source_target_pairs={{0,8},{4,12},{8,0},{12,4},{16,24},{20,28},{24,16},{28,20},{32,40},... | collective-permute-start | bytes 393224 | tf_op jit(solution)/shard_map/ppermute | solution.py:48
  14.5 19.0 %collective-permute-start.1 = (f32[20,128]{1,0:T(8,128)S(1)}, f32[20,128]{1,0:T(8,128)S(1)}, u32[]{:S(2)}, u32[]{:S(2)}) collective-permute-start(f32[20,128]{1,0:T(8,128)S(1)} %pad_maximum_fusion.9), channel_id=1, source_target_pairs={{0,96},{4,100},{8,104},{12,108},{16,112},{20,116},{24,120},{28,124... | collective-permute-start | bytes 30728 | tf_op jit(solution)/shard_map/ppermute | solution.py:48
  33.5 24.6 %all-to-all-start = ((f32[4,32,2048]{2,1,0:T(8,128)}), f32[4,32,2048]{2,1,0:T(8,128)S(1)}, u32[]{:S(2)}, u32[]{:S(2)}) async-start(f32[4,32,2048]{2,1,0:T(8,128)} %bitcast.36), calls=%async_computation | async-start | bytes 2097152 | tf_op jit(solution)/shard_map/all_to_all | solution.py:289
  38.3 24.5 %copy-start.13 = (f32[2,32,128]{2,1,0:T(8,128)S(1)}, f32[2,32,128]{2,1,0:T(8,128)}, u32[]{:S(2)}) copy-start(f32[2,32,128]{2,1,0:T(8,128)} %get-tuple-element.38) | copy-start | bytes 98308
  38.3 116.3 %all-gather.3.cloned.1.call-start = ((), (), s32[]{:S(2)}) async-start(), calls=%async_computation.2 | async-start | bytes 1966080 | tf_op jit(solution)/shard_map/all_gather | solution.py:308
  38.3 19.7 %collective-permute-start.4 = (f32[2,256,128]{2,1,0:T(8,128)S(1)}, f32[2,256,128]{2,1,0:T(8,128)S(1)}, u32[]{:S(2)}, u32[]{:S(2)}) collective-permute-start(f32[2,256,128]{2,1,0:T(8,128)S(1)} %pad_maximum_fusion.4), channel_id=1, source_target_pairs={{0,3},{1,2},{2,1},{3,0},{4,7},{5,6},{6,5},{7,4},{8,11},{9,10},{10,... | collective-permute-start | bytes 786440 | tf_op jit(solution)/shard_map/ppermute | solution.py:48
  42.8 15.2 %collective-permute-start.3 = (f32[2,256,128]{2,1,0:T(8,128)S(1)}, f32[2,256,128]{2,1,0:T(8,128)S(1)}, u32[]{:S(2)}, u32[]{:S(2)}) collective-permute-start(f32[2,256,128]{2,1,0:T(8,128)S(1)} %pad_maximum_fusion.4), channel_id=1, source_target_pairs={{0,2},{1,3},{2,0},{3,1},{4,6},{5,7},{6,4},{7,5},{8,10},{9,11},{10,... | collective-permute-start | bytes 786440 | tf_op jit(solution)/shard_map/ppermute | solution.py:48
  45.2 12.8 %collective-permute-start.2 = (f32[2,256,128]{2,1,0:T(8,128)S(1)}, f32[2,256,128]{2,1,0:T(8,128)S(1)}, u32[]{:S(2)}, u32[]{:S(2)}) collective-permute-start(f32[2,256,128]{2,1,0:T(8,128)S(1)} %pad_maximum_fusion.4), channel_id=1, source_target_pairs={{0,1},{1,0},{2,3},{3,2},{4,5},{5,4},{6,7},{7,6},{8,9},{9,8},{10,11... | collective-permute-start | bytes 786440 | tf_op jit(solution)/shard_map/ppermute | solution.py:48
  47.4 5.9 %collective-permute-start.5 = (f32[1,8,128]{2,1,0:T(8,128)S(1)}, f32[1,8,128]{2,1,0:T(8,128)S(1)}, u32[]{:S(2)}, u32[]{:S(2)}) collective-permute-start(f32[1,8,128]{2,1,0:T(8,128)S(1)} %maximum_bitcast_fusion.1), channel_id=1, source_target_pairs={{0,384},{4,388},{8,392},{12,396},{16,400},{20,404},{24,408},{28,41... | collective-permute-start | bytes 12296 | tf_op jit(solution)/shard_map/ppermute | solution.py:48
  53.4 4.6 %collective-permute-start.6 = (f32[3,16,128]{2,1,0:T(8,128)S(1)}, f32[3,16,128]{2,1,0:T(8,128)S(1)}, u32[]{:S(2)}, u32[]{:S(2)}) collective-permute-start(f32[3,16,128]{2,1,0:T(8,128)S(1)} %pad_maximum_fusion.8), channel_id=1, source_target_pairs={{0,128},{4,132},{8,136},{12,140},{16,144},{20,148},{24,152},{28,15... | collective-permute-start | bytes 73736 | tf_op jit(solution)/shard_map/ppermute | solution.py:48
  58.1 9.8 %collective-permute-start.7 = (f32[4,2,256,128]{3,2,1,0:T(8,128)S(1)}, f32[4,2,256,128]{3,2,1,0:T(8,128)S(1)}, u32[]{:S(2)}, u32[]{:S(2)}) collective-permute-start(f32[4,2,256,128]{3,2,1,0:T(8,128)S(1)} %pad_maximum_fusion.refs_1_.m1), channel_id=1, source_target_pairs={{0,4},{4,0},{8,12},{12,8},{16,20},{20,16},{24,28},{28,24},{32,36},... | collective-permute-start | bytes 3145736 | tf_op jit(solution)/shard_map/ppermute | solution.py:48
  62.7 13.9 %collective-permute-start.9 = (f32[5,32,128]{2,1,0:T(8,128)S(1)}, f32[5,32,128]{2,1,0:T(8,128)S(1)}, u32[]{:S(2)}, u32[]{:S(2)}) collective-permute-start(f32[5,32,128]{2,1,0:T(8,128)S(1)} %constant_dynamic-update-slice_fusion), channel_id=1, source_target_pairs={{0,32},{4,36},{8,40},{12,44},{16,48},{20,52},{24,56},{28,60},{32,0... | collective-permute-start | bytes 245768 | tf_op jit(solution)/shard_map/ppermute | solution.py:48
  68.9 28.0 %copy-start.7 = (f32[32,512]{1,0:T(8,128)}, f32[32,512]{1,0:T(8,128)S(1)}, u32[]{:S(2)}) copy-start(f32[32,512]{1,0:T(8,128)S(1)} %get-tuple-element.51.z1) | copy-start | bytes 196612
  68.9 15.6 %collective-permute-start.8 = (f32[32,1536]{1,0:T(8,128)S(1)}, f32[32,1536]{1,0:T(8,128)S(1)}, u32[]{:S(2)}, u32[]{:S(2)}) collective-permute-start(f32[32,1536]{1,0:T(8,128)S(1)} %get-tuple-element.40), channel_id=1, source_target_pairs={{0,16},{4,20},{8,24},{12,28},{16,0},{20,4},{24,8},{28,12},{32,48},... | collective-permute-start | bytes 589832 | tf_op jit(solution)/shard_map/ppermute | solution.py:48
  84.5 10.4 %collective-permute-start.10 = (f32[5,64,128]{2,1,0:T(8,128)S(1)}, f32[5,64,128]{2,1,0:T(8,128)S(1)}, u32[]{:S(2)}, u32[]{:S(2)}) collective-permute-start(f32[5,64,128]{2,1,0:T(8,128)S(1)} %pad_maximum_fusion.5), channel_id=1, source_target_pairs={{0,16},{4,20},{8,24},{12,28},{16,0},{20,4},{24,8},{28,12},{32,48},... | collective-permute-start | bytes 491528 | tf_op jit(solution)/shard_map/ppermute | solution.py:48
  95.0 10.7 %collective-permute-start.11 = (f32[5,128,128]{2,1,0:T(8,128)S(1)}, f32[5,128,128]{2,1,0:T(8,128)S(1)}, u32[]{:S(2)}, u32[]{:S(2)}) collective-permute-start(f32[5,128,128]{2,1,0:T(8,128)S(1)} %pad_maximum_fusion.3), channel_id=1, source_target_pairs={{0,8},{4,12},{8,0},{12,4},{16,24},{20,28},{24,16},{28,20},{32,40},... | collective-permute-start | bytes 983048 | tf_op jit(solution)/shard_map/ppermute | solution.py:48
  107.6 29.2 %all-to-all-start.1 = ((f32[4,2,256,128]{3,2,1,0:T(8,128)}), f32[4,2,256,128]{3,2,1,0:T(8,128)S(1)}, u32[]{:S(2)}, u32[]{:S(2)}) async-start(f32[4,2,256,128]{3,2,1,0:T(8,128)} %broadcast_in_dim.14), calls=%async_computation.1 | async-start | bytes 2097152 | tf_op jit(solution)/shard_map/all_to_all | solution.py:256
  111.6 25.2 %collective-permute-start.12 = (f32[32,1536]{1,0:T(8,128)S(1)}, f32[32,1536]{1,0:T(8,128)S(1)}, u32[]{:S(2)}, u32[]{:S(2)}) collective-permute-start(f32[32,1536]{1,0:T(8,128)S(1)} %add.24.refs_0_), channel_id=1, source_target_pairs={{0,32},{4,36},{8,40},{12,44},{16,48},{20,52},{24,56},{28,60},{32,0... | collective-permute-start | bytes 589832 | tf_op jit(solution)/shard_map/ppermute | solution.py:48
  136.8 4.7 %collective-permute-start.13 = (f32[4,2,256,128]{3,2,1,0:T(8,128)S(1)}, f32[4,2,256,128]{3,2,1,0:T(8,128)S(1)}, u32[]{:S(2)}, u32[]{:S(2)}) collective-permute-start(f32[4,2,256,128]{3,2,1,0:T(8,128)S(1)} %all-to-all-done.1.refs_2_.m2), channel_id=1, source_target_pairs={{0,4},{4,0},{8,12},{12,8},{16,20},{20,16},{24,28},{28,24},{32,36},... | collective-permute-start | bytes 3145736 | tf_op jit(solution)/shard_map/ppermute | solution.py:48
  144.0 10.5 %collective-permute-start.14 = (f32[32,1024]{1,0:T(8,128)S(1)}, f32[32,1024]{1,0:T(8,128)S(1)}, u32[]{:S(2)}, u32[]{:S(2)}) collective-permute-start(f32[32,1024]{1,0:T(8,128)S(1)} %get-tuple-element.47), channel_id=1, source_target_pairs={{0,96},{4,100},{8,104},{12,108},{16,112},{20,116},{24,120},{28,124... | collective-permute-start | bytes 393224 | tf_op jit(solution)/shard_map/ppermute | solution.py:48
  154.5 18.9 %copy-start.8 = (f32[32,512]{1,0:T(8,128)S(1)}, f32[32,512]{1,0:T(8,128)}, u32[]{:S(2)}) copy-start(f32[32,512]{1,0:T(8,128)} %copy-done.7) | copy-start | bytes 196612
  154.5 18.9 %copy-start.10 = (f32[32,512]{1,0:T(8,128)S(1)}, f32[32,512]{1,0:T(8,128)}, u32[]{:S(2)}) copy-start(f32[32,512]{1,0:T(8,128)} %copy-done.9) | copy-start | bytes 196612
  154.6 10.2 %collective-permute-start.16 = (f32[4,3,256,128]{3,2,1,0:T(8,128)}, f32[4,3,256,128]{3,2,1,0:T(8,128)S(1)}, u32[]{:S(2)}, u32[]{:S(2)}) collective-permute-start(f32[4,3,256,128]{3,2,1,0:T(8,128)} %bitcast.31), channel_id=1, source_target_pairs={{0,4},{4,0},{8,12},{12,8},{16,20},{20,16},{24,28},{28,24},{32,36},... | collective-permute-start | bytes 4718600 | tf_op jit(solution)/shard_map/ppermute | solution.py:48
  157.8 7.0 %collective-permute-start.15 = (f32[32,1024]{1,0:T(8,128)S(1)}, f32[32,1024]{1,0:T(8,128)S(1)}, u32[]{:S(2)}, u32[]{:S(2)}) collective-permute-start(f32[32,1024]{1,0:T(8,128)S(1)} %add.25.refs_0_), channel_id=1, source_target_pairs={{0,128},{4,132},{8,136},{12,140},{16,144},{20,148},{24,152},{28,15... | collective-permute-start | bytes 393224 | tf_op jit(solution)/shard_map/ppermute | solution.py:48
  167.2 6.2 %collective-permute-start.17 = (f32[32,512]{1,0:T(8,128)S(1)}, f32[32,512]{1,0:T(8,128)S(1)}, u32[]{:S(2)}, u32[]{:S(2)}) collective-permute-start(f32[32,512]{1,0:T(8,128)S(1)} %get-tuple-element.50.right), channel_id=1, source_target_pairs={{0,384},{4,388},{8,392},{12,396},{16,400},{20,404},{24,408},{28,41... | collective-permute-start | bytes 196616 | tf_op jit(solution)/shard_map/ppermute | solution.py:48
  173.4 17.8 %copy-start.1 = (f32[21,128,128]{2,1,0:T(8,128)S(1)}, f32[21,128,128]{2,1,0:T(8,128)}, u32[]{:S(2)}) copy-start(f32[21,128,128]{2,1,0:T(8,128)} %blocks.1) | copy-start | bytes 4128772
  173.4 17.8 %copy-start.5 = (f32[7,128,128]{2,1,0:T(8,128)S(1)}, f32[7,128,128]{2,1,0:T(8,128)}, u32[]{:S(2)}) copy-start(f32[7,128,128]{2,1,0:T(8,128)} %inverse.1) | copy-start | bytes 1376260
  173.5 17.8 %copy-start.6 = (f32[896,128]{1,0:T(8,128)S(1)}, f32[896,128]{1,0:T(8,128)}, u32[]{:S(2)}) copy-start(f32[896,128]{1,0:T(8,128)} %get-tuple-element.28.y) | copy-start | bytes 1376260
  173.5 17.8 %copy-start.11 = (s32[5]{0:T(128)S(1)}, s32[5]{0:T(128)}, u32[]{:S(2)}) copy-start(s32[5]{0:T(128)} %stack.59.where) | copy-start | bytes 64
  173.5 17.8 %copy-start.12 = (s32[1,21]{1,0:T(1,128)S(1)}, s32[1,21]{1,0:T(1,128)}, u32[]{:S(2)}) copy-start(s32[1,21]{1,0:T(1,128)} %pattern.3) | copy-start | bytes 256
  177.0 7.9 %collective-permute-start.18 = (f32[32,2048]{1,0:T(8,128)S(1)}, f32[32,2048]{1,0:T(8,128)S(1)}, u32[]{:S(2)}, u32[]{:S(2)}) collective-permute-start(f32[32,2048]{1,0:T(8,128)S(1)} %shard_map.99), channel_id=1, source_target_pairs={{0,8},{4,12},{8,0},{12,4},{16,24},{20,28},{24,16},{28,20},{32,40},... | collective-permute-start | bytes 786440 | tf_op jit(solution)/shard_map/ppermute | solution.py:48
  184.9 6.3 %collective-permute-start.19 = (f32[2,32,2048]{2,1,0:T(8,128)S(1)}, f32[2,32,2048]{2,1,0:T(8,128)S(1)}, u32[]{:S(2)}, u32[]{:S(2)}) collective-permute-start(f32[2,32,2048]{2,1,0:T(8,128)S(1)} %pad_maximum_fusion.2.near), channel_id=1, source_target_pairs={{0,4},{4,0},{8,12},{12,8},{16,20},{20,16},{24,28},{28,24},{32,36},... | collective-permute-start | bytes 1572872 | tf_op jit(solution)/shard_map/ppermute | solution.py:48
  (5 other events, 24.4 us)
Sparse Core Ops, SparseCore 0:
  106.6 33.2 all-gather.2
